TPU v7x, 32 devices: a whole 2x2x4 slice. The times are simulated.
32 devices in a mesh: dp: 2 (over x), rows: 4 (over y, core), cols: 4 (over z).
Axes of the slice: x: 2, y: 2, z: 4, core: 2. Of those that a mesh axis runs over, the one named last changes fastest.
Arguments:
- hidden_in: bfloat16 [4096, 1536], P(('dp', 'rows'), 'cols'), may hold values from -6 to 6
- lengths: int32 [2, 2], P('dp'), may hold values from 128 to 1792, as said below
- norm1_gain: float32 [1536], P('cols'), may hold values from 0.5 to 1.5
- z_weight: bfloat16 [1536, 3072], P('cols', 'rows'), may hold values from -0.15625 to 0.15625
- x_weight: bfloat16 [1536, 3072], P('cols', 'rows'), may hold values from -0.15625 to 0.15625
- bcdt_weight: bfloat16 [1536, 304], P('cols'), may hold values from -0.15625 to 0.15625
- conv_x_weight: float32 [4, 3072], P(None, 'rows'), may hold values from -3 to 3
- conv_x_bias: float32 [3072], P('rows'), may hold values from -3 to 3
- conv_bc_weight: float32 [4, 256], replicated, may hold values from -3 to 3
- conv_bc_bias: float32 [256], replicated, may hold values from -3 to 3
- a_log: float32 [48], P('rows'), may hold values from -1 to 1
- d_skip: float32 [48], P('rows'), may hold values from 0.5 to 1.5
- dt_bias: float32 [48], P('rows'), may hold values from -8 to -2
- gate_gain: float32 [3072], P('rows'), may hold values from 0.5 to 1.5
- mix_out_weight: bfloat16 [3072, 1536], P('rows', 'cols'), may hold values from -0.109375 to 0.109375
- norm2_gain: float32 [1536], P('cols'), may hold values from 0.5 to 1.5
- q_weight: bfloat16 [1536, 1536], P('cols', 'rows'), may hold values from -0.15625 to 0.15625
- k_weight: bfloat16 [1536, 1536], P('cols', 'rows'), may hold values from -0.15625 to 0.15625
- v_weight: bfloat16 [1536, 1536], P('cols', 'rows'), may hold values from -0.15625 to 0.15625
- att_out_weight: bfloat16 [1536, 1536], P('rows', 'cols'), may hold values from -1.25 to 1.25
- norm3_gain: float32 [1536], P('cols'), may hold values from 0.5 to 1.5
- up_weight: bfloat16 [1536, 6144], P('cols', 'rows'), may hold values from -0.15625 to 0.15625
- down_weight: bfloat16 [6144, 1536], P('rows', 'cols'), may hold values from -0.078125 to 0.078125
- grad_output: bfloat16 [4096, 1536], P(('dp', 'rows'), 'cols'), may hold values from -6 to 6
Outputs:
- output: bfloat16 [4096, 1536], P(('dp', 'rows'), 'cols')
- input_grad: float32 [4096, 1536], P(('dp', 'rows'), 'cols')
- norm1_gain_grad: float32 [1536], replicated
- z_weight_grad: float32 [1536, 3072], P('cols', 'rows')
- x_weight_grad: float32 [1536, 3072], P('cols', 'rows')
- bcdt_weight_grad: float32 [1536, 304], replicated
- conv_x_weight_grad: float32 [4, 3072], replicated
- conv_x_bias_grad: float32 [3072], replicated
- conv_bc_weight_grad: float32 [4, 256], replicated
- conv_bc_bias_grad: float32 [256], replicated
- a_log_grad: float32 [48], replicated
- d_skip_grad: float32 [48], replicated
- dt_bias_grad: float32 [48], replicated
- gate_gain_grad: float32 [3072], replicated
- mix_out_weight_grad: float32 [3072, 1536], P('rows', 'cols')
- norm2_gain_grad: float32 [1536], replicated
- q_weight_grad: float32 [1536, 1536], P('cols', 'rows')
- k_weight_grad: float32 [1536, 1536], P('cols', 'rows')
- v_weight_grad: float32 [1536, 1536], P('cols', 'rows')
- att_out_weight_grad: float32 [1536, 1536], P('rows', 'cols')
- norm3_gain_grad: float32 [1536], replicated
- up_weight_grad: float32 [1536, 6144], P('cols', 'rows')
- down_weight_grad: float32 [6144, 1536], P('rows', 'cols')
Inputs may be any that keep to these rules, and one draw needn't show every extreme that they name: `lengths`: row g holds the two packed sequences of group g, in order from place 0, then padding: the first is longer than three quarters of 2048, the two together take at most 2048 places.
All inputs are finite; a program needn't handle non-finite values.
Results may differ from a plain program's by a relative error of at most 0.018.
Values may be sent and summed in bfloat16 or wider, within the bound.
A program may use at most 256 MiB of HBM per device.

v0:
```python
from functools import partial

import jax
import jax.numpy as jnp
from jax import lax
from jax.sharding import PartitionSpec as P

D = 1536
HEADS = 48
HEAD_DIM = 64
STATE = 128
CONV = 4
SPAN = 256
AHEAD_DIM = 64
INNER = 3072


EPS = 1e-05
HIGH = lax.Precision.HIGHEST


def from_behind(value, axis, steps):
    count = lax.axis_size(axis)
    initial, last = (max(0, -steps), min(count, count - steps))
    return lax.ppermute(value, axis, [(source, source + steps) for source in range(initial, last)])


def carried_in(part, axis, combine, identity):
    place = lax.axis_index(axis)
    gathered = jax.tree.map(lambda a: lax.all_gather(a, axis), part)
    state = jax.tree.map(lambda a, e: jnp.zeros_like(a) + jnp.asarray(e, a.dtype), part, identity)

    def one(turn, state):
        return combine(
            state, jax.tree.map(lambda a: lax.dynamic_index_in_dim(a, turn, 0, False), gathered)
        )

    return lax.fori_loop(0, place, one, state)


def prefix(x, axis, combine, identity):
    count, mine = (lax.axis_size(axis), lax.axis_index(axis))
    everything = jax.tree.map(
        lambda part, kind: lax.all_gather(part.astype(kind), axis),
        x,
        jax.tree.map(lambda a: jnp.bfloat16 if a.dtype == jnp.float32 else a.dtype, x),
    )
    start = jax.tree.map(
        lambda part, zero: jnp.broadcast_to(jnp.asarray(zero, part.dtype), part.shape), x, identity
    )

    def turn(k, before):
        at = count - 1 - k
        reached = at > mine
        new = combine(
            before, jax.tree.map(lambda part, own: part[at].astype(own.dtype), everything, x)
        )
        return jax.tree.map(lambda a, b: jnp.where(reached, a, b), new, before)

    return lax.fori_loop(0, count, turn, start)


def rows_gather(shard):
    return lax.all_gather(shard, "rows", axis=0, tiled=True)


def cols_gather(shard):
    return lax.all_gather(shard, "cols", axis=0, tiled=True)


def cols_sum(partial_sum):
    return lax.psum_scatter(partial_sum, "cols", scatter_dimension=0, tiled=True)


def rows_sum(partial_sum):
    return lax.psum_scatter(partial_sum, "rows", scatter_dimension=0, tiled=True)


def grid_total(partial_sum):
    return lax.psum(partial_sum, ("rows", "cols"))


def block_dot(left, right):
    return jnp.dot(left, right, preferred_element_type=jnp.float32)


def dot_trans(left, right):
    return lax.dot_general(
        left, right, (((1,), (1,)), ((), ())), preferred_element_type=jnp.float32
    )


def dot_rows(left, right):
    return lax.dot_general(
        left, right, (((0,), (0,)), ((), ())), preferred_element_type=jnp.float32
    )


def segments_of(places, seq_lens):
    first_part = (places >= seq_lens[0]).astype(jnp.int32)
    second_part = (places >= seq_lens[0] + seq_lens[1]).astype(jnp.int32)
    return jnp.where(places < 0, -1, first_part + second_part)


def place_block(piece, block_idx, full_len, axis_dim):
    full_shape = piece.shape[:axis_dim] + (full_len,) + piece.shape[axis_dim + 1 :]
    return lax.dynamic_update_slice_in_dim(
        jnp.zeros(full_shape, jnp.float32), piece, block_idx * piece.shape[axis_dim], axis_dim
    )


def token_total(partial_sum, block_idx, total_rows):
    length = partial_sum.shape[0]
    spread = place_block(partial_sum, block_idx, total_rows, 0)
    return lax.dynamic_slice_in_dim(grid_total(spread), block_idx * length, length, 0)


def norm_apply(resid, gain, block_idx, total_rows):
    scaling = lax.rsqrt(
        token_total(jnp.sum(resid * resid, axis=1), block_idx, total_rows) / D + EPS
    )
    return (scaling, (resid * scaling[:, None] * gain[None, :]).astype(jnp.bfloat16))


def norm_back(resid, gain, scaling, upstream, block_idx, total_rows):
    gain_grad = jnp.sum(resid * scaling[:, None] * upstream, axis=0)
    tilted = upstream * gain[None, :]
    project = token_total(jnp.sum(resid * tilted, axis=1), block_idx, total_rows) / D
    return (scaling[:, None] * tilted - resid * (scaling**3 * project)[:, None], gain_grad)


def conv_keep(places, segment, seq_lens):
    masks = []
    for offset in range(CONV):
        earlier = segments_of(places - (CONV - 1 - offset), seq_lens)
        masks.append((earlier == segment).astype(jnp.float32))
    return jnp.stack(masks)


def depth_conv(conv_masks, extended, weight, conv_bias):
    length = conv_masks.shape[1]
    summed = conv_bias[None, :]
    for offset in range(CONV):
        summed = (
            summed
            + weight[offset][None, :]
            * extended[offset : offset + length]
            * conv_masks[offset][:, None]
        )
    return summed


def mamba_pre(
    conv_masks,
    ext_x,
    ext_bc,
    dt_raw,
    conv_x_weight,
    conv_x_bias,
    conv_bc_weight,
    conv_bc_bias,
    dt_bias,
    a_log,
):
    length = dt_raw.shape[0]
    signal = jax.nn.silu(depth_conv(conv_masks, ext_x, conv_x_weight, conv_x_bias))
    signal = signal.reshape(length, a_log.shape[0], HEAD_DIM)
    bc_act = jax.nn.silu(depth_conv(conv_masks, ext_bc, conv_bc_weight, conv_bc_bias))
    step_size = jax.nn.softplus(dt_raw + dt_bias[None, :])
    rate = -jnp.exp(a_log)[None, :] * step_size
    return (signal, bc_act[:, :STATE], bc_act[:, STATE:], step_size, rate)


def ssd_block(carried, w_block, b_block, c_block, r_block, s_block, prior_seg):
    length = r_block.shape[0]
    cumulative = jnp.cumsum(r_block, axis=0)
    order = jnp.arange(length, dtype=jnp.int32)
    allowed = (order[None, :] <= order[:, None]) & (s_block[None, :] == s_block[:, None])
    gaps = cumulative[:, None, :] - cumulative[None, :, :]
    decay = jnp.where(allowed[:, :, None], jnp.exp(jnp.where(allowed[:, :, None], gaps, 0.0)), 0.0)
    scores = jnp.einsum("pn,qn->pq", c_block, b_block, precision=HIGH)
    mixing = scores[:, :, None] * decay
    result = jnp.einsum("pqh,qhm->phm", mixing, w_block, precision=HIGH)
    reach = (s_block == prior_seg).astype(jnp.float32)[:, None] * jnp.exp(cumulative)
    result = (
        result + jnp.einsum("pn,hmn->phm", c_block, carried, precision=HIGH) * reach[:, :, None]
    )
    tail_decay = (
        jnp.exp(cumulative[-1][None, :] - cumulative)
        * (s_block == s_block[-1]).astype(jnp.float32)[:, None]
    )
    local_state = jnp.einsum("qh,qhm,qn->hmn", tail_decay, w_block, b_block, precision=HIGH)
    through = jnp.exp(cumulative[-1]) * (s_block[-1] == prior_seg).astype(jnp.float32)
    return (result, through[:, None, None] * carried + local_state)


def ssd_local(inner_seg, prior_seg, signal, b_matrix, c_matrix, step_size, rate):
    length = rate.shape[0]
    blocks = length // SPAN
    heads_loc = rate.shape[1]
    weighted = signal * step_size[:, :, None]
    priors = jnp.concatenate([prior_seg[None], inner_seg[:-1]]).reshape(blocks, SPAN)[:, 0]
    pieces = (
        weighted.reshape(blocks, SPAN, heads_loc, HEAD_DIM),
        b_matrix.reshape(blocks, SPAN, STATE),
        c_matrix.reshape(blocks, SPAN, STATE),
        rate.reshape(blocks, SPAN, heads_loc),
        inner_seg.reshape(blocks, SPAN),
        priors,
    )

    def block_step(carried, piece_set):
        w_block, b_block, c_block, r_block, s_block, prior_one = piece_set
        result, next_state = ssd_block(
            carried, w_block, b_block, c_block, r_block, s_block, prior_one
        )
        return (next_state, result)

    zero_state = jnp.zeros((heads_loc, HEAD_DIM, STATE), jnp.float32)
    last_state, y_blocks = lax.scan(block_step, zero_state, pieces)
    through = jnp.exp(jnp.sum(rate, axis=0)) * (inner_seg[-1] == prior_seg).astype(jnp.float32)
    return (y_blocks.reshape(length, heads_loc, HEAD_DIM), last_state, through)


def carry_in(inner_seg, prior_seg, c_matrix, rate, entering):
    reach = (
        jnp.exp(jnp.cumsum(rate, axis=0)) * (inner_seg == prior_seg).astype(jnp.float32)[:, None]
    )
    return jnp.einsum("pn,hmn->phm", c_matrix, entering, precision=HIGH) * reach[:, :, None]


def join_states(earlier, latter):
    return (earlier[0] * latter[0], latter[0][:, None, None] * earlier[1] + latter[1])


def join_back(earlier, latter):
    return (earlier[0] * latter[0], latter[1] + latter[0][:, None, None] * earlier[1])


def attend_head(allowed, piece_set):
    q_head, k_head, v_head = piece_set
    scores = jnp.where(allowed, dot_trans(q_head, k_head) * AHEAD_DIM ** (-0.5), -jnp.inf)
    row_top = jnp.max(scores, axis=1, keepdims=True)
    powers = jnp.exp(scores - row_top)
    totals = jnp.sum(powers, axis=1, keepdims=True)
    probs = (powers / totals).astype(jnp.bfloat16)
    return (block_dot(probs, v_head), (row_top + jnp.log(totals))[:, 0])


def attend_back(allowed, piece_set):
    q_head, k_head, v_head, d_out, log_total = piece_set
    scores = jnp.where(allowed, dot_trans(q_head, k_head) * AHEAD_DIM ** (-0.5), -jnp.inf)
    probs = jnp.exp(scores - log_total[:, None])
    d_probs = dot_trans(d_out, v_head)
    spread = jnp.sum(probs * d_probs, axis=1, keepdims=True)
    d_scores = (probs * (d_probs - spread) * AHEAD_DIM ** (-0.5)).astype(jnp.bfloat16)
    d_query = block_dot(d_scores, k_head)
    d_key = dot_rows(d_scores, q_head)
    d_value = dot_rows(probs.astype(jnp.bfloat16), d_out)
    return (d_query, d_key, d_value)


def split_heads(flat, rows_count, heads_count):
    return flat.reshape(rows_count, heads_count, AHEAD_DIM).transpose(1, 0, 2)


def per_device(
    hidden_in,
    lengths,
    norm1_gain,
    z_weight,
    x_weight,
    bcdt_weight,
    conv_x_weight,
    conv_x_bias,
    conv_bc_weight,
    conv_bc_bias,
    a_log,
    d_skip,
    dt_bias,
    gate_gain,
    mix_out_weight,
    norm2_gain,
    q_weight,
    k_weight,
    v_weight,
    att_out_weight,
    norm3_gain,
    up_weight,
    down_weight,
    grad_output,
):
    row_idx = lax.axis_index("rows")
    col_idx = lax.axis_index("cols")
    tok_rows = hidden_in.shape[0]
    total_rows = tok_rows * lax.axis_size("rows")
    tok_cols = total_rows // lax.axis_size("cols")
    inner_loc = z_weight.shape[1]
    heads_loc = a_log.shape[0]
    att_loc = q_weight.shape[1]
    heads_att = att_loc // AHEAD_DIM
    seq_lens = lengths[0]
    resid_places = row_idx * tok_rows + jnp.arange(tok_rows, dtype=jnp.int32)
    inner_places = col_idx * tok_cols + jnp.arange(tok_cols, dtype=jnp.int32)
    key_places = jnp.arange(total_rows, dtype=jnp.int32)
    valid_rows = (resid_places < seq_lens[0] + seq_lens[1]).astype(jnp.float32)
    inner_seg = segments_of(inner_places, seq_lens)
    prior_seg = segments_of(col_idx * tok_cols - 1, seq_lens)
    key_seg = segments_of(key_places, seq_lens)
    lead_row = (row_idx == 0).astype(jnp.float32)
    hidden = hidden_in.astype(jnp.float32)
    scale_one, normed_one = norm_apply(hidden, norm1_gain, row_idx, total_rows)
    main_weight = jnp.concatenate([z_weight, x_weight], axis=1)
    in_weight = jnp.concatenate([main_weight, bcdt_weight], axis=1)
    whole_one = rows_gather(normed_one)
    projected = cols_sum(block_dot(whole_one, in_weight))
    gate_pre = projected[:, :inner_loc]
    x_pre = projected[:, inner_loc : 2 * inner_loc]
    bc_pre = projected[:, 2 * inner_loc : 2 * inner_loc + 2 * STATE]
    dt_all = projected[:, 2 * inner_loc + 2 * STATE :]
    dt_raw = lax.dynamic_slice_in_dim(dt_all, row_idx * heads_loc, heads_loc, 1)
    x_tail, bc_tail = from_behind(
        (x_pre[tok_cols - CONV + 1 :], bc_pre[tok_cols - CONV + 1 :]), "cols", 1
    )
    conv_masks = conv_keep(inner_places, inner_seg, seq_lens)
    ext_x = jnp.concatenate([x_tail, x_pre], axis=0)
    ext_bc = jnp.concatenate([bc_tail, bc_pre], axis=0)
    pre_out, pre_back = jax.vjp(
        partial(mamba_pre, conv_masks),
        ext_x,
        ext_bc,
        dt_raw,
        conv_x_weight,
        conv_x_bias,
        conv_bc_weight,
        conv_bc_bias,
        dt_bias,
        a_log,
    )
    signal, b_matrix, c_matrix, step_size, rate = pre_out
    ssd_out, ssd_back = jax.vjp(
        partial(ssd_local, inner_seg, prior_seg), signal, b_matrix, c_matrix, step_size, rate
    )
    mixed_zero, state_loc, through = ssd_out
    carried = carried_in(
        (through, state_loc),
        "cols",
        join_states,
        (jnp.ones_like(through), jnp.zeros_like(state_loc)),
    )
    entering = carried[1]
    corr_out, corr_back = jax.vjp(partial(carry_in, inner_seg, prior_seg), c_matrix, rate, entering)
    mixed = mixed_zero + corr_out + d_skip[None, :, None] * signal
    flat_mixed = mixed.reshape(tok_cols, inner_loc)
    silu_pair = jax.vjp(jax.nn.silu, gate_pre)
    gated = flat_mixed * silu_pair[0]
    gate_scale = lax.rsqrt(
        token_total(jnp.sum(gated * gated, axis=1), col_idx, total_rows) / INNER + EPS
    )
    gated_out = (gated * gate_scale[:, None] * gate_gain[None, :]).astype(jnp.bfloat16)
    whole_gated = cols_gather(gated_out)
    hidden_one = hidden + rows_sum(block_dot(whole_gated, mix_out_weight))
    scale_two, normed_two = norm_apply(hidden_one, norm2_gain, row_idx, total_rows)
    qkv_weight = jnp.concatenate([q_weight, k_weight, v_weight], axis=1)
    whole_two = rows_gather(normed_two)
    qkv_all = cols_sum(block_dot(whole_two, qkv_weight)).astype(jnp.bfloat16)
    queries = qkv_all[:, :att_loc]
    keys_vals = qkv_all[:, att_loc:]
    whole_kv = cols_gather(keys_vals)
    allowed = (key_places[None, :] <= inner_places[:, None]) & (
        key_seg[None, :] == inner_seg[:, None]
    )
    q_heads = split_heads(queries, tok_cols, heads_att)
    k_heads = split_heads(whole_kv[:, :att_loc], total_rows, heads_att)
    v_heads = split_heads(whole_kv[:, att_loc:], total_rows, heads_att)
    att_vals, log_totals = lax.map(partial(attend_head, allowed), (q_heads, k_heads, v_heads))
    attended = att_vals.transpose(1, 0, 2).reshape(tok_cols, att_loc).astype(jnp.bfloat16)
    whole_att = cols_gather(attended)
    hidden_two = hidden_one + rows_sum(block_dot(whole_att, att_out_weight))
    scale_three, normed_three = norm_apply(hidden_two, norm3_gain, row_idx, total_rows)
    whole_three = rows_gather(normed_three)
    activated = cols_sum(block_dot(whole_three, up_weight))
    gelu_pair = jax.vjp(partial(jax.nn.gelu, approximate=True), activated)
    hidden_act = gelu_pair[0].astype(jnp.bfloat16)
    whole_act = cols_gather(hidden_act)
    hidden_three = hidden_two + rows_sum(block_dot(whole_act, down_weight))
    output = (hidden_three * valid_rows[:, None]).astype(jnp.bfloat16)
    upstream = grad_output.astype(jnp.float32) * valid_rows[:, None]
    whole_grad = rows_gather(upstream.astype(jnp.bfloat16))
    d_act = cols_sum(dot_trans(whole_grad, down_weight))
    act_back = cols_gather(hidden_act)
    down_grad = dot_rows(act_back, whole_grad)
    d_pre = gelu_pair[1](d_act)[0].astype(jnp.bfloat16)
    whole_dpre = cols_gather(d_pre)
    d_normed_three = rows_sum(dot_trans(whole_dpre, up_weight))
    three_back = rows_gather(normed_three)
    up_grad = dot_rows(three_back, whole_dpre)
    d_norm_three, gain_three_grad = norm_back(
        hidden_two, norm3_gain, scale_three, d_normed_three, row_idx, total_rows
    )
    upstream_two = upstream + d_norm_three
    whole_grad = rows_gather(upstream_two.astype(jnp.bfloat16))
    d_att = cols_sum(dot_trans(whole_grad, att_out_weight)).astype(jnp.bfloat16)
    att_back = cols_gather(attended)
    att_out_grad = dot_rows(att_back, whole_grad)
    kv_back = cols_gather(keys_vals)
    k_again = split_heads(kv_back[:, :att_loc], total_rows, heads_att)
    v_again = split_heads(kv_back[:, att_loc:], total_rows, heads_att)
    d_heads = split_heads(d_att, tok_cols, heads_att)
    d_query, d_key, d_value = lax.map(
        partial(attend_back, allowed), (q_heads, k_again, v_again, d_heads, log_totals)
    )
    d_query = d_query.transpose(1, 0, 2).reshape(tok_cols, att_loc)
    d_kv_part = jnp.concatenate(
        [
            d_key.transpose(1, 0, 2).reshape(total_rows, att_loc),
            d_value.transpose(1, 0, 2).reshape(total_rows, att_loc),
        ],
        axis=1,
    )
    d_kv = cols_sum(d_kv_part)
    d_qkv = jnp.concatenate([d_query, d_kv], axis=1).astype(jnp.bfloat16)
    whole_dqkv = cols_gather(d_qkv)
    d_normed_two = rows_sum(dot_trans(whole_dqkv, qkv_weight))
    two_back = rows_gather(normed_two)
    qkv_grad = dot_rows(two_back, whole_dqkv)
    d_norm_two, gain_two_grad = norm_back(
        hidden_one, norm2_gain, scale_two, d_normed_two, row_idx, total_rows
    )
    upstream_one = upstream_two + d_norm_two
    whole_grad = rows_gather(upstream_one.astype(jnp.bfloat16))
    d_gated_out = cols_sum(dot_trans(whole_grad, mix_out_weight))
    gated_back = cols_gather(gated_out)
    mix_out_grad = dot_rows(gated_back, whole_grad)
    gate_gain_grad = jnp.sum(gated * gate_scale[:, None] * d_gated_out, axis=0)
    tilted = d_gated_out * gate_gain[None, :]
    project = token_total(jnp.sum(gated * tilted, axis=1), col_idx, total_rows) / INNER
    d_gated = gate_scale[:, None] * tilted - gated * (gate_scale**3 * project)[:, None]
    d_gate_pre = silu_pair[1](d_gated * flat_mixed)[0]
    d_mixed = (d_gated * silu_pair[0]).reshape(tok_cols, heads_loc, HEAD_DIM)
    d_skip_grad = jnp.sum(d_mixed * signal, axis=(0, 2))
    d_c_carry, d_rate_carry, local_enter = corr_back(d_mixed)
    returned = prefix(
        (through, local_enter),
        "cols",
        join_back,
        (jnp.ones_like(through), jnp.zeros_like(local_enter)),
    )
    leaving = returned[1]
    d_through = jnp.sum(leaving * entering, axis=(1, 2))
    d_signal, d_b_matrix, d_c_matrix, d_step, d_rate = ssd_back((d_mixed, leaving, d_through))
    pre_grads = pre_back(
        (
            d_signal + d_mixed * d_skip[None, :, None],
            d_b_matrix,
            d_c_matrix + d_c_carry,
            d_step,
            d_rate + d_rate_carry,
        )
    )
    (
        d_ext_x,
        d_ext_bc,
        d_dt_raw,
        conv_x_weight_grad,
        conv_x_bias_grad,
        conv_bc_weight_grad,
        conv_bc_bias_grad,
        dt_bias_grad,
        a_log_grad,
    ) = pre_grads
    sent_x, sent_bc = from_behind((d_ext_x[: CONV - 1], d_ext_bc[: CONV - 1]), "cols", -1)
    d_x_pre = d_ext_x[CONV - 1 :].at[tok_cols - CONV + 1 :].add(sent_x)
    d_bc_pre = d_ext_bc[CONV - 1 :].at[tok_cols - CONV + 1 :].add(sent_bc)
    d_main = jnp.concatenate([d_gate_pre, d_x_pre], axis=1).astype(jnp.bfloat16)
    d_bcdt_loc = jnp.concatenate([d_bc_pre, place_block(d_dt_raw, row_idx, HEADS, 1)], axis=1)
    d_bcdt_full = grid_total(place_block(d_bcdt_loc, col_idx, total_rows, 0)).astype(jnp.bfloat16)
    whole_main = cols_gather(d_main)
    d_normed_one = rows_sum(
        dot_trans(whole_main, main_weight) + lead_row * dot_trans(d_bcdt_full, bcdt_weight)
    )
    one_back = rows_gather(normed_one)
    main_grad = dot_rows(one_back, whole_main)
    bcdt_grad = lead_row * dot_rows(one_back, d_bcdt_full)
    d_norm_one, gain_one_grad = norm_back(
        hidden, norm1_gain, scale_one, d_normed_one, row_idx, total_rows
    )
    input_grad = upstream_one + d_norm_one
    summed_big = (
        lax.psum(main_grad[:, :inner_loc].astype(jnp.bfloat16), "dp").astype(jnp.float32),
        lax.psum(main_grad[:, inner_loc:].astype(jnp.bfloat16), "dp").astype(jnp.float32),
        lax.psum(mix_out_grad.astype(jnp.bfloat16), "dp").astype(jnp.float32),
        lax.psum(qkv_grad[:, :att_loc].astype(jnp.bfloat16), "dp").astype(jnp.float32),
        lax.psum(qkv_grad[:, att_loc : 2 * att_loc].astype(jnp.bfloat16), "dp").astype(jnp.float32),
        lax.psum(qkv_grad[:, 2 * att_loc :].astype(jnp.bfloat16), "dp").astype(jnp.float32),
        lax.psum(att_out_grad.astype(jnp.bfloat16), "dp").astype(jnp.float32),
        lax.psum(up_grad.astype(jnp.bfloat16), "dp").astype(jnp.float32),
        lax.psum(down_grad.astype(jnp.bfloat16), "dp").astype(jnp.float32),
    )
    summed_small = lax.psum(
        (
            place_block(gain_one_grad, col_idx, D, 0),
            place_block(bcdt_grad, col_idx, D, 0),
            place_block(conv_x_weight_grad, row_idx, INNER, 1),
            place_block(conv_x_bias_grad, row_idx, INNER, 0),
            conv_bc_weight_grad,
            conv_bc_bias_grad,
            place_block(a_log_grad, row_idx, HEADS, 0),
            place_block(d_skip_grad, row_idx, HEADS, 0),
            place_block(dt_bias_grad, row_idx, HEADS, 0),
            place_block(gate_gain_grad, row_idx, INNER, 0),
            place_block(gain_two_grad, col_idx, D, 0),
            place_block(gain_three_grad, col_idx, D, 0),
        ),
        ("dp", "rows", "cols"),
    )
    return (
        output,
        input_grad,
        summed_small[0],
        summed_big[0],
        summed_big[1],
        summed_small[1],
        summed_small[2],
        summed_small[3],
        summed_small[4],
        summed_small[5],
        summed_small[6],
        summed_small[7],
        summed_small[8],
        summed_small[9],
        summed_big[2],
        summed_small[10],
        summed_big[3],
        summed_big[4],
        summed_big[5],
        summed_big[6],
        summed_small[11],
        summed_big[7],
        summed_big[8],
    )


def solution(mesh):
    placed = (
        P(("dp", "rows"), "cols"),
        P("dp", None),
        P("cols"),
        P("cols", "rows"),
        P("cols", "rows"),
        P("cols", None),
        P(None, "rows"),
        P("rows"),
        P(),
        P(),
        P("rows"),
        P("rows"),
        P("rows"),
        P("rows"),
        P("rows", "cols"),
        P("cols"),
        P("cols", "rows"),
        P("cols", "rows"),
        P("cols", "rows"),
        P("rows", "cols"),
        P("cols"),
        P("cols", "rows"),
        P("rows", "cols"),
        P(("dp", "rows"), "cols"),
    )
    return jax.shard_map(
        per_device,
        mesh=mesh,
        in_specs=placed,
        out_specs=(
            P(("dp", "rows"), "cols"),
            P(("dp", "rows"), "cols"),
            P(),
            P("cols", "rows"),
            P("cols", "rows"),
            P(),
            P(),
            P(),
            P(),
            P(),
            P(),
            P(),
            P(),
            P(),
            P("rows", "cols"),
            P(),
            P("cols", "rows"),
            P("cols", "rows"),
            P("cols", "rows"),
            P("rows", "cols"),
            P(),
            P("cols", "rows"),
            P("rows", "cols"),
        ),
        check_vma=False,
    )
```

profile of v0, /device:TPU:0, one launch (start us, length us, event | category | flops | bytes accessed | tf_op | source)
XLA Modules:
  0.0 3269.4 jit_solution(7420646685623587898)
XLA Ops:
  8.9 36.0 %psum.210 = f32[2048]{0:T(1024)S(1)} all-reduce(f32[2048]{0:T(1024)S(1)} %dynamic_update_slice.260), channel_id=1, replica_groups=mesh['dp'=2,'rows'=4,'cols'=4] {'rows','cols'}, use_global_device_ids=true, to_apply=%region_1.2 | all-reduce | flops 2048 | bytes 16384 | tf_op jit(solution)/shard_map/psum | solution.py:80
  47.8 16.7 all-gather.19.cloned.1.call-done
  64.5 9.1 fusion.182
  81.0 244.8 %reduce-scatter.14.cloned.1.call-done = f32[512,1840]{0,1:T(8,128)} async-done(((f32[2048,1840]{0,1:T(8,128)}), f32[512,1840]{0,1:T(8,128)}) %reduce-scatter.14.cloned.1.call-update) | async-done | bytes 3768336 | tf_op jit(solution)/shard_map/reduce_scatter | solution.py:72
  346.3 7.1 fusion.177
  360.1 87.4 %while.136 = (s32[]{:T(128)}, f32[12,64,128]{2,1,0:T(8,128)S(1)}, f32[2,256,12,64]{1,0,3,2:T(2,128)}, pred[2,256,256,12]{2,1,3,0:T(32,128)(4,1)}, f32[2,256,256,...) while((s32[]{:T(128)}, f32[12,64,128]{2,1,0:T(8,128)S(1)}, ...), condition=%wide.region_6.7_spmd.clone, body=%wide.region_3.6_spmd.clone.sunk | while | flops 1316793344 | bytes 32349332 | solution.py:220
  378.6 16.8 dynamic_update_slice.371
  422.3 16.8 dynamic_update_slice.371
  453.4 12.8 all-reduce.20
  473.2 14.0 all-gather.45.cloned.1.call-done
  495.8 34.5 %psum.211 = f32[2048]{0:T(1024)S(1)} all-reduce(f32[2048]{0:T(1024)S(1)} %dynamic_update_slice.261), channel_id=1, replica_groups=mesh['dp'=2,'rows'=4,'cols'=4] {'rows','cols'}, use_global_device_ids=true, to_apply=%region_13.14 | all-reduce | flops 2048 | bytes 16384 | tf_op jit(solution)/shard_map/psum | solution.py:80
  532.6 60.8 %all-gather.21.cloned.1.call-done = bf16[2048,768]{0,1:T(8,128)(2,1)} async-done(((bf16[512,768]{0,1:T(8,128)(2,1)}), bf16[2048,768]{0,1:T(8,128)(2,1)}) %all-gather.21.cloned.1.call-update) | async-done | bytes 3145744 | tf_op jit(solution)/shard_map/all_gather | solution.py:68
  598.9 36.7 %reduce-scatter.16.cloned.1.call-done = f32[512,384]{1,0:T(8,128)} async-done(((f32[2048,384]{1,0:T(8,128)}), f32[512,384]{1,0:T(8,128)}) %reduce-scatter.16.cloned.1.call-update) | async-done | bytes 786448 | tf_op jit(solution)/shard_map/reduce_scatter | solution.py:76
  637.2 33.3 %psum.212 = f32[2048]{0:T(1024)S(1)} all-reduce(f32[2048]{0:T(1024)S(1)} %dynamic_update_slice.262), channel_id=1, replica_groups=mesh['dp'=2,'rows'=4,'cols'=4] {'rows','cols'}, use_global_device_ids=true, to_apply=%region_16.17 | all-reduce | flops 2048 | bytes 16384 | tf_op jit(solution)/shard_map/psum | solution.py:80
  672.7 16.6 all-gather.23.cloned.1.call-done
  689.4 7.8 fusion.274
  697.3 161.4 %reduce-scatter.18.cloned.1.call-done = f32[512,1152]{1,0:T(8,128)} async-done(((f32[2048,1152]{1,0:T(8,128)}), f32[512,1152]{1,0:T(8,128)}) %reduce-scatter.18.cloned.1.call-update) | async-done | bytes 2359312 | tf_op jit(solution)/shard_map/reduce_scatter | solution.py:72
  863.6 62.4 %all-gather.25.cloned.1.call-done = bf16[2048,768]{1,0:T(8,128)(2,1)} async-done(((bf16[512,768]{1,0:T(8,128)(2,1)}), bf16[2048,768]{1,0:T(8,128)(2,1)}) %all-gather.25.cloned.1.call-update) | async-done | bytes 3145744 | tf_op jit(solution)/shard_map/all_gather | solution.py:68
  942.1 54.0 %while.134 = (s32[]{:T(128)}, bf16[6,512,64]{1,2,0:T(8,128)(2,1)S(1)}, f32[6,512]{1,0:T(8,128)}, bf16[6,512,64]{2,1,0:T(8,128)(2,1)}, bf16[6,2048,64]{2,1,0:T(8,...) while((s32[]{:T(128)}, ...), condition=%wide.region_21.22_spmd.clone, body=%wide.region_18.21_spmd.clone.sunk | while | flops 279969280 | bytes 30705804 | solution.py:376
  996.9 35.9 %all-gather.27.cloned.1.call-done = bf16[2048,384]{0,1:T(8,128)(2,1)} async-done(((bf16[512,384]{0,1:T(8,128)(2,1)}), bf16[2048,384]{0,1:T(8,128)(2,1)}) %all-gather.27.cloned.1.call-update) | async-done | bytes 1572880 | tf_op jit(solution)/shard_map/all_gather | solution.py:68
  1039.0 35.0 %reduce-scatter.20.cloned.1.call-done = f32[512,384]{1,0:T(8,128)} async-done(((f32[2048,384]{1,0:T(8,128)}), f32[512,384]{1,0:T(8,128)}) %reduce-scatter.20.cloned.1.call-update) | async-done | bytes 786448 | tf_op jit(solution)/shard_map/reduce_scatter | solution.py:76
  1075.6 33.8 %psum.213 = f32[2048]{0:T(1024)S(1)} all-reduce(f32[2048]{0:T(1024)S(1)} %dynamic_update_slice.263), channel_id=1, replica_groups=mesh['dp'=2,'rows'=4,'cols'=4] {'rows','cols'}, use_global_device_ids=true, to_apply=%region_24.25 | all-reduce | flops 2048 | bytes 16384 | tf_op jit(solution)/shard_map/psum | solution.py:80
  1110.5 9.8 fusion.278
  1120.4 7.6 all-gather.29.cloned.1.call-done
  1128.0 7.8 fusion.276
  1135.9 206.5 %reduce-scatter.26.cloned.1.call-done = f32[512,1536]{1,0:T(8,128)} async-done(((f32[2048,1536]{1,0:T(8,128)}), f32[512,1536]{1,0:T(8,128)}) %reduce-scatter.26.cloned.1.call-update) | async-done | bytes 3145744 | tf_op jit(solution)/shard_map/reduce_scatter | solution.py:72
  1342.3 215.2 %reduce-scatter.22.cloned.1.call-done = f32[512,1536]{1,0:T(8,128)} async-done(((f32[2048,1536]{1,0:T(8,128)}), f32[512,1536]{1,0:T(8,128)}) %reduce-scatter.22.cloned.1.call-update) | async-done | bytes 3145744 | tf_op jit(solution)/shard_map/reduce_scatter | solution.py:72
  1563.7 115.9 %all-gather.35.cloned.1.call-done = bf16[2048,1536]{1,0:T(8,128)(2,1)} async-done(((bf16[512,1536]{1,0:T(8,128)(2,1)}), bf16[2048,1536]{1,0:T(8,128)(2,1)}) %all-gather.35.cloned.1.call-update) | async-done | bytes 6291472 | tf_op jit(solution)/shard_map/all_gather | solution.py:68
  1679.7 7.9 fusion.279
  1687.6 107.2 %all-gather.31.cloned.1.call-done = bf16[2048,1536]{1,0:T(8,128)(2,1)} async-done(((bf16[512,1536]{1,0:T(8,128)(2,1)}), bf16[2048,1536]{1,0:T(8,128)(2,1)}) %all-gather.31.cloned.1.call-update) | async-done | bytes 6291472 | tf_op jit(solution)/shard_map/all_gather | solution.py:68
  1794.8 7.8 fusion.277
  1802.7 30.8 reduce-scatter.28.cloned.1.call-done
  1835.7 33.7 %psum.214 = f32[2048]{0:T(1024)S(1)} all-reduce(f32[2048]{0:T(1024)S(1)} %dynamic_update_slice.264), channel_id=1, replica_groups=mesh['dp'=2,'rows'=4,'cols'=4] {'rows','cols'}, use_global_device_ids=true, to_apply=%region_30.31 | all-reduce | flops 2048 | bytes 16384 | tf_op jit(solution)/shard_map/psum | solution.py:80
  1876.7 19.7 all-gather.37.cloned.1.call-done
  1900.7 60.3 %reduce-scatter.30.cloned.1.call-done = f32[512,384]{1,0:T(8,128)} async-done(((f32[2048,384]{1,0:T(8,128)}), f32[512,384]{1,0:T(8,128)}) %reduce-scatter.30.cloned.1.call-update) | async-done | bytes 786448 | tf_op jit(solution)/shard_map/reduce_scatter | solution.py:72
  1962.4 69.1 %while.135 = (s32[]{:T(128)}, bf16[6,512,64]{1,2,0:T(8,128)(2,1)S(1)}, f32[6,2048,64]{1,2,0:T(8,128)}, f32[6,2048,64]{1,2,0:T(8,128)}, bf16[6,512,64]{2,1,0:T(8,...) while((s32[]{:T(128)}, ...), condition=%wide.region_34.35_spmd.clone, body=%wide.region_32.34_spmd.clone.sunk | while | flops 684719616 | bytes 34630784 | solution.py:410
  2031.6 6.2 pad_maximum_fusion
  2037.8 110.9 %reduce-scatter.32.cloned.1.call-done = f32[512,768]{0,1:T(8,128)} async-done(((f32[2048,768]{0,1:T(8,128)}), f32[512,768]{0,1:T(8,128)}) %reduce-scatter.32.cloned.1.call-update) | async-done | bytes 1572880 | tf_op jit(solution)/shard_map/reduce_scatter | solution.py:72
  2151.4 90.0 %all-gather.39.cloned.1.call-done = bf16[2048,1152]{0,1:T(8,128)(2,1)} async-done(((bf16[512,1152]{0,1:T(8,128)(2,1)}), bf16[2048,1152]{0,1:T(8,128)(2,1)}) %all-gather.39.cloned.1.call-update) | async-done | bytes 4718608 | tf_op jit(solution)/shard_map/all_gather | solution.py:68
  2241.4 7.0 fusion.281
  2248.5 36.5 %reduce-scatter.34.cloned.1.call-done = f32[512,384]{1,0:T(8,128)} async-done(((f32[2048,384]{1,0:T(8,128)}), f32[512,384]{1,0:T(8,128)}) %reduce-scatter.34.cloned.1.call-update) | async-done | bytes 786448 | tf_op jit(solution)/shard_map/reduce_scatter | solution.py:76
  2287.2 33.3 %psum.215 = f32[2048]{0:T(1024)S(1)} all-reduce(f32[2048]{0:T(1024)S(1)} %dynamic_update_slice.265), channel_id=1, replica_groups=mesh['dp'=2,'rows'=4,'cols'=4] {'rows','cols'}, use_global_device_ids=true, to_apply=%region_38.39 | all-reduce | flops 2048 | bytes 16384 | tf_op jit(solution)/shard_map/psum | solution.py:80
  2322.6 17.8 all-gather.41.cloned.1.call-done
  2340.4 5.8 fusion.282
  2347.8 11.9 all-reduce.21
  2359.8 97.5 %reduce-scatter.36.cloned.1.call-done = f32[512,768]{0,1:T(8,128)} async-done(((f32[2048,768]{0,1:T(8,128)}), f32[512,768]{0,1:T(8,128)}) %reduce-scatter.36.cloned.1.call-update) | async-done | bytes 1572880 | tf_op jit(solution)/shard_map/reduce_scatter | solution.py:72
  2459.9 33.9 %psum.216 = f32[2048]{0:T(1024)S(1)} all-reduce(f32[2048]{0:T(1024)S(1)} %dynamic_update_slice.266), channel_id=1, replica_groups=mesh['dp'=2,'rows'=4,'cols'=4] {'rows','cols'}, use_global_device_ids=true, to_apply=%region_41.42 | all-reduce | flops 2048 | bytes 16384 | tf_op jit(solution)/shard_map/psum | solution.py:80
  2503.5 17.2 all-gather.2
  2525.3 122.2 %while.133 = (s32[]{:T(128)}, f32[12,64,128]{2,1,0:T(8,128)S(1)}, f32[2,256,12,64]{1,0,3,2:T(2,128)}, f32[2,256,128]{2,1,0:T(8,128)}, f32[2,256,128]{2,1,0:T(8,1...) while((s32[]{:T(128)}, f32[12,64,128]{2,1,0:T(8,128)S(1)}, ...), condition=%wide.region_53.54_spmd, body=%wide.region_44.53_spmd.sunk | while | flops 2625927168 | bytes 50645296 | solution.py:220
  2533.3 6.8 fusion.390
  2561.1 16.7 dynamic_update_slice.353
  2594.1 6.8 fusion.390
  2621.9 16.7 dynamic_update_slice.353
  2659.5 6.4 collective-permute-done.2
  2670.1 7.1 convolution_convert_fusion.2
  2677.2 7.9 convolution_convert_fusion.1
  2693.6 89.6 %all-gather.43.cloned.1.call-done = bf16[2048,1536]{0,1:T(8,128)(2,1)} async-done(((bf16[512,1536]{0,1:T(8,128)(2,1)}), bf16[2048,1536]{0,1:T(8,128)(2,1)}) %all-gather.43.cloned.1.call-update) | async-done | bytes 6291472 | tf_op jit(solution)/shard_map/all_gather | solution.py:68
  2783.2 5.9 convolution_convert_fusion.3
  2818.2 114.1 %all-reduce.34 = bf16[2048,304]{0,1:T(8,128)(2,1)S(1)} all-reduce(f32[2048,304]{0,1:T(8,128)} %maximum_dynamic-update-slice_fusion), channel_id=1, replica_groups=mesh['dp'=2,'rows'=4,'cols'=4] {'rows','cols'}, use_global_device_ids=true, to_apply=%region_59.60 | all-reduce | flops 622592 | bytes 3735552 | tf_op jit(solution)/shard_map/psum | solution.py:80
  2932.4 6.1 fusion.189
  2960.2 16.8 reduce-scatter.38.cloned.1.call-done
  2979.1 33.7 %psum.218 = f32[2048]{0:T(1024)S(1)} all-reduce(f32[2048]{0:T(1024)S(1)} %dynamic_update_slice.269), channel_id=1, replica_groups=mesh['dp'=2,'rows'=4,'cols'=4] {'rows','cols'}, use_global_device_ids=true, to_apply=%region_62.63 | all-reduce | flops 2048 | bytes 16384 | tf_op jit(solution)/shard_map/psum | solution.py:80
  3014.8 102.0 %all-reduce.29.cloned.1.call-done = f32[1536,304]{0,1:T(8,128)} async-done(((f32[1536,304]{0,1:T(8,128)}), f32[1536,304]{0,1:T(8,128)}) %all-reduce.29.cloned.1.call-update) | async-done | bytes 1867792 | tf_op jit(solution)/shard_map/psum | solution.py:500
  3116.8 135.4 %all-reduce.31.cloned.1.call-done = (f32[1536]{0:T(1024)}, f32[4,3072]{1,0:T(4,128)}, f32[3072]{0:T(1024)}, f32[4,256]{1,0:T(4,128)}, f32[256]{0:T(256)}, /*inde...) async-done(((f32[1536]{0:T(1024)}, f32[4,3072]{1,0:T(4,128)}, f32[3072]{0:T(1024)}, f32[4,256]{1,0:T(4,128)}, ...) | async-done | bytes 97872 | tf_op jit(solution)/shard_map/psum | solution.py:500
  (1011 shorter events, 482.3 us)
Async XLA Ops:
  7.2 1120.8 %copy-start = (bf16[384,1536]{1,0:T(8,128)(2,1)S(1)}, bf16[384,1536]{1,0:T(8,128)(2,1)}, u32[]{:S(2)}) copy-start(bf16[384,1536]{1,0:T(8,128)(2,1)} %param.61) | copy-start | bytes 3538948
  7.2 57.2 %all-gather.19.cloned.1.call-start = ((), (), s32[]{:S(2)}) async-start(), calls=%async_computation.13 | async-start | bytes 1966080 | tf_op jit(solution)/shard_map/all_gather | solution.py:64
  47.5 278.3 %reduce-scatter.14.cloned.1.call-start = ((), (), s32[]{:S(2)}) async-start(), calls=%async_computation.14 | async-start | bytes 18841600 | tf_op jit(solution)/shard_map/reduce_scatter | solution.py:72
  73.6 263.2 %copy-start.174 = (f32[12]{0:T(128)S(1)}, f32[12]{0:T(128)}, u32[]{:S(2)}) copy-start(f32[12]{0:T(128)} %param.52) | copy-start | bytes 148
  73.6 413.5 %all-gather.45.cloned.1.call-start = ((), (), s32[]{:S(2)}) async-start(), calls=%async_computation.40 | async-start | bytes 1966080 | tf_op jit(solution)/shard_map/all_gather | solution.py:30
  77.4 260.1 %copy-start.161 = (s32[512]{0:T(512)}, s32[512]{0:T(512)S(1)}, u32[]{:S(2)}) copy-start(s32[512]{0:T(512)S(1)} %add_select_fusion) | copy-start | bytes 6148
  80.1 266.2 %copy-start.101 = (f32[512]{0:T(512)}, f32[512]{0:T(512)S(1)}, u32[]{:S(2)}) copy-start(f32[512]{0:T(512)S(1)} %get-tuple-element.2104) | copy-start | bytes 6148
  80.8 265.5 %copy-start.103 = (f32[512]{0:T(512)}, f32[512]{0:T(512)S(1)}, u32[]{:S(2)}) copy-start(f32[512]{0:T(512)S(1)} %get-tuple-element.2102) | copy-start | bytes 6148
  80.8 265.5 %copy-start.105 = (f32[512]{0:T(512)}, f32[512]{0:T(512)S(1)}, u32[]{:S(2)}) copy-start(f32[512]{0:T(512)S(1)} %get-tuple-element.2103) | copy-start | bytes 6148
  80.8 265.5 %copy-start.115 = (f32[768]{0:T(1024)}, f32[768]{0:T(1024)S(1)}, u32[]{:S(2)}) copy-start(f32[768]{0:T(1024)S(1)} %get-tuple-element.1829) | copy-start | bytes 9220
  80.8 265.5 %copy-start.117 = (f32[768]{0:T(1024)}, f32[768]{0:T(1024)S(1)}, u32[]{:S(2)}) copy-start(f32[768]{0:T(1024)S(1)} %get-tuple-element.1830) | copy-start | bytes 9220
  80.8 265.5 %copy-start.119 = (f32[768]{0:T(1024)}, f32[768]{0:T(1024)S(1)}, u32[]{:S(2)}) copy-start(f32[768]{0:T(1024)S(1)} %get-tuple-element.1831) | copy-start | bytes 9220
  80.9 265.5 %copy-start.121 = (f32[768]{0:T(1024)}, f32[768]{0:T(1024)S(1)}, u32[]{:S(2)}) copy-start(f32[768]{0:T(1024)S(1)} %get-tuple-element.1832) | copy-start | bytes 9220
  80.9 256.6 %copy-start.176 = (f32[12]{0:T(128)}, f32[12]{0:T(128)S(1)}, u32[]{:S(2)}) copy-start(f32[12]{0:T(128)S(1)} %exponential_negate_fusion) | copy-start | bytes 148
  80.9 260.7 %copy-start.149 = (f32[1,256]{1,0:T(1,128)}, f32[1,256]{1,0:T(1,128)S(1)}, u32[]{:S(2)}) copy-start(f32[1,256]{1,0:T(1,128)S(1)} %get-tuple-element.2092) | copy-start | bytes 3076
  80.9 260.7 %copy-start.151 = (f32[1,256]{1,0:T(1,128)}, f32[1,256]{1,0:T(1,128)S(1)}, u32[]{:S(2)}) copy-start(f32[1,256]{1,0:T(1,128)S(1)} %get-tuple-element.2093) | copy-start | bytes 3076
  80.9 260.7 %copy-start.153 = (f32[1,256]{1,0:T(1,128)}, f32[1,256]{1,0:T(1,128)S(1)}, u32[]{:S(2)}) copy-start(f32[1,256]{1,0:T(1,128)S(1)} %get-tuple-element.2094) | copy-start | bytes 3076
  80.9 260.7 %copy-start.155 = (f32[1,256]{1,0:T(1,128)}, f32[1,256]{1,0:T(1,128)S(1)}, u32[]{:S(2)}) copy-start(f32[1,256]{1,0:T(1,128)S(1)} %get-tuple-element.2095) | copy-start | bytes 3076
  327.0 18.6 collective-permute-start
  331.4 10.2 collective-permute-start.1
  448.3 145.2 %all-gather.21.cloned.1.call-start = ((), (), s32[]{:S(2)}) async-start(), calls=%async_computation.15 | async-start | bytes 3932160 | tf_op jit(solution)/shard_map/all_gather | solution.py:68
  531.5 62.0 %copy-start.68 = (bf16[768,384]{1,0:T(8,128)(2,1)S(1)}, bf16[768,384]{1,0:T(8,128)(2,1)}, u32[]{:S(2)}) copy-start(bf16[768,384]{1,0:T(8,128)(2,1)} %param.54) | copy-start | bytes 1769476
  532.6 103.0 %reduce-scatter.16.cloned.1.call-start = ((), (), s32[]{:S(2)}) async-start(), calls=%async_computation.16 | async-start | bytes 3932160 | tf_op jit(solution)/shard_map/reduce_scatter | solution.py:76
  598.8 71.8 %copy-start.133 = (f32[384]{0:T(512)S(1)}, f32[384]{0:T(512)}, u32[]{:S(2)}) copy-start(f32[384]{0:T(512)} %param.55) | copy-start | bytes 4612
  598.8 72.8 %copy-start.92 = (bf16[384,384]{1,0:T(8,128)(2,1)S(1)}, bf16[384,384]{1,0:T(8,128)(2,1)}, u32[]{:S(2)}) copy-start(bf16[384,384]{1,0:T(8,128)(2,1)} %param.56) | copy-start | bytes 884740
  598.8 90.5 %all-gather.23.cloned.1.call-start = ((), (), s32[]{:S(2)}) async-start(), calls=%async_computation.17 | async-start | bytes 1966080 | tf_op jit(solution)/shard_map/all_gather | solution.py:64
  671.5 187.2 %reduce-scatter.18.cloned.1.call-start = ((), (), s32[]{:S(2)}) async-start(), calls=%async_computation.18 | async-start | bytes 11796480 | tf_op jit(solution)/shard_map/reduce_scatter | solution.py:72
  697.3 228.7 %all-gather.25.cloned.1.call-start = ((), (), s32[]{:S(2)}) async-start(), calls=%async_computation.19 | async-start | bytes 3932160 | tf_op jit(solution)/shard_map/all_gather | solution.py:68
  861.4 171.4 %all-gather.27.cloned.1.call-start = ((), (), s32[]{:S(2)}) async-start(), calls=%async_computation.20 | async-start | bytes 1966080 | tf_op jit(solution)/shard_map/all_gather | solution.py:68
  942.1 90.8 %copy-start.60 = (bf16[384,384]{1,0:T(8,128)(2,1)S(1)}, bf16[384,384]{1,0:T(8,128)(2,1)}, u32[]{:S(2)}) copy-start(bf16[384,384]{1,0:T(8,128)(2,1)} %param.59) | copy-start | bytes 884740
  996.9 77.1 %reduce-scatter.20.cloned.1.call-start = ((), (), s32[]{:S(2)}) async-start(), calls=%async_computation.21 | async-start | bytes 3932160 | tf_op jit(solution)/shard_map/reduce_scatter | solution.py:76
  1037.1 73.4 %all-gather.33.cloned.1.call-start = ((), (), s32[]{:S(2)}) async-start(), calls=%async_computation.26 | async-start | bytes 1966080 | tf_op jit(solution)/shard_map/all_gather | solution.py:64
  1038.9 70.6 %copy-start.132 = (f32[384]{0:T(512)S(1)}, f32[384]{0:T(512)}, u32[]{:S(2)}) copy-start(f32[384]{0:T(512)} %param.60) | copy-start | bytes 4612
  1038.9 89.0 %all-gather.29.cloned.1.call-start = ((), (), s32[]{:S(2)}) async-start(), calls=%async_computation.22 | async-start | bytes 1966080 | tf_op jit(solution)/shard_map/all_gather | solution.py:64
  1110.4 231.9 %reduce-scatter.26.cloned.1.call-start = ((), (), s32[]{:S(2)}) async-start(), calls=%async_computation.27 | async-start | bytes 15728640 | tf_op jit(solution)/shard_map/reduce_scatter | solution.py:72
  1120.3 437.2 %reduce-scatter.22.cloned.1.call-start = ((), (), s32[]{:S(2)}) async-start(), calls=%async_computation.23 | async-start | bytes 15728640 | tf_op jit(solution)/shard_map/reduce_scatter | solution.py:72
  1135.8 543.8 %all-gather.35.cloned.1.call-start = ((), (), s32[]{:S(2)}) async-start(), calls=%async_computation.28 | async-start | bytes 7864320 | tf_op jit(solution)/shard_map/all_gather | solution.py:68
  1563.1 231.7 %all-gather.31.cloned.1.call-start = ((), (), s32[]{:S(2)}) async-start(), calls=%async_computation.24 | async-start | bytes 7864320 | tf_op jit(solution)/shard_map/all_gather | solution.py:68
  1563.7 269.8 %reduce-scatter.28.cloned.1.call-start = ((), (), s32[]{:S(2)}) async-start(), calls=%async_computation.29 | async-start | bytes 3932160 | tf_op jit(solution)/shard_map/reduce_scatter | solution.py:76
  1687.5 107.3 %copy-start.59 = (bf16[1536,384]{1,0:T(8,128)(2,1)S(1)}, bf16[1536,384]{1,0:T(8,128)(2,1)}, u32[]{:S(2)}) copy-start(bf16[1536,384]{1,0:T(8,128)(2,1)} %param.62) | copy-start | bytes 3538948
  1687.5 186.7 %reduce-scatter.24.cloned.1.call-start = ((), (), s32[]{:S(2)}) async-start(), calls=%async_computation.25 | async-start | bytes 3932160 | tf_op jit(solution)/shard_map/reduce_scatter | solution.py:76
  1802.6 71.6 %copy-start.56 = (bf16[512,384]{1,0:T(8,128)(2,1)S(1)}, bf16[512,384]{1,0:T(8,128)(2,1)}, u32[]{:S(2)}) copy-start(bf16[512,384]{1,0:T(8,128)(2,1)} %param.63) | copy-start | bytes 1179652
  1802.7 93.7 %all-gather.37.cloned.1.call-start = ((), (), s32[]{:S(2)}) async-start(), calls=%async_computation.30 | async-start | bytes 1966080 | tf_op jit(solution)/shard_map/all_gather | solution.py:64
  1876.6 84.4 %reduce-scatter.30.cloned.1.call-start = ((), (), s32[]{:S(2)}) async-start(), calls=%async_computation.31 | async-start | bytes 3932160 | tf_op jit(solution)/shard_map/reduce_scatter | solution.py:72
  1900.6 61.8 %copy-start.160 = (s32[2048]{0:T(1024)S(1)}, s32[2048]{0:T(1024)}, u32[]{:S(2)}) copy-start(s32[2048]{0:T(1024)} %copy-done.159) | copy-start | bytes 24580
  1900.6 61.8 %copy-start.163 = (s32[512]{0:T(512)S(1)}, s32[512]{0:T(512)}, u32[]{:S(2)}) copy-start(s32[512]{0:T(512)} %copy-done.161) | copy-start | bytes 6148
  1900.6 61.8 %copy-start.181 = (s32[512]{0:T(512)S(1)}, s32[512]{0:T(512)}, u32[]{:S(2)}) copy-start(s32[512]{0:T(512)} %copy-done.180) | copy-start | bytes 6148
  1900.6 248.1 %reduce-scatter.32.cloned.1.call-start = ((), (), s32[]{:S(2)}) async-start(), calls=%async_computation.32 | async-start | bytes 7864320 | tf_op jit(solution)/shard_map/reduce_scatter | solution.py:72
  2037.8 203.7 %all-gather.39.cloned.1.call-start = ((), (), s32[]{:S(2)}) async-start(), calls=%async_computation.33 | async-start | bytes 5898240 | tf_op jit(solution)/shard_map/all_gather | solution.py:68
  2151.4 133.6 %reduce-scatter.34.cloned.1.call-start = ((), (), s32[]{:S(2)}) async-start(), calls=%async_computation.34 | async-start | bytes 3932160 | tf_op jit(solution)/shard_map/reduce_scatter | solution.py:76
  2248.5 91.9 %all-gather.41.cloned.1.call-start = ((), (), s32[]{:S(2)}) async-start(), calls=%async_computation.35 | async-start | bytes 1966080 | tf_op jit(solution)/shard_map/all_gather | solution.py:64
  2322.6 134.7 %reduce-scatter.36.cloned.1.call-start = ((), (), s32[]{:S(2)}) async-start(), calls=%async_computation.36 | async-start | bytes 7864320 | tf_op jit(solution)/shard_map/reduce_scatter | solution.py:72
  2346.2 111.1 %copy-start.18 = (f32[512,768]{0,1:T(8,128)S(1)}, f32[512,768]{0,1:T(8,128)}, u32[]{:S(2)}) copy-start(f32[512,768]{0,1:T(8,128)} %copy-done.17) | copy-start | bytes 4718596
  2346.2 111.1 %copy-start.114 = (f32[768]{0:T(1024)S(1)}, f32[768]{0:T(1024)}, u32[]{:S(2)}) copy-start(f32[768]{0:T(1024)} %param.53) | copy-start | bytes 9220
  2346.2 111.1 %copy-start.131 = (f32[512]{0:T(512)S(1)}, f32[512]{0:T(512)}, u32[]{:S(2)}) copy-start(f32[512]{0:T(512)} %copy-done.130) | copy-start | bytes 6148
  2346.2 437.0 %all-gather.43.cloned.1.call-start = ((), (), s32[]{:S(2)}) async-start(), calls=%async_computation.37 | async-start | bytes 7864320 | tf_op jit(solution)/shard_map/all_gather | solution.py:68
  2656.3 9.7 collective-permute-start.2
  2670.0 278.5 %all-reduce.33.cloned.1.call-start = ((), (), s32[]{:S(2)}) async-start(), calls=%async_computation.42 | async-start | bytes 10616832 | tf_op jit(solution)/shard_map/psum | solution.py:490
  2790.2 186.8 %reduce-scatter.38.cloned.1.call-start = ((), (), s32[]{:S(2)}) async-start(), calls=%async_computation.38 | async-start | bytes 3932160 | tf_op jit(solution)/shard_map/reduce_scatter | solution.py:76
  2800.0 14.1 collective-permute-start.3
  2818.2 114.1 %copy-start.71 = (bf16[384,768]{1,0:T(8,128)(2,1)S(1)}, bf16[384,768]{1,0:T(8,128)(2,1)}, u32[]{:S(2)}) copy-start(bf16[384,768]{1,0:T(8,128)(2,1)} %param.44) | copy-start | bytes 1769476
  2818.2 114.1 %copy-start.73 = (bf16[384,768]{1,0:T(8,128)(2,1)S(1)}, bf16[384,768]{1,0:T(8,128)(2,1)}, u32[]{:S(2)}) copy-start(bf16[384,768]{1,0:T(8,128)(2,1)} %param.43) | copy-start | bytes 1769476
  2941.4 175.4 %all-reduce.29.cloned.1.call-start = ((), (), s32[]{:S(2)}) async-start(), calls=%async_computation.39 | async-start | bytes 3735552 | tf_op jit(solution)/shard_map/psum | solution.py:500
  2945.7 306.5 %all-reduce.31.cloned.1.call-start = ((), (), s32[]{:S(2)}) async-start(), calls=%async_computation.41 | async-start | bytes 209920 | tf_op jit(solution)/shard_map/psum | solution.py:500
  (208 other events, 1501.1 us)
Sparse Core Ops, SparseCore 0:
  47.6 16.8 all-gather.18
  73.7 252.0 reduce-scatter.13
  448.4 38.7 all-gather.44
  532.7 60.6 all-gather.20
  598.9 36.6 reduce-scatter.15
  671.6 17.6 all-gather.22
  697.4 161.2 reduce-scatter.17
  861.6 64.3 all-gather.24
  997.0 35.7 all-gather.26
  1037.2 36.7 reduce-scatter.19
  1076.3 19.9 all-gather.32
  1110.5 17.3 all-gather.28
  1130.4 211.8 reduce-scatter.25
  1344.7 212.8 reduce-scatter.21
  1563.2 116.3 all-gather.34
  1681.2 113.5 all-gather.30
  1797.3 36.1 reduce-scatter.27
  1835.9 38.3 reduce-scatter.23
  1876.8 19.5 all-gather.36
  1900.7 60.2 reduce-scatter.29
  2037.9 110.7 reduce-scatter.31
  2151.5 89.9 all-gather.38
  2248.6 36.3 reduce-scatter.33
  2322.7 17.6 all-gather.40
  2346.3 110.8 reduce-scatter.35
  2670.2 112.9 all-gather.42
  2790.3 132.9 all-reduce.32
  2941.5 35.4 reduce-scatter.37
  2983.9 132.8 all-reduce.28
  3125.9 126.2 all-reduce.30
where the time goes:
time: 3280 us; the launch traced here: 3270 us
  waiting for transfers between devices  2160 us (66%)
  blocking collectives  428 us (13%)
  matrix products  276 us (8%)
  local copies, waits for them, and re-layouts  216 us (7%)
  other arithmetic  155 us (5%)
    reduce_scatter x7, waiting for transfers between devices, cols_sum(): lax.psum_scatter(partial_sum, 'cols', scatter_dimension=0, tiled=True)  1100 us
    all_gather x7, waiting for transfers between devices, cols_gather(): return lax.all_gather(shard, 'cols', axis=0, tiled=True)  562 us
    psum x9, blocking collectives, grid_total(): return lax.psum(partial_sum, ('rows', 'cols'))  386 us
    psum x2, waiting for transfers between devices, per_device(): lax.psum((place_block(gain_one_grad, col_idx, D, 0), place_block(bcdt_gra...  237 us
    reduce_scatter x6, waiting for transfers between devices, rows_sum(): lax.psum_scatter(partial_sum, 'rows', scatter_dimension=0, tiled=True)  161 us
    dot_general x25, matrix products, dot_trans(): lax.dot_general(left, right, (((1,), (1,)), ((), ())), preferred_element_...  86.3 us
    all_gather x6, waiting for transfers between devices, rows_gather(): return lax.all_gather(shard, 'rows', axis=0, tiled=True)  78.4 us
    dynamic_update_slice x20, local copies, waits for them, and re-layouts, ssd_local(): last_state, y_blocks = lax.scan(block_step, zero_state, pieces)  77.5 us
  transfers between devices with their start and end apart: 34, of which 30 were waited for; matrix products, arithmetic and copies ran while one was open for 4% of the time, Pallas kernels for 0%

commit v1 on v0

v1 whole, which is shorter than its diff:
```python
import functools
import jax, jax.numpy as jnp
from jax import lax
from jax.experimental import pallas as pl
from jax.experimental.pallas import tpu as pltpu
MESH = pl.DeviceIdType.MESH
NC = 4
F32, BF = jnp.float32, jnp.bfloat16


def copy_to(src, dst, send, recv, dev):
    return pltpu.make_async_remote_copy(src_ref=src, dst_ref=dst, send_sem=send, recv_sem=recv, device_id=dev, device_id_type=MESH)


def greet(r, c):
    barrier = pltpu.get_barrier_semaphore()
    pl.semaphore_signal(barrier, inc=1, device_id={"rows": r ^ 1}, device_id_type=MESH)
    pl.semaphore_signal(barrier, inc=1, device_id={"rows": r ^ 2}, device_id_type=MESH)

    @pl.when(c > 0)
    def _():
        pl.semaphore_signal(barrier, inc=1, device_id={"cols": c - 1}, device_id_type=MESH)

    @pl.when(c < NC - 1)
    def _():
        pl.semaphore_signal(barrier, inc=1, device_id={"cols": c + 1}, device_id_type=MESH)

    count = 2 + jnp.where(c > 0, 1, 0) + jnp.where(c < NC - 1, 1, 0)
    pl.semaphore_wait(barrier, count)


def ag_kernel(native, x_ref, out_ref, recv, zr_s, zl_s, y_s, k_s, loc):
    r, c = lax.axis_index("rows"), lax.axis_index("cols")
    S, W = x_ref.shape
    greet(r, c)

    def slab(rr, cc):
        if native:
            return out_ref.at[pl.ds(pl.multiple_of(rr * S, 16), S), pl.ds(pl.multiple_of(cc * W, 128), W)]
        return out_ref.at[pl.ds(pl.multiple_of((rr * NC + cc) * S, 16), S)]

    def right(cc, src):
        return copy_to(src, slab(r, cc), zr_s.at[cc], recv.at[r * NC + cc], {"cols": c + 1})

    def left(cc, src):
        return copy_to(src, slab(r, cc), zl_s.at[cc], recv.at[r * NC + cc], {"cols": c - 1})

    def ycopy(cc, src):
        return copy_to(src, slab(r, cc), y_s.at[cc], recv.at[r * NC + cc], {"rows": r ^ 2})

    def kcopy(rr, cc, src):
        return copy_to(src, slab(rr, cc), k_s.at[(rr >> 1) * NC + cc], recv.at[rr * NC + cc], {"rows": r ^ 1})

    def got(rr, cc):
        copy_to(slab(rr, cc), slab(rr, cc), k_s.at[0], recv.at[rr * NC + cc], {"rows": r ^ 1}).wait_recv()

    @pl.when(c < NC - 1)
    def _():
        right(c, x_ref).start()

    @pl.when(c > 0)
    def _():
        left(c, x_ref).start()
    ycopy(c, x_ref).start()
    kcopy(r, c, x_ref).start()
    own = pltpu.make_async_copy(x_ref, slab(r, c), loc)
    own.start()

    def from_y(cc):
        got(r ^ 2, cc)
        kcopy(r ^ 2, cc, slab(r ^ 2, cc)).start()

    for d in range(1, NC):
        @pl.when(c >= d)
        def _():
            cc = c - d
            got(r, cc)

            @pl.when(c < NC - 1)
            def _():
                right(cc, slab(r, cc)).start()
            ycopy(cc, slab(r, cc)).start()
            kcopy(r, cc, slab(r, cc)).start()

        @pl.when(c + d < NC)
        def _():
            cc = c + d
            got(r, cc)

            @pl.when(c > 0)
            def _():
                left(cc, slab(r, cc)).start()
            ycopy(cc, slab(r, cc)).start()
            kcopy(r, cc, slab(r, cc)).start()
        if d == 1:
            from_y(c)
        else:
            @pl.when(c >= d - 1)
            def _():
                from_y(c - (d - 1))

            @pl.when(c + d - 1 < NC)
            def _():
                from_y(c + d - 1)
    d = NC

    @pl.when(c >= d - 1)
    def _():
        from_y(c - (d - 1))

    @pl.when(c + d - 1 < NC)
    def _():
        from_y(c + d - 1)
    for cc in range(NC):
        got(r ^ 1, cc)
        got(r ^ 3, cc)
    own.wait()
    for cc in range(NC):
        y_c = ycopy(cc, slab(r, cc))
        y_c.wait_send()
        kcopy(r, cc, slab(r, cc)).wait_send()
        kcopy(r ^ 2, cc, slab(r ^ 2, cc)).wait_send()

        @pl.when((cc <= c) & (c < NC - 1))
        def _():
            right(cc, slab(r, cc)).wait_send()

        @pl.when((cc >= c) & (c > 0))
        def _():
            left(cc, slab(r, cc)).wait_send()


def gather16(x, cid, native):
    S, D = x.shape
    return pl.pallas_call(
        functools.partial(ag_kernel, native),
        out_shape=jax.ShapeDtypeStruct((4 * S, NC * D) if native else (16 * S, D), x.dtype),
        in_specs=[pl.BlockSpec(memory_space=pltpu.VMEM)],
        out_specs=pl.BlockSpec(memory_space=pltpu.VMEM),
        scratch_shapes=[pltpu.SemaphoreType.DMA((16,)), pltpu.SemaphoreType.DMA((NC,)), pltpu.SemaphoreType.DMA((NC,)),
                        pltpu.SemaphoreType.DMA((NC,)), pltpu.SemaphoreType.DMA((2 * NC,)), pltpu.SemaphoreType.DMA],
        compiler_params=pltpu.CompilerParams(collective_id=cid, has_side_effects=True, vmem_limit_bytes=48 << 20),
        cost_estimate=pl.CostEstimate(flops=0, bytes_accessed=64 << 20, transcendentals=0),
    )(x)


def all_gather16(x, cid):
    return gather16(x, cid, False)


def gather_native(x, cid):
    return gather16(x, cid, True)


def rs_kernel(p_ref, o_ref, k_buf, y_buf, l_buf, r_buf, k_out, y_out, zr_out, zl_out,
              k_s, k_r, y_s, y_r, zr_s, zr_r, zl_s, zl_r):
    r, c = lax.axis_index("rows"), lax.axis_index("cols")
    S, D = o_ref.shape
    yy, kk = r >> 1, r & 1
    greet(r, c)

    def mine(rr, cc):
        return p_ref.at[pl.ds(pl.multiple_of((rr * NC + cc) * S, 16), S)]

    def kcopy(y2, cc):
        return copy_to(mine(y2 * 2 + (1 - kk), cc), k_buf.at[y2, cc], k_s.at[y2 * NC + cc], k_r.at[y2 * NC + cc], {"rows": r ^ 1})

    def ycopy(cc):
        return copy_to(y_out.at[cc], y_buf.at[cc], y_s.at[cc], y_r.at[cc], {"rows": r ^ 2})

    def rcopy(cc):
        return copy_to(zr_out.at[cc], r_buf.at[cc], zr_s.at[cc], zr_r.at[cc], {"cols": c + 1})

    def lcopy(cc):
        return copy_to(zl_out.at[cc], l_buf.at[cc], zl_s.at[cc], zl_r.at[cc], {"cols": c - 1})

    def order(f):
        for d in range(NC - 1, 0, -1):
            @pl.when(c + d < NC)
            def _():
                f(c + d)

            @pl.when(c >= d)
            def _():
                f(c - d)
        f(c)

    def start_k(cc):
        kcopy(1 - yy, cc).start()
    order(start_k)

    def start_k2(cc):
        kcopy(yy, cc).start()
    order(start_k2)

    def do_y(cc):
        kcopy(1 - yy, cc).wait_recv()
        y_out[cc] = (mine((1 - yy) * 2 + kk, cc)[...].astype(F32) + k_buf[1 - yy, cc].astype(F32)).astype(BF)
        ycopy(cc).start()
    order(do_y)

    def partial(cc):
        kcopy(yy, cc).wait_recv()
        a = mine(r, cc)[...].astype(F32) + k_buf[yy, cc].astype(F32)
        ycopy(cc).wait_recv()
        return a + y_buf[cc].astype(F32)

    for d in range(NC - 1, 0, -1):
        @pl.when(c + d < NC)
        def _():
            cc = c + d
            a = partial(cc)
            zr_out[cc] = a.astype(BF)

            @pl.when(c > 0)
            def _():
                rcopy(cc).wait_recv()
                zr_out[cc] = (zr_out[cc].astype(F32) + r_buf[cc].astype(F32)).astype(BF)
            rcopy(cc).start()

        @pl.when(c >= d)
        def _():
            cc = c - d
            a = partial(cc)
            zl_out[cc] = a.astype(BF)

            @pl.when(c < NC - 1)
            def _():
                lcopy(cc).wait_recv()
                zl_out[cc] = (zl_out[cc].astype(F32) + l_buf[cc].astype(F32)).astype(BF)
            lcopy(cc).start()
    o_ref[...] = partial(c)

    @pl.when(c > 0)
    def _():
        rcopy(c).wait_recv()
        o_ref[...] += r_buf[c].astype(F32)

    @pl.when(c < NC - 1)
    def _():
        lcopy(c).wait_recv()
        o_ref[...] += l_buf[c].astype(F32)

    def fin(cc):
        kcopy(1 - yy, cc).wait_send()
        kcopy(yy, cc).wait_send()
        ycopy(cc).wait_send()
    order(fin)
    for d in range(NC - 1, 0, -1):
        @pl.when(c + d < NC)
        def _():
            rcopy(c + d).wait_send()

        @pl.when(c >= d)
        def _():
            lcopy(c - d).wait_send()


def reduce_scatter16(p, cid):
    T, D = p.shape
    S = T // 16
    buf = lambda n: pltpu.VMEM((n, S, D), BF)
    sem = lambda n: pltpu.SemaphoreType.DMA((n,))
    return pl.pallas_call(
        rs_kernel,
        out_shape=jax.ShapeDtypeStruct((S, D), F32),
        in_specs=[pl.BlockSpec(memory_space=pltpu.VMEM)],
        out_specs=pl.BlockSpec(memory_space=pltpu.VMEM),
        scratch_shapes=[pltpu.VMEM((2, NC, S, D), BF), buf(NC), buf(NC), buf(NC), buf(NC), buf(NC), buf(NC), buf(NC),
                        sem(8), sem(8), sem(4), sem(4), sem(4), sem(4), sem(4), sem(4)],
        compiler_params=pltpu.CompilerParams(collective_id=cid, has_side_effects=True, vmem_limit_bytes=56 << 20),
        cost_estimate=pl.CostEstimate(flops=0, bytes_accessed=64 << 20, transcendentals=0),
    )(p)


P = jax.sharding.PartitionSpec
HEAD_DIM = 64
STATE = 128
CONV = 4
SPAN = 256
AHEAD_DIM = 64
EPS = 1e-05
HIGH = lax.Precision.HIGHEST


def dot(a, b):
    return jnp.dot(a, b, preferred_element_type=F32)


def dot_t(a, b):
    return lax.dot_general(a, b, (((1,), (1,)), ((), ())), preferred_element_type=F32)


def t_dot(a, b):
    return lax.dot_general(a, b, (((0,), (0,)), ((), ())), preferred_element_type=F32)


def segments_of(places, seq_lens):
    first = (places >= seq_lens[0]).astype(jnp.int32)
    second = (places >= seq_lens[0] + seq_lens[1]).astype(jnp.int32)
    return jnp.where(places < 0, -1, first + second)


def cols_swap(pieces):
    c = lax.axis_index("cols")
    out = jnp.zeros_like(pieces)
    own = lax.dynamic_index_in_dim(pieces, c, 0, True)
    out = lax.dynamic_update_slice_in_dim(out, own, c, 0)
    for s in range(1, NC):
        away = lax.dynamic_index_in_dim(pieces, (c + s) % NC, 0, True)
        came = lax.ppermute(away, "cols", [(i, (i + s) % NC) for i in range(NC)])
        out = lax.dynamic_update_slice_in_dim(out, came, (c - s) % NC, 0)
    return out


def spread_in(w):
    d, n = w.shape
    return cols_swap(w.reshape(d, NC, n // NC).transpose(1, 0, 2)).reshape(d * NC, n // NC)


def spread_pair(w):
    d, n = w.shape
    halves = w.reshape(d, 2, n // 2).transpose(1, 0, 2)
    return cols_swap(jnp.repeat(halves, NC // 2, axis=0)).reshape(d * NC, n // 2)


def spread_out(w):
    n, d = w.shape
    return cols_swap(w.reshape(NC, n // NC, d)).transpose(1, 0, 2).reshape(n // NC, d * NC)


def spread_out_pair(w):
    n, d = w.shape
    halves = jnp.repeat(w.reshape(2, n // 2, d), NC // 2, axis=0)
    return cols_swap(halves).transpose(1, 0, 2).reshape(n // 2, d * NC)


def both_groups(x):
    if lax.axis_size("dp") == 2:
        return x.astype(F32) + lax.ppermute(x, "dp", [(0, 1), (1, 0)]).astype(F32)
    return lax.psum(x, "dp").astype(F32)


def back_in(g):
    d, n = g.shape
    got = both_groups(cols_swap(g.astype(BF).reshape(NC, d // NC, n)))
    return got.transpose(1, 0, 2).reshape(d // NC, NC * n)


def back_in_pair(g):
    d, n = g.shape
    got = both_groups(cols_swap(g.astype(BF).reshape(NC, d // NC, n)))
    got = got.reshape(2, NC // 2, d // NC, n).sum(1)
    return got.transpose(1, 0, 2).reshape(d // NC, 2 * n)


def back_out(g):
    n, d = g.shape
    got = both_groups(cols_swap(g.astype(BF).reshape(n, NC, d // NC).transpose(1, 0, 2)))
    return got.reshape(NC * n, d // NC)


def back_out_pair(g):
    n, d = g.shape
    got = both_groups(cols_swap(g.astype(BF).reshape(n, NC, d // NC).transpose(1, 0, 2)))
    got = got.reshape(2, NC // 2, n, d // NC).sum(1)
    return got.reshape(2 * n, d // NC)


def place_block(piece, start, full_len, axis):
    shape = piece.shape[:axis] + (full_len,) + piece.shape[axis + 1:]
    return lax.dynamic_update_slice_in_dim(jnp.zeros(shape, piece.dtype), piece, start, axis)


def rms_scale(x):
    return lax.rsqrt(jnp.mean(x * x, axis=1, keepdims=True) + EPS)


def norm_back(x, gain, scale, up):
    gain_grad = jnp.sum(x * scale * up, axis=0)
    tilted = up * gain[None, :]
    project = jnp.mean(x * tilted, axis=1, keepdims=True)
    return scale * tilted - x * (scale**3 * project), gain_grad


def depth_conv(masks, x, weight, bias):
    total = bias[None, :] + weight[CONV - 1][None, :] * x
    for s in range(1, CONV):
        shifted = jnp.concatenate([jnp.zeros((s, x.shape[1]), F32), x[:-s]], axis=0)
        total = total + weight[CONV - 1 - s][None, :] * shifted * masks[s - 1][:, None]
    return total


def mixer_pre(masks, x_pre, bc_pre, dt_raw, conv_w, conv_b, bc_w, bc_b, dt_bias, a_log):
    signal = jax.nn.silu(depth_conv(masks, x_pre, conv_w, conv_b))
    bc = jax.nn.silu(depth_conv(masks, bc_pre, bc_w, bc_b))
    step = jax.nn.softplus(dt_raw + dt_bias[None, :])
    rate = -jnp.exp(a_log)[None, :] * step
    return signal, bc[:, :STATE], bc[:, STATE:], step, rate


def ssd(seg, signal, bm, cm, step, rate):
    T, H = rate.shape
    nb = T // SPAN
    sb = seg.reshape(nb, SPAN)
    prior = jnp.concatenate([jnp.full((1,), -1, jnp.int32), sb[:-1, -1]])
    cum = jnp.cumsum(rate.reshape(nb, SPAN, H), axis=1).transpose(0, 2, 1)
    w = (signal.reshape(T, H, HEAD_DIM) * step[:, :, None]).reshape(nb, SPAN, H, HEAD_DIM).transpose(0, 2, 1, 3)
    b = bm.reshape(nb, SPAN, STATE)
    cc = cm.reshape(nb, SPAN, STATE)
    order = jnp.arange(SPAN, dtype=jnp.int32)
    allowed = (order[None, None, :] <= order[None, :, None]) & (sb[:, None, :] == sb[:, :, None])
    gaps = cum[:, :, :, None] - cum[:, :, None, :]
    decay = jnp.exp(jnp.where(allowed[:, None], gaps, -1e30))
    scores = jnp.einsum("bpn,bqn->bpq", cc, b, precision=HIGH)
    y = jnp.einsum("bhpq,bhqm->bhpm", scores[:, None] * decay, w, precision=HIGH)
    last = cum[:, :, -1]
    tail = jnp.exp(last[:, :, None] - cum) * (sb == sb[:, -1:]).astype(F32)[:, None, :]
    local = jnp.einsum("bhqm,bqn->bhmn", tail[..., None] * w, b, precision=HIGH)
    through = jnp.exp(last) * (sb[:, -1] == prior).astype(F32)[:, None]
    reach = jnp.exp(cum) * (sb == prior[:, None]).astype(F32)[:, None, :]
    state = jnp.zeros((H, HEAD_DIM, STATE), F32)
    states = []
    for i in range(nb):
        states.append(state)
        state = through[i][:, None, None] * state + local[i]
    states = jnp.stack(states)
    y = y + jnp.einsum("bpn,bhmn->bhpm", cc, states, precision=HIGH) * reach[..., None]
    return y.transpose(0, 2, 1, 3).reshape(T, H * HEAD_DIM)


def attend_head(allowed, piece):
    q, k, v = piece
    s = jnp.where(allowed, dot_t(q, k) * AHEAD_DIM ** (-0.5), -jnp.inf)
    top = jnp.max(s, axis=1, keepdims=True)
    e = jnp.exp(s - top)
    tot = jnp.sum(e, axis=1, keepdims=True)
    return dot((e / tot).astype(BF), v), (top + jnp.log(tot))[:, 0]


def attend_back(allowed, piece):
    q, k, v, do, lse = piece
    s = jnp.where(allowed, dot_t(q, k) * AHEAD_DIM ** (-0.5), -jnp.inf)
    p = jnp.exp(s - lse[:, None])
    dp = dot_t(do, v)
    ds = (p * (dp - jnp.sum(p * dp, axis=1, keepdims=True)) * AHEAD_DIM ** (-0.5)).astype(BF)
    return dot(ds, k), t_dot(ds, q), t_dot(p.astype(BF), do)


def heads_first(x):
    n, w = x.shape
    return x.reshape(n, w // AHEAD_DIM, AHEAD_DIM).transpose(1, 0, 2)


def heads_last(x):
    h, n, w = x.shape
    return x.transpose(1, 0, 2).reshape(n, h * w)


def per_device(hidden_in, lengths, norm1_gain, z_weight, x_weight, bcdt_weight, conv_x_weight, conv_x_bias,
               conv_bc_weight, conv_bc_bias, a_log, d_skip, dt_bias, gate_gain, mix_out_weight, norm2_gain,
               q_weight, k_weight, v_weight, att_out_weight, norm3_gain, up_weight, down_weight, grad_output):
    r, c = lax.axis_index("rows"), lax.axis_index("cols")
    rows = lax.axis_size("rows")
    tok_rows, feat = hidden_in.shape
    T, D = tok_rows * rows, feat * NC
    S = T // (rows * NC)
    slab = r * NC + c
    inner = z_weight.shape[1] * rows
    wide = z_weight.shape[1] // NC
    heads_row = a_log.shape[0]
    heads = heads_row // NC
    n_heads = heads_row * rows
    seq_lens = lengths[0]
    places = jnp.arange(T, dtype=jnp.int32)
    seg = segments_of(places, seq_lens)
    valid = (places < seq_lens[0] + seq_lens[1]).astype(F32)
    my_valid = lax.dynamic_slice_in_dim(valid, slab * S, S, 0)[:, None]
    pad = 128

    gains = lax.all_gather(jnp.stack([norm1_gain, norm2_gain, norm3_gain]), "cols", axis=1, tiled=True)
    hidden_all = gather_native(hidden_in, 0)
    w_z = spread_in(z_weight)
    w_x = spread_in(x_weight)
    w_bcdt = lax.all_gather(bcdt_weight, "cols", axis=0, tiled=True)
    w_in = jnp.concatenate([w_z, w_x, w_bcdt], axis=1)
    w_mix = spread_out(mix_out_weight)
    w_qkv = jnp.concatenate([spread_pair(q_weight), spread_pair(k_weight), spread_pair(v_weight)], axis=1)
    w_o = spread_out_pair(att_out_weight)
    w_up = spread_in(up_weight)
    w_down = spread_out(down_weight)
    grad_all = gather_native(grad_output, 0)

    hid_all = hidden_all.astype(F32)
    u1 = (hid_all * rms_scale(hid_all) * gains[0][None, :]).astype(BF)
    proj = dot(u1, w_in)
    z_pre, x_pre = proj[:, :wide], proj[:, wide:2 * wide]
    bc_pre = proj[:, 2 * wide:2 * wide + 2 * STATE]
    dt_raw = lax.dynamic_slice_in_dim(proj[:, 2 * wide + 2 * STATE:], slab * heads, heads, 1)
    masks = jnp.stack([(segments_of(places - s, seq_lens) == seg).astype(F32) for s in range(1, CONV)])
    mine = lambda a, n: lax.dynamic_slice_in_dim(a, c * n, n, a.ndim - 1)
    pre_out, pre_back = jax.vjp(
        functools.partial(mixer_pre, masks), x_pre, bc_pre, dt_raw, mine(conv_x_weight, wide), mine(conv_x_bias, wide),
        conv_bc_weight, conv_bc_bias, mine(dt_bias, heads), mine(a_log, heads))
    signal = pre_out[0]
    y_ssd, ssd_back = jax.vjp(functools.partial(ssd, seg), *pre_out)
    skip = jnp.repeat(mine(d_skip, heads), HEAD_DIM)[None, :]
    y = y_ssd + skip * signal
    silu_z, silu_back = jax.vjp(jax.nn.silu, z_pre)
    gated = y * silu_z
    my_gate_gain = mine(gate_gain, wide)[None, :]
    mixg = (gated * my_gate_gain).astype(BF)
    squares = jnp.sum(gated * gated, axis=1, keepdims=True)
    part = jnp.concatenate([dot(mixg, w_mix), jnp.broadcast_to(squares, (T, pad))], axis=1).astype(BF)
    summed = reduce_scatter16(part, 2)
    gate_scale = lax.rsqrt(summed[:, D:D + 1] / inner + EPS)
    mix_out = summed[:, :D] * gate_scale
    h0 = lax.dynamic_slice_in_dim(hidden_all, slab * S, S, 0).astype(F32)
    h1 = h0 + mix_out
    s2 = rms_scale(h1)
    u2 = all_gather16((h1 * s2 * gains[1][None, :]).astype(BF), 1)

    qkv = dot(u2, w_qkv).astype(BF)
    att = w_o.shape[0]
    odd = c % 2
    blk = T // 4
    b0, b1 = jnp.where(odd == 1, 1, 0), jnp.where(odd == 1, 2, 3)

    def pick(x):
        return jnp.concatenate([lax.dynamic_slice_in_dim(x, b0 * blk, blk, 0), lax.dynamic_slice_in_dim(x, b1 * blk, blk, 0)], axis=0)

    def unpick(x):
        out = jnp.zeros((T,) + x.shape[1:], x.dtype)
        out = lax.dynamic_update_slice_in_dim(out, x[:blk], b0 * blk, 0)
        return lax.dynamic_update_slice_in_dim(out, x[blk:], b1 * blk, 0)

    q_h = heads_first(pick(qkv[:, :att]))
    k_h, v_h = heads_first(qkv[:, att:2 * att]), heads_first(qkv[:, 2 * att:])
    q_places, q_seg = pick(places), pick(seg)
    allowed = (places[None, :] <= q_places[:, None]) & (seg[None, :] == q_seg[:, None])
    att_h, lse = lax.map(functools.partial(attend_head, allowed), (q_h, k_h, v_h))
    attended = heads_last(att_h).astype(BF)
    h2 = h1 + reduce_scatter16(unpick(dot(attended, w_o).astype(BF)), 3)
    s3 = rms_scale(h2)
    u3 = all_gather16((h2 * s3 * gains[2][None, :]).astype(BF), 1)

    act, = (dot(u3, w_up),)
    gelu, gelu_back = jax.vjp(functools.partial(jax.nn.gelu, approximate=True), act)
    hid = gelu.astype(BF)
    h3 = h2 + reduce_scatter16(dot(hid, w_down).astype(BF), 3)
    out_slab = (h3 * my_valid).astype(BF)
    output = cols_swap(out_slab.reshape(S, NC, feat).transpose(1, 0, 2)).reshape(NC * S, feat)

    g3 = (grad_all.astype(F32) * valid[:, None]).astype(BF)
    g3_mine = lax.dynamic_slice_in_dim(g3, slab * S, S, 0).astype(F32)
    d_act = gelu_back(dot_t(g3, w_down))[0].astype(BF)
    down_grad = back_out(t_dot(hid, g3))
    up_grad = back_in(t_dot(u3, d_act))
    d_u3 = reduce_scatter16(dot_t(d_act, w_up).astype(BF), 3)
    d_n3, gain3_grad = norm_back(h2, gains[2], s3, d_u3)
    dh2 = g3_mine + d_n3
    g2 = all_gather16(dh2.astype(BF), 1)
    g2_sel = pick(g2)
    d_att = heads_first(dot_t(g2_sel, w_o).astype(BF))
    o_grad = back_out_pair(t_dot(attended, g2_sel))
    dq, dk, dv = lax.map(functools.partial(attend_back, allowed), (q_h, k_h, v_h, d_att, lse))
    d_qkv = jnp.concatenate([unpick(heads_last(dq)), heads_last(dk), heads_last(dv)], axis=1).astype(BF)
    qkv_grad = t_dot(u2, d_qkv)
    q_grad, k_grad, v_grad = (back_in_pair(qkv_grad[:, i * att:(i + 1) * att]) for i in range(3))
    d_u2 = reduce_scatter16(dot_t(d_qkv, w_qkv).astype(BF), 3)
    d_n2, gain2_grad = norm_back(h1, gains[1], s2, d_u2)
    dh1 = dh2 + d_n2
    tilt = gate_scale * gate_scale * jnp.sum(dh1 * mix_out, axis=1, keepdims=True) / inner
    tilt_hi = tilt.astype(BF)
    tilt_lo = (tilt - tilt_hi.astype(F32)).astype(BF)
    tail = jnp.concatenate([jnp.broadcast_to(tilt_hi, (S, pad // 2)), jnp.broadcast_to(tilt_lo, (S, pad // 2))], axis=1)
    g1_ext = all_gather16(jnp.concatenate([(dh1 * gate_scale).astype(BF), tail], axis=1), 4)
    g1 = g1_ext[:, :D]
    tilt_all = g1_ext[:, D:D + 1].astype(F32) + g1_ext[:, D + pad // 2:D + pad // 2 + 1].astype(F32)
    d_mix = dot_t(g1, w_mix)
    mix_grad = back_out(t_dot(mixg, g1))
    gate_gain_grad = jnp.sum(gated * d_mix, axis=0)
    d_gated = d_mix * my_gate_gain - gated * tilt_all
    d_z = silu_back(d_gated * y)[0]
    d_y = d_gated * silu_z
    d_skip_grad = jnp.sum((d_y * signal).reshape(T, heads, HEAD_DIM), axis=(0, 2))
    d_signal, d_b, d_c, d_step, d_rate = ssd_back(d_y)
    pre_grads = pre_back((d_signal + d_y * skip, d_b, d_c, d_step, d_rate))
    d_x, d_bc, d_dt, cxw_grad, cxb_grad, cbw_grad, cbb_grad, dt_bias_grad, a_log_grad = pre_grads
    d_bcdt = jnp.concatenate([d_bc, place_block(d_dt, slab * heads, n_heads, 1)], axis=1)
    d_in = jnp.concatenate([d_z, d_x, d_bcdt], axis=1).astype(BF)
    in_grad = t_dot(u1, d_in)
    z_grad, x_grad = back_in(in_grad[:, :wide]), back_in(in_grad[:, wide:2 * wide])
    d_u1 = reduce_scatter16(dot_t(d_in, w_in).astype(BF), 3)
    d_n1, gain1_grad = norm_back(h0, gains[0], rms_scale(h0), d_u1)
    in_slab = dh1 + d_n1
    input_grad = cols_swap(in_slab.reshape(S, NC, feat).transpose(1, 0, 2)).reshape(NC * S, feat)

    small = lax.psum((
        gain1_grad, in_grad[:, 2 * wide:], place_block(cxw_grad, slab * wide, inner, 1), place_block(cxb_grad, slab * wide, inner, 0),
        cbw_grad, cbb_grad, place_block(a_log_grad, slab * heads, n_heads, 0), place_block(d_skip_grad, slab * heads, n_heads, 0),
        place_block(dt_bias_grad, slab * heads, n_heads, 0), place_block(gate_gain_grad, slab * wide, inner, 0),
        gain2_grad, gain3_grad), ("dp", "rows", "cols"))
    return (output, input_grad, small[0], z_grad, x_grad, small[1], small[2], small[3], small[4], small[5], small[6], small[7],
            small[8], small[9], mix_grad, small[10], q_grad, k_grad, v_grad, o_grad, small[11], up_grad, down_grad)


def solution(mesh):
    assert mesh.shape["rows"] == 4 and mesh.shape["cols"] == NC
    token = P(("dp", "rows"), "cols")
    w_in, w_out = P("cols", "rows"), P("rows", "cols")
    row, col, whole = P("rows"), P("cols"), P()
    placed = (token, P("dp", None), col, w_in, w_in, P("cols", None), P(None, "rows"), row, whole, whole, row, row, row, row,
              w_out, col, w_in, w_in, w_in, w_out, col, w_in, w_out, token)
    given = (token, token, whole, w_in, w_in, whole, whole, whole, whole, whole, whole, whole, whole, whole, w_out, whole,
             w_in, w_in, w_in, w_out, whole, w_in, w_out)
    return jax.shard_map(per_device, mesh=mesh, in_specs=placed, out_specs=given, check_vma=False)
```

time: 3280 us -> 1560 us (0.48)
  waiting for transfers between devices: 2160 us -> 174 us
  Pallas kernels: 0 us -> 569 us
  blocking collectives: 428 us -> 36.5 us
  local copies, waits for them, and re-layouts: 216 us -> 336 us
  starting transfers between devices: 12.3 us -> 93.6 us
  matrix products: 276 us -> 200 us
  other arithmetic: 155 us -> 116 us
    reduce_scatter x13 -> x0, waiting for transfers between devices: 1260 us -> none  [the longest x7 1100 us: cols_sum(): lax.psum_scatter(partial_sum, 'cols', scatter_dimension=0, tiled=True)]
    all_gather x14 -> x0, waiting for transfers between devices: 654 us -> none  [the longest x7 562 us: cols_gather(): return lax.all_gather(shard, 'cols', axis=0, tiled=True)]
    pallas_call x0 -> x12, Pallas kernels: none -> 569 us  [the longest x6 293 us: reduce_scatter16(): pl.pallas_call(rs_kernel, out_shape=jax.ShapeDtypeStruct((S, D), F32), in...]
    psum x9 -> x0, blocking collectives: 386 us -> none  [grid_total(): return lax.psum(partial_sum, ('rows', 'cols'))]
    psum x3 -> x2, waiting for transfers between devices: 237 us -> 0.02 us  [per_device(): lax.psum((gain1_grad, in_grad[:, 2 * wide:], place_block(cxw_grad, slab *...]
    ppermute x4 -> x69, waiting for transfers between devices: 6.67 us -> 174 us  [the longest x9 99.9 us: both_groups(): return x.astype(F32) + lax.ppermute(x, 'dp', [(0, 1), (1, 0)]).astype(F32)]
    ppermute x4 -> x69, starting transfers between devices: 10.7 us -> 93.6 us  [the longest x60 89.4 us: cols_swap(): came = lax.ppermute(away, 'cols', [(i, (i + s) % NC) for i in range(NC)])]
    dot_general x89 -> x51, matrix products: 276 us -> 200 us  [the longest x15 61.5 us: dot_t(): lax.dot_general(a, b, (((1,), (1,)), ((), ())), preferred_element_type=F32)]
  transfers between devices with their start and end apart: 34 -> 71, of which waited for: 30 -> 26; matrix products, arithmetic and copies ran while one was open for 4% -> 25% of each run, Pallas kernels for 0% -> 22%
where the time goes in v1:
time: 1560 us; the launch traced here: 1550 us
  Pallas kernels  569 us (36%)
  local copies, waits for them, and re-layouts  336 us (22%)
  matrix products  200 us (13%)
  waiting for transfers between devices  174 us (11%)
  other arithmetic  116 us (7%)
  starting transfers between devices  93.6 us (6%)
  blocking collectives  36.5 us (2%)
  between operations  20 us (1%)
    pallas_call x6, Pallas kernels, reduce_scatter16(): pl.pallas_call(rs_kernel, out_shape=jax.ShapeDtypeStruct((S, D), F32), in...  293 us
    pallas_call x6, Pallas kernels, gather16(): pl.pallas_call(functools.partial(ag_kernel, native), out_shape=jax.ShapeD...  276 us
    dynamic_update_slice x58, local copies, waits for them, and re-layouts, cols_swap(): out = lax.dynamic_update_slice_in_dim(out, came, (c - s) % NC, 0)  110 us
    ppermute x9, waiting for transfers between devices, both_groups(): return x.astype(F32) + lax.ppermute(x, 'dp', [(0, 1), (1, 0)]).astype(F32)  99.9 us
    ppermute x60, starting transfers between devices, cols_swap(): came = lax.ppermute(away, 'cols', [(i, (i + s) % NC) for i in range(NC)])  89.4 us
    unnamed x654, local copies, waits for them, and re-layouts  77.2 us
    ppermute x60, waiting for transfers between devices, cols_swap(): came = lax.ppermute(away, 'cols', [(i, (i + s) % NC) for i in range(NC)])  74.4 us
    dot_general x15, matrix products, dot_t(): lax.dot_general(a, b, (((1,), (1,)), ((), ())), preferred_element_type=F32)  61.5 us
  transfers between devices with their start and end apart: 71, of which 26 were waited for; matrix products, arithmetic and copies ran while one was open for 25% of the time, Pallas kernels for 22%

profile of v1, /device:TPU:0, one launch (start us, length us, event | category | flops | bytes accessed | tf_op | source)
XLA Modules:
  0.0 1546.6 jit_solution(1756381031358615924)
XLA Ops:
  30.3 23.4 %all_gather.7 = bf16[1536,304]{0,1:T(8,128)(2,1)S(1)} all-gather(bf16[384,304]{0,1:T(8,128)(2,1)S(1)} %copy-done.131), channel_id=1, replica_groups=mesh['dp'=2,'rows'=4,'cols'=4] {'cols'}, dimensions={0}, use_global_device_ids=true | all-gather | bytes 1167360 | tf_op jit(solution)/shard_map/all_gather | solution.py:485
  53.7 44.6 %shard_map.407 = bf16[2048,1536]{1,0:T(8,128)(2,1)} custom-call(bf16[512,384]{1,0:T(8,128)(2,1)S(1)} %copy-done), custom_call_target="tpu_custom_call" | custom-call | bytes 67108864 | tf_op jit(solution)/shard_map/pallas_call | solution.py:135
  103.2 13.2 all_gather.6
  128.2 40.6 %shard_map.413 = bf16[2048,1536]{1,0:T(8,128)(2,1)} custom-call(bf16[512,384]{1,0:T(8,128)(2,1)S(1)} %copy-done.1), custom_call_target="tpu_custom_call" | custom-call | bytes 67108864 | tf_op jit(solution)/shard_map/pallas_call | solution.py:135
  200.1 6.6 dynamic_update_slice.299
  207.7 6.6 dynamic_update_slice.315
  235.4 5.8 collective-permute-done.1
  294.0 8.5 fusion.101
  305.1 6.6 dynamic_update_slice.300
  314.7 6.6 dynamic_update_slice.301
  321.3 6.7 dynamic_update_slice.302
  337.3 53.6 %shard_map.408 = f32[128,1664]{1,0:T(8,128)} custom-call(bf16[2048,1664]{1,0:T(8,128)(2,1)} %pad_maximum_fusion.p_ref), custom_call_target="tpu_custom_call" | custom-call | bytes 67108864 | tf_op jit(solution)/shard_map/pallas_call | solution.py:264
  400.5 62.8 %shard_map.409 = bf16[2048,1536]{1,0:T(8,128)(2,1)} custom-call(bf16[128,1536]{1,0:T(8,128)(2,1)S(1)} %multiply_convert_fusion.7.x_ref), custom_call_target="tpu_custom_call" | custom-call | bytes 67108864 | tf_op jit(solution)/shard_map/pallas_call | solution.py:135
  479.4 35.7 %while.28 = (s32[]{:T(128)}, bf16[3,1024,64]{1,2,0:T(8,128)(2,1)S(1)}, f32[3,1024]{1,0:T(4,128)S(1)}, bf16[3,1024,64]{2,1,0:T(8,128)(2,1)S(1)}, bf16[3,2048,64]{...) while((s32[]{:T(128)}, ...), condition=%wide.region_8.9_spmd.clone, body=%wide.region_5.8_spmd.clone.sunk | while | flops 559938560 | bytes 60352652 | solution.py:541
  486.1 5.2 fusion.269
  498.0 5.2 fusion.269
  509.9 5.2 fusion.269
  518.9 5.7 dynamic_update_slice.316
  524.8 5.8 dynamic_update_slice.317
  533.0 5.7 dynamic_update_slice.318
  544.1 48.0 %shard_map.410 = f32[128,1536]{1,0:T(8,128)} custom-call(bf16[2048,1536]{1,0:T(8,128)(2,1)} %copy-done.4), custom_call_target="tpu_custom_call" | custom-call | bytes 67108864 | tf_op jit(solution)/shard_map/pallas_call | solution.py:264
  595.1 41.1 %shard_map.411 = bf16[2048,1536]{1,0:T(8,128)(2,1)} custom-call(bf16[128,1536]{1,0:T(8,128)(2,1)S(1)} %multiply_convert_fusion.6.x_ref), custom_call_target="tpu_custom_call" | custom-call | bytes 67108864 | tf_op jit(solution)/shard_map/pallas_call | solution.py:135
  650.7 6.0 fusion.213
  656.7 7.7 convolution_convert_fusion.8
  664.4 5.1 fusion.68
  674.1 5.9 convolution_convert_fusion.3.p_ref
  679.9 47.7 %shard_map.414 = f32[128,1536]{1,0:T(8,128)} custom-call(bf16[2048,1536]{1,0:T(8,128)(2,1)} %convolution_convert_fusion.3.p_ref), custom_call_target="tpu_custom_call" | custom-call | bytes 67108864 | tf_op jit(solution)/shard_map/pallas_call | solution.py:264
  730.9 41.5 %shard_map.415 = bf16[2048,1536]{1,0:T(8,128)(2,1)} custom-call(bf16[128,1536]{1,0:T(8,128)(2,1)S(1)} %fusion.192.x_ref), custom_call_target="tpu_custom_call" | custom-call | bytes 67108864 | tf_op jit(solution)/shard_map/pallas_call | solution.py:135
  777.8 33.7 %while.29 = (s32[]{:T(128)}, bf16[3,1024,64]{1,2,0:T(8,128)(2,1)S(1)}, bf16[3,2048,64]{1,2,0:T(8,128)(2,1)}, bf16[3,2048,64]{1,2,0:T(8,128)(2,1)}, bf16[3,1024,6...) while((s32[]{:T(128)}, ...), condition=%wide.region_13.14_spmd.clone, body=%wide.region_11.13_spmd.clone.sunk | while | flops 1369439232 | bytes 73245968 | solution.py:566
  812.7 8.2 convolution_convert_fusion.6
  820.9 8.6 convolution_convert_fusion.2.p_ref
  829.5 6.5 convolution_convert_fusion.4.p_ref
  836.0 46.4 %shard_map.416 = f32[128,1536]{1,0:T(8,128)} custom-call(bf16[2048,1536]{1,0:T(8,128)(2,1)} %convolution_convert_fusion.2.p_ref), custom_call_target="tpu_custom_call" | custom-call | bytes 67108864 | tf_op jit(solution)/shard_map/pallas_call | solution.py:264
  884.5 47.9 %shard_map.412 = f32[128,1536]{1,0:T(8,128)} custom-call(bf16[2048,1536]{1,0:T(8,128)(2,1)} %convolution_convert_fusion.4.p_ref), custom_call_target="tpu_custom_call" | custom-call | bytes 67108864 | tf_op jit(solution)/shard_map/pallas_call | solution.py:264
  935.7 45.3 %shard_map.417 = bf16[2048,1664]{1,0:T(8,128)(2,1)} custom-call(bf16[128,1664]{1,0:T(8,128)(2,1)S(1)} %concatenate.73.x_ref), custom_call_target="tpu_custom_call" | custom-call | bytes 67108864 | tf_op jit(solution)/shard_map/pallas_call | solution.py:135
  981.1 5.2 fusion.79
  987.0 6.0 multiply_reduce_fusion.7
  1000.0 9.8 fusion.61
  1013.1 4.7 fusion.119
  1018.4 6.6 bitcast_add_fusion
  1042.0 5.7 convolution_add_fusion
  1064.0 7.5 reduce-window.16
  1076.1 4.7 fusion.194
  1084.8 7.4 fusion.210
  1092.2 7.4 convolution_convert_fusion.1.p_ref
  1133.1 49.7 %shard_map.418 = f32[128,1536]{1,0:T(8,128)} custom-call(bf16[2048,1536]{1,0:T(8,128)(2,1)} %convolution_convert_fusion.1.p_ref), custom_call_target="tpu_custom_call" | custom-call | bytes 67108864 | tf_op jit(solution)/shard_map/pallas_call | solution.py:264
  1222.0 6.7 dynamic_update_slice.354
  1233.3 5.0 collective-permute-done.28
  1247.5 4.9 collective-permute-done.54
  1270.2 5.4 collective-permute-done.45
  1276.3 5.0 collective-permute-done.46
  1290.5 4.9 collective-permute-done.38
  1323.5 6.6 dynamic_update_slice.355
  1333.3 6.6 dynamic_update_slice.356
  1342.3 6.6 dynamic_update_slice.357
  1359.4 7.0 collective-permute-done.31
  1383.5 13.0 collective-permute-done.62
  1399.8 7.4 collective-permute-done.60
  1407.3 13.9 collective-permute-done.52
  1422.2 11.7 collective-permute-done.48
  1449.4 10.5 collective-permute-done.40
  1462.7 11.1 collective-permute-done.36
  1476.6 26.3 %collective-permute-done.64 = bf16[4,384,384]{2,1,0:T(8,128)(2,1)} collective-permute-done((bf16[4,384,384]{2,1,0:T(8,128)(2,1)S(1)}, bf16[4,384,384]{2,1,0:T(8,128)(2,1)}, u32[]{:S(2)}, u32[]{:S(2)}) %collective-permute-start.64) | collective-permute-done | bytes 1179680 | tf_op jit(solution)/shard_map/ppermute | solution.py:340
  1509.4 16.6 %collective-permute-done.68 = bf16[4,384,384]{2,1,0:T(8,128)(2,1)} collective-permute-done((bf16[4,384,384]{2,1,0:T(8,128)(2,1)}, bf16[4,384,384]{2,1,0:T(8,128)(2,1)}, u32[]{:S(2)}, u32[]{:S(2)}) %collective-permute-start.68) | collective-permute-done | bytes 1179680 | tf_op jit(solution)/shard_map/ppermute | solution.py:340
  (1202 shorter events, 558.0 us)
Async XLA Ops:
  7.2 1522.1 %all-reduce.43.cloned.1.call-start = ((), (), s32[]{:S(2)}) async-start(), calls=%async_computation.1 | async-start | bytes 209920 | tf_op jit(solution)/shard_map/psum | solution.py:599
  9.5 204.8 %collective-permute-start.9 = (bf16[1,384,192]{1,2,0:T(8,128)(2,1)}, bf16[1,384,192]{1,2,0:T(8,128)(2,1)}, u32[]{:S(2)}, u32[]{:S(2)}) collective-permute-start(bf16[1,384,192]{1,2,0:T(8,128)(2,1)} %get-tuple-element.625), channel_id=1, source_target_pairs={{0,1},{1,2},{2,3},{3,0},{4,5},{5,6},{6,7},{7,4},{8,9},{9,10},{10,1... | collective-permute-start | bytes 442376 | tf_op jit(solution)/shard_map/ppermute | solution.py:311
  12.5 207.5 %collective-permute-start.10 = (bf16[1,384,192]{1,2,0:T(8,128)(2,1)}, bf16[1,384,192]{1,2,0:T(8,128)(2,1)}, u32[]{:S(2)}, u32[]{:S(2)}) collective-permute-start(bf16[1,384,192]{1,2,0:T(8,128)(2,1)} %get-tuple-element.624), channel_id=1, source_target_pairs={{0,2},{1,3},{2,0},{3,1},{4,6},{5,7},{6,4},{7,5},{8,10},{9,11},{10,... | collective-permute-start | bytes 442376 | tf_op jit(solution)/shard_map/ppermute | solution.py:311
  16.2 202.2 %collective-permute-start.3 = (bf16[1,384,192]{1,2,0:T(8,128)(2,1)}, bf16[1,384,192]{1,2,0:T(8,128)(2,1)}, u32[]{:S(2)}, u32[]{:S(2)}) collective-permute-start(bf16[1,384,192]{1,2,0:T(8,128)(2,1)} %get-tuple-element.633), channel_id=1, source_target_pairs={{0,1},{1,2},{2,3},{3,0},{4,5},{5,6},{6,7},{7,4},{8,9},{9,10},{10,1... | collective-permute-start | bytes 442376 | tf_op jit(solution)/shard_map/ppermute | solution.py:311
  17.0 205.2 %collective-permute-start.4 = (bf16[1,384,192]{1,2,0:T(8,128)(2,1)}, bf16[1,384,192]{1,2,0:T(8,128)(2,1)}, u32[]{:S(2)}, u32[]{:S(2)}) collective-permute-start(bf16[1,384,192]{1,2,0:T(8,128)(2,1)} %get-tuple-element.632), channel_id=1, source_target_pairs={{0,2},{1,3},{2,0},{3,1},{4,6},{5,7},{6,4},{7,5},{8,10},{9,11},{10,... | collective-permute-start | bytes 442376 | tf_op jit(solution)/shard_map/ppermute | solution.py:311
  18.1 208.9 %collective-permute-start.11 = (bf16[1,384,192]{1,2,0:T(8,128)(2,1)}, bf16[1,384,192]{1,2,0:T(8,128)(2,1)}, u32[]{:S(2)}, u32[]{:S(2)}) collective-permute-start(bf16[1,384,192]{1,2,0:T(8,128)(2,1)} %get-tuple-element.623), channel_id=1, source_target_pairs={{0,3},{1,0},{2,1},{3,2},{4,7},{5,4},{6,5},{7,6},{8,11},{9,8},{10,9... | collective-permute-start | bytes 442376 | tf_op jit(solution)/shard_map/ppermute | solution.py:311
  214.3 13.3 collective-permute-start.5
  218.4 12.4 collective-permute-start
  220.0 21.2 %collective-permute-start.1 = (bf16[1,384,192]{1,2,0:T(8,128)(2,1)}, bf16[1,384,192]{1,2,0:T(8,128)(2,1)S(1)}, u32[]{:S(2)}, u32[]{:S(2)}) collective-permute-start(bf16[1,384,192]{1,2,0:T(8,128)(2,1)} %get-tuple-element.635), channel_id=1, source_target_pairs={{0,2},{1,3},{2,0},{3,1},{4,6},{5,7},{6,4},{7,5},{8,10},{9,11},{10,... | collective-permute-start | bytes 442376 | tf_op jit(solution)/shard_map/ppermute | solution.py:311
  222.2 20.0 %collective-permute-start.2 = (bf16[1,384,192]{1,2,0:T(8,128)(2,1)}, bf16[1,384,192]{1,2,0:T(8,128)(2,1)S(1)}, u32[]{:S(2)}, u32[]{:S(2)}) collective-permute-start(bf16[1,384,192]{1,2,0:T(8,128)(2,1)} %get-tuple-element.634), channel_id=1, source_target_pairs={{0,3},{1,0},{2,1},{3,2},{4,7},{5,4},{6,5},{7,6},{8,11},{9,8},{10,9... | collective-permute-start | bytes 442376 | tf_op jit(solution)/shard_map/ppermute | solution.py:311
  227.0 77.1 %collective-permute-start.6 = (bf16[1,192,384]{2,0,1:T(2,128)(2,1)}, bf16[1,192,384]{2,0,1:T(2,128)(2,1)}, u32[]{:S(2)}, u32[]{:S(2)}) collective-permute-start(bf16[1,192,384]{2,0,1:T(2,128)(2,1)} %copy.1394), channel_id=1, source_target_pairs={{0,1},{1,2},{2,3},{3,0},{4,5},{5,6},{6,7},{7,4},{8,9},{9,10},{10,1... | collective-permute-start | bytes 442376 | tf_op jit(solution)/shard_map/ppermute | solution.py:311
  227.6 84.2 %collective-permute-start.7 = (bf16[1,192,384]{2,0,1:T(2,128)(2,1)}, bf16[1,192,384]{2,0,1:T(2,128)(2,1)}, u32[]{:S(2)}, u32[]{:S(2)}) collective-permute-start(bf16[1,192,384]{2,0,1:T(2,128)(2,1)} %copy.1395), channel_id=1, source_target_pairs={{0,2},{1,3},{2,0},{3,1},{4,6},{5,7},{6,4},{7,5},{8,10},{9,11},{10,... | collective-permute-start | bytes 442376 | tf_op jit(solution)/shard_map/ppermute | solution.py:311
  230.8 90.5 %collective-permute-start.8 = (bf16[1,192,384]{2,0,1:T(2,128)(2,1)S(1)}, bf16[1,192,384]{2,0,1:T(2,128)(2,1)}, u32[]{:S(2)}, u32[]{:S(2)}) collective-permute-start(bf16[1,192,384]{2,0,1:T(2,128)(2,1)S(1)} %copy-done.130), channel_id=1, source_target_pairs={{0,3},{1,0},{2,1},{3,2},{4,7},{5,4},{6,5},{7,6},{8,11},{9,8},{10,9... | collective-permute-start | bytes 442376 | tf_op jit(solution)/shard_map/ppermute | solution.py:311
  241.2 152.9 %collective-permute-start.15 = (bf16[1,384,192]{1,2,0:T(8,128)(2,1)}, bf16[1,384,192]{1,2,0:T(8,128)(2,1)}, u32[]{:S(2)}, u32[]{:S(2)}) collective-permute-start(bf16[1,384,192]{1,2,0:T(8,128)(2,1)} %get-tuple-element.617), channel_id=1, source_target_pairs={{0,1},{1,2},{2,3},{3,0},{4,5},{5,6},{6,7},{7,4},{8,9},{9,10},{10,1... | collective-permute-start | bytes 442376 | tf_op jit(solution)/shard_map/ppermute | solution.py:311
  242.2 155.4 %collective-permute-start.16 = (bf16[1,384,192]{1,2,0:T(8,128)(2,1)}, bf16[1,384,192]{1,2,0:T(8,128)(2,1)}, u32[]{:S(2)}, u32[]{:S(2)}) collective-permute-start(bf16[1,384,192]{1,2,0:T(8,128)(2,1)} %get-tuple-element.616), channel_id=1, source_target_pairs={{0,2},{1,3},{2,0},{3,1},{4,6},{5,7},{6,4},{7,5},{8,10},{9,11},{10,... | collective-permute-start | bytes 442376 | tf_op jit(solution)/shard_map/ppermute | solution.py:311
  304.1 94.4 %collective-permute-start.12 = (bf16[1,384,192]{1,2,0:T(8,128)(2,1)}, bf16[1,384,192]{1,2,0:T(8,128)(2,1)}, u32[]{:S(2)}, u32[]{:S(2)}) collective-permute-start(bf16[1,384,192]{1,2,0:T(8,128)(2,1)} %get-tuple-element.621), channel_id=1, source_target_pairs={{0,1},{1,2},{2,3},{3,0},{4,5},{5,6},{6,7},{7,4},{8,9},{9,10},{10,1... | collective-permute-start | bytes 442376 | tf_op jit(solution)/shard_map/ppermute | solution.py:311
  311.8 151.5 %collective-permute-start.13 = (bf16[1,384,192]{1,2,0:T(8,128)(2,1)}, bf16[1,384,192]{1,2,0:T(8,128)(2,1)}, u32[]{:S(2)}, u32[]{:S(2)}) collective-permute-start(bf16[1,384,192]{1,2,0:T(8,128)(2,1)} %get-tuple-element.620), channel_id=1, source_target_pairs={{0,2},{1,3},{2,0},{3,1},{4,6},{5,7},{6,4},{7,5},{8,10},{9,11},{10,... | collective-permute-start | bytes 442376 | tf_op jit(solution)/shard_map/ppermute | solution.py:311
  321.3 144.4 %collective-permute-start.14 = (bf16[1,384,192]{1,2,0:T(8,128)(2,1)}, bf16[1,384,192]{1,2,0:T(8,128)(2,1)S(1)}, u32[]{:S(2)}, u32[]{:S(2)}) collective-permute-start(bf16[1,384,192]{1,2,0:T(8,128)(2,1)} %get-tuple-element.619), channel_id=1, source_target_pairs={{0,3},{1,0},{2,1},{3,2},{4,7},{5,4},{6,5},{7,6},{8,11},{9,8},{10,9... | collective-permute-start | bytes 442376 | tf_op jit(solution)/shard_map/ppermute | solution.py:311
  394.2 72.6 %collective-permute-start.17 = (bf16[1,384,192]{1,2,0:T(8,128)(2,1)S(1)}, bf16[1,384,192]{1,2,0:T(8,128)(2,1)S(1)}, u32[]{:S(2)}, u32[]{:S(2)}) collective-permute-start(bf16[1,384,192]{1,2,0:T(8,128)(2,1)S(1)} %copy-done.146), channel_id=1, source_target_pairs={{0,3},{1,0},{2,1},{3,2},{4,7},{5,4},{6,5},{7,6},{8,11},{9,8},{10,9... | collective-permute-start | bytes 442376 | tf_op jit(solution)/shard_map/ppermute | solution.py:311
  397.5 117.6 %collective-permute-start.18 = (bf16[1,192,384]{2,0,1:T(2,128)(2,1)}, bf16[1,192,384]{2,0,1:T(2,128)(2,1)}, u32[]{:S(2)}, u32[]{:S(2)}) collective-permute-start(bf16[1,192,384]{2,0,1:T(2,128)(2,1)} %get-tuple-element.613), channel_id=1, source_target_pairs={{0,1},{1,2},{2,3},{3,0},{4,5},{5,6},{6,7},{7,4},{8,9},{9,10},{10,1... | collective-permute-start | bytes 442376 | tf_op jit(solution)/shard_map/ppermute | solution.py:311
  398.6 126.1 %collective-permute-start.19 = (bf16[1,192,384]{2,0,1:T(2,128)(2,1)}, bf16[1,192,384]{2,0,1:T(2,128)(2,1)}, u32[]{:S(2)}, u32[]{:S(2)}) collective-permute-start(bf16[1,192,384]{2,0,1:T(2,128)(2,1)} %get-tuple-element.612), channel_id=1, source_target_pairs={{0,2},{1,3},{2,0},{3,1},{4,6},{5,7},{6,4},{7,5},{8,10},{9,11},{10,... | collective-permute-start | bytes 442376 | tf_op jit(solution)/shard_map/ppermute | solution.py:311
  463.3 67.3 %collective-permute-start.20 = (bf16[1,192,384]{2,0,1:T(2,128)(2,1)}, bf16[1,192,384]{2,0,1:T(2,128)(2,1)}, u32[]{:S(2)}, u32[]{:S(2)}) collective-permute-start(bf16[1,192,384]{2,0,1:T(2,128)(2,1)} %get-tuple-element.611), channel_id=1, source_target_pairs={{0,3},{1,0},{2,1},{3,2},{4,7},{5,4},{6,5},{7,6},{8,11},{9,8},{10,9... | collective-permute-start | bytes 442376 | tf_op jit(solution)/shard_map/ppermute | solution.py:311
  465.7 179.6 %collective-permute-start.21 = (bf16[1,384,384]{2,1,0:T(8,128)(2,1)}, bf16[1,384,384]{2,1,0:T(8,128)(2,1)}, u32[]{:S(2)}, u32[]{:S(2)}) collective-permute-start(bf16[1,384,384]{2,1,0:T(8,128)(2,1)} %bitcast.52), channel_id=1, source_target_pairs={{0,1},{1,2},{2,3},{3,0},{4,5},{5,6},{6,7},{7,4},{8,9},{9,10},{10,1... | collective-permute-start | bytes 884744 | tf_op jit(solution)/shard_map/ppermute | solution.py:311
  466.8 180.5 %collective-permute-start.22 = (bf16[1,384,384]{2,1,0:T(8,128)(2,1)}, bf16[1,384,384]{2,1,0:T(8,128)(2,1)}, u32[]{:S(2)}, u32[]{:S(2)}) collective-permute-start(bf16[1,384,384]{2,1,0:T(8,128)(2,1)} %bitcast.53), channel_id=1, source_target_pairs={{0,2},{1,3},{2,0},{3,1},{4,6},{5,7},{6,4},{7,5},{8,10},{9,11},{10,... | collective-permute-start | bytes 884744 | tf_op jit(solution)/shard_map/ppermute | solution.py:311
  515.1 121.2 %collective-permute-start.24 = (bf16[1,384,384]{2,1,0:T(8,128)(2,1)}, bf16[1,384,384]{2,1,0:T(8,128)(2,1)}, u32[]{:S(2)}, u32[]{:S(2)}) collective-permute-start(bf16[1,384,384]{2,1,0:T(8,128)(2,1)} %get-tuple-element.573), channel_id=1, source_target_pairs={{0,1},{1,2},{2,3},{3,0},{4,5},{5,6},{6,7},{7,4},{8,9},{9,10},{10,1... | collective-permute-start | bytes 884744 | tf_op jit(solution)/shard_map/ppermute | solution.py:311
  524.7 115.5 %collective-permute-start.25 = (bf16[1,384,384]{2,1,0:T(8,128)(2,1)}, bf16[1,384,384]{2,1,0:T(8,128)(2,1)}, u32[]{:S(2)}, u32[]{:S(2)}) collective-permute-start(bf16[1,384,384]{2,1,0:T(8,128)(2,1)} %get-tuple-element.572), channel_id=1, source_target_pairs={{0,2},{1,3},{2,0},{3,1},{4,6},{5,7},{6,4},{7,5},{8,10},{9,11},{10,... | collective-permute-start | bytes 884744 | tf_op jit(solution)/shard_map/ppermute | solution.py:311
  530.6 111.3 %collective-permute-start.26 = (bf16[1,384,384]{2,1,0:T(8,128)(2,1)}, bf16[1,384,384]{2,1,0:T(8,128)(2,1)}, u32[]{:S(2)}, u32[]{:S(2)}) collective-permute-start(bf16[1,384,384]{2,1,0:T(8,128)(2,1)} %get-tuple-element.571), channel_id=1, source_target_pairs={{0,3},{1,0},{2,1},{3,2},{4,7},{5,4},{6,5},{7,6},{8,11},{9,8},{10,9... | collective-permute-start | bytes 884744 | tf_op jit(solution)/shard_map/ppermute | solution.py:311
  636.3 12.7 collective-permute-start.23
  1107.7 188.6 %collective-permute-start.57 = (bf16[1,192,384]{2,1,0:T(8,128)(2,1)}, bf16[1,192,384]{2,1,0:T(8,128)(2,1)}, u32[]{:S(2)}, u32[]{:S(2)}) collective-permute-start(bf16[1,192,384]{2,1,0:T(8,128)(2,1)} %bitcast.500), channel_id=1, source_target_pairs={{0,1},{1,2},{2,3},{3,0},{4,5},{5,6},{6,7},{7,4},{8,9},{9,10},{10,1... | collective-permute-start | bytes 442376 | tf_op jit(solution)/shard_map/ppermute | solution.py:311
  1109.2 187.1 %collective-permute-start.58 = (bf16[1,192,384]{2,1,0:T(8,128)(2,1)}, bf16[1,192,384]{2,1,0:T(8,128)(2,1)}, u32[]{:S(2)}, u32[]{:S(2)}) collective-permute-start(bf16[1,192,384]{2,1,0:T(8,128)(2,1)} %bitcast.499), channel_id=1, source_target_pairs={{0,2},{1,3},{2,0},{3,1},{4,6},{5,7},{6,4},{7,5},{8,10},{9,11},{10,... | collective-permute-start | bytes 442376 | tf_op jit(solution)/shard_map/ppermute | solution.py:311
  1111.4 189.1 %collective-permute-start.59 = (bf16[1,192,384]{2,1,0:T(8,128)(2,1)}, bf16[1,192,384]{2,1,0:T(8,128)(2,1)}, u32[]{:S(2)}, u32[]{:S(2)}) collective-permute-start(bf16[1,192,384]{2,1,0:T(8,128)(2,1)} %bitcast.498), channel_id=1, source_target_pairs={{0,3},{1,0},{2,1},{3,2},{4,7},{5,4},{6,5},{7,6},{8,11},{9,8},{10,9... | collective-permute-start | bytes 442376 | tf_op jit(solution)/shard_map/ppermute | solution.py:311
  1115.9 127.2 %collective-permute-start.53 = (bf16[1,384,192]{1,2,0:T(8,128)(2,1)}, bf16[1,384,192]{1,2,0:T(8,128)(2,1)}, u32[]{:S(2)}, u32[]{:S(2)}) collective-permute-start(bf16[1,384,192]{1,2,0:T(8,128)(2,1)} %copy.1422), channel_id=1, source_target_pairs={{0,1},{1,2},{2,3},{3,0},{4,5},{5,6},{6,7},{7,4},{8,9},{9,10},{10,1... | collective-permute-start | bytes 442376 | tf_op jit(solution)/shard_map/ppermute | solution.py:311
  1191.3 39.9 %collective-permute-start.27 = (bf16[1,128,384]{2,1,0:T(8,128)(2,1)}, bf16[1,128,384]{2,1,0:T(8,128)(2,1)}, u32[]{:S(2)}, u32[]{:S(2)}) collective-permute-start(bf16[1,128,384]{2,1,0:T(8,128)(2,1)} %bitcast.508), channel_id=1, source_target_pairs={{0,1},{1,2},{2,3},{3,0},{4,5},{5,6},{6,7},{7,4},{8,9},{9,10},{10,1... | collective-permute-start | bytes 294920 | tf_op jit(solution)/shard_map/ppermute | solution.py:311
  1203.4 326.1 %all-reduce.41.cloned.1.call-start = ((), (), s32[]{:S(2)}) async-start(), calls=%async_computation | async-start | bytes 3735552 | tf_op jit(solution)/shard_map/psum | solution.py:599
  1243.1 9.3 collective-permute-start.54
  1243.2 10.6 collective-permute-start.55
  1252.4 8.9 collective-permute-start.49
  1253.8 13.5 collective-permute-start.50
  1269.4 12.0 collective-permute-start.46
  1283.0 12.4 collective-permute-start.38
  1289.8 12.8 collective-permute-start.39
  1295.3 8.8 collective-permute-start.33
  1296.3 25.4 %collective-permute-start.41 = (bf16[1,192,384]{2,1,0:T(8,128)(2,1)}, bf16[1,192,384]{2,1,0:T(8,128)(2,1)}, u32[]{:S(2)}, u32[]{:S(2)}) collective-permute-start(bf16[1,192,384]{2,1,0:T(8,128)(2,1)} %bitcast.504), channel_id=1, source_target_pairs={{0,1},{1,2},{2,3},{3,0},{4,5},{5,6},{6,7},{7,4},{8,9},{9,10},{10,1... | collective-permute-start | bytes 442376 | tf_op jit(solution)/shard_map/ppermute | solution.py:311
  1296.3 33.7 %collective-permute-start.42 = (bf16[1,192,384]{2,1,0:T(8,128)(2,1)}, bf16[1,192,384]{2,1,0:T(8,128)(2,1)}, u32[]{:S(2)}, u32[]{:S(2)}) collective-permute-start(bf16[1,192,384]{2,1,0:T(8,128)(2,1)} %bitcast.503), channel_id=1, source_target_pairs={{0,2},{1,3},{2,0},{3,1},{4,6},{5,7},{6,4},{7,5},{8,10},{9,11},{10,... | collective-permute-start | bytes 442376 | tf_op jit(solution)/shard_map/ppermute | solution.py:311
  1300.4 39.5 %collective-permute-start.43 = (bf16[1,192,384]{2,1,0:T(8,128)(2,1)}, bf16[1,192,384]{2,1,0:T(8,128)(2,1)}, u32[]{:S(2)}, u32[]{:S(2)}) collective-permute-start(bf16[1,192,384]{2,1,0:T(8,128)(2,1)} %bitcast.502), channel_id=1, source_target_pairs={{0,3},{1,0},{2,1},{3,2},{4,7},{5,4},{6,5},{7,6},{8,11},{9,8},{10,9... | collective-permute-start | bytes 442376 | tf_op jit(solution)/shard_map/ppermute | solution.py:311
  1302.6 46.3 %collective-permute-start.34 = (bf16[1,384,192]{1,2,0:T(8,128)(2,1)}, bf16[1,384,192]{1,2,0:T(8,128)(2,1)}, u32[]{:S(2)}, u32[]{:S(2)}) collective-permute-start(bf16[1,384,192]{1,2,0:T(8,128)(2,1)} %copy.1403), channel_id=1, source_target_pairs={{0,2},{1,3},{2,0},{3,1},{4,6},{5,7},{6,4},{7,5},{8,10},{9,11},{10,... | collective-permute-start | bytes 442376 | tf_op jit(solution)/shard_map/ppermute | solution.py:311
  1304.1 47.2 %collective-permute-start.35 = (bf16[1,384,192]{1,2,0:T(8,128)(2,1)}, bf16[1,384,192]{1,2,0:T(8,128)(2,1)}, u32[]{:S(2)}, u32[]{:S(2)}) collective-permute-start(bf16[1,384,192]{1,2,0:T(8,128)(2,1)} %copy.1404), channel_id=1, source_target_pairs={{0,3},{1,0},{2,1},{3,2},{4,7},{5,4},{6,5},{7,6},{8,11},{9,8},{10,9... | collective-permute-start | bytes 442376 | tf_op jit(solution)/shard_map/ppermute | solution.py:311
  1321.7 51.8 %collective-permute-start.65 = (bf16[1,384,384]{2,1,0:T(8,128)(2,1)}, bf16[1,384,384]{2,1,0:T(8,128)(2,1)}, u32[]{:S(2)}, u32[]{:S(2)}) collective-permute-start(bf16[1,384,384]{2,1,0:T(8,128)(2,1)} %bitcast.659), channel_id=1, source_target_pairs={{0,1},{1,2},{2,3},{3,0},{4,5},{5,6},{6,7},{7,4},{8,9},{9,10},{10,1... | collective-permute-start | bytes 884744 | tf_op jit(solution)/shard_map/ppermute | solution.py:311
  1330.1 45.9 %collective-permute-start.66 = (bf16[1,384,384]{2,1,0:T(8,128)(2,1)}, bf16[1,384,384]{2,1,0:T(8,128)(2,1)}, u32[]{:S(2)}, u32[]{:S(2)}) collective-permute-start(bf16[1,384,384]{2,1,0:T(8,128)(2,1)} %bitcast.658), channel_id=1, source_target_pairs={{0,2},{1,3},{2,0},{3,1},{4,6},{5,7},{6,4},{7,5},{8,10},{9,11},{10,... | collective-permute-start | bytes 884744 | tf_op jit(solution)/shard_map/ppermute | solution.py:311
  1340.0 37.8 %collective-permute-start.67 = (bf16[1,384,384]{2,1,0:T(8,128)(2,1)}, bf16[1,384,384]{2,1,0:T(8,128)(2,1)}, u32[]{:S(2)}, u32[]{:S(2)}) collective-permute-start(bf16[1,384,384]{2,1,0:T(8,128)(2,1)} %bitcast.657), channel_id=1, source_target_pairs={{0,3},{1,0},{2,1},{3,2},{4,7},{5,4},{6,5},{7,6},{8,11},{9,8},{10,9... | collective-permute-start | bytes 884744 | tf_op jit(solution)/shard_map/ppermute | solution.py:311
  1351.4 15.0 collective-permute-start.31
  1357.2 12.5 collective-permute-start.32
  1366.3 17.0 %collective-permute-start.61 = (bf16[1,384,384]{2,1,0:T(8,128)(2,1)}, bf16[1,384,384]{2,1,0:T(8,128)(2,1)S(1)}, u32[]{:S(2)}, u32[]{:S(2)}) collective-permute-start(bf16[1,384,384]{2,1,0:T(8,128)(2,1)} %get-tuple-element.565), channel_id=1, source_target_pairs={{0,1},{1,2},{2,3},{3,0},{4,5},{5,6},{6,7},{7,4},{8,9},{9,10},{10,1... | collective-permute-start | bytes 884744 | tf_op jit(solution)/shard_map/ppermute | solution.py:311
  1369.7 26.8 %collective-permute-start.62 = (bf16[1,384,384]{2,1,0:T(8,128)(2,1)}, bf16[1,384,384]{2,1,0:T(8,128)(2,1)S(1)}, u32[]{:S(2)}, u32[]{:S(2)}) collective-permute-start(bf16[1,384,384]{2,1,0:T(8,128)(2,1)} %get-tuple-element.564), channel_id=1, source_target_pairs={{0,2},{1,3},{2,0},{3,1},{4,6},{5,7},{6,4},{7,5},{8,10},{9,11},{10,... | collective-permute-start | bytes 884744 | tf_op jit(solution)/shard_map/ppermute | solution.py:311
  1373.5 23.0 %collective-permute-start.63 = (bf16[1,384,384]{2,1,0:T(8,128)(2,1)}, bf16[1,384,384]{2,1,0:T(8,128)(2,1)S(1)}, u32[]{:S(2)}, u32[]{:S(2)}) collective-permute-start(bf16[1,384,384]{2,1,0:T(8,128)(2,1)} %get-tuple-element.563), channel_id=1, source_target_pairs={{0,3},{1,0},{2,1},{3,2},{4,7},{5,4},{6,5},{7,6},{8,11},{9,8},{10,9... | collective-permute-start | bytes 884744 | tf_op jit(solution)/shard_map/ppermute | solution.py:311
  1376.0 22.7 %collective-permute-start.56 = (bf16[4,384,192]{1,2,0:T(8,128)(2,1)S(1)}, bf16[4,384,192]{1,2,0:T(8,128)(2,1)S(1)}, u32[]{:S(2)}, u32[]{:S(2)}) collective-permute-start(bf16[4,384,192]{1,2,0:T(8,128)(2,1)S(1)} %constant_dynamic-update-slice_fusion.6), channel_id=1, source_target_pairs={{0,16},{16,0},{1,17},{17,1},{2,18},{18,2},{3,19},{19,3},{4,20},{20... | collective-permute-start | bytes 1769480 | tf_op jit(solution)/shard_map/ppermute | solution.py:340
  1377.7 29.5 %collective-permute-start.60 = (bf16[4,192,384]{2,0,1:T(4,128)(2,1)S(1)}, bf16[4,192,384]{2,0,1:T(4,128)(2,1)S(1)}, u32[]{:S(2)}, u32[]{:S(2)}) collective-permute-start(bf16[4,192,384]{2,0,1:T(4,128)(2,1)S(1)} %dynamic_update_slice.373), channel_id=1, source_target_pairs={{0,16},{16,0},{1,17},{17,1},{2,18},{18,2},{3,19},{19,3},{4,20},{20... | collective-permute-start | bytes 1769480 | tf_op jit(solution)/shard_map/ppermute | solution.py:340
  1383.4 37.8 %collective-permute-start.52 = (bf16[4,384,192]{1,2,0:T(8,128)(2,1)S(1)}, bf16[4,384,192]{1,2,0:T(8,128)(2,1)S(1)}, u32[]{:S(2)}, u32[]{:S(2)}) collective-permute-start(bf16[4,384,192]{1,2,0:T(8,128)(2,1)S(1)} %constant_dynamic-update-slice_fusion.9), channel_id=1, source_target_pairs={{0,16},{16,0},{1,17},{17,1},{2,18},{18,2},{3,19},{19,3},{4,20},{20... | collective-permute-start | bytes 1769480 | tf_op jit(solution)/shard_map/ppermute | solution.py:340
  1396.5 37.4 %collective-permute-start.48 = (bf16[4,384,192]{1,2,0:T(8,128)(2,1)}, bf16[4,384,192]{1,2,0:T(8,128)(2,1)S(1)}, u32[]{:S(2)}, u32[]{:S(2)}) collective-permute-start(bf16[4,384,192]{1,2,0:T(8,128)(2,1)} %constant_dynamic-update-slice_fusion.12), channel_id=1, source_target_pairs={{0,16},{16,0},{1,17},{17,1},{2,18},{18,2},{3,19},{19,3},{4,20},{20... | collective-permute-start | bytes 1769480 | tf_op jit(solution)/shard_map/ppermute | solution.py:340
  1396.6 50.4 %collective-permute-start.44 = (bf16[4,192,384]{2,0,1:T(4,128)(2,1)}, bf16[4,192,384]{2,0,1:T(4,128)(2,1)}, u32[]{:S(2)}, u32[]{:S(2)}) collective-permute-start(bf16[4,192,384]{2,0,1:T(4,128)(2,1)} %dynamic_update_slice.357), channel_id=1, source_target_pairs={{0,16},{16,0},{1,17},{17,1},{2,18},{18,2},{3,19},{19,3},{4,20},{20... | collective-permute-start | bytes 1769480 | tf_op jit(solution)/shard_map/ppermute | solution.py:340
  1398.7 61.3 %collective-permute-start.40 = (bf16[4,384,192]{1,2,0:T(8,128)(2,1)}, bf16[4,384,192]{1,2,0:T(8,128)(2,1)}, u32[]{:S(2)}, u32[]{:S(2)}) collective-permute-start(bf16[4,384,192]{1,2,0:T(8,128)(2,1)} %constant_dynamic-update-slice_fusion.15), channel_id=1, source_target_pairs={{0,16},{16,0},{1,17},{17,1},{2,18},{18,2},{3,19},{19,3},{4,20},{20... | collective-permute-start | bytes 1769480 | tf_op jit(solution)/shard_map/ppermute | solution.py:340
  1407.2 66.6 %collective-permute-start.36 = (bf16[4,384,192]{1,2,0:T(8,128)(2,1)}, bf16[4,384,192]{1,2,0:T(8,128)(2,1)}, u32[]{:S(2)}, u32[]{:S(2)}) collective-permute-start(bf16[4,384,192]{1,2,0:T(8,128)(2,1)} %constant_dynamic-update-slice_fusion.18), channel_id=1, source_target_pairs={{0,16},{16,0},{1,17},{17,1},{2,18},{18,2},{3,19},{19,3},{4,20},{20... | collective-permute-start | bytes 1769480 | tf_op jit(solution)/shard_map/ppermute | solution.py:340
  1421.2 81.7 %collective-permute-start.64 = (bf16[4,384,384]{2,1,0:T(8,128)(2,1)S(1)}, bf16[4,384,384]{2,1,0:T(8,128)(2,1)}, u32[]{:S(2)}, u32[]{:S(2)}) collective-permute-start(bf16[4,384,384]{2,1,0:T(8,128)(2,1)S(1)} %constant_dynamic-update-slice_fusion.3), channel_id=1, source_target_pairs={{0,16},{16,0},{1,17},{17,1},{2,18},{18,2},{3,19},{19,3},{4,20},{20... | collective-permute-start | bytes 3538952 | tf_op jit(solution)/shard_map/ppermute | solution.py:340
  1433.9 92.2 %collective-permute-start.68 = (bf16[4,384,384]{2,1,0:T(8,128)(2,1)}, bf16[4,384,384]{2,1,0:T(8,128)(2,1)}, u32[]{:S(2)}, u32[]{:S(2)}) collective-permute-start(bf16[4,384,384]{2,1,0:T(8,128)(2,1)} %constant_dynamic-update-slice_fusion), channel_id=1, source_target_pairs={{0,16},{16,0},{1,17},{17,1},{2,18},{18,2},{3,19},{19,3},{4,20},{20... | collective-permute-start | bytes 3538952 | tf_op jit(solution)/shard_map/ppermute | solution.py:340
  (315 other events, 5403.3 us)
Sparse Core Ops, SparseCore 0:
  1203.5 141.4 all-reduce.42
  1351.8 160.0 all-reduce.40

commit v2 on v1

v2 whole, which is shorter than its diff:
```python
import functools
import jax, jax.numpy as jnp
from jax import lax
from jax.experimental import pallas as pl
from jax.experimental.pallas import tpu as pltpu
MESH = pl.DeviceIdType.MESH
NC = 4
F32, BF = jnp.float32, jnp.bfloat16


def copy_to(src, dst, send, recv, dev):
    return pltpu.make_async_remote_copy(src_ref=src, dst_ref=dst, send_sem=send, recv_sem=recv, device_id=dev, device_id_type=MESH)


def greet(r, c, kinds=()):
    barrier = pltpu.get_barrier_semaphore()
    all_cols = any(kind != "dp" for kind in kinds)
    pl.semaphore_signal(barrier, inc=1, device_id={"rows": r ^ 1}, device_id_type=MESH)
    pl.semaphore_signal(barrier, inc=1, device_id={"rows": r ^ 2}, device_id_type=MESH)
    count = 2
    if all_cols:
        for s in range(1, NC):
            pl.semaphore_signal(barrier, inc=1, device_id={"cols": lax.rem(c + s, NC)}, device_id_type=MESH)
        count += NC - 1
    else:
        @pl.when(c > 0)
        def _():
            pl.semaphore_signal(barrier, inc=1, device_id={"cols": c - 1}, device_id_type=MESH)

        @pl.when(c < NC - 1)
        def _():
            pl.semaphore_signal(barrier, inc=1, device_id={"cols": c + 1}, device_id_type=MESH)
        count = count + jnp.where(c > 0, 1, 0) + jnp.where(c < NC - 1, 1, 0)
    if "dp" in kinds or "swap2" in kinds:
        groups = lax.axis_size("dp")
        for s in range(1, groups):
            pl.semaphore_signal(barrier, inc=1, device_id={"dp": lax.rem(lax.axis_index("dp") + s, groups)}, device_id_type=MESH)
        count = count + groups - 1
    pl.semaphore_wait(barrier, count)


def riders(kinds, ins, outs, send, recv, loc):
    r, c, g = lax.axis_index("rows"), lax.axis_index("cols"), lax.axis_index("dp")
    groups = lax.axis_size("dp")
    remote, local, late = [], [], []
    for e, kind in enumerate(kinds):
        src, dst = ins[e], outs[e]
        if kind == "dp":
            for s in range(1, groups):
                remote.append(copy_to(src, dst.at[s - 1], send.at[e, s - 1], recv.at[e, s - 1], {"dp": lax.rem(g + s, groups)}))
        elif kind == "swap":
            for s in range(1, NC):
                to = lax.rem(c + s, NC)
                remote.append(copy_to(src.at[to], dst.at[c], send.at[e, s - 1], recv.at[e, s - 1], {"cols": to}))
            local.append(pltpu.make_async_copy(src.at[c], dst.at[c], loc.at[e]))
        else:
            half = g if kind == "swap2" else r & 1
            other = {"dp": 1 - g} if kind == "swap2" else {"rows": r ^ 1}
            for s in range(1, NC):
                to, came = lax.rem(c + s, NC), lax.rem(c + NC - s, NC)
                first = copy_to(src.at[to, half] if kind == "swap2" else src.at[half], dst.at[c, half],
                                send.at[e, s - 1], recv.at[e, s - 1], {"cols": to})
                late.append((first, copy_to(dst.at[came, half], dst.at[came, half], send.at[e, NC + s - 1], recv.at[e, NC + s - 1], other)))
            if kind == "swap2":
                local.append(pltpu.make_async_copy(src.at[c], dst.at[c], loc.at[e]))
            else:
                local.append(pltpu.make_async_copy(src, dst.at[c], loc.at[e]))

    def start():
        for first, _ in late:
            first.start()
        for one in remote + local:
            one.start()

    def finish():
        for first, second in late:
            first.wait_recv()
            second.start()
        for one in remote + local:
            one.wait()
        for first, second in late:
            first.wait_send()
            second.wait()
    return start, finish


def rider_parts(kinds, arrays):
    groups = lax.axis_size("dp")
    shapes = []
    for kind, a in zip(kinds, arrays):
        lead = {"swap": (), "swap2": (), "bcast2": (NC,), "dp": (groups - 1,)}[kind]
        shapes.append(jax.ShapeDtypeStruct(lead + a.shape, a.dtype))
    n, most = len(kinds), max(2 * NC, groups)
    sems = [pltpu.SemaphoreType.DMA((n, most)), pltpu.SemaphoreType.DMA((n, most)), pltpu.SemaphoreType.DMA((n,))] if n else []
    return shapes, sems


SMALL = 96


def sum_groups(x_ref, others, held, dp_s, dp_r, n):
    g, groups = lax.axis_index("dp"), lax.axis_size("dp")
    copies = [copy_to(x_ref, others.at[s - 1], dp_s.at[s - 1], dp_r.at[s - 1], {"dp": lax.rem(g + s, groups)}) for s in range(1, groups)]
    for one in copies:
        one.start()
    total = x_ref[...]
    for s, one in enumerate(copies):
        one.wait()
        total = total + others[s]
    part = (lax.broadcasted_iota(jnp.int32, total.shape, 0) - SMALL) // n
    rest = total - total.astype(BF).astype(F32)
    rest2 = rest - rest.astype(BF).astype(F32)
    second, third = (part == 1) | (part == 4), (part == 2) | (part == 5)
    held[...] = jnp.where(second, rest, jnp.where(third, rest2, total)).astype(BF)
    return held


def ag_kernel(native, total, at, kinds, *refs):
    n = len(kinds)
    x_ref, ins, out_ref, outs = refs[0], refs[1:1 + n], refs[1 + n], refs[2 + n:2 + 2 * n]
    recv, zr_s, zl_s, y_s, k_s, loc, *sems = refs[2 + 2 * n:]
    r, c = lax.axis_index("rows"), lax.axis_index("cols")
    S, W = x_ref.shape
    greet(r, c, kinds)
    if total:
        others, held, dp_s, dp_r, *sems = sems
    ride, alight = riders(kinds, ins, outs, *sems) if n else (lambda: None, lambda: None)
    if total:
        x_ref = sum_groups(x_ref, others, held, dp_s, dp_r, total)

    def slab(rr, cc):
        if native:
            return out_ref.at[pl.ds(pl.multiple_of(rr * S, 16), S), pl.ds(pl.multiple_of(cc * W, 128), W)]
        return out_ref.at[pl.ds(pl.multiple_of((rr * NC + cc) * S, 16), S)]

    def right(cc, src):
        return copy_to(src, slab(r, cc), zr_s.at[cc], recv.at[r * NC + cc], {"cols": c + 1})

    def left(cc, src):
        return copy_to(src, slab(r, cc), zl_s.at[cc], recv.at[r * NC + cc], {"cols": c - 1})

    def ycopy(cc, src):
        return copy_to(src, slab(r, cc), y_s.at[cc], recv.at[r * NC + cc], {"rows": r ^ 2})

    def kcopy(rr, cc, src):
        return copy_to(src, slab(rr, cc), k_s.at[(rr >> 1) * NC + cc], recv.at[rr * NC + cc], {"rows": r ^ 1})

    def got(rr, cc):
        copy_to(slab(rr, cc), slab(rr, cc), k_s.at[0], recv.at[rr * NC + cc], {"rows": r ^ 1}).wait_recv()

    @pl.when(c < NC - 1)
    def _():
        right(c, x_ref).start()

    @pl.when(c > 0)
    def _():
        left(c, x_ref).start()
    ycopy(c, x_ref).start()
    kcopy(r, c, x_ref).start()
    own = pltpu.make_async_copy(x_ref, slab(r, c), loc)
    own.start()
    if at == 0:
        ride()

    def from_y(cc):
        got(r ^ 2, cc)
        kcopy(r ^ 2, cc, slab(r ^ 2, cc)).start()

    for d in range(1, NC):
        @pl.when(c >= d)
        def _():
            cc = c - d
            got(r, cc)

            @pl.when(c < NC - 1)
            def _():
                right(cc, slab(r, cc)).start()
            ycopy(cc, slab(r, cc)).start()
            kcopy(r, cc, slab(r, cc)).start()

        @pl.when(c + d < NC)
        def _():
            cc = c + d
            got(r, cc)

            @pl.when(c > 0)
            def _():
                left(cc, slab(r, cc)).start()
            ycopy(cc, slab(r, cc)).start()
            kcopy(r, cc, slab(r, cc)).start()
        if d == at:
            ride()
        if d == 1:
            from_y(c)
        else:
            @pl.when(c >= d - 1)
            def _():
                from_y(c - (d - 1))

            @pl.when(c + d - 1 < NC)
            def _():
                from_y(c + d - 1)
    d = NC

    @pl.when(c >= d - 1)
    def _():
        from_y(c - (d - 1))

    @pl.when(c + d - 1 < NC)
    def _():
        from_y(c + d - 1)
    for cc in range(NC):
        got(r ^ 1, cc)
        got(r ^ 3, cc)
    own.wait()
    for cc in range(NC):
        y_c = ycopy(cc, slab(r, cc))
        y_c.wait_send()
        kcopy(r, cc, slab(r, cc)).wait_send()
        kcopy(r ^ 2, cc, slab(r ^ 2, cc)).wait_send()

        @pl.when((cc <= c) & (c < NC - 1))
        def _():
            right(cc, slab(r, cc)).wait_send()

        @pl.when((cc >= c) & (c > 0))
        def _():
            left(cc, slab(r, cc)).wait_send()
    alight()


def gather16(x, cid, native, kinds, arrays, total=0, at=0):
    S, D = x.shape
    shapes, sems = rider_parts(kinds, arrays)
    if total:
        groups = lax.axis_size("dp")
        sems = [pltpu.VMEM((groups - 1, S, D), F32), pltpu.VMEM((S, D), BF), pltpu.SemaphoreType.DMA((groups - 1,)),
                pltpu.SemaphoreType.DMA((groups - 1,))] + sems
    any_space = pl.BlockSpec(memory_space=pl.ANY)
    return pl.pallas_call(
        functools.partial(ag_kernel, native, total, at, tuple(kinds)),
        out_shape=[jax.ShapeDtypeStruct((4 * S, NC * D) if native else (16 * S, D), BF)] + shapes,
        in_specs=[pl.BlockSpec(memory_space=pltpu.VMEM)] + [any_space] * len(kinds),
        out_specs=[pl.BlockSpec(memory_space=pltpu.VMEM)] + [any_space] * len(kinds),
        scratch_shapes=[pltpu.SemaphoreType.DMA((16,)), pltpu.SemaphoreType.DMA((NC,)), pltpu.SemaphoreType.DMA((NC,)),
                        pltpu.SemaphoreType.DMA((NC,)), pltpu.SemaphoreType.DMA((2 * NC,)), pltpu.SemaphoreType.DMA] + sems,
        compiler_params=pltpu.CompilerParams(collective_id=cid, has_side_effects=True, vmem_limit_bytes=48 << 20),
        cost_estimate=pl.CostEstimate(flops=0, bytes_accessed=64 << 20, transcendentals=0),
    )(x, *arrays)


def all_gather16(x, cid, kinds=(), arrays=()):
    return gather16(x, cid, False, kinds, arrays, 0, 3)


def gather_native(x, cid, kinds=(), arrays=()):
    return gather16(x, cid, True, kinds, arrays)


def rs_kernel(kinds, *refs):
    n = len(kinds)
    p_ref, ins, o_ref, outs = refs[0], refs[1:1 + n], refs[1 + n], refs[2 + n:2 + 2 * n]
    (k_buf, y_buf, l_buf, r_buf, y_out, zr_out, zl_out,
     k_s, k_r, y_s, y_r, zr_s, zr_r, zl_s, zl_r, *sems) = refs[2 + 2 * n:]
    r, c = lax.axis_index("rows"), lax.axis_index("cols")
    S, D = o_ref.shape
    yy, kk = r >> 1, r & 1
    greet(r, c, kinds)
    ride, alight = riders(kinds, ins, outs, *sems) if n else (lambda: None, lambda: None)

    def mine(rr, cc):
        return p_ref.at[pl.ds(pl.multiple_of((rr * NC + cc) * S, 16), S)]

    def kcopy(y2, cc):
        return copy_to(mine(y2 * 2 + (1 - kk), cc), k_buf.at[y2, cc], k_s.at[y2 * NC + cc], k_r.at[y2 * NC + cc], {"rows": r ^ 1})

    def ycopy(cc):
        return copy_to(y_out.at[cc], y_buf.at[cc], y_s.at[cc], y_r.at[cc], {"rows": r ^ 2})

    def rcopy(cc):
        return copy_to(zr_out.at[cc], r_buf.at[cc], zr_s.at[cc], zr_r.at[cc], {"cols": c + 1})

    def lcopy(cc):
        return copy_to(zl_out.at[cc], l_buf.at[cc], zl_s.at[cc], zl_r.at[cc], {"cols": c - 1})

    def order(f):
        for d in range(NC - 1, 0, -1):
            @pl.when(c + d < NC)
            def _():
                f(c + d)

            @pl.when(c >= d)
            def _():
                f(c - d)
        f(c)

    def start_k(cc):
        kcopy(1 - yy, cc).start()
    order(start_k)

    def start_k2(cc):
        kcopy(yy, cc).start()
    order(start_k2)
    ride()

    def do_y(cc):
        kcopy(1 - yy, cc).wait_recv()
        y_out[cc] = (mine((1 - yy) * 2 + kk, cc)[...].astype(F32) + k_buf[1 - yy, cc].astype(F32)).astype(BF)
        ycopy(cc).start()
    order(do_y)

    def partial(cc):
        kcopy(yy, cc).wait_recv()
        a = mine(r, cc)[...].astype(F32) + k_buf[yy, cc].astype(F32)
        ycopy(cc).wait_recv()
        return a + y_buf[cc].astype(F32)

    for d in range(NC - 1, 0, -1):
        @pl.when(c + d < NC)
        def _():
            cc = c + d
            a = partial(cc)
            zr_out[cc] = a.astype(BF)

            @pl.when(c > 0)
            def _():
                rcopy(cc).wait_recv()
                zr_out[cc] = (zr_out[cc].astype(F32) + r_buf[cc].astype(F32)).astype(BF)
            rcopy(cc).start()

        @pl.when(c >= d)
        def _():
            cc = c - d
            a = partial(cc)
            zl_out[cc] = a.astype(BF)

            @pl.when(c < NC - 1)
            def _():
                lcopy(cc).wait_recv()
                zl_out[cc] = (zl_out[cc].astype(F32) + l_buf[cc].astype(F32)).astype(BF)
            lcopy(cc).start()
    o_ref[...] = partial(c)

    @pl.when(c > 0)
    def _():
        rcopy(c).wait_recv()
        o_ref[...] += r_buf[c].astype(F32)

    @pl.when(c < NC - 1)
    def _():
        lcopy(c).wait_recv()
        o_ref[...] += l_buf[c].astype(F32)

    def fin(cc):
        kcopy(1 - yy, cc).wait_send()
        kcopy(yy, cc).wait_send()
        ycopy(cc).wait_send()
    order(fin)
    for d in range(NC - 1, 0, -1):
        @pl.when(c + d < NC)
        def _():
            rcopy(c + d).wait_send()

        @pl.when(c >= d)
        def _():
            lcopy(c - d).wait_send()
    alight()


def reduce_scatter16(p, cid, kinds=(), arrays=()):
    T, D = p.shape
    S = T // 16
    buf = lambda n: pltpu.VMEM((n, S, D), BF)
    sem = lambda n: pltpu.SemaphoreType.DMA((n,))
    shapes, sems = rider_parts(kinds, arrays)
    any_space = pl.BlockSpec(memory_space=pl.ANY)
    return pl.pallas_call(
        functools.partial(rs_kernel, tuple(kinds)),
        out_shape=[jax.ShapeDtypeStruct((S, D), F32)] + shapes,
        in_specs=[pl.BlockSpec(memory_space=pltpu.VMEM)] + [any_space] * len(kinds),
        out_specs=[pl.BlockSpec(memory_space=pltpu.VMEM)] + [any_space] * len(kinds),
        scratch_shapes=[pltpu.VMEM((2, NC, S, D), BF), buf(NC), buf(NC), buf(NC), buf(NC), buf(NC), buf(NC),
                        sem(8), sem(8), sem(4), sem(4), sem(4), sem(4), sem(4), sem(4)] + sems,
        compiler_params=pltpu.CompilerParams(collective_id=cid, has_side_effects=True, vmem_limit_bytes=56 << 20),
        cost_estimate=pl.CostEstimate(flops=0, bytes_accessed=64 << 20, transcendentals=0),
    )(p, *arrays)


HEAD_DIM = 64
STATE = 128
CONV = 4
SPAN = 256
HIGH = lax.Precision.HIGHEST
WIDE = 192
MIX = 2 * STATE + WIDE


def mm(a, b, ca=1, cb=0):
    return lax.dot_general(a.astype(BF), b.astype(BF), (((ca,), (cb,)), ((), ())), preferred_element_type=F32)


def exact(a, b, ca=1, cb=0):
    return lax.dot_general(a, b, (((ca,), (cb,)), ((), ())), preferred_element_type=F32, precision=HIGH)


def seg_at(place, l0, l1):
    return jnp.where(place < 0, -1, jnp.where(place >= l0, 1, 0) + jnp.where(place >= l0 + l1, 1, 0))


def sigmoid(x):
    return 1.0 / (1.0 + jnp.exp(-x))


def by_head(a, lane):
    return jnp.where(lane < HEAD_DIM, a[:, 0:1], jnp.where(lane < 2 * HEAD_DIM, a[:, 1:2], a[:, 2:3]))


def head_sums(a):
    i = lax.broadcasted_iota(jnp.int32, (WIDE, 128), 0)
    j = lax.broadcasted_iota(jnp.int32, (WIDE, 128), 1)
    return exact(a, jnp.where(i // HEAD_DIM == j, 1.0, 0.0).astype(F32))


class Block:
    def __init__(self, blk, lens, proj, before, cw, pv):
        self.l0, self.l1 = lens[0], lens[1]
        self.start = blk * SPAN
        v = proj[:, :MIX]
        self.place = self.start + lax.broadcasted_iota(jnp.int32, (SPAN, 1), 0)
        self.seg = seg_at(self.place, self.l0, self.l1)
        ext = jnp.concatenate([before[:, :MIX], v], axis=0)
        acc = cw[4:5] + cw[3:4] * v
        self.shifted = [v]
        for s in range(1, CONV):
            keep = jnp.where(seg_at(self.place - s, self.l0, self.l1) == self.seg, 1.0, 0.0)
            moved = ext[8 - s:8 - s + SPAN] * keep
            self.shifted.append(moved)
            acc = acc + cw[3 - s:4 - s] * moved
        self.acc = acc
        self.gate = sigmoid(acc)
        act = acc * self.gate
        self.b, self.c, self.x = act[:, :STATE], act[:, STATE:2 * STATE], act[:, 2 * STATE:]
        self.z = proj[:, MIX:MIX + WIDE]
        self.zs = sigmoid(self.z)
        self.raw = proj[:, MIX + WIDE:] + pv[2:3, :128]
        self.dt = jnp.maximum(self.raw, 0.0) + jnp.log1p(jnp.exp(-jnp.abs(self.raw)))
        self.rate = pv[3:4, :128] * self.dt
        i = lax.broadcasted_iota(jnp.int32, (SPAN, SPAN), 0)
        j = lax.broadcasted_iota(jnp.int32, (SPAN, SPAN), 1)
        self.low = jnp.where(j <= i, 1.0, 0.0).astype(F32)
        self.cum = exact(self.low, self.rate)
        self.cum_t = self.cum.T
        seg_row = seg_at(self.start + lax.broadcasted_iota(jnp.int32, (1, SPAN), 1), self.l0, self.l1)
        self.allowed = (j <= i) & (seg_row == self.seg)
        self.scores = mm(self.c, self.b, 1, 1)
        self.lane = lax.broadcasted_iota(jnp.int32, (SPAN, WIDE), 1)
        self.w = self.x * by_head(self.dt, self.lane)
        prior = seg_at(self.start - 1, self.l0, self.l1)
        last = seg_at(self.start + SPAN - 1, self.l0, self.l1)
        end = self.cum[SPAN - 1:SPAN]
        self.e = by_head(jnp.exp(self.cum), self.lane) * jnp.where(self.seg == prior, 1.0, 0.0)
        self.tail = by_head(jnp.exp(end - self.cum), self.lane) * jnp.where(self.seg == last, 1.0, 0.0)
        self.through = jnp.exp(end) * jnp.where(last == prior, 1.0, 0.0)
        row = lax.broadcasted_iota(jnp.int32, (WIDE, 1), 0)
        self.through_rows = jnp.where(row < HEAD_DIM, self.through[:, 0:1],
                                      jnp.where(row < 2 * HEAD_DIM, self.through[:, 1:2], self.through[:, 2:3]))

    def decay(self, h):
        return jnp.exp(jnp.where(self.allowed, self.cum[:, h:h + 1] - self.cum_t[h:h + 1, :], -1e30))

    def of_head(self, a, h):
        return jnp.where(self.lane // HEAD_DIM == h, a, 0.0)


def mixer_fwd_kernel(lens, proj, before, cw, pv, mixg, squares, y_out, states, state):
    blk = pl.program_id(0)

    @pl.when(blk == 0)
    def _():
        state[...] = jnp.zeros_like(state)
    k = Block(blk, lens, proj[...], before[...], cw[...], pv[...])
    s_in = state[...]
    states[0] = s_in
    y = mm(k.c, s_in, 1, 1) * k.e
    for h in range(3):
        y = y + mm(k.scores * k.decay(h), k.of_head(k.w, h))
    y = y + pv[1:2, :WIDE] * k.x
    state[...] = k.through_rows * s_in + mm(k.tail * k.w, k.b, 0, 0)
    y_out[...] = y
    gated = y * k.z * k.zs
    mixg[...] = (gated * pv[0:1, :WIDE]).astype(BF)
    squares[...] = jnp.broadcast_to(jnp.sum(gated * gated, axis=1, keepdims=True), squares.shape).astype(BF)


def mixer_bwd_kernel(lens, proj, before, cw, pv, y_ref, states, d_mix, extra, d_in, taps, rows, d_state, later):
    step = pl.program_id(0)
    blk = pl.num_programs(0) - 1 - step

    @pl.when(step == 0)
    def _():
        d_state[...] = jnp.zeros_like(d_state)
        later[...] = jnp.zeros_like(later)
        taps[...] = jnp.zeros_like(taps)
        rows[...] = jnp.zeros_like(rows)
    k = Block(blk, lens, proj[...], before[...], cw[...], pv[...])
    y, dm, s_in, ds = y_ref[...], d_mix[...], states[0], d_state[...]
    tilt = extra[:, 0:1].astype(F32) + extra[:, 64:65].astype(F32)
    silu_z = k.z * k.zs
    gated = y * silu_z
    d_gated = dm * pv[0:1, :WIDE] - gated * tilt
    d_z = d_gated * y * (k.zs * (1.0 + k.z * (1.0 - k.zs)))
    dy = d_gated * silu_z
    zeros = jnp.zeros((SPAN, 128), F32)
    lane = lax.broadcasted_iota(jnp.int32, (SPAN, 128), 1)
    top = lax.broadcasted_iota(jnp.int32, (128, SPAN), 0)
    d_cum, cols = zeros, jnp.zeros((128, SPAN), F32)
    d_scores = jnp.zeros((SPAN, SPAN), F32)
    dw = jnp.zeros((SPAN, WIDE), F32)
    for h in range(3):
        decay = k.decay(h)
        mixing = k.scores * decay
        dyh = k.of_head(dy, h).astype(BF)
        d_mixing = mm(dyh, k.w, 1, 1)
        d_scores = d_scores + d_mixing * decay
        moved = d_mixing * mixing
        d_cum = jnp.where(lane == h, jnp.sum(moved, axis=1, keepdims=True), d_cum)
        cols = jnp.where(top == h, jnp.sum(moved, axis=0, keepdims=True), cols)
        dw = dw + mm(mixing, dyh, 0, 0)
    e_dy, tail_w = k.e * dy, k.tail * k.w
    back = mm(k.b, ds, 1, 1)
    dw = dw + k.tail * back
    d_c = mm(d_scores, k.b) + mm(e_dy, s_in)
    d_b = mm(d_scores, k.c, 0, 0) + mm(tail_w, ds)
    through_state = mm(k.c, s_in, 1, 1) * k.e
    left = head_sums(tail_w * back)
    d_cum = d_cum - cols.T + head_sums(dy * through_state) - left
    own = jnp.sum(ds * s_in, axis=1, keepdims=True)
    of_row = lax.broadcasted_iota(jnp.int32, (WIDE, 128), 0) // HEAD_DIM
    own = jnp.sum(jnp.where(of_row == lax.broadcasted_iota(jnp.int32, (WIDE, 128), 1), own, 0.0), axis=0, keepdims=True)
    at_end = jnp.sum(left, axis=0, keepdims=True) + k.through * own
    is_last = lax.broadcasted_iota(jnp.int32, (SPAN, 128), 0) == SPAN - 1
    d_cum = d_cum + jnp.where(is_last, at_end, 0.0)
    d_rate = exact(k.low, d_cum, 0, 0)
    d_dt = head_sums(dw * k.x) + d_rate * pv[3:4, :128]
    d_raw = jnp.where(lane < 3, d_dt * sigmoid(k.raw), 0.0)
    d_x = dw * by_head(k.dt, k.lane) + pv[1:2, :WIDE] * dy
    d_pre = jnp.concatenate([d_b, d_c, d_x], axis=1) * (k.gate * (1.0 + k.acc * (1.0 - k.gate)))
    wide_rows = [jnp.sum(gated * dm, axis=0, keepdims=True), jnp.sum(dy * k.x, axis=0, keepdims=True)]
    thin_rows = [jnp.sum(d_raw, axis=0, keepdims=True), jnp.sum(d_rate * k.rate, axis=0, keepdims=True)]
    for i, one in enumerate(wide_rows):
        rows[i:i + 1, :WIDE] += one
    for i, one in enumerate(thin_rows):
        rows[2 + i:3 + i, :128] += one
    for s in range(CONV):
        taps[3 - s:4 - s] += jnp.sum(d_pre * k.shifted[s], axis=0, keepdims=True)
    taps[4:5] += jnp.sum(d_pre, axis=0, keepdims=True)
    ext = jnp.concatenate([d_pre, later[...]], axis=0)
    place = k.start + lax.broadcasted_iota(jnp.int32, (SPAN + 8, 1), 0)
    seg = seg_at(place, k.l0, k.l1)
    d_v = cw[3:4] * d_pre
    for s in range(1, CONV):
        keep = jnp.where(seg_at(place - s, k.l0, k.l1) == seg, 1.0, 0.0)
        d_v = d_v + cw[3 - s:4 - s] * (ext * keep)[s:s + SPAN]
    later[...] = d_pre[:8]
    d_in[...] = jnp.concatenate([d_v, d_z, d_raw], axis=1).astype(BF)
    d_state[...] = k.through_rows * ds + mm(e_dy, k.c, 0, 0)


def mixer_specs(n, order):
    block = lambda width: pl.BlockSpec((SPAN, width), lambda i: (order(i), 0))
    whole = lambda shape: pl.BlockSpec(shape, lambda i: (0, 0))
    before = pl.BlockSpec((8, MIX + WIDE + 128), lambda i: (jnp.maximum(order(i) * (SPAN // 8) - 1, 0), 0))
    return block, whole, [pl.BlockSpec(memory_space=pltpu.SMEM), block(MIX + WIDE + 128), before, whole((8, MIX)), whole((8, 256))]


def mixer_fwd(lens, proj, cw, pv):
    T = proj.shape[0]
    n = T // SPAN
    block, whole, first = mixer_specs(n, lambda i: i)
    return pl.pallas_call(
        mixer_fwd_kernel,
        grid=(n,),
        in_specs=first,
        out_specs=[block(WIDE), block(128), block(WIDE), pl.BlockSpec((1, WIDE, STATE), lambda i: (i, 0, 0))],
        out_shape=[jax.ShapeDtypeStruct((T, WIDE), BF), jax.ShapeDtypeStruct((T, 128), BF), jax.ShapeDtypeStruct((T, WIDE), F32),
                   jax.ShapeDtypeStruct((n, WIDE, STATE), F32)],
        scratch_shapes=[pltpu.VMEM((WIDE, STATE), F32)],
        compiler_params=pltpu.CompilerParams(vmem_limit_bytes=48 << 20, dimension_semantics=("arbitrary",)),
        cost_estimate=pl.CostEstimate(flops=4 << 30, bytes_accessed=16 << 20, transcendentals=4 << 20),
    )(lens, proj, proj, cw, pv)


def mixer_bwd(lens, proj, cw, pv, y, states, d_mix, g1_ext):
    T = proj.shape[0]
    n = T // SPAN
    order = lambda i: n - 1 - i
    block, whole, first = mixer_specs(n, order)
    at = g1_ext.shape[1] // 128 - 1
    return pl.pallas_call(
        mixer_bwd_kernel,
        grid=(n,),
        in_specs=first + [block(WIDE), pl.BlockSpec((1, WIDE, STATE), lambda i: (order(i), 0, 0)), block(WIDE),
                          pl.BlockSpec((SPAN, 128), lambda i: (order(i), at))],
        out_specs=[block(MIX + WIDE + 128), whole((8, MIX)), whole((8, 256))],
        out_shape=[jax.ShapeDtypeStruct((T, MIX + WIDE + 128), BF), jax.ShapeDtypeStruct((8, MIX), F32),
                   jax.ShapeDtypeStruct((8, 256), F32)],
        scratch_shapes=[pltpu.VMEM((WIDE, STATE), F32), pltpu.VMEM((8, MIX), F32)],
        compiler_params=pltpu.CompilerParams(vmem_limit_bytes=48 << 20, dimension_semantics=("arbitrary",)),
        cost_estimate=pl.CostEstimate(flops=12 << 30, bytes_accessed=24 << 20, transcendentals=8 << 20),
    )(lens, proj, proj, cw, pv, y, states, d_mix, g1_ext)


AHEAD_DIM = 64
SCALE = AHEAD_DIM ** (-0.5)
LOW = -1e30


def att_allowed(lens, i, j, n, flip):
    a, b = lax.broadcasted_iota(jnp.int32, (n, 1), 0), lax.broadcasted_iota(jnp.int32, (1, n), 1)
    qp, kp = (i * n + b, j * n + a) if flip else (i * n + a, j * n + b)
    return (kp <= qp) & (seg_at(kp, lens[0], lens[1]) == seg_at(qp, lens[0], lens[1]))


def att_fwd_kernel(lens, odd, qkv, attended, o_ref, lse):
    i = pl.program_id(0)
    n = o_ref.shape[0]
    lane = lax.broadcasted_iota(jnp.int32, (n, WIDE), 1)
    thin = lax.broadcasted_iota(jnp.int32, (n, 128), 1)
    mine = jnp.where((i == 0) | (i == 3), 0, 1) == odd[0]

    @pl.when(jnp.logical_not(mine))
    def _():
        attended[...] = jnp.zeros_like(attended)
        o_ref[...] = jnp.zeros_like(o_ref)
        lse[...] = jnp.zeros_like(lse)

    @pl.when(mine)
    def _():
        q = qkv[pl.ds(i * n, n), :WIDE] * jnp.asarray(SCALE, BF)
        heads = [jnp.where(lane // AHEAD_DIM == h, q, jnp.zeros_like(q)) for h in range(3)]

        def body(j, carry):
            tops, sums, acc = carry
            k, v = qkv[pl.ds(j * n, n), WIDE:2 * WIDE], qkv[pl.ds(j * n, n), 2 * WIDE:]
            allowed = att_allowed(lens, i, j, n, False)
            new_tops, new_sums = [], []
            for h in range(3):
                s = jnp.where(allowed, mm(heads[h], k, 1, 1), LOW)
                top = jnp.maximum(tops[h], jnp.max(s, axis=1, keepdims=True))
                p = jnp.exp(s - top)
                fade = jnp.exp(tops[h] - top)
                new_tops.append(top)
                new_sums.append(sums[h] * fade + jnp.sum(p, axis=1, keepdims=True))
                acc = jnp.where(lane // AHEAD_DIM == h, acc * fade + mm(p, v), acc)
            return tuple(new_tops), tuple(new_sums), acc

        zero = jnp.zeros((n, 1), F32)
        start = (tuple(zero + LOW for _ in range(3)), (zero,) * 3, jnp.zeros((n, WIDE), F32))
        tops, sums, acc = lax.fori_loop(0, i + 1, body, start)
        pick = lambda a: jnp.where(lane < AHEAD_DIM, a[0], jnp.where(lane < 2 * AHEAD_DIM, a[1], a[2]))
        out = acc / pick(sums)
        o_ref[...] = out
        attended[...] = out.astype(BF)
        logs = [t + jnp.log(s) for t, s in zip(tops, sums)]
        lse[...] = jnp.where(thin == 0, logs[0], jnp.where(thin == 1, logs[1], logs[2]))


def att_bwd_kernel(lens, odd, qkv, d_att, o_ref, lse, d_qkv, dk, dv):
    i = pl.program_id(0)
    n = lse.shape[0]
    lane = lax.broadcasted_iota(jnp.int32, (n, WIDE), 1)
    mine = jnp.where((i == 0) | (i == 3), 0, 1) == odd[0]

    @pl.when(i == 0)
    def _():
        dk[...] = jnp.zeros_like(dk)
        dv[...] = jnp.zeros_like(dv)

    @pl.when(jnp.logical_not(mine))
    def _():
        d_qkv[pl.ds(i * n, n), :WIDE] = jnp.zeros((n, WIDE), BF)

    @pl.when(mine)
    def _():
        q = qkv[pl.ds(i * n, n), :WIDE]
        do = d_att[...]
        delta = head_sums(o_ref[...] * do.astype(F32)).T
        logs = lse[...].T
        none = jnp.zeros_like(q)
        qs = [jnp.where(lane // AHEAD_DIM == h, q, none) for h in range(3)]
        dos = [jnp.where(lane // AHEAD_DIM == h, do, none) for h in range(3)]

        def body(j, dq):
            at = pl.ds(j * n, n)
            k, v = qkv[at, WIDE:2 * WIDE], qkv[at, 2 * WIDE:]
            allowed = att_allowed(lens, i, j, n, True)
            for h in range(3):
                s = mm(k, qs[h], 1, 1) * SCALE
                p = jnp.exp(jnp.where(allowed, s, LOW) - logs[h:h + 1])
                ds = (p * (mm(v, dos[h], 1, 1) - delta[h:h + 1]) * SCALE).astype(BF)
                dv[at, :] += mm(p, dos[h])
                dk[at, :] += mm(ds, qs[h])
                dq = jnp.where(lane // AHEAD_DIM == h, dq + mm(ds, k, 0, 0), dq)
            return dq

        dq = lax.fori_loop(0, i + 1, body, jnp.zeros((n, WIDE), F32))
        d_qkv[pl.ds(i * n, n), :WIDE] = dq.astype(BF)

    @pl.when(i == pl.num_programs(0) - 1)
    def _():
        d_qkv[:, WIDE:2 * WIDE] = dk[...].astype(BF)
        d_qkv[:, 2 * WIDE:] = dv[...].astype(BF)


def att_call(kernel, T, ins, blocked, out_specs, out_shape, scratch):
    n = T // 4
    smem = pl.BlockSpec(memory_space=pltpu.SMEM)
    specs = [smem, smem, pl.BlockSpec((T, 3 * WIDE), lambda i: (0, 0))]
    specs += [pl.BlockSpec((n, a.shape[1]), lambda i: (i, 0)) for a in blocked]
    return pl.pallas_call(
        kernel, grid=(4,), in_specs=specs, out_specs=out_specs, out_shape=out_shape, scratch_shapes=scratch,
        compiler_params=pltpu.CompilerParams(vmem_limit_bytes=56 << 20, dimension_semantics=("arbitrary",)),
        cost_estimate=pl.CostEstimate(flops=8 << 30, bytes_accessed=16 << 20, transcendentals=8 << 20),
    )(*ins, *blocked)


def att_fwd(lens, odd, qkv):
    T = qkv.shape[0]
    block = lambda w: pl.BlockSpec((T // 4, w), lambda i: (i, 0))
    return att_call(att_fwd_kernel, T, (lens, odd, qkv), (), [block(WIDE), block(WIDE), block(128)],
                    [jax.ShapeDtypeStruct((T, WIDE), BF), jax.ShapeDtypeStruct((T, WIDE), F32), jax.ShapeDtypeStruct((T, 128), F32)], [])


def att_bwd(lens, odd, qkv, d_att, o, lse):
    T = qkv.shape[0]
    return att_call(att_bwd_kernel, T, (lens, odd, qkv), (d_att, o, lse), pl.BlockSpec((T, 3 * WIDE), lambda i: (0, 0)),
                    jax.ShapeDtypeStruct((T, 3 * WIDE), BF), [pltpu.VMEM((T, WIDE), F32), pltpu.VMEM((T, WIDE), F32)])


P = jax.sharding.PartitionSpec
EPS = 1e-05


def dot(a, b):
    return jnp.dot(a, b, preferred_element_type=F32)


def dot_t(a, b):
    return lax.dot_general(a, b, (((1,), (1,)), ((), ())), preferred_element_type=F32)


def t_dot(a, b):
    return lax.dot_general(a, b, (((0,), (0,)), ((), ())), preferred_element_type=F32)


def cols_swap(pieces):
    c = lax.axis_index("cols")
    out = jnp.zeros_like(pieces)
    own = lax.dynamic_index_in_dim(pieces, c, 0, True)
    out = lax.dynamic_update_slice_in_dim(out, own, c, 0)
    for s in range(1, NC):
        away = lax.dynamic_index_in_dim(pieces, (c + s) % NC, 0, True)
        came = lax.ppermute(away, "cols", [(i, (i + s) % NC) for i in range(NC)])
        out = lax.dynamic_update_slice_in_dim(out, came, (c - s) % NC, 0)
    return out


def split_in(w):
    d, n = w.shape
    return w.reshape(d, NC, n // NC).transpose(1, 0, 2)


def split_pair(w):
    d, n = w.shape
    return jnp.repeat(w.reshape(d, 2, n // 2).transpose(1, 0, 2), NC // 2, axis=0)


def whole_out(got):
    return got.transpose(1, 0, 2).reshape(got.shape[1], -1)


def split_grad(g):
    n, d = g.shape
    return g.astype(BF).reshape(n, NC, d // NC).transpose(1, 0, 2)


def pair_sum(got):
    return got.astype(F32).reshape((2, NC // 2) + got.shape[1:]).sum(1).astype(BF)


def group_sum(own, others):
    return own.astype(F32) + others.astype(F32).sum(0)


def beside(a):
    k, d, n = a.shape
    return a.transpose(1, 0, 2).reshape(d, k * n)


def place_block(piece, start, full_len, axis):
    shape = piece.shape[:axis] + (full_len,) + piece.shape[axis + 1:]
    return lax.dynamic_update_slice_in_dim(jnp.zeros(shape, piece.dtype), piece, start, axis)


def rms_scale(x):
    return lax.rsqrt(jnp.mean(x * x, axis=1, keepdims=True) + EPS)


def norm_back(x, gain, scale, up):
    gain_grad = jnp.sum(x * scale * up, axis=0)
    tilted = up * gain[None, :]
    project = jnp.mean(x * tilted, axis=1, keepdims=True)
    return scale * tilted - x * (scale**3 * project), gain_grad


def per_device(hidden_in, lengths, norm1_gain, z_weight, x_weight, bcdt_weight, conv_x_weight, conv_x_bias,
               conv_bc_weight, conv_bc_bias, a_log, d_skip, dt_bias, gate_gain, mix_out_weight, norm2_gain,
               q_weight, k_weight, v_weight, att_out_weight, norm3_gain, up_weight, down_weight, grad_output):
    r, c = lax.axis_index("rows"), lax.axis_index("cols")
    rows = lax.axis_size("rows")
    tok_rows, feat = hidden_in.shape
    T, D = tok_rows * rows, feat * NC
    S = T // (rows * NC)
    slab = r * NC + c
    inner = z_weight.shape[1] * rows
    wide = z_weight.shape[1] // NC
    heads_row = a_log.shape[0]
    heads = heads_row // NC
    n_heads = heads_row * rows
    seq_lens = lengths[0]
    places = jnp.arange(T, dtype=jnp.int32)
    valid = (places < seq_lens[0] + seq_lens[1]).astype(F32)
    my_valid = lax.dynamic_slice_in_dim(valid, slab * S, S, 0)[:, None]
    pad = 128

    pair = "swap2" if lax.axis_size("dp") == 2 else "swap"

    def halved(a):
        return a.reshape(a.shape[0], 2, -1, a.shape[2]) if pair == "swap2" else a

    def joined(a):
        return a.reshape(a.shape[0], -1, a.shape[-1])

    zx_pieces = halved(jnp.concatenate([split_in(x_weight), split_in(z_weight)], axis=2))
    mix_pieces = halved(mix_out_weight.reshape(NC, -1, feat))
    bcdt_width = bcdt_weight.shape[1]
    bcdt_pad = -bcdt_width % 128
    bcdt_piece = jnp.pad(bcdt_weight, ((0, 0), (0, bcdt_pad))).reshape(2, feat // 2, -1)
    gain_piece = jnp.broadcast_to(jnp.pad(jnp.stack([norm1_gain, norm2_gain, norm3_gain]), ((0, 5), (0, 0)))[None], (2, 8, feat))
    hidden_all, w_zx, mix_got, w_bcdt, gains = gather_native(
        hidden_in, 0, (pair, pair, "bcast2", "bcast2"), (zx_pieces, mix_pieces, bcdt_piece, gain_piece))
    w_mix = whole_out(joined(mix_got))
    gains = gains[:, 0, :3].transpose(1, 0, 2).reshape(3, D)
    w_bcdt = w_bcdt.reshape(D, -1)
    w_dt = jnp.pad(lax.dynamic_slice_in_dim(w_bcdt, 2 * STATE + slab * heads, heads, 1), ((0, 0), (0, 128 - heads)))
    w_in = jnp.concatenate([w_bcdt[:, :2 * STATE], w_zx.reshape(D, 2 * wide), w_dt], axis=1)
    qkv_pieces = halved(jnp.concatenate([split_pair(q_weight), split_pair(k_weight), split_pair(v_weight)], axis=2))
    o_pieces = halved(jnp.repeat(att_out_weight.reshape(2, -1, feat), NC // 2, axis=0))
    grad_output, hidden_all = lax.optimization_barrier((grad_output, hidden_all))
    grad_all = lax.all_gather(grad_output, ("rows", "cols"), axis=0)
    grad_all = grad_all.reshape(rows, NC, tok_rows, feat).transpose(0, 2, 1, 3).reshape(T, D)

    hid_all = hidden_all.astype(F32)
    u1 = (hid_all * rms_scale(hid_all) * gains[0][None, :]).astype(BF)
    proj = dot(u1, w_in)
    mine = lambda a, n: lax.dynamic_slice_in_dim(a, c * n, n, a.ndim - 1)
    cw = jnp.concatenate([conv_bc_weight, mine(conv_x_weight, wide)], axis=1)
    cw = jnp.concatenate([cw, jnp.concatenate([conv_bc_bias, mine(conv_x_bias, wide)])[None], jnp.zeros((3, MIX), F32)])
    wide_row = lambda a: jnp.pad(a, (0, 256 - a.shape[0]))[None]
    pv = jnp.concatenate([wide_row(mine(gate_gain, wide)), wide_row(jnp.repeat(mine(d_skip, heads), HEAD_DIM)),
                          wide_row(mine(dt_bias, heads)), wide_row(-jnp.exp(mine(a_log, heads))), jnp.zeros((4, 256), F32)])
    mixg, squares, y, states = mixer_fwd(seq_lens, proj, cw, pv)
    part = jnp.concatenate([dot(mixg, w_mix).astype(BF), squares], axis=1)
    summed, qkv_got, o_got = reduce_scatter16(part, 2, (pair, pair), (qkv_pieces, o_pieces))
    w_qkv, w_o = qkv_got.reshape(D, -1), whole_out(joined(o_got))
    gate_scale = lax.rsqrt(summed[:, D:D + 1] / inner + EPS)
    mix_out = summed[:, :D] * gate_scale
    h0 = lax.dynamic_slice_in_dim(hidden_all, slab * S, S, 0).astype(F32)
    h1 = h0 + mix_out
    s2 = rms_scale(h1)
    u2, up_got = all_gather16((h1 * s2 * gains[1][None, :]).astype(BF), 3, (pair,), (halved(split_in(up_weight)),))
    w_up = up_got.reshape(D, -1)

    qkv = dot(u2, w_qkv).astype(BF)
    att = w_o.shape[0]
    odd = (c % 2)[None]
    attended, att_exact, lse = att_fwd(seq_lens, odd, qkv)
    att_part, down_got = reduce_scatter16(dot(attended, w_o).astype(BF), 4, (pair,), (halved(down_weight.reshape(NC, -1, feat)),))
    w_down = whole_out(joined(down_got))
    h2 = h1 + att_part
    s3 = rms_scale(h2)
    u3, = all_gather16((h2 * s3 * gains[2][None, :]).astype(BF), 1)

    act, = (dot(u3, w_up),)
    gelu, gelu_back = jax.vjp(functools.partial(jax.nn.gelu, approximate=True), act)
    hid = gelu.astype(BF)
    h3 = h2 + lax.psum_scatter(dot(hid, w_down).astype(BF), ("rows", "cols"), scatter_dimension=0, tiled=True).astype(F32)
    out_slab = (h3 * my_valid).astype(BF)
    output = cols_swap(out_slab.reshape(S, NC, feat).transpose(1, 0, 2)).reshape(NC * S, feat)

    g3 = (grad_all.astype(F32) * valid[:, None]).astype(BF)
    g3_mine = lax.dynamic_slice_in_dim(g3, slab * S, S, 0).astype(F32)
    d_act = gelu_back(dot_t(g3, w_down))[0].astype(BF)
    down_pieces = split_grad(t_dot(hid, g3))
    up_pieces = t_dot(u3, d_act).astype(BF).reshape(NC, feat, -1)
    d_u3, down_back = reduce_scatter16(dot_t(d_act, w_up).astype(BF), 6, ("swap",), (down_pieces,))
    d_n3, gain3_grad = norm_back(h2, gains[2], s3, d_u3)
    dh2 = g3_mine + d_n3
    g2, up_back, down_other = all_gather16(dh2.astype(BF), 7, ("swap", "dp"), (up_pieces, down_back))
    down_grad = group_sum(down_back, down_other).reshape(-1, feat)
    d_att = dot_t(g2, w_o).astype(BF)
    o_pieces = split_grad(t_dot(attended, g2))
    d_qkv = att_bwd(seq_lens, odd, qkv, d_att, att_exact, lse)
    qkv_pieces = t_dot(u2, d_qkv).astype(BF).reshape(NC, feat, -1)
    d_u2, o_back, up_other = reduce_scatter16(dot_t(d_qkv, w_qkv).astype(BF), 8, ("swap", "dp"), (o_pieces, up_back))
    up_grad = beside(group_sum(up_back, up_other))
    o_back = pair_sum(o_back)
    d_n2, gain2_grad = norm_back(h1, gains[1], s2, d_u2)
    dh1 = dh2 + d_n2
    tilt = gate_scale * gate_scale * jnp.sum(dh1 * mix_out, axis=1, keepdims=True) / inner
    tilt_hi = tilt.astype(BF)
    tilt_lo = (tilt - tilt_hi.astype(F32)).astype(BF)
    tail = jnp.concatenate([jnp.broadcast_to(tilt_hi, (S, pad // 2)), jnp.broadcast_to(tilt_lo, (S, pad // 2))], axis=1)
    g1_ext, qkv_back, o_other = all_gather16(jnp.concatenate([(dh1 * gate_scale).astype(BF), tail], axis=1), 9, ("swap", "dp"), (qkv_pieces, o_back))
    o_grad = group_sum(o_back, o_other).reshape(-1, feat)
    qkv_back = pair_sum(qkv_back)
    g1 = g1_ext[:, :D]
    d_mix = dot_t(g1, w_mix)
    mix_pieces = split_grad(t_dot(mixg, g1))
    d_in, tap_grads, row_grads = mixer_bwd(seq_lens, proj, cw, pv, y, states, d_mix, g1_ext)
    cbw_grad, cxw_grad = tap_grads[:CONV, :2 * STATE], tap_grads[:CONV, 2 * STATE:]
    cbb_grad, cxb_grad = tap_grads[CONV, :2 * STATE], tap_grads[CONV, 2 * STATE:]
    gate_gain_grad, dt_bias_grad, a_log_grad = row_grads[0, :wide], row_grads[2, :heads], row_grads[3, :heads]
    d_skip_grad = row_grads[1, :wide].reshape(heads, HEAD_DIM).sum(1)
    in_grad = t_dot(u1, d_in)
    zx_pieces = in_grad[:, 2 * STATE:2 * STATE + 2 * wide].astype(BF).reshape(NC, feat, -1)
    slabs = rows * NC
    dt_grads = place_block(in_grad[:, 2 * STATE + 2 * wide:2 * STATE + 2 * wide + heads].astype(BF), slab * heads, bcdt_width + bcdt_pad - 2 * STATE, 1)
    bcdt_part = jnp.concatenate([in_grad[:, :2 * STATE].astype(BF), dt_grads], axis=1).reshape(slabs, SMALL, -1)
    misc = jnp.concatenate([cbw_grad.reshape(-1), cbb_grad] + [
        place_block(a, slab * heads, n_heads, 0) for a in (a_log_grad, d_skip_grad, dt_bias_grad)])
    n_misc = misc.shape[0]
    small = jnp.concatenate([gain2_grad[None], gain3_grad[None], place_block(cxw_grad, slab * wide, inner, 1).reshape(-1, D),
                             place_block(cxb_grad, slab * wide, inner, 0).reshape(-1, D),
                             place_block(gate_gain_grad, slab * wide, inner, 0).reshape(-1, D), jnp.pad(misc, (0, D - n_misc))[None]])
    thin = bcdt_width + bcdt_pad
    four = D // thin
    small = jnp.pad(small, ((0, slabs - small.shape[0]), (0, 0))).reshape(slabs, four, thin)
    small_hi = small.astype(BF)
    small_lo = (small - small_hi.astype(F32)).astype(BF)
    side = jnp.concatenate([bcdt_part, small_hi, small_lo, jnp.zeros((slabs, S - SMALL - 2 * four, thin), BF)], axis=1)
    payload = jnp.concatenate([dot_t(d_in, w_in).astype(BF), side.reshape(T, thin)], axis=1)
    d_u1, zx_back, mix_back, qkv_other = reduce_scatter16(
        payload, 10, ("swap", "swap", "dp"), (zx_pieces, mix_pieces, qkv_back))
    rest, d_u1 = d_u1[:, D:], d_u1[:, :D]
    qkv_sum = group_sum(qkv_back, qkv_other)
    q_grad, k_grad, v_grad = (beside(qkv_sum[:, :, i * att:(i + 1) * att]) for i in range(3))
    d_n1, gain1_grad = norm_back(h0, gains[0], rms_scale(h0), d_u1)
    in_slab = dh1 + d_n1
    own = rest[SMALL:SMALL + four] + rest[SMALL + four:SMALL + 2 * four]
    gain1_rows = gain1_grad.reshape(four, thin)
    mine_small = jnp.concatenate([rest[:SMALL], own, own, own, gain1_rows, gain1_rows, gain1_rows,
                                  jnp.zeros((S - SMALL - 6 * four, thin), F32)])
    rest_all, in_got, zx_other, mix_other = gather16(
        mine_small, 11, False, ("swap", "dp", "dp"), (in_slab.reshape(S, NC, feat).transpose(1, 0, 2), zx_back, mix_back), four)
    rest_all = rest_all.reshape(slabs, S, thin)
    bcdt_grad = rest_all[:, :SMALL].reshape(D, thin)[:, :bcdt_width].astype(F32)
    tail_rows = rest_all[:, SMALL:SMALL + 6 * four].astype(F32).reshape(slabs, 6, D)
    small = tail_rows[:, 0] + tail_rows[:, 1] + tail_rows[:, 2]
    gain1_grad = (tail_rows[:, 3] + tail_rows[:, 4] + tail_rows[:, 5]).sum(0)
    per_inner = inner // D
    edges = [2 + CONV * per_inner, 2 + (CONV + 1) * per_inner, 2 + (CONV + 2) * per_inner]
    cxw_sum = small[2:edges[0]].reshape(CONV, inner)
    cxb_sum, gate_gain_sum = small[edges[0]:edges[1]].reshape(-1), small[edges[1]:edges[2]].reshape(-1)
    misc = small[edges[2]]
    cbw_sum, cbb_sum = misc[:CONV * 2 * STATE].reshape(CONV, 2 * STATE), misc[CONV * 2 * STATE:(CONV + 1) * 2 * STATE]
    a_log_sum, d_skip_sum, dt_bias_sum = jnp.split(misc[n_misc - 3 * n_heads:n_misc], 3)
    input_grad = in_got.reshape(NC * S, feat)
    zx_sum = group_sum(zx_back, zx_other)
    x_grad, z_grad = beside(zx_sum[:, :, :wide]), beside(zx_sum[:, :, wide:])
    mix_grad = group_sum(mix_back, mix_other).reshape(-1, feat)

    return (output, input_grad, gain1_grad, z_grad, x_grad, bcdt_grad, cxw_sum, cxb_sum, cbw_sum, cbb_sum, a_log_sum, d_skip_sum,
            dt_bias_sum, gate_gain_sum, mix_grad, small[0], q_grad, k_grad, v_grad, o_grad, small[1], up_grad, down_grad)


def solution(mesh):
    assert mesh.shape["rows"] == 4 and mesh.shape["cols"] == NC
    token = P(("dp", "rows"), "cols")
    w_in, w_out = P("cols", "rows"), P("rows", "cols")
    row, col, whole = P("rows"), P("cols"), P()
    placed = (token, P("dp", None), col, w_in, w_in, P("cols", None), P(None, "rows"), row, whole, whole, row, row, row, row,
              w_out, col, w_in, w_in, w_in, w_out, col, w_in, w_out, token)
    given = (token, token, whole, w_in, w_in, whole, whole, whole, whole, whole, whole, whole, whole, whole, w_out, whole,
             w_in, w_in, w_in, w_out, whole, w_in, w_out)
    return jax.shard_map(per_device, mesh=mesh, in_specs=placed, out_specs=given, check_vma=False)
```

time: 1560 us -> 1150 us (0.74)
  Pallas kernels: 569 us -> 797 us
  local copies, waits for them, and re-layouts: 336 us -> 129 us
  waiting for transfers between devices: 174 us -> 4.82 us
  starting transfers between devices: 93.6 us -> 4.37 us
  matrix products: 200 us -> 112 us
  other arithmetic: 116 us -> 79.5 us
  blocking collectives: 36.5 us -> 0 us
    pallas_call x12 -> x15, Pallas kernels: 569 us -> 797 us  [the longest x6 371 us: gather16(): pl.pallas_call(functools.partial(ag_kernel, native, total, at, tuple(kind...]
    dynamic_update_slice x58 -> x3, local copies, waits for them, and re-layouts: 110 us -> 0.06 us  [cols_swap(): out = lax.dynamic_update_slice_in_dim(out, came, (c - s) % NC, 0)]
    ppermute x9 -> x0, waiting for transfers between devices: 99.9 us -> none  [both_groups(): return x.astype(F32) + lax.ppermute(x, 'dp', [(0, 1), (1, 0)]).astype(F32)]
    ppermute x60 -> x3, starting transfers between devices: 89.4 us -> 4 us  [cols_swap(): came = lax.ppermute(away, 'cols', [(i, (i + s) % NC) for i in range(NC)])]
    ppermute x60 -> x3, waiting for transfers between devices: 74.4 us -> 4.76 us  [cols_swap(): came = lax.ppermute(away, 'cols', [(i, (i + s) % NC) for i in range(NC)])]
    dot_general x12 -> x0, matrix products: 52.7 us -> none  [the longest x3 24.9 us: ssd(): jnp.einsum('bhpq,bhqm->bhpm', scores[:, None] * decay, w, precision=HIGH)]
    all_gather x2 -> x0, blocking collectives: 36.5 us -> none  [the longest x1 23.4 us: per_device(): w_bcdt = lax.all_gather(bcdt_weight, 'cols', axis=0, tiled=True)]
    unnamed x654 -> x192, local copies, waits for them, and re-layouts: 77.2 us -> 46.9 us
  transfers between devices with their start and end apart: 71 -> 5, of which waited for: 26 -> 2; matrix products, arithmetic and copies ran while one was open for 25% -> 14% of each run, Pallas kernels for 22% -> 41%
where the time goes in v2:
time: 1150 us; the launch traced here: 1140 us
  Pallas kernels  797 us (69%)
  local copies, waits for them, and re-layouts  129 us (11%)
  matrix products  112 us (10%)
  other arithmetic  79.5 us (7%)
  between operations  17.2 us (1%)
    pallas_call x6, Pallas kernels, gather16(): pl.pallas_call(functools.partial(ag_kernel, native, total, at, tuple(kind...  371 us
    pallas_call x5, Pallas kernels, reduce_scatter16(): pl.pallas_call(functools.partial(rs_kernel, tuple(kinds)), out_shape=[jax...  340 us
    unnamed x192, local copies, waits for them, and re-layouts  46.9 us
    dot_general x6, matrix products, t_dot(): lax.dot_general(a, b, (((0,), (0,)), ((), ())), preferred_element_type=F32)  38.4 us
    pallas_call x2, Pallas kernels, att_call(): pl.pallas_call(kernel, grid=(4,), in_specs=specs, out_specs=out_specs, ou...  37.7 us
    dot_general x6, matrix products, dot(): return jnp.dot(a, b, preferred_element_type=F32)  37.3 us
    dot_general x6, matrix products, dot_t(): lax.dot_general(a, b, (((1,), (1,)), ((), ())), preferred_element_type=F32)  36.5 us
    pallas_call x1, Pallas kernels, mixer_bwd(): pl.pallas_call(mixer_bwd_kernel, grid=(n,), in_specs=first + [block(WIDE)...  32.3 us
  transfers between devices with their start and end apart: 5, of which 2 were waited for; matrix products, arithmetic and copies ran while one was open for 14% of the time, Pallas kernels for 41%

profile of v2, /device:TPU:0, one launch (start us, length us, event | category | flops | bytes accessed | tf_op | source)
XLA Modules:
  0.0 1144.0 jit_solution(17108455588947577475)
XLA Ops:
  14.6 95.4 %shard_map.407 = (bf16[2048,1536]{1,0:T(8,128)(2,1)}, bf16[4,2,192,384]{3,2,1,0:T(8,128)(2,1)S(1)}, bf16[4,2,96,384]{3,2,1,0:T(8,128)(2,1)S(1)}, bf16[4,2,192,38...) custom-call(bf16[512,384]{1,0:T(8,128)(2,1)S(1)} %copy-done.19, bf16[4,2,192,384]{3,2,1,0:T(8,128)(2,1)S(1)} %bitcast.207, ...), custom_call_target="tpu_custom_call" | custom-call | bytes 67108864 | tf_op jit(solution)/shard_map/pallas_call | solution.py:240
  126.5 2.1 pad_maximum_fusion.2.refs_1_
  128.5 4.2 fusion
  133.2 8.0 fusion.21.proj.before
  141.2 16.0 %shard_map.408 = (bf16[2048,192]{1,0:T(8,128)(2,1)S(1)}, bf16[2048,128]{1,0:T(8,128)(2,1)S(1)}, f32[2048,192]{1,0:T(8,128)S(1)}, f32[8,192,128]{2,1,0:T(8,128)S(1)}) custom-call(s32[2]{0:T(128)S(1)} %bitcast.218, f32[2048,768]{1,0:T(8,128)} %fusion.21.proj.before, f32[2048,768]{1,0:T(8,128)} %fusion.21.proj.before, f32[8,448]{1,0:T(8,128)S(1)} %maximum_maximum_fusion.1.cw, ...), custom_call_target="tpu_custom_call" | custom-call | flops 4294967296 | bytes 16777216 | tf_op jit(solution)/shard_map/pallas_call | solution.py:580
  159.2 3.3 pad_maximum_fusion.1.refs_0_
  163.3 80.6 %shard_map.409 = (f32[128,1664]{1,0:T(8,128)}, bf16[4,2,192,576]{3,2,1,0:T(8,128)(2,1)}, bf16[4,2,96,384]{3,2,1,0:T(8,128)(2,1)}) custom-call(bf16[2048,1664]{1,0:T(8,128)(2,1)} %pad_maximum_fusion.1.refs_0_, bf16[4,2,192,576]{3,2,1,0:T(8,128)(2,1)} %pad_maximum_fusion.2.refs_1_, bf16[4,2,96,384]{3,2,1,0:T(8,128)(2,1)} %bitcast.252), custom_call_target="tpu_custom_call" | custom-call | bytes 67108864 | tf_op jit(solution)/shard_map/pallas_call | solution.py:377
  248.9 51.3 %shard_map.410 = (bf16[2048,1536]{1,0:T(8,128)(2,1)}, bf16[4,2,192,384]{3,2,1,0:T(8,128)(2,1)S(1)}) custom-call(bf16[128,1536]{1,0:T(8,128)(2,1)S(1)} %multiply_convert_fusion.6.refs_0_, bf16[4,2,192,384]{3,2,1,0:T(8,128)(2,1)S(1)} %bitcast.206), custom_call_target="tpu_custom_call" | custom-call | bytes 67108864 | tf_op jit(solution)/shard_map/pallas_call | solution.py:240
  300.2 8.8 convolution_convert_fusion.7.qkv
  309.0 16.7 %shard_map.411 = (bf16[2048,192]{1,0:T(8,128)(2,1)}, f32[2048,192]{1,0:T(8,128)}, f32[2048,128]{1,0:T(8,128)}) custom-call(s32[2]{0:T(128)} %bitcast.216, s32[1]{0:T(128)} %bitcast.30.odd, bf16[2048,576]{1,0:T(8,128)(2,1)} %convolution_convert_fusion.7.qkv), custom_call_target="tpu_custom_call" | custom-call | flops 8589934592 | bytes 16777216 | tf_op jit(solution)/shard_map/pallas_call | solution.py:720
  325.7 5.7 convolution_convert_fusion.1.refs_0_
  331.4 64.1 %shard_map.412 = (f32[128,1536]{1,0:T(8,128)}, bf16[4,2,192,384]{3,2,1,0:T(8,128)(2,1)}) custom-call(bf16[2048,1536]{1,0:T(8,128)(2,1)} %convolution_convert_fusion.1.refs_0_, bf16[4,2,192,384]{3,2,1,0:T(8,128)(2,1)} %bitcast.265), custom_call_target="tpu_custom_call" | custom-call | bytes 67108864 | tf_op jit(solution)/shard_map/pallas_call | solution.py:377
  397.0 41.9 %shard_map.413 = bf16[2048,1536]{1,0:T(8,128)(2,1)} custom-call(bf16[128,1536]{1,0:T(8,128)(2,1)S(1)} %multiply_convert_fusion.5.refs_0_), custom_call_target="tpu_custom_call" | custom-call | bytes 67108864 | tf_op jit(solution)/shard_map/pallas_call | solution.py:240
  442.6 4.1 convert.22
  446.7 12.6 %multiply_convert_fusion = bf16[4,4,512,384]{3,1,2,0:T(4,128)(2,1)} fusion(f32[4,512]{1,0:T(4,128)S(1)} %fusion.35, f32[4,4,512,384]{3,2,1,0:T(8,128)S(1)} %convert.22), kind=kLoop, calls=%fused_computation.5 | loop fusion | flops 6291456 | bytes 18882560 | tf_op jit(solution)/shard_map/convert_element_type | solution.py:901
  459.3 4.1 copy.179
  463.4 3.4 fusion.49
  466.9 6.4 fusion.14
  474.9 6.7 convolution_convert_fusion.5
  482.4 12.9 %copy.134 = f32[4,4,512,384]{3,1,2,0:T(4,128)} copy(bf16[4,4,512,384]{3,2,1,0:T(8,128)(2,1)} %bitcast.228) | data formatting | bytes 18874368 | tf_op jit(solution)/shard_map/convert_element_type | solution.py:901
  495.3 11.3 copy.178
  506.6 8.0 multiply_convert_fusion.1
  514.6 7.4 convolution_convert_fusion.10
  525.2 6.8 convolution_convert_fusion.4.refs_0_
  532.0 73.0 %shard_map.414 = (f32[128,1536]{1,0:T(8,128)}, bf16[4,384,384]{2,1,0:T(8,128)(2,1)}) custom-call(bf16[2048,1536]{1,0:T(8,128)(2,1)} %convolution_convert_fusion.4.refs_0_, bf16[4,384,384]{2,1,0:T(8,128)(2,1)} %bitcast.237), custom_call_target="tpu_custom_call" | custom-call | bytes 67108864 | tf_op jit(solution)/shard_map/pallas_call | solution.py:377
  608.1 6.4 convolution_convert_fusion.9
  614.4 61.6 %shard_map.415 = (bf16[2048,1536]{1,0:T(8,128)(2,1)}, bf16[4,384,384]{2,1,0:T(8,128)(2,1)S(1)}, bf16[1,4,384,384]{3,2,1,0:T(8,128)(2,1)S(1)}) custom-call(bf16[128,1536]{1,0:T(8,128)(2,1)S(1)} %fusion.46.refs_0_, bf16[4,384,384]{2,1,0:T(8,128)(2,1)S(1)} %bitcast.212, bf16[4,384,384]{2,1,0:T(8,128)(2,1)S(1)} %copy-done.3), custom_call_target="tpu_custom_call" | custom-call | bytes 67108864 | tf_op jit(solution)/shard_map/pallas_call | solution.py:240
  676.1 5.1 convolution_convert_fusion.11
  682.1 2.2 convolution_convert_fusion.12
  685.6 21.1 %shard_map.416 = bf16[2048,576]{1,0:T(8,128)(2,1)} custom-call(s32[2]{0:T(128)} %bitcast.217, s32[1]{0:T(128)} %bitcast.30.odd, bf16[2048,576]{1,0:T(8,128)(2,1)} %convolution_convert_fusion.7.qkv, bf16[2048,192]{1,0:T(8,128)(2,1)} %copy.138.d_att, f32[2048,192]{1,0:T(8,128)} %get-tuple-element.88.o_ref, f32[2048,128]{1,0:T(8,128)} %get-tuple-element.89.lse), custom_call_target="tpu_custom_call" | custom-call | flops 8589934592 | bytes 16777216 | tf_op jit(solution)/shard_map/pallas_call | solution.py:720
  706.6 8.8 convolution_convert_fusion.3.refs_0_
  715.4 43.8 %shard_map.417 = (f32[128,1536]{1,0:T(8,128)}, bf16[4,192,384]{2,1,0:T(8,128)(2,1)}, bf16[1,4,384,384]{3,2,1,0:T(8,128)(2,1)}) custom-call(bf16[2048,1536]{1,0:T(8,128)(2,1)} %convolution_convert_fusion.3.refs_0_, bf16[4,192,384]{2,1,0:T(8,128)(2,1)} %bitcast.261, bf16[4,384,384]{2,1,0:T(8,128)(2,1)} %copy-done.4), custom_call_target="tpu_custom_call" | custom-call | bytes 67108864 | tf_op jit(solution)/shard_map/pallas_call | solution.py:377
  759.2 3.1 fusion.19
  762.3 3.1 copy.155
  765.4 3.0 copy.162
  768.5 8.6 convolution_convert_fusion.8
  777.1 2.7 copy.142
  785.5 3.6 multiply_reduce_fusion.2
  790.7 71.4 %shard_map.418 = (bf16[2048,1664]{1,0:T(8,128)(2,1)}, bf16[4,384,576]{2,1,0:T(8,128)(2,1)S(1)}, bf16[1,2,192,384]{3,2,1,0:T(8,128)(2,1)S(1)}) custom-call(bf16[128,1664]{1,0:T(8,128)(2,1)S(1)} %concatenate.63.refs_0_, bf16[4,384,576]{2,1,0:T(8,128)(2,1)S(1)} %bitcast.205, bf16[2,192,384]{2,1,0:T(8,128)(2,1)S(1)} %bitcast_reduce_fusion.1.refs_2_), custom_call_target="tpu_custom_call" | custom-call | bytes 67108864 | tf_op jit(solution)/shard_map/pallas_call | solution.py:240
  862.2 5.6 fusion.5.d_mix
  867.9 32.3 %shard_map.419 = (bf16[2048,768]{1,0:T(8,128)(2,1)}, f32[8,448]{1,0:T(8,128)S(1)}, f32[8,256]{1,0:T(8,128)S(1)}) custom-call(s32[2]{0:T(128)S(1)} %bitcast.219, f32[2048,768]{1,0:T(8,128)} %fusion.21.proj.before, f32[2048,768]{1,0:T(8,128)} %fusion.21.proj.before, f32[8,448]{1,0:T(8,128)S(1)} %copy-done.23, f32[8,256]{1,0:T(8,128)S(1)} %copy-done.25, ...), custom_call_target="tpu_custom_call" | custom-call | flops 12884901888 | bytes 25165824 | tf_op jit(solution)/shard_map/pallas_call | solution.py:599
  900.3 9.7 convolution_convert_fusion
  910.0 8.7 convolution_convert_fusion.6
  918.9 2.2 fusion.15
  922.5 2.5 copy.145
  928.3 2.4 concatenate.66
  933.0 1.9 copy.193
  938.3 6.4 pad_maximum_fusion.refs_0_
  944.7 78.8 %shard_map.420 = (f32[128,1920]{1,0:T(8,128)}, bf16[4,384,384]{2,1,0:T(8,128)(2,1)}, bf16[4,192,384]{2,1,0:T(8,128)(2,1)}, bf16[1,2,384,576]{3,2,1,0:T(8,128)(2,1)}) custom-call(bf16[2048,1920]{1,0:T(8,128)(2,1)} %pad_maximum_fusion.refs_0_, bf16[4,384,384]{2,1,0:T(8,128)(2,1)} %bitcast.240, bf16[4,192,384]{2,1,0:T(8,128)(2,1)} %bitcast.262, ...), custom_call_target="tpu_custom_call" | custom-call | bytes 67108864 | tf_op jit(solution)/shard_map/pallas_call | solution.py:377
  1031.1 49.1 %shard_map.421 = (bf16[2048,384]{1,0:T(8,128)(2,1)}, f32[4,128,384]{2,1,0:T(8,128)S(1)}, bf16[1,4,384,384]{3,2,1,0:T(8,128)(2,1)S(1)}, bf16[1,4,192,384]{3,2,1,0:T(8,128)(2,1)S(1)}) custom-call(f32[128,384]{1,0:T(8,128)S(1)} %concatenate.69.refs_0_, f32[4,128,384]{2,1,0:T(8,128)S(1)} %bitcast.208, bf16[4,384,384]{2,1,0:T(8,128)(2,1)S(1)} %copy-done.2, ...), custom_call_target="tpu_custom_call" | custom-call | bytes 67108864 | tf_op jit(solution)/shard_map/pallas_call | solution.py:240
  1082.9 2.5 slice.234
  1085.4 1.8 slice_convert_fusion.1
  1087.2 2.0 reshape.439
  1089.2 4.5 slice_add_fusion
  1103.6 2.2 copy.160
  1105.9 2.2 copy.154
  1108.1 2.1 copy.161
  1110.2 2.3 convert_add_fusion.5
  1114.7 2.7 copy.156
  1118.8 2.7 copy.157
  1125.8 1.9 collective-permute-start.1
  1127.7 2.0 collective-permute-start.2
  1131.1 2.1 collective-permute-done
  1133.3 2.6 collective-permute-done.1
  (346 shorter events, 94.2 us)
Async XLA Ops:
  7.2 116.7 %copy-start = (f32[4,768]{1,0:T(4,128)S(1)}, f32[4,768]{1,0:T(4,128)}, u32[]{:S(2)}) copy-start(f32[4,768]{1,0:T(4,128)} %param.30) | copy-start | bytes 36868
  7.2 435.3 %all-gather.3.cloned.1.call-start = ((), (), s32[]{:S(2)}) async-start(), calls=%async_computation.2 | async-start | bytes 6684672 | tf_op jit(solution)/shard_map/all_gather | solution.py:860
  111.7 5.9 copy-start.58
  111.7 673.8 %reduce-scatter.2.cloned.1.call-start = ((), (), s32[]{:S(2)}) async-start(), calls=%async_computation.1 | async-start | bytes 6684672 | tf_op jit(solution)/shard_map/reduce_scatter | solution.py:897
  114.5 18.6 %copy-start.62 = (f32[1536]{0:T(1024)}, f32[1536]{0:T(1024)S(1)}, u32[]{:S(2)}) copy-start(f32[1536]{0:T(1024)S(1)} %mul.312) | copy-start | bytes 18436
  117.6 39.7 %copy-start.47 = (bf16[24,8,4,384]{3,1,2,0:T(8,128)(2,1)}, bf16[24,8,4,384]{3,1,2,0:T(8,128)(2,1)S(1)}, u32[]{:S(2)}) copy-start(bf16[24,8,4,384]{3,1,2,0:T(8,128)(2,1)S(1)} %copy.176) | copy-start | bytes 1769476
  117.6 6.1 copy-start.74
  117.6 6.3 copy-start.71
  123.9 17.3 %copy-start.24 = (f32[8,256]{1,0:T(8,128)}, f32[8,256]{1,0:T(8,128)S(1)}, u32[]{:S(2)}) copy-start(f32[8,256]{1,0:T(8,128)S(1)} %concatenate.57.pv) | copy-start | bytes 24580
  124.0 9.1 slice-start
  126.5 6.7 slice-start.1
  128.5 4.3 copy-start.67
  128.5 4.6 copy-start.31
  128.5 4.6 copy-start.52
  132.8 8.4 copy-start.65
  132.9 8.3 copy-start.22
  133.1 8.1 copy-start.55
  133.2 8.1 copy-start.27
  248.8 146.7 %copy-start.38 = (f32[128,1536]{1,0:T(8,128)}, f32[128,1536]{1,0:T(8,128)S(1)}, u32[]{:S(2)}) copy-start(f32[128,1536]{1,0:T(8,128)S(1)} %get-tuple-element.175) | copy-start | bytes 2359300
  248.8 535.1 %copy-start.68 = (f32[128]{0:T(128)}, f32[128]{0:T(128)S(1)}, u32[]{:S(2)}) copy-start(f32[128]{0:T(128)S(1)} %get-tuple-element.176) | copy-start | bytes 1540
  309.0 16.7 %copy-start.48 = (bf16[24,8,4,384]{3,1,2,0:T(8,128)(2,1)S(1)}, bf16[24,8,4,384]{3,1,2,0:T(8,128)(2,1)}, u32[]{:S(2)}) copy-start(bf16[24,8,4,384]{3,1,2,0:T(8,128)(2,1)} %copy.177) | copy-start | bytes 1769476
  396.8 209.7 %copy-start.39 = (f32[128,1536]{1,0:T(8,128)}, f32[128,1536]{1,0:T(8,128)S(1)}, u32[]{:S(2)}) copy-start(f32[128,1536]{1,0:T(8,128)S(1)} %get-tuple-element.173) | copy-start | bytes 2359300
  397.0 43.6 %copy-start.28 = (s32[1,2]{1,0:T(1,128)S(1)}, s32[1,2]{1,0:T(1,128)}, u32[]{:S(2)}) copy-start(s32[1,2]{1,0:T(1,128)} %param.25) | copy-start | bytes 28
  459.3 7.6 slice-start.2
  608.0 6.4 copy-start.3
  614.4 61.7 %copy-start.40 = (bf16[2048,192]{1,0:T(8,128)(2,1)S(1)}, bf16[2048,192]{1,0:T(8,128)(2,1)}, u32[]{:S(2)}) copy-start(bf16[2048,192]{1,0:T(8,128)(2,1)} %get-tuple-element.77) | copy-start | bytes 2359300
  676.1 5.1 copy-start.4
  676.1 5.1 copy-start.11
  676.1 6.0 copy-start.37
  676.1 6.0 copy-start.49
  685.6 21.1 %copy-start.73 = (bf16[4,2,192,576]{3,2,1,0:T(8,128)(2,1)S(1)}, bf16[4,2,192,576]{3,2,1,0:T(8,128)(2,1)}, u32[]{:S(2)}) copy-start(bf16[4,2,192,576]{3,2,1,0:T(8,128)(2,1)} %get-tuple-element.76) | copy-start | bytes 5308420
  715.4 43.8 %copy-start.5 = (bf16[4,384,384]{2,1,0:T(8,128)(2,1)S(1)}, bf16[4,384,384]{2,1,0:T(8,128)(2,1)}, u32[]{:S(2)}) copy-start(bf16[4,384,384]{2,1,0:T(8,128)(2,1)} %copy-done.4) | copy-start | bytes 3538948
  862.1 5.7 copy-start.9
  862.1 5.7 copy-start.20
  862.1 5.7 copy-start.23
  862.2 5.7 copy-start.25
  862.2 5.7 copy-start.29
  862.2 5.7 copy-start.34
  862.2 5.7 copy-start.36
  867.9 32.4 %copy-start.32 = (bf16[4,2,192,384]{3,2,1,0:T(8,128)(2,1)S(1)}, bf16[4,2,192,384]{3,2,1,0:T(8,128)(2,1)}, u32[]{:S(2)}) copy-start(bf16[4,2,192,384]{3,2,1,0:T(8,128)(2,1)} %copy-done.30) | copy-start | bytes 3538948
  867.9 32.4 %copy-start.53 = (bf16[1536,256]{1,0:T(8,128)(2,1)S(1)}, bf16[1536,256]{1,0:T(8,128)(2,1)}, u32[]{:S(2)}) copy-start(bf16[1536,256]{1,0:T(8,128)(2,1)} %slice.222) | copy-start | bytes 2359300
  867.9 32.4 %copy-start.56 = (bf16[1536,3]{1,0:T(8,128)(2,1)S(1)}, bf16[1536,3]{1,0:T(8,128)(2,1)}, u32[]{:S(2)}) copy-start(bf16[1536,3]{1,0:T(8,128)(2,1)} %copy-done.55) | copy-start | bytes 27652
  900.3 9.7 copy-start.63
  900.3 9.7 copy-start.66
  900.3 9.7 copy-start.77
  900.3 18.5 %slice-start.5 = ((s8[6815744]{0:T(1024)(128)(4,1)}), s8[2621440]{0:T(1024)(128)(4,1)S(1)}, s32[]{:S(2)}) async-start(s8[6815744]{0:T(1024)(128)(4,1)} %bitcast.297), calls=%async_computation.8 | async-start | bytes 5242880
  910.0 8.8 copy-start.8
  910.0 8.8 slice-start.6
  921.4 13.6 %slice-start.4 = ((bf16[1536,768]{0,1:T(8,128)(2,1)}), bf16[1536,384]{0,1:T(8,128)(2,1)S(1)}, s32[]{:S(2)}) async-start(bf16[1536,768]{0,1:T(8,128)(2,1)} %copy-done.45), calls=%async_computation.7 | async-start | bytes 2359296 | tf_op jit(solution)/shard_map/slice | solution.py:936
  922.5 13.9 %copy-start.10 = (bf16[4,384,576]{2,1,0:T(8,128)(2,1)S(1)}, bf16[4,384,576]{2,1,0:T(8,128)(2,1)}, u32[]{:S(2)}) copy-start(bf16[4,384,576]{2,1,0:T(8,128)(2,1)} %copy-done.9) | copy-start | bytes 5308420
  933.0 4.8 copy-start.60
  933.0 4.8 copy-start.61
  933.0 4.8 copy-start.72
  944.7 80.5 %copy-start.64 = (f32[1536]{0:T(1024)S(1)}, f32[1536]{0:T(1024)}, u32[]{:S(2)}) copy-start(f32[1536]{0:T(1024)} %copy-done.62) | copy-start | bytes 18436
  944.7 82.0 %copy-start.69 = (f32[128]{0:T(128)S(1)}, f32[128]{0:T(128)}, u32[]{:S(2)}) copy-start(f32[128]{0:T(128)} %copy-done.68) | copy-start | bytes 1540
  944.7 82.1 %copy-start.43 = (f32[128,1536]{1,0:T(8,128)S(1)}, f32[128,1536]{1,0:T(8,128)}, u32[]{:S(2)}) copy-start(f32[128,1536]{1,0:T(8,128)} %copy-done.42) | copy-start | bytes 2359300
  1082.9 13.4 %copy-start.21 = (bf16[1,2,192,384]{3,2,1,0:T(8,128)(2,1)S(1)}, bf16[1,2,192,384]{3,2,1,0:T(8,128)(2,1)}, u32[]{:S(2)}) copy-start(bf16[1,2,192,384]{3,2,1,0:T(8,128)(2,1)} %copy-done.20) | copy-start | bytes 884740
  1082.9 14.3 %copy-start.41 = (bf16[2,384,576]{2,1,0:T(8,128)(2,1)S(1)}, bf16[2,384,576]{2,1,0:T(8,128)(2,1)}, u32[]{:S(2)}) copy-start(bf16[2,384,576]{2,1,0:T(8,128)(2,1)} %bitcast_reduce_fusion.refs_3_) | copy-start | bytes 2654212
  1103.6 8.8 copy-start.14
  1121.6 15.4 %copy-start.1 = (f32[4,768]{1,0:T(4,128)S(1)}, f32[4,768]{1,0:T(4,128)}, u32[]{:S(2)}) copy-start(f32[4,768]{1,0:T(4,128)} %param.30) | copy-start | bytes 36868
  1123.5 12.5 %copy-start.16 = (f32[4,128,384]{2,1,0:T(8,128)S(1)}, f32[4,128,384]{2,1,0:T(8,128)}, u32[]{:S(2)}) copy-start(f32[4,128,384]{2,1,0:T(8,128)} %copy-done.15) | copy-start | bytes 2359300
  1125.7 7.6 collective-permute-start
  1125.8 10.2 collective-permute-start.1
  1127.7 8.2 collective-permute-start.2
  (26 other events, 61.3 us)
Sparse Core Ops, SparseCore 0:
  111.8 60.7 all-gather.2
  481.7 110.6 reduce-scatter.1

commit v3 on v2

--- a/solution.py
+++ b/solution.py
@@ -31,7 +31,7 @@
         def _():
             pl.semaphore_signal(barrier, inc=1, device_id={"cols": c + 1}, device_id_type=MESH)
         count = count + jnp.where(c > 0, 1, 0) + jnp.where(c < NC - 1, 1, 0)
-    if "dp" in kinds or "swap2" in kinds:
+    if any(kind in ("dp", "swap2", "reduce") for kind in kinds):
         groups = lax.axis_size("dp")
         for s in range(1, groups):
             pl.semaphore_signal(barrier, inc=1, device_id={"dp": lax.rem(lax.axis_index("dp") + s, groups)}, device_id_type=MESH)
@@ -39,59 +39,95 @@
     pl.semaphore_wait(barrier, count)
 
 
-def riders(kinds, ins, outs, send, recv, loc):
-    r, c, g = lax.axis_index("rows"), lax.axis_index("cols"), lax.axis_index("dp")
-    groups = lax.axis_size("dp")
-    remote, local, late = [], [], []
-    for e, kind in enumerate(kinds):
-        src, dst = ins[e], outs[e]
-        if kind == "dp":
-            for s in range(1, groups):
-                remote.append(copy_to(src, dst.at[s - 1], send.at[e, s - 1], recv.at[e, s - 1], {"dp": lax.rem(g + s, groups)}))
-        elif kind == "swap":
-            for s in range(1, NC):
-                to = lax.rem(c + s, NC)
-                remote.append(copy_to(src.at[to], dst.at[c], send.at[e, s - 1], recv.at[e, s - 1], {"cols": to}))
-            local.append(pltpu.make_async_copy(src.at[c], dst.at[c], loc.at[e]))
-        else:
-            half = g if kind == "swap2" else r & 1
-            other = {"dp": 1 - g} if kind == "swap2" else {"rows": r ^ 1}
+class Riders:
+    def __init__(self, kinds, ins, outs, send, recv, loc, *held):
+        r, c, g = lax.axis_index("rows"), lax.axis_index("cols"), lax.axis_index("dp")
+        groups = lax.axis_size("dp")
+        self.remote, self.local, self.late, self.sums = [], [], [], []
+        held = iter(held)
+        for e, kind in enumerate(kinds):
+            src, dst = ins[e], outs[e]
+            if kind == "dp":
+                for s in range(1, groups):
+                    self.remote.append(copy_to(src, dst.at[s - 1], send.at[e, s - 1], recv.at[e, s - 1], {"dp": lax.rem(g + s, groups)}))
+                continue
+            if kind == "swap":
+                for s in range(1, NC):
+                    to = lax.rem(c + s, NC)
+                    self.remote.append(copy_to(src.at[to], dst.at[c], send.at[e, s - 1], recv.at[e, s - 1], {"cols": to}))
+                self.local.append(pltpu.make_async_copy(src.at[c], dst.at[c], loc.at[e]))
+                continue
+            half = r & 1 if kind == "bcast2" else g
+            other = {"rows": r ^ 1} if kind == "bcast2" else {"dp": 1 - g}
+            pairs = []
+            if kind == "reduce":
+                own, got = next(held), next(held)
+                first = copy_to(src.at[:, 1 - g], got, send.at[e, 2 * NC - 1], recv.at[e, 2 * NC - 1], other)
+                self.sums.append((first, pltpu.make_async_copy(src.at[:, g], own, loc.at[e]), own, got, pairs))
+                piece = lambda to: own.at[to]
+                keep = pltpu.make_async_copy(own.at[c], dst.at[c, g], loc.at[e])
+                pairs.append((None, keep, copy_to(own.at[c], dst.at[c, g], send.at[e, NC - 1], recv.at[e, NC - 1], other)))
+            elif kind == "swap2":
+                piece = lambda to: src.at[to, half]
+                self.local.append(pltpu.make_async_copy(src.at[c], dst.at[c], loc.at[e]))
+            else:
+                piece = lambda to: src.at[half]
+                self.local.append(pltpu.make_async_copy(src, dst.at[c], loc.at[e]))
             for s in range(1, NC):
                 to, came = lax.rem(c + s, NC), lax.rem(c + NC - s, NC)
-                first = copy_to(src.at[to, half] if kind == "swap2" else src.at[half], dst.at[c, half],
-                                send.at[e, s - 1], recv.at[e, s - 1], {"cols": to})
-                late.append((first, copy_to(dst.at[came, half], dst.at[came, half], send.at[e, NC + s - 1], recv.at[e, NC + s - 1], other)))
-            if kind == "swap2":
-                local.append(pltpu.make_async_copy(src.at[c], dst.at[c], loc.at[e]))
-            else:
-                local.append(pltpu.make_async_copy(src, dst.at[c], loc.at[e]))
-
-    def start():
-        for first, _ in late:
+                first = copy_to(piece(to), dst.at[c, half], send.at[e, s - 1], recv.at[e, s - 1], {"cols": to})
+                pairs.append((first, None, copy_to(dst.at[came, half], dst.at[came, half], send.at[e, NC + s - 1], recv.at[e, NC + s - 1], other)))
+            if kind != "reduce":
+                self.late.extend(pairs)
+
+    def start(self):
+        for first, keep, own, got, pairs in self.sums:
             first.start()
-        for one in remote + local:
+            keep.start()
+        for first, _, _ in self.late:
+            first.start()
+        for one in self.remote + self.local:
             one.start()
 
-    def finish():
-        for first, second in late:
+    def add(self):
+        for first, keep, own, got, pairs in self.sums:
+            keep.wait()
+            first.wait()
+            own[...] = (own[...].astype(F32) + got[...].astype(F32)).astype(BF)
+            for one, local, second in pairs:
+                if one is None:
+                    local.start()
+                    second.start()
+                else:
+                    one.start()
+
+    def relay(self):
+        for first, _, second in self.late + [p for one in self.sums for p in one[4] if p[0] is not None]:
             first.wait_recv()
             second.start()
-        for one in remote + local:
+
+    def finish(self):
+        for one in self.remote + self.local:
             one.wait()
-        for first, second in late:
-            first.wait_send()
+        for first, local, second in self.late + [p for one in self.sums for p in one[4]]:
+            if first is None:
+                local.wait()
+            else:
+                first.wait_send()
             second.wait()
-    return start, finish
 
 
 def rider_parts(kinds, arrays):
     groups = lax.axis_size("dp")
     shapes = []
     for kind, a in zip(kinds, arrays):
-        lead = {"swap": (), "swap2": (), "bcast2": (NC,), "dp": (groups - 1,)}[kind]
+        lead = {"swap": (), "swap2": (), "reduce": (), "bcast2": (NC,), "dp": (groups - 1,)}[kind]
         shapes.append(jax.ShapeDtypeStruct(lead + a.shape, a.dtype))
     n, most = len(kinds), max(2 * NC, groups)
     sems = [pltpu.SemaphoreType.DMA((n, most)), pltpu.SemaphoreType.DMA((n, most)), pltpu.SemaphoreType.DMA((n,))] if n else []
+    for kind, a in zip(kinds, arrays):
+        if kind == "reduce":
+            sems += [pltpu.VMEM(a.shape[:1] + a.shape[2:], a.dtype)] * 2
     return shapes, sems
 
 
@@ -115,18 +151,14 @@
     return held
 
 
-def ag_kernel(native, total, at, kinds, *refs):
+def ag_kernel(native, at, kinds, *refs):
     n = len(kinds)
     x_ref, ins, out_ref, outs = refs[0], refs[1:1 + n], refs[1 + n], refs[2 + n:2 + 2 * n]
     recv, zr_s, zl_s, y_s, k_s, loc, *sems = refs[2 + 2 * n:]
     r, c = lax.axis_index("rows"), lax.axis_index("cols")
     S, W = x_ref.shape
     greet(r, c, kinds)
-    if total:
-        others, held, dp_s, dp_r, *sems = sems
-    ride, alight = riders(kinds, ins, outs, *sems) if n else (lambda: None, lambda: None)
-    if total:
-        x_ref = sum_groups(x_ref, others, held, dp_s, dp_r, total)
+    riding = Riders(kinds, ins, outs, *sems) if n else Riders((), (), (), None, None, None)
 
     def slab(rr, cc):
         if native:
@@ -160,7 +192,7 @@
     own = pltpu.make_async_copy(x_ref, slab(r, c), loc)
     own.start()
     if at == 0:
-        ride()
+        riding.start()
 
     def from_y(cc):
         got(r ^ 2, cc)
@@ -189,7 +221,7 @@
             ycopy(cc, slab(r, cc)).start()
             kcopy(r, cc, slab(r, cc)).start()
         if d == at:
-            ride()
+            riding.start()
         if d == 1:
             from_y(c)
         else:
@@ -226,19 +258,16 @@
         @pl.when((cc >= c) & (c > 0))
         def _():
             left(cc, slab(r, cc)).wait_send()
-    alight()
-
-
-def gather16(x, cid, native, kinds, arrays, total=0, at=0):
+    riding.relay()
+    riding.finish()
+
+
+def gather16(x, cid, native, kinds, arrays, at=0):
     S, D = x.shape
     shapes, sems = rider_parts(kinds, arrays)
-    if total:
-        groups = lax.axis_size("dp")
-        sems = [pltpu.VMEM((groups - 1, S, D), F32), pltpu.VMEM((S, D), BF), pltpu.SemaphoreType.DMA((groups - 1,)),
-                pltpu.SemaphoreType.DMA((groups - 1,))] + sems
     any_space = pl.BlockSpec(memory_space=pl.ANY)
     return pl.pallas_call(
-        functools.partial(ag_kernel, native, total, at, tuple(kinds)),
+        functools.partial(ag_kernel, native, at, tuple(kinds)),
         out_shape=[jax.ShapeDtypeStruct((4 * S, NC * D) if native else (16 * S, D), BF)] + shapes,
         in_specs=[pl.BlockSpec(memory_space=pltpu.VMEM)] + [any_space] * len(kinds),
         out_specs=[pl.BlockSpec(memory_space=pltpu.VMEM)] + [any_space] * len(kinds),
@@ -249,141 +278,8 @@
     )(x, *arrays)
 
 
-def all_gather16(x, cid, kinds=(), arrays=()):
-    return gather16(x, cid, False, kinds, arrays, 0, 3)
-
-
 def gather_native(x, cid, kinds=(), arrays=()):
     return gather16(x, cid, True, kinds, arrays)
-
-
-def rs_kernel(kinds, *refs):
-    n = len(kinds)
-    p_ref, ins, o_ref, outs = refs[0], refs[1:1 + n], refs[1 + n], refs[2 + n:2 + 2 * n]
-    (k_buf, y_buf, l_buf, r_buf, y_out, zr_out, zl_out,
-     k_s, k_r, y_s, y_r, zr_s, zr_r, zl_s, zl_r, *sems) = refs[2 + 2 * n:]
-    r, c = lax.axis_index("rows"), lax.axis_index("cols")
-    S, D = o_ref.shape
-    yy, kk = r >> 1, r & 1
-    greet(r, c, kinds)
-    ride, alight = riders(kinds, ins, outs, *sems) if n else (lambda: None, lambda: None)
-
-    def mine(rr, cc):
-        return p_ref.at[pl.ds(pl.multiple_of((rr * NC + cc) * S, 16), S)]
-
-    def kcopy(y2, cc):
-        return copy_to(mine(y2 * 2 + (1 - kk), cc), k_buf.at[y2, cc], k_s.at[y2 * NC + cc], k_r.at[y2 * NC + cc], {"rows": r ^ 1})
-
-    def ycopy(cc):
-        return copy_to(y_out.at[cc], y_buf.at[cc], y_s.at[cc], y_r.at[cc], {"rows": r ^ 2})
-
-    def rcopy(cc):
-        return copy_to(zr_out.at[cc], r_buf.at[cc], zr_s.at[cc], zr_r.at[cc], {"cols": c + 1})
-
-    def lcopy(cc):
-        return copy_to(zl_out.at[cc], l_buf.at[cc], zl_s.at[cc], zl_r.at[cc], {"cols": c - 1})
-
-    def order(f):
-        for d in range(NC - 1, 0, -1):
-            @pl.when(c + d < NC)
-            def _():
-                f(c + d)
-
-            @pl.when(c >= d)
-            def _():
-                f(c - d)
-        f(c)
-
-    def start_k(cc):
-        kcopy(1 - yy, cc).start()
-    order(start_k)
-
-    def start_k2(cc):
-        kcopy(yy, cc).start()
-    order(start_k2)
-    ride()
-
-    def do_y(cc):
-        kcopy(1 - yy, cc).wait_recv()
-        y_out[cc] = (mine((1 - yy) * 2 + kk, cc)[...].astype(F32) + k_buf[1 - yy, cc].astype(F32)).astype(BF)
-        ycopy(cc).start()
-    order(do_y)
-
-    def partial(cc):
-        kcopy(yy, cc).wait_recv()
-        a = mine(r, cc)[...].astype(F32) + k_buf[yy, cc].astype(F32)
-        ycopy(cc).wait_recv()
-        return a + y_buf[cc].astype(F32)
-
-    for d in range(NC - 1, 0, -1):
-        @pl.when(c + d < NC)
-        def _():
-            cc = c + d
-            a = partial(cc)
-            zr_out[cc] = a.astype(BF)
-
-            @pl.when(c > 0)
-            def _():
-                rcopy(cc).wait_recv()
-                zr_out[cc] = (zr_out[cc].astype(F32) + r_buf[cc].astype(F32)).astype(BF)
-            rcopy(cc).start()
-
-        @pl.when(c >= d)
-        def _():
-            cc = c - d
-            a = partial(cc)
-            zl_out[cc] = a.astype(BF)
-
-            @pl.when(c < NC - 1)
-            def _():
-                lcopy(cc).wait_recv()
-                zl_out[cc] = (zl_out[cc].astype(F32) + l_buf[cc].astype(F32)).astype(BF)
-            lcopy(cc).start()
-    o_ref[...] = partial(c)
-
-    @pl.when(c > 0)
-    def _():
-        rcopy(c).wait_recv()
-        o_ref[...] += r_buf[c].astype(F32)
-
-    @pl.when(c < NC - 1)
-    def _():
-        lcopy(c).wait_recv()
-        o_ref[...] += l_buf[c].astype(F32)
-
-    def fin(cc):
-        kcopy(1 - yy, cc).wait_send()
-        kcopy(yy, cc).wait_send()
-        ycopy(cc).wait_send()
-    order(fin)
-    for d in range(NC - 1, 0, -1):
-        @pl.when(c + d < NC)
-        def _():
-            rcopy(c + d).wait_send()
-
-        @pl.when(c >= d)
-        def _():
-            lcopy(c - d).wait_send()
-    alight()
-
-
-def reduce_scatter16(p, cid, kinds=(), arrays=()):
-    T, D = p.shape
-    S = T // 16
-    buf = lambda n: pltpu.VMEM((n, S, D), BF)
-    sem = lambda n: pltpu.SemaphoreType.DMA((n,))
-    shapes, sems = rider_parts(kinds, arrays)
-    any_space = pl.BlockSpec(memory_space=pl.ANY)
-    return pl.pallas_call(
-        functools.partial(rs_kernel, tuple(kinds)),
-        out_shape=[jax.ShapeDtypeStruct((S, D), F32)] + shapes,
-        in_specs=[pl.BlockSpec(memory_space=pltpu.VMEM)] + [any_space] * len(kinds),
-        out_specs=[pl.BlockSpec(memory_space=pltpu.VMEM)] + [any_space] * len(kinds),
-        scratch_shapes=[pltpu.VMEM((2, NC, S, D), BF), buf(NC), buf(NC), buf(NC), buf(NC), buf(NC), buf(NC),
-                        sem(8), sem(8), sem(4), sem(4), sem(4), sem(4), sem(4), sem(4)] + sems,
-        compiler_params=pltpu.CompilerParams(collective_id=cid, has_side_effects=True, vmem_limit_bytes=56 << 20),
-        cost_estimate=pl.CostEstimate(flops=0, bytes_accessed=64 << 20, transcendentals=0),
-    )(p, *arrays)
 
 
 HEAD_DIM = 64
@@ -737,8 +633,503 @@
                     jax.ShapeDtypeStruct((T, 3 * WIDE), BF), [pltpu.VMEM((T, WIDE), F32), pltpu.VMEM((T, WIDE), F32)])
 
 
+VMEM, ANY = pltpu.VMEM, pl.ANY
+
+
+HALVES = 2
+
+
+class Sum:
+    def __init__(self, r, c, partial, bufs):
+        self.r, self.c, self.partial = r, c, partial
+        self.yy, self.kk = r >> 1, r & 1
+        (self.part, self.p_out, self.k_buf, self.y_out, self.y_buf, self.zr_out, self.zl_out, self.r_buf, self.l_buf,
+         self.k_s, self.k_r, self.y_s, self.y_r, self.zr_s, self.zr_r, self.zl_s, self.zl_r) = bufs
+        self.cut = self.part.shape[1] // HALVES
+
+    @staticmethod
+    def scratch(S, W):
+        buf, sem = (lambda *n: VMEM(n + (S, W), BF)), (lambda n: pltpu.SemaphoreType.DMA((n,)))
+        return [VMEM((NC, S, W), F32), buf(2, NC), buf(2, NC)] + [buf(NC)] * 6 + [sem(2 * NC), sem(2 * NC)] + [sem(HALVES * NC)] * 6
+
+    def k_copy(self, y, cc):
+        i = y * NC + cc
+        return copy_to(self.p_out.at[y, cc], self.k_buf.at[y, cc], self.k_s.at[i], self.k_r.at[i], {"rows": self.r ^ 1})
+
+    def piece(self, src, dst, send, recv, cc, h, to):
+        at, i = pl.ds(h * self.cut, self.cut), cc * HALVES + h
+        return copy_to(src.at[cc, at], dst.at[cc, at], send.at[i], recv.at[i], to)
+
+    def y_copy(self, cc, h):
+        return self.piece(self.y_out, self.y_buf, self.y_s, self.y_r, cc, h, {"rows": self.r ^ 2})
+
+    def r_copy(self, cc, h):
+        return self.piece(self.zr_out, self.r_buf, self.zr_s, self.zr_r, cc, h, {"cols": self.c + 1})
+
+    def l_copy(self, cc, h):
+        return self.piece(self.zl_out, self.l_buf, self.zl_s, self.zl_r, cc, h, {"cols": self.c - 1})
+
+    def nth(self, j):
+        return jnp.where(self.c < NC // 2, NC - 1 - j, j)
+
+    def each(self, f):
+        def body(j, carry):
+            f(self.nth(j))
+            return carry
+        lax.fori_loop(0, NC, body, 0)
+
+    def to_core(self):
+        def half(i, carry):
+            y = jnp.where(i == 0, 1 - self.yy, self.yy)
+
+            def one(cc):
+                self.p_out[y, cc] = self.partial(y * 2 + (1 - self.kk), cc).astype(BF)
+                self.k_copy(y, cc).start()
+            self.each(one)
+            return carry
+        lax.fori_loop(0, 2, half, 0)
+
+    def to_y(self):
+        def one(cc):
+            mine = self.partial((1 - self.yy) * 2 + self.kk, cc)
+            self.k_copy(1 - self.yy, cc).wait_recv()
+            self.y_out[cc] = (mine + self.k_buf[1 - self.yy, cc].astype(F32)).astype(BF)
+            for h in range(HALVES):
+                self.y_copy(cc, h).start()
+        self.each(one)
+
+    def own(self):
+        def one(cc):
+            mine = self.partial(self.r, cc)
+            self.k_copy(self.yy, cc).wait_recv()
+            self.part[cc] = mine + self.k_buf[self.yy, cc].astype(F32)
+        self.each(one)
+
+    def step(self, j):
+        c, cc = self.c, self.nth(j)
+        for h in range(HALVES):
+            at = pl.ds(h * self.cut, self.cut)
+            self.y_copy(cc, h).wait_recv()
+            self.part[cc, at] += self.y_buf[cc, at].astype(F32)
+
+            @pl.when(cc > c)
+            def _():
+                @pl.when(c > 0)
+                def _():
+                    self.r_copy(cc, h).wait_recv()
+                    self.part[cc, at] += self.r_buf[cc, at].astype(F32)
+                self.zr_out[cc, at] = self.part[cc, at].astype(BF)
+                self.r_copy(cc, h).start()
+
+            @pl.when(cc < c)
+            def _():
+                @pl.when(c < NC - 1)
+                def _():
+                    self.l_copy(cc, h).wait_recv()
+                    self.part[cc, at] += self.l_buf[cc, at].astype(F32)
+                self.zl_out[cc, at] = self.part[cc, at].astype(BF)
+                self.l_copy(cc, h).start()
+
+    def last(self, total):
+        c = self.c
+        total[...] = self.part[c]
+
+        @pl.when(c > 0)
+        def _():
+            for h in range(HALVES):
+                self.r_copy(c, h).wait_recv()
+            total[...] += self.r_buf[c].astype(F32)
+
+        @pl.when(c < NC - 1)
+        def _():
+            for h in range(HALVES):
+                self.l_copy(c, h).wait_recv()
+            total[...] += self.l_buf[c].astype(F32)
+
+    def finish(self):
+        def one(cc):
+            self.k_copy(0, cc).wait_send()
+            self.k_copy(1, cc).wait_send()
+            for h in range(HALVES):
+                self.y_copy(cc, h).wait_send()
+
+                @pl.when(cc > self.c)
+                def _():
+                    self.r_copy(cc, h).wait_send()
+
+                @pl.when(cc < self.c)
+                def _():
+                    self.l_copy(cc, h).wait_send()
+        self.each(one)
+
+
+class Gather:
+    def __init__(self, r, c, out, S, sems, use=None):
+        self.r, self.c, self.out, self.S, self.use = r, c, out, S, use
+        self.recv, self.zr_s, self.zl_s, self.y_s, self.k_s = sems
+
+    @staticmethod
+    def scratch():
+        return [pltpu.SemaphoreType.DMA((HALVES * n,)) for n in (4 * NC, NC, NC, NC, 2 * NC)]
+
+    def slab(self, rr, cc):
+        return self.out.at[pl.ds(pl.multiple_of((rr * NC + cc) * self.S, 16), self.S)]
+
+    def move(self, rr, cc, h, sem, to):
+        cut = self.S // HALVES
+        ref = self.out.at[pl.ds(pl.multiple_of((rr * NC + cc) * self.S + h * cut, 16), cut)]
+        return copy_to(ref, ref, sem, self.recv.at[(rr * NC + cc) * HALVES + h], to)
+
+    def right(self, cc, h):
+        return self.move(self.r, cc, h, self.zr_s.at[cc * HALVES + h], {"cols": self.c + 1})
+
+    def left(self, cc, h):
+        return self.move(self.r, cc, h, self.zl_s.at[cc * HALVES + h], {"cols": self.c - 1})
+
+    def y_copy(self, cc, h):
+        return self.move(self.r, cc, h, self.y_s.at[cc * HALVES + h], {"rows": self.r ^ 2})
+
+    def k_copy(self, rr, cc, h):
+        return self.move(rr, cc, h, self.k_s.at[((rr >> 1) * NC + cc) * HALVES + h], {"rows": self.r ^ 1})
+
+    def got(self, rr, cc, h):
+        self.k_copy(rr, cc, h).wait_recv()
+
+    def pass_on(self, cc, h):
+        c = self.c
+
+        @pl.when((cc <= c) & (c < NC - 1))
+        def _():
+            self.right(cc, h).start()
+
+        @pl.when((cc >= c) & (c > 0))
+        def _():
+            self.left(cc, h).start()
+        self.y_copy(cc, h).start()
+        self.k_copy(self.r, cc, h).start()
+
+    def begin(self):
+        for h in range(HALVES):
+            self.pass_on(self.c, h)
+
+    def sides(self, off, f):
+        for h in range(HALVES):
+            for s in (-1, 1):
+                cc = self.c + s * off
+                fits = (cc >= 0) & (cc < NC) & (off < NC)
+                if s == 1:
+                    fits = fits & (off > 0)
+
+                @pl.when(fits)
+                def _():
+                    f(cc, h)
+
+    def forward(self, d):
+        def along(cc, h):
+            self.got(self.r, cc, h)
+            self.pass_on(cc, h)
+
+        def across(cc, h):
+            self.got(self.r ^ 2, cc, h)
+            self.k_copy(self.r ^ 2, cc, h).start()
+        self.sides(d, along)
+        self.sides(d - 1, across)
+
+    def uses(self, d):
+        def one(i, carry):
+            kind, s = i >> 1, (i & 1) * 2 - 1
+            off = d - jnp.where(kind == 0, 0, jnp.where(kind == 3, 2, 1))
+            rr = self.r ^ jnp.where(kind == 0, 0, jnp.where(kind == 1, 2, jnp.where(kind == 2, 1, 3)))
+            cc = self.c + s * off
+            fits = (off >= 0) & (off < NC) & (cc >= 0) & (cc < NC) & ((s < 0) | (off > 0))
+
+            @pl.when(fits)
+            def _():
+                @pl.when(kind >= 2)
+                def _():
+                    for h in range(HALVES):
+                        self.got(rr, cc, h)
+                if self.use is not None:
+                    self.use(rr, cc)
+            return carry
+        lax.fori_loop(0, 8, one, 0)
+
+    def stage(self, d):
+        self.forward(d)
+        self.uses(d)
+
+    def finish(self):
+        def body(cc, carry):
+            for h in range(HALVES):
+                self.y_copy(cc, h).wait_send()
+                self.k_copy(self.r, cc, h).wait_send()
+                self.k_copy(self.r ^ 2, cc, h).wait_send()
+
+                @pl.when((cc <= self.c) & (self.c < NC - 1))
+                def _():
+                    self.right(cc, h).wait_send()
+
+                @pl.when((cc >= self.c) & (self.c > 0))
+                def _():
+                    self.left(cc, h).wait_send()
+            return carry
+        lax.fori_loop(0, NC, body, 0)
+
+
+def link_call(kernel, cid, ins, in_spaces, outs, out_spaces, scratch, flops):
+    return pl.pallas_call(
+        kernel,
+        out_shape=[jax.ShapeDtypeStruct(s, d) for s, d in outs],
+        in_specs=[pl.BlockSpec(memory_space=s) for s in in_spaces],
+        out_specs=[pl.BlockSpec(memory_space=s) for s in out_spaces],
+        scratch_shapes=scratch,
+        compiler_params=pltpu.CompilerParams(collective_id=cid, has_side_effects=True, vmem_limit_bytes=60 << 20),
+        cost_estimate=pl.CostEstimate(flops=flops, bytes_accessed=96 << 20, transcendentals=0),
+    )(*ins)
+
+
+def link_kernel(spec, *refs):
+    it = iter(refs)
+    take = lambda n: [next(it) for _ in range(n)]
+    maybe = lambda key, n=1: take(n) if spec[key] else [None] * n
+    a, w1 = take(2)
+    side, = maybe("side")
+    mid_in = take(spec["n_mid"])
+    w2, = take(1) if spec["w2"] in ("in", "in_t") else [None]
+    a2, v2 = maybe("more_sum", 2)
+    slab2, = maybe("more_gather")
+    early_in = take(len(spec["early"]))
+    late_in = take(sum(src is None for _, src in spec["late"]))
+    u_all = next(it)
+    mid_out = take(spec["n_mid_out"])
+    post_out = take(spec["n_post"])
+    sum2, = maybe("more_sum")
+    all2, = maybe("more_gather")
+    early_out, late_out = take(len(spec["early"])), take(len(spec["late"]))
+    total, = take(1)
+    sum_bufs, gather_sems = take(17), take(5)
+    sum2_bufs = take(18) if spec["more_sum"] else []
+    gather2_sems = take(6) if spec["more_gather"] else []
+    small = take(6) if spec["small"] else None
+    early_sems, late_sems = take(spec["n_early_sems"]), take(spec["n_late_sems"])
+    r, c = lax.axis_index("rows"), lax.axis_index("cols")
+    S, W = total.shape
+    D = w1.shape[0] if spec["w1_t"] else w1.shape[1]
+    late_kinds = tuple(kind for kind, _ in spec["late"])
+    greet(r, c, spec["early"] + late_kinds + (("dp",) if spec["small"] else ()))
+    none = [None] * 3
+    early = Riders(spec["early"], early_in, early_out, *(early_sems or none))
+    late_in = iter(late_in)
+    sources = [next(late_in) if src is None else mid_out[src] for _, src in spec["late"]]
+    late = Riders(late_kinds, sources, late_out, *(late_sems or none))
+    rows_of = lambda rr, cc: pl.ds(pl.multiple_of((rr * NC + cc) * S, 16), S)
+
+    def partial(rr, cc):
+        p = mm(a[rows_of(rr, cc), :], w1[...], 1, 1 if spec["w1_t"] else 0)
+        return p if side is None else jnp.concatenate([p, side[rows_of(rr, cc), :].astype(F32)], axis=1)
+
+    def use(rr, cc):
+        w = early_out[0][...].reshape(D, -1) if spec["w2"] == "rider" else w2[...]
+        u = u_all[rows_of(rr, cc), :D] if u_all.shape[1] > D else u_all[rows_of(rr, cc), :]
+        spec["post"](mm(u, w, 1, 1 if spec["w2"] == "in_t" else 0), rows_of(rr, cc), post_out)
+
+    summing = Sum(r, c, partial, sum_bufs)
+    gather = Gather(r, c, u_all, S, gather_sems, use if spec["w2"] else None)
+    summing2 = gather2 = None
+    if spec["more_gather"]:
+        gather2 = Gather(r, c, all2, S, gather2_sems[:5])
+        own2 = pltpu.make_async_copy(slab2, gather2.slab(r, c), gather2_sems[5])
+        own2.start()
+    summing.to_core()
+    early.start()
+    summing.to_y()
+    if gather2:
+        own2.wait()
+        gather2.begin()
+    if spec["more_sum"]:
+        summing2 = Sum(r, c, lambda rr, cc: mm(a2[rows_of(rr, cc), :], v2[...]), sum2_bufs[:17])
+        summing2.to_core()
+        summing2.to_y()
+        summing2.own()
+    summing.own()
+    summing.step(0)
+    summing.step(1)
+    early.add()
+    summing.step(2)
+    if gather2:
+        gather2.stage(1)
+    summing.step(3)
+    summing.last(total)
+    if spec["small"]:
+        mine, others, held, dp_s, dp_r, loc = small
+        spec["mid"](total, mid_in, mid_out, mine)
+        late.start()
+        sum_groups(mine, others, held, dp_s, dp_r, 4)
+        place = pltpu.make_async_copy(held, gather.slab(r, c), loc)
+        place.start()
+        place.wait()
+        gather.begin()
+    else:
+        u_all[rows_of(r, c), :] = spec["mid"](total, mid_in, mid_out)
+        gather.begin()
+        late.start()
+    if spec["w2"] == "rider":
+        early.relay()
+        gather.forward(1)
+        early.finish()
+    if spec["w2"]:
+        use(r, c)
+    for d in range(1, NC + 2):
+        if summing2 and d <= NC:
+            summing2.step(d - 1)
+        if gather2 and d < NC + 1:
+            gather2.stage(d + 1)
+        if d > 1 or spec["w2"] != "rider":
+            gather.forward(d)
+        gather.uses(d)
+        if d == 2 and spec["w2"] != "rider":
+            early.relay()
+    gather.finish()
+    summing.finish()
+    if gather2:
+        gather2.finish()
+    if summing2:
+        summing2.last(sum2_bufs[17])
+        sum2[...] = sum2_bufs[17][...]
+        summing2.finish()
+    late.add()
+    late.relay()
+    if spec["w2"] != "rider":
+        early.finish()
+    late.finish()
+
+
+def link(cid, a, w1, mid, mid_in, mid_out, *, w1_t=False, side=None, w2=None, w2_kind=None, post=None, post_out=(), early=(), early_in=(),
+         late=(), late_in=(), extra=0, small=0, more_sum=None, more_gather=None):
+    T = a.shape[0]
+    D = w1.shape[0] if w1_t else w1.shape[1]
+    S = T // (4 * NC)
+    W = D + (0 if side is None else side.shape[1])
+    width = small or D + extra
+    early_shapes, early_sems = rider_parts(early, early_in)
+    late_it = iter(late_in)
+    late_arrays = [next(late_it) if src is None else jax.ShapeDtypeStruct(*mid_out[src]) for _, src in late]
+    late_shapes, late_sems = rider_parts(tuple(k for k, _ in late), late_arrays)
+    spec = dict(w1_t=w1_t, side=side is not None, mid=mid, n_mid=len(mid_in), n_mid_out=len(mid_out), w2=w2_kind, post=post,
+                n_post=len(post_out), early=tuple(early), late=tuple(late), small=small, more_sum=more_sum is not None,
+                more_gather=more_gather is not None, n_early_sems=len(early_sems), n_late_sems=len(late_sems))
+    ins = [a, w1] + ([side] if side is not None else []) + list(mid_in) + ([w2] if w2 is not None else [])
+    ins += list(more_sum or ()) + ([more_gather] if more_gather is not None else [])
+    in_spaces = [VMEM] * len(ins) + [ANY] * (len(early_in) + len(late_in))
+    ins += list(early_in) + list(late_in)
+    outs = [((T, width), BF)] + list(mid_out) + list(post_out)
+    if more_sum is not None:
+        outs.append(((S, D), F32))
+    if more_gather is not None:
+        outs.append(((T, D), BF))
+    out_spaces = [VMEM] * len(outs) + [ANY] * len(early_shapes + late_shapes)
+    if w2_kind == "rider":
+        out_spaces[len(outs)] = VMEM
+    outs += [(s.shape, s.dtype) for s in early_shapes + late_shapes]
+    scratch = [VMEM((S, W), F32)] + Sum.scratch(S, W) + Gather.scratch()
+    if more_sum is not None:
+        scratch += Sum.scratch(S, D) + [VMEM((S, D), F32)]
+    if more_gather is not None:
+        scratch += Gather.scratch() + [pltpu.SemaphoreType.DMA]
+    if small:
+        groups = lax.axis_size("dp")
+        scratch += [VMEM((S, small), F32), VMEM((groups - 1, S, small), F32), VMEM((S, small), BF), pltpu.SemaphoreType.DMA((groups - 1,)),
+                    pltpu.SemaphoreType.DMA((groups - 1,)), pltpu.SemaphoreType.DMA]
+    scratch += early_sems + late_sems
+    return link_call(functools.partial(link_kernel, spec), cid, ins, in_spaces, outs, out_spaces, scratch, 8 << 30)
+
+
+EPS = 1e-05
+
+
+def norm_scale(x):
+    return lax.rsqrt(jnp.mean(x * x, axis=1, keepdims=True) + EPS)
+
+
+def norm_grad(x, gain, up, gain_grad):
+    s = norm_scale(x)
+    gain_grad[0:1] = jnp.sum(x * s * up, axis=0, keepdims=True)
+    tilted = up * gain
+    return s * tilted - x * (s * s * s * jnp.mean(x * tilted, axis=1, keepdims=True))
+
+
+def mid_mixer(inner, total, ins, outs):
+    h0, gain = ins
+    h1, mix_out, gate_scale = outs
+    D = h0.shape[1]
+    s = lax.rsqrt(total[:, D:D + 1] / inner + EPS)
+    out = total[:, :D] * s
+    mix_out[...] = out
+    gate_scale[...] = jnp.broadcast_to(s, gate_scale.shape)
+    h = h0[...].astype(F32) + out
+    h1[...] = h
+    return (h * norm_scale(h) * gain[...]).astype(BF)
+
+
+def mid_attention(total, ins, outs):
+    h1, gain = ins
+    h = h1[...] + total[...]
+    outs[0][...] = h
+    return (h * norm_scale(h) * gain[...]).astype(BF)
+
+
+def mid_ff_back(total, ins, outs):
+    h2, gain, grad = ins
+    dh2, gain_grad = outs
+    d = grad[...].astype(F32) + norm_grad(h2[...], gain[...], total[...], gain_grad)
+    dh2[...] = d
+    return d.astype(BF)
+
+
+def mid_att_back(inner, total, ins, outs):
+    h1, gain, dh2, mix_out, gate_scale = ins
+    dh1, gain_grad = outs
+    d = dh2[...] + norm_grad(h1[...], gain[...], total[...], gain_grad)
+    dh1[...] = d
+    s = gate_scale[:, 0:1]
+    tilt = s * s * jnp.sum(d * mix_out[...], axis=1, keepdims=True) / inner
+    high = tilt.astype(BF).astype(F32)
+    lane = lax.broadcasted_iota(jnp.int32, (d.shape[0], 128), 1)
+    return jnp.concatenate([d * s, jnp.where(lane < 64, high, tilt - high)], axis=1).astype(BF)
+
+
+def mid_mixer_back(total, ins, outs, small):
+    h0, gain, dh1 = ins
+    in_slab, gain_grad = outs
+    D = h0.shape[1]
+    thin = small.shape[1]
+    four = D // thin
+    d = dh1[...] + norm_grad(h0[...].astype(F32), gain[...], total[:, :D], gain_grad)
+    feat = D // NC
+    for i in range(NC):
+        in_slab[i] = d[:, i * feat:(i + 1) * feat]
+    rest = total[:, D:]
+    small[...] = jnp.zeros_like(small)
+    small[:SMALL] = rest[:SMALL]
+    own = rest[SMALL:SMALL + four] + rest[SMALL + four:SMALL + 2 * four]
+    row = gain_grad[0:1]
+    for i in range(3):
+        small[SMALL + i * four:SMALL + (i + 1) * four] = own
+        for j in range(four):
+            at = SMALL + (3 + i) * four + j
+            small[at:at + 1] = row[:, j * thin:(j + 1) * thin]
+
+
+def post_plain(p, at, outs):
+    outs[0][at, :] = p.astype(outs[0].dtype)
+
+
+def post_gelu(p, at, outs):
+    outs[0][at, :] = p
+    outs[1][at, :] = (0.5 * p * (1.0 + jnp.tanh(0.7978845608028654 * (p + 0.044715 * (p * p * p))))).astype(BF)
+
+
 P = jax.sharding.PartitionSpec
-EPS = 1e-05
 
 
 def dot(a, b):
@@ -751,18 +1142,6 @@
 
 def t_dot(a, b):
     return lax.dot_general(a, b, (((0,), (0,)), ((), ())), preferred_element_type=F32)
-
-
-def cols_swap(pieces):
-    c = lax.axis_index("cols")
-    out = jnp.zeros_like(pieces)
-    own = lax.dynamic_index_in_dim(pieces, c, 0, True)
-    out = lax.dynamic_update_slice_in_dim(out, own, c, 0)
-    for s in range(1, NC):
-        away = lax.dynamic_index_in_dim(pieces, (c + s) % NC, 0, True)
-        came = lax.ppermute(away, "cols", [(i, (i + s) % NC) for i in range(NC)])
-        out = lax.dynamic_update_slice_in_dim(out, came, (c - s) % NC, 0)
-    return out
 
 
 def split_in(w):
@@ -785,11 +1164,7 @@
 
 
 def pair_sum(got):
-    return got.astype(F32).reshape((2, NC // 2) + got.shape[1:]).sum(1).astype(BF)
-
-
-def group_sum(own, others):
-    return own.astype(F32) + others.astype(F32).sum(0)
+    return got.astype(F32).reshape((2, NC // 2) + got.shape[1:]).sum(1)
 
 
 def beside(a):
@@ -804,13 +1179,6 @@
 
 def rms_scale(x):
     return lax.rsqrt(jnp.mean(x * x, axis=1, keepdims=True) + EPS)
-
-
-def norm_back(x, gain, scale, up):
-    gain_grad = jnp.sum(x * scale * up, axis=0)
-    tilted = up * gain[None, :]
-    project = jnp.mean(x * tilted, axis=1, keepdims=True)
-    return scale * tilted - x * (scale**3 * project), gain_grad
 
 
 def per_device(hidden_in, lengths, norm1_gain, z_weight, x_weight, bcdt_weight, conv_x_weight, conv_x_bias,
@@ -829,6 +1197,7 @@
     n_heads = heads_row * rows
     seq_lens = lengths[0]
     places = jnp.arange(T, dtype=jnp.int32)
+    one_f32, row8 = ((S, D), F32), ((8, D), F32)
     valid = (places < seq_lens[0] + seq_lens[1]).astype(F32)
     my_valid = lax.dynamic_slice_in_dim(valid, slab * S, S, 0)[:, None]
     pad = 128
@@ -856,9 +1225,6 @@
     w_in = jnp.concatenate([w_bcdt[:, :2 * STATE], w_zx.reshape(D, 2 * wide), w_dt], axis=1)
     qkv_pieces = halved(jnp.concatenate([split_pair(q_weight), split_pair(k_weight), split_pair(v_weight)], axis=2))
     o_pieces = halved(jnp.repeat(att_out_weight.reshape(2, -1, feat), NC // 2, axis=0))
-    grad_output, hidden_all = lax.optimization_barrier((grad_output, hidden_all))
-    grad_all = lax.all_gather(grad_output, ("rows", "cols"), axis=0)
-    grad_all = grad_all.reshape(rows, NC, tok_rows, feat).transpose(0, 2, 1, 3).reshape(T, D)
 
     hid_all = hidden_all.astype(F32)
     u1 = (hid_all * rms_scale(hid_all) * gains[0][None, :]).astype(BF)
@@ -870,77 +1236,67 @@
     pv = jnp.concatenate([wide_row(mine(gate_gain, wide)), wide_row(jnp.repeat(mine(d_skip, heads), HEAD_DIM)),
                           wide_row(mine(dt_bias, heads)), wide_row(-jnp.exp(mine(a_log, heads))), jnp.zeros((4, 256), F32)])
     mixg, squares, y, states = mixer_fwd(seq_lens, proj, cw, pv)
-    part = jnp.concatenate([dot(mixg, w_mix).astype(BF), squares], axis=1)
-    summed, qkv_got, o_got = reduce_scatter16(part, 2, (pair, pair), (qkv_pieces, o_pieces))
+    h0 = lax.dynamic_slice_in_dim(hidden_all, slab * S, S, 0)
+    att3 = qkv_pieces.shape[-1]
+    u2, h1, mix_out, gate_scale, qkv, qkv_got, o_got, grad_got = link(
+        1, mixg, w_mix, functools.partial(mid_mixer, inner), (h0, gains[1:2]), (one_f32, one_f32, ((S, 128), F32)), side=squares,
+        w2_kind="rider", post=post_plain, post_out=(((T, att3), BF),), early=(pair, pair), early_in=(qkv_pieces, o_pieces),
+        late=(("swap", None),), late_in=(grad_output.reshape(NC, S, feat),))
     w_qkv, w_o = qkv_got.reshape(D, -1), whole_out(joined(o_got))
-    gate_scale = lax.rsqrt(summed[:, D:D + 1] / inner + EPS)
-    mix_out = summed[:, :D] * gate_scale
-    h0 = lax.dynamic_slice_in_dim(hidden_all, slab * S, S, 0).astype(F32)
-    h1 = h0 + mix_out
-    s2 = rms_scale(h1)
-    u2, up_got = all_gather16((h1 * s2 * gains[1][None, :]).astype(BF), 3, (pair,), (halved(split_in(up_weight)),))
-    w_up = up_got.reshape(D, -1)
-
-    qkv = dot(u2, w_qkv).astype(BF)
-    att = w_o.shape[0]
+    g3_mine = (grad_got.transpose(1, 0, 2).reshape(S, D).astype(F32) * my_valid).astype(BF)
+    att = att3 // 3
+
     odd = (c % 2)[None]
     attended, att_exact, lse = att_fwd(seq_lens, odd, qkv)
-    att_part, down_got = reduce_scatter16(dot(attended, w_o).astype(BF), 4, (pair,), (halved(down_weight.reshape(NC, -1, feat)),))
-    w_down = whole_out(joined(down_got))
-    h2 = h1 + att_part
-    s3 = rms_scale(h2)
-    u3, = all_gather16((h2 * s3 * gains[2][None, :]).astype(BF), 1)
-
-    act, = (dot(u3, w_up),)
-    gelu, gelu_back = jax.vjp(functools.partial(jax.nn.gelu, approximate=True), act)
-    hid = gelu.astype(BF)
-    h3 = h2 + lax.psum_scatter(dot(hid, w_down).astype(BF), ("rows", "cols"), scatter_dimension=0, tiled=True).astype(F32)
-    out_slab = (h3 * my_valid).astype(BF)
-    output = cols_swap(out_slab.reshape(S, NC, feat).transpose(1, 0, 2)).reshape(NC * S, feat)
-
-    g3 = (grad_all.astype(F32) * valid[:, None]).astype(BF)
-    g3_mine = lax.dynamic_slice_in_dim(g3, slab * S, S, 0).astype(F32)
+    hidden_units = up_weight.shape[1] // NC
+    u3, h2, act, hid, g3, up_got, down_got = link(
+        2, attended, w_o, mid_attention, (h1, gains[2:3]), (one_f32,), w2_kind="rider", post=post_gelu,
+        post_out=(((T, hidden_units), F32), ((T, hidden_units), BF)), early=(pair,), early_in=(halved(split_in(up_weight)),),
+        late=((pair, None),), late_in=(halved(down_weight.reshape(NC, -1, feat)),), more_gather=g3_mine)
+    w_up, w_down = up_got.reshape(D, -1), whole_out(joined(down_got))
+    gelu_back = jax.vjp(functools.partial(jax.nn.gelu, approximate=True), act)[1]
+
+    reduce = "reduce" if pair == "swap2" else "swap"
+
+    def settle(got):
+        return joined(got) if reduce == "reduce" else lax.psum(got, "dp")
+
     d_act = gelu_back(dot_t(g3, w_down))[0].astype(BF)
-    down_pieces = split_grad(t_dot(hid, g3))
-    up_pieces = t_dot(u3, d_act).astype(BF).reshape(NC, feat, -1)
-    d_u3, down_back = reduce_scatter16(dot_t(d_act, w_up).astype(BF), 6, ("swap",), (down_pieces,))
-    d_n3, gain3_grad = norm_back(h2, gains[2], s3, d_u3)
-    dh2 = g3_mine + d_n3
-    g2, up_back, down_other = all_gather16(dh2.astype(BF), 7, ("swap", "dp"), (up_pieces, down_back))
-    down_grad = group_sum(down_back, down_other).reshape(-1, feat)
-    d_att = dot_t(g2, w_o).astype(BF)
-    o_pieces = split_grad(t_dot(attended, g2))
+    down_pieces = halved(split_grad(t_dot(hid, g3)))
+    up_pieces = halved(t_dot(u3, d_act).astype(BF).reshape(NC, feat, -1))
+    g2, dh2, gain3_rows, d_att, ff_out, down_back, up_back = link(
+        3, d_act, w_up, mid_ff_back, (h2, gains[2:3], g3_mine), (one_f32, row8), w1_t=True, w2=w_o, w2_kind="in_t", post=post_plain,
+        post_out=(((T, att), BF),), early=(reduce, reduce), early_in=(down_pieces, up_pieces), more_sum=(hid, w_down))
+    out_slab = ((h2 + ff_out) * my_valid).astype(BF)
+    o_pieces = halved(split_grad(t_dot(attended, g2)))
     d_qkv = att_bwd(seq_lens, odd, qkv, d_att, att_exact, lse)
-    qkv_pieces = t_dot(u2, d_qkv).astype(BF).reshape(NC, feat, -1)
-    d_u2, o_back, up_other = reduce_scatter16(dot_t(d_qkv, w_qkv).astype(BF), 8, ("swap", "dp"), (o_pieces, up_back))
-    up_grad = beside(group_sum(up_back, up_other))
-    o_back = pair_sum(o_back)
-    d_n2, gain2_grad = norm_back(h1, gains[1], s2, d_u2)
-    dh1 = dh2 + d_n2
-    tilt = gate_scale * gate_scale * jnp.sum(dh1 * mix_out, axis=1, keepdims=True) / inner
-    tilt_hi = tilt.astype(BF)
-    tilt_lo = (tilt - tilt_hi.astype(F32)).astype(BF)
-    tail = jnp.concatenate([jnp.broadcast_to(tilt_hi, (S, pad // 2)), jnp.broadcast_to(tilt_lo, (S, pad // 2))], axis=1)
-    g1_ext, qkv_back, o_other = all_gather16(jnp.concatenate([(dh1 * gate_scale).astype(BF), tail], axis=1), 9, ("swap", "dp"), (qkv_pieces, o_back))
-    o_grad = group_sum(o_back, o_other).reshape(-1, feat)
-    qkv_back = pair_sum(qkv_back)
+    qkv_pieces = halved(t_dot(u2, d_qkv).astype(BF).reshape(NC, feat, -1))
+    g1_ext, dh1, gain2_rows, d_mix, o_back, qkv_back, out_got = link(
+        4, d_qkv, w_qkv, functools.partial(mid_att_back, inner), (h1, gains[1:2], dh2, mix_out, gate_scale), (one_f32, row8), w1_t=True,
+        w2=w_mix, w2_kind="in_t", post=post_plain, post_out=(((T, wide), F32),), extra=128,
+        early=(reduce, reduce), early_in=(o_pieces, qkv_pieces), late=(("swap", None),), late_in=(out_slab.reshape(S, NC, feat).transpose(1, 0, 2),))
     g1 = g1_ext[:, :D]
-    d_mix = dot_t(g1, w_mix)
-    mix_pieces = split_grad(t_dot(mixg, g1))
+    output = out_got.reshape(NC * S, feat)
+    down_grad = settle(down_back).astype(F32).reshape(-1, feat)
+    up_grad = beside(settle(up_back)).astype(F32)
+    o_grad = pair_sum(settle(o_back)).reshape(-1, feat)
+    qkv_sum = pair_sum(settle(qkv_back))
+    q_grad, k_grad, v_grad = (beside(qkv_sum[:, :, i * att:(i + 1) * att]) for i in range(3))
+    mix_pieces = halved(split_grad(t_dot(mixg, g1)))
     d_in, tap_grads, row_grads = mixer_bwd(seq_lens, proj, cw, pv, y, states, d_mix, g1_ext)
     cbw_grad, cxw_grad = tap_grads[:CONV, :2 * STATE], tap_grads[:CONV, 2 * STATE:]
     cbb_grad, cxb_grad = tap_grads[CONV, :2 * STATE], tap_grads[CONV, 2 * STATE:]
     gate_gain_grad, dt_bias_grad, a_log_grad = row_grads[0, :wide], row_grads[2, :heads], row_grads[3, :heads]
     d_skip_grad = row_grads[1, :wide].reshape(heads, HEAD_DIM).sum(1)
     in_grad = t_dot(u1, d_in)
-    zx_pieces = in_grad[:, 2 * STATE:2 * STATE + 2 * wide].astype(BF).reshape(NC, feat, -1)
+    zx_pieces = halved(in_grad[:, 2 * STATE:2 * STATE + 2 * wide].astype(BF).reshape(NC, feat, -1))
     slabs = rows * NC
     dt_grads = place_block(in_grad[:, 2 * STATE + 2 * wide:2 * STATE + 2 * wide + heads].astype(BF), slab * heads, bcdt_width + bcdt_pad - 2 * STATE, 1)
     bcdt_part = jnp.concatenate([in_grad[:, :2 * STATE].astype(BF), dt_grads], axis=1).reshape(slabs, SMALL, -1)
     misc = jnp.concatenate([cbw_grad.reshape(-1), cbb_grad] + [
         place_block(a, slab * heads, n_heads, 0) for a in (a_log_grad, d_skip_grad, dt_bias_grad)])
     n_misc = misc.shape[0]
-    small = jnp.concatenate([gain2_grad[None], gain3_grad[None], place_block(cxw_grad, slab * wide, inner, 1).reshape(-1, D),
+    small = jnp.concatenate([gain2_rows[:1], gain3_rows[:1], place_block(cxw_grad, slab * wide, inner, 1).reshape(-1, D),
                              place_block(cxb_grad, slab * wide, inner, 0).reshape(-1, D),
                              place_block(gate_gain_grad, slab * wide, inner, 0).reshape(-1, D), jnp.pad(misc, (0, D - n_misc))[None]])
     thin = bcdt_width + bcdt_pad
@@ -949,20 +1305,9 @@
     small_hi = small.astype(BF)
     small_lo = (small - small_hi.astype(F32)).astype(BF)
     side = jnp.concatenate([bcdt_part, small_hi, small_lo, jnp.zeros((slabs, S - SMALL - 2 * four, thin), BF)], axis=1)
-    payload = jnp.concatenate([dot_t(d_in, w_in).astype(BF), side.reshape(T, thin)], axis=1)
-    d_u1, zx_back, mix_back, qkv_other = reduce_scatter16(
-        payload, 10, ("swap", "swap", "dp"), (zx_pieces, mix_pieces, qkv_back))
-    rest, d_u1 = d_u1[:, D:], d_u1[:, :D]
-    qkv_sum = group_sum(qkv_back, qkv_other)
-    q_grad, k_grad, v_grad = (beside(qkv_sum[:, :, i * att:(i + 1) * att]) for i in range(3))
-    d_n1, gain1_grad = norm_back(h0, gains[0], rms_scale(h0), d_u1)
-    in_slab = dh1 + d_n1
-    own = rest[SMALL:SMALL + four] + rest[SMALL + four:SMALL + 2 * four]
-    gain1_rows = gain1_grad.reshape(four, thin)
-    mine_small = jnp.concatenate([rest[:SMALL], own, own, own, gain1_rows, gain1_rows, gain1_rows,
-                                  jnp.zeros((S - SMALL - 6 * four, thin), F32)])
-    rest_all, in_got, zx_other, mix_other = gather16(
-        mine_small, 11, False, ("swap", "dp", "dp"), (in_slab.reshape(S, NC, feat).transpose(1, 0, 2), zx_back, mix_back), four)
+    rest_all, _, _, zx_back, mix_back, in_got = link(
+        5, d_in, w_in, mid_mixer_back, (h0, gains[0:1], dh1), (((NC, S, feat), F32), row8), w1_t=True, side=side.reshape(T, thin), small=thin,
+        early=(reduce, reduce), early_in=(zx_pieces, mix_pieces), late=(("swap", 0),))
     rest_all = rest_all.reshape(slabs, S, thin)
     bcdt_grad = rest_all[:, :SMALL].reshape(D, thin)[:, :bcdt_width].astype(F32)
     tail_rows = rest_all[:, SMALL:SMALL + 6 * four].astype(F32).reshape(slabs, 6, D)
@@ -976,10 +1321,9 @@
     cbw_sum, cbb_sum = misc[:CONV * 2 * STATE].reshape(CONV, 2 * STATE), misc[CONV * 2 * STATE:(CONV + 1) * 2 * STATE]
     a_log_sum, d_skip_sum, dt_bias_sum = jnp.split(misc[n_misc - 3 * n_heads:n_misc], 3)
     input_grad = in_got.reshape(NC * S, feat)
-    zx_sum = group_sum(zx_back, zx_other)
+    zx_sum = settle(zx_back).astype(F32)
     x_grad, z_grad = beside(zx_sum[:, :, :wide]), beside(zx_sum[:, :, wide:])
-    mix_grad = group_sum(mix_back, mix_other).reshape(-1, feat)
-
+    mix_grad = settle(mix_back).astype(F32).reshape(-1, feat)
     return (output, input_grad, gain1_grad, z_grad, x_grad, bcdt_grad, cxw_sum, cxb_sum, cbw_sum, cbb_sum, a_log_sum, d_skip_sum,
             dt_bias_sum, gate_gain_sum, mix_grad, small[0], q_grad, k_grad, v_grad, o_grad, small[1], up_grad, down_grad)
 

time: 1150 us -> 933 us (0.81)
  matrix products: 112 us -> 48.6 us
  local copies, waits for them, and re-layouts: 129 us -> 65.9 us
  other arithmetic: 79.5 us -> 25.5 us
  Pallas kernels: 797 us -> 782 us
  between operations: 17.2 us -> 3.12 us
    dot_general x6 -> x1, matrix products: 37.3 us -> 7.78 us  [dot(): return jnp.dot(a, b, preferred_element_type=F32)]
    dot_general x6 -> x1, matrix products: 36.5 us -> 8.49 us  [dot_t(): lax.dot_general(a, b, (((1,), (1,)), ((), ())), preferred_element_type=F32)]
    convert_element_type x8 -> x5, other arithmetic: 27.6 us -> 7.6 us  [the longest x1 2.15 us: per_device(): mix_grad = settle(mix_back).astype(F32).reshape(-1, feat)]
    unnamed x192 -> x122, local copies, waits for them, and re-layouts: 46.9 us -> 28.6 us
    pallas_call x11 -> x6, Pallas kernels: 711 us -> 696 us  [the longest x5 600 us: link_call(): pl.pallas_call(kernel, out_shape=[jax.ShapeDtypeStruct(s, d) for s, d in...]
    convert_element_type x4, local copies, waits for them, and re-layouts: 18.6 us -> 5.98 us  [the longest x1 3.97 us: per_device(): qkv_pieces = halved(t_dot(u2, d_qkv).astype(BF).reshape(NC, feat, -1))]
    transpose x8 -> x4, local copies, waits for them, and re-layouts: 12.7 us -> 1.07 us  [beside(): return a.transpose(1, 0, 2).reshape(d, k * n)]
  transfers between devices with their start and end apart: 5 -> 0, of which waited for: 2 -> 0; matrix products, arithmetic and copies ran while one was open for 14% -> 0% of each run, Pallas kernels for 41% -> 0%
where the time goes in v3:
time: 933 us; the launch traced here: 925 us
  Pallas kernels  782 us (84%)
  local copies, waits for them, and re-layouts  65.9 us (7%)
  matrix products  48.6 us (5%)
  other arithmetic  25.5 us (3%)
    pallas_call x5, Pallas kernels, link_call(): pl.pallas_call(kernel, out_shape=[jax.ShapeDtypeStruct(s, d) for s, d in...  600 us
    pallas_call x1, Pallas kernels, gather16(): pl.pallas_call(functools.partial(ag_kernel, native, at, tuple(kinds)), ou...  95.4 us
    pallas_call x2, Pallas kernels, att_call(): pl.pallas_call(kernel, grid=(4,), in_specs=specs, out_specs=out_specs, ou...  37.6 us
    dot_general x6, matrix products, t_dot(): lax.dot_general(a, b, (((0,), (0,)), ((), ())), preferred_element_type=F32)  32.4 us
    pallas_call x1, Pallas kernels, mixer_bwd(): pl.pallas_call(mixer_bwd_kernel, grid=(n,), in_specs=first + [block(WIDE)...  32.3 us
    unnamed x122, local copies, waits for them, and re-layouts  28.6 us

profile of v3, /device:TPU:0, one launch (start us, length us, event | category | flops | bytes accessed | tf_op | source)
XLA Modules:
  0.0 924.8 jit_solution(14262122698339081177)
XLA Ops:
  4.4 1.4 copy.100
  5.8 1.4 copy.101
  8.6 1.1 copy-done.2
  9.7 1.0 copy-done.5
  10.7 95.4 %shard_map.407 = (bf16[2048,1536]{1,0:T(8,128)(2,1)}, bf16[4,2,192,384]{3,2,1,0:T(8,128)(2,1)S(1)}, bf16[4,2,96,384]{3,2,1,0:T(8,128)(2,1)S(1)}, bf16[4,2,192,38...) custom-call(bf16[512,384]{1,0:T(8,128)(2,1)S(1)} %copy-done.5, bf16[4,2,192,384]{3,2,1,0:T(8,128)(2,1)S(1)} %bitcast.169, ...), custom_call_target="tpu_custom_call" | custom-call | bytes 67108864 | tf_op jit(solution)/shard_map/pallas_call | solution.py:269
  106.1 0.8 copy-done.3
  107.9 4.2 fusion
  112.5 7.8 fusion.18.proj.before
  121.3 15.9 %shard_map.408 = (bf16[2048,192]{1,0:T(8,128)(2,1)S(1)}, bf16[2048,128]{1,0:T(8,128)(2,1)S(1)}, f32[2048,192]{1,0:T(8,128)S(1)}, f32[8,192,128]{2,1,0:T(8,128)S(1)}) custom-call(s32[2]{0:T(128)S(1)} %bitcast.179, f32[2048,768]{1,0:T(8,128)} %fusion.18.proj.before, f32[2048,768]{1,0:T(8,128)} %fusion.18.proj.before, f32[8,448]{1,0:T(8,128)S(1)} %maximum_maximum_fusion.1.cw, ...), custom_call_target="tpu_custom_call" | custom-call | flops 4294967296 | bytes 16777216 | tf_op jit(solution)/shard_map/pallas_call | solution.py:476
  137.2 1.3 copy-done.10
  138.5 0.9 copy-done.12
  140.2 1.8 constant_dynamic-slice_fusion.refs_3_
  142.5 0.9 copy.145
  143.9 1.2 copy.107
  145.3 0.9 broadcast_in_dim.70
  146.2 1.2 copy.109
  147.6 3.3 pad_maximum_fusion.refs_5_
  150.9 0.9 broadcast_in_dim.72
  151.7 103.2 %shard_map.409 = (bf16[2048,1536]{1,0:T(8,128)(2,1)}, f32[128,1536]{1,0:T(8,128)}, f32[128,1536]{1,0:T(8,128)}, f32[128,128]{1,0:T(8,128)}, bf16[2048,576]{1,0:T...) custom-call(bf16[2048,192]{1,0:T(8,128)(2,1)} %copy-done.12, ...), custom_call_target="tpu_custom_call" | custom-call | flops 8589934592 | bytes 100663296 | tf_op jit(solution)/shard_map/pallas_call | solution.py:880
  255.0 16.7 %shard_map.410 = (bf16[2048,192]{1,0:T(8,128)(2,1)}, f32[2048,192]{1,0:T(8,128)}, f32[2048,128]{1,0:T(8,128)}) custom-call(s32[2]{0:T(128)} %bitcast.177, s32[1]{0:T(128)} %bitcast.1.odd, bf16[2048,576]{1,0:T(8,128)(2,1)} %get-tuple-element.78.qkv), custom_call_target="tpu_custom_call" | custom-call | flops 8589934592 | bytes 16777216 | tf_op jit(solution)/shard_map/pallas_call | solution.py:616
  274.2 0.9 multiply_convert_fusion.1.refs_4_
  275.5 0.9 copy.146
  276.4 1.1 copy.155
  277.5 140.2 %shard_map.411 = (bf16[2048,1536]{1,0:T(8,128)(2,1)}, f32[128,1536]{1,0:T(8,128)}, f32[2048,384]{1,0:T(8,128)}, bf16[2048,384]{1,0:T(8,128)(2,1)}, bf16[2048,153...) custom-call(bf16[2048,192]{1,0:T(8,128)(2,1)} %get-tuple-element.79.refs_0_, ...), custom_call_target="tpu_custom_call" | custom-call | flops 8589934592 | bytes 100663296 | tf_op jit(solution)/shard_map/pallas_call | solution.py:880
  417.8 2.3 copy.114
  420.4 8.5 fusion.12.refs_0_
  428.9 4.5 convolution_convert_fusion.2
  433.4 2.6 convolution_convert_fusion.3
  436.1 1.1 copy.154
  437.2 128.5 %shard_map.412 = (bf16[2048,1536]{1,0:T(8,128)(2,1)}, f32[128,1536]{1,0:T(8,128)}, f32[8,1536]{1,0:T(8,128)}, bf16[2048,192]{1,0:T(8,128)(2,1)}, f32[128,1536]{1...) custom-call(bf16[2048,384]{1,0:T(8,128)(2,1)} %copy-done.42, ...), custom_call_target="tpu_custom_call" | custom-call | flops 8589934592 | bytes 100663296 | tf_op jit(solution)/shard_map/pallas_call | solution.py:880
  565.7 1.5 multiply_convert_fusion
  567.4 0.9 copy.119
  568.3 20.9 %shard_map.413.refs_0_ = bf16[2048,576]{1,0:T(8,128)(2,1)} custom-call(s32[2]{0:T(128)} %bitcast.178, s32[1]{0:T(128)} %bitcast.1.odd, bf16[2048,576]{1,0:T(8,128)(2,1)} %get-tuple-element.78.qkv, bf16[2048,192]{1,0:T(8,128)(2,1)} %get-tuple-element.90.d_att, f32[2048,192]{1,0:T(8,128)} %get-tuple-element.91.o_ref, f32[2048,128]{1,0:T(8,128)} %get-tuple-element.92.lse), custom_call_target="tpu_custom_call" | custom-call | flops 8589934592 | bytes 16777216 | tf_op jit(solution)/shard_map/pallas_call | solution.py:616
  589.3 8.6 convolution_convert_fusion.1
  597.9 4.0 copy.117
  601.9 4.2 convolution_convert_fusion.4
  606.1 0.9 copy.157
  607.0 114.5 %shard_map.414 = (bf16[2048,1664]{1,0:T(8,128)(2,1)}, f32[128,1536]{1,0:T(8,128)}, f32[8,1536]{1,0:T(8,128)}, f32[2048,192]{1,0:T(8,128)}, bf16[4,2,96,384]{3,2,...) custom-call(bf16[2048,576]{1,0:T(8,128)(2,1)} %shard_map.413.refs_0_, ...), custom_call_target="tpu_custom_call" | custom-call | flops 8589934592 | bytes 100663296 | tf_op jit(solution)/shard_map/pallas_call | solution.py:880
  721.5 4.4 fusion.13
  725.9 0.9 copy.156
  726.8 32.3 %shard_map.415 = (bf16[2048,768]{1,0:T(8,128)(2,1)}, f32[8,448]{1,0:T(8,128)S(1)}, f32[8,256]{1,0:T(8,128)S(1)}) custom-call(s32[2]{0:T(128)S(1)} %bitcast.180, f32[2048,768]{1,0:T(8,128)} %fusion.18.proj.before, f32[2048,768]{1,0:T(8,128)} %fusion.18.proj.before, f32[8,448]{1,0:T(8,128)S(1)} %maximum_maximum_fusion.1.cw, f32[8,256]{1,0:T(8,128)S(1)} %copy-done.6, ...), custom_call_target="tpu_custom_call" | custom-call | flops 12884901888 | bytes 25165824 | tf_op jit(solution)/shard_map/pallas_call | solution.py:495
  759.1 8.0 convolution_convert_fusion
  767.3 1.3 copy-done.17
  768.9 1.1 pad_maximum_fusion.2
  770.0 1.7 copy.120
  775.5 1.7 maximum_maximum_fusion
  777.2 1.4 copy.121
  778.6 1.6 fusion.16.refs_1_
  780.3 114.0 %shard_map.416 = (bf16[2048,384]{1,0:T(8,128)(2,1)}, f32[4,128,384]{2,1,0:T(8,128)}, f32[8,1536]{1,0:T(8,128)}, bf16[4,2,192,384]{3,2,1,0:T(8,128)(2,1)}, bf16[4...) custom-call(bf16[2048,768]{1,0:T(8,128)(2,1)} %get-tuple-element.105.refs_0_, bf16[1536,768]{1,0:T(8,128)(2,1)} %fusion.16.refs_1_, ...), custom_call_target="tpu_custom_call" | custom-call | flops 8589934592 | bytes 100663296 | tf_op jit(solution)/shard_map/pallas_call | solution.py:880
  894.3 1.4 bitcast_convert_fusion.1
  896.2 1.5 copy.136
  897.7 2.7 copy.129
  900.8 1.4 copy.130
  902.7 1.8 copy.131
  904.5 1.0 slice_convert_fusion.1
  905.6 1.0 slice_add_fusion
  910.5 2.2 bitcast_convert_fusion.2
  913.6 1.1 copy.132
  914.9 1.1 copy.133
  916.2 1.1 copy.134
  917.2 2.0 convert_reduce_fusion.1
  919.6 1.7 copy.144
  921.3 1.7 bitcast_convert_fusion
  923.7 0.9 copy.176
  (205 shorter events, 23.5 us)
Async XLA Ops:
  0.7 119.6 %copy-start = (f32[4,768]{1,0:T(4,128)S(1)}, f32[4,768]{1,0:T(4,128)}, u32[]{:S(2)}) copy-start(f32[4,768]{1,0:T(4,128)} %param.30) | copy-start | bytes 36868
  7.2 1.4 copy-start.37
  7.3 0.9 copy-start.35
  7.3 1.2 copy-start.38
  7.3 1.2 copy-start.39
  8.6 1.1 copy-start.2
  9.7 1.0 copy-start.5
  106.1 0.8 copy-start.3
  107.1 5.1 copy-start.22
  107.9 4.6 copy-start.16
  112.2 8.1 copy-start.19
  112.5 8.6 copy-start.40
  112.5 8.7 copy-start.36
  112.5 8.8 copy-start.6
  112.5 8.8 copy-start.7
  121.3 20.8 %copy-start.4 = (bf16[4,2,96,384]{3,2,1,0:T(8,128)(2,1)S(1)}, bf16[4,2,96,384]{3,2,1,0:T(8,128)(2,1)}, u32[]{:S(2)}) copy-start(bf16[4,2,96,384]{3,2,1,0:T(8,128)(2,1)} %copy-done.3) | copy-start | bytes 1769476
  137.2 1.3 copy-start.10
  138.5 0.9 copy-start.12
  139.4 0.8 copy-start.14
  140.2 3.2 copy-start.34
  147.6 3.3 copy-start.33
  254.9 16.7 %copy-start.32 = (bf16[4,128,384]{2,1,0:T(8,128)(2,1)S(1)}, bf16[4,128,384]{2,1,0:T(8,128)(2,1)}, u32[]{:S(2)}) copy-start(bf16[4,128,384]{2,1,0:T(8,128)(2,1)} %get-tuple-element.82) | copy-start | bytes 1179652
  271.6 0.7 copy-start.8
  271.6 3.4 copy-start.30
  271.7 4.7 copy-start.27
  417.8 2.6 copy-start.43
  420.1 8.8 slice-start.5
  420.1 13.3 %slice-start.3 = ((s8[6291456]{0:T(1024)(128)(4,1)}), s8[4194304]{0:T(1024)(128)(4,1)S(1)}, s32[]{:S(2)}) async-start(s8[6291456]{0:T(1024)(128)(4,1)} %bitcast.258), calls=%async_computation.3 | async-start | bytes 8388608
  420.3 8.5 copy-start.28
  420.3 8.5 slice-start.6
  420.3 13.1 %slice-start.4 = ((s8[6291456]{0:T(1024)(128)(4,1)}), s8[2097152]{0:T(1024)(128)(4,1)S(1)}, s32[]{:S(2)}) async-start(s8[6291456]{0:T(1024)(128)(4,1)} %bitcast.258), calls=%async_computation.4 | async-start | bytes 4194304
  428.9 4.5 copy-start.42
  428.9 4.5 copy-start.41
  597.9 4.0 copy-start.18
  607.0 114.5 %copy-start.13 = (bf16[2048,192]{1,0:T(8,128)(2,1)S(1)}, bf16[2048,192]{1,0:T(8,128)(2,1)}, u32[]{:S(2)}) copy-start(bf16[2048,192]{1,0:T(8,128)(2,1)} %copy-done.12) | copy-start | bytes 2359300
  721.5 5.3 copy-start.9
  721.5 5.3 copy-start.11
  721.5 5.3 copy-start.15
  721.5 37.6 %slice-start = ((s8[6291456]{0:T(1024)(128)(4,1)}), s8[4194304]{0:T(1024)(128)(4,1)S(1)}, s32[]{:S(2)}) async-start(s8[6291456]{0:T(1024)(128)(4,1)} %bitcast.181), calls=%async_computation | async-start | bytes 8388608
  726.8 32.3 %slice-start.1 = ((s8[6291456]{0:T(1024)(128)(4,1)}), s8[2097152]{0:T(1024)(128)(4,1)S(1)}, s32[]{:S(2)}) async-start(s8[6291456]{0:T(1024)(128)(4,1)} %bitcast.181), calls=%async_computation.1 | async-start | bytes 4194304
  767.2 1.4 copy-start.17
  775.5 1.7 slice-start.2
  777.2 1.4 copy-start.20
  777.2 1.4 copy-start.23
  900.8 1.6 copy-start.24
  905.5 7.1 copy-start.21
  914.9 4.4 copy-start.26
  919.5 1.7 copy-start.25
  921.3 1.7 copy-start.31
  921.3 2.4 copy-start.29
  921.3 3.3 copy-start.1

commit v4 on v3

--- a/solution.py
+++ b/solution.py
@@ -12,17 +12,19 @@
     return pltpu.make_async_remote_copy(src_ref=src, dst_ref=dst, send_sem=send, recv_sem=recv, device_id=dev, device_id_type=MESH)
 
 
-def greet(r, c, kinds=()):
+def greet(r, c, kinds=(), partners=True):
     barrier = pltpu.get_barrier_semaphore()
-    all_cols = any(kind != "dp" for kind in kinds)
-    pl.semaphore_signal(barrier, inc=1, device_id={"rows": r ^ 1}, device_id_type=MESH)
-    pl.semaphore_signal(barrier, inc=1, device_id={"rows": r ^ 2}, device_id_type=MESH)
-    count = 2
+    all_cols = any(kind not in ("dp", "half", "spread") for kind in kinds)
+    count = 0
+    if partners:
+        pl.semaphore_signal(barrier, inc=1, device_id={"rows": r ^ 1}, device_id_type=MESH)
+        pl.semaphore_signal(barrier, inc=1, device_id={"rows": r ^ 2}, device_id_type=MESH)
+        count = 2
     if all_cols:
         for s in range(1, NC):
             pl.semaphore_signal(barrier, inc=1, device_id={"cols": lax.rem(c + s, NC)}, device_id_type=MESH)
         count += NC - 1
-    else:
+    elif partners:
         @pl.when(c > 0)
         def _():
             pl.semaphore_signal(barrier, inc=1, device_id={"cols": c - 1}, device_id_type=MESH)
@@ -31,7 +33,7 @@
         def _():
             pl.semaphore_signal(barrier, inc=1, device_id={"cols": c + 1}, device_id_type=MESH)
         count = count + jnp.where(c > 0, 1, 0) + jnp.where(c < NC - 1, 1, 0)
-    if any(kind in ("dp", "swap2", "reduce") for kind in kinds):
+    if any(kind in ("dp", "swap2", "half", "spread", "reduce") for kind in kinds):
         groups = lax.axis_size("dp")
         for s in range(1, groups):
             pl.semaphore_signal(barrier, inc=1, device_id={"dp": lax.rem(lax.axis_index("dp") + s, groups)}, device_id_type=MESH)
@@ -47,6 +49,23 @@
         held = iter(held)
         for e, kind in enumerate(kinds):
             src, dst = ins[e], outs[e]
+            if kind == "half":
+                self.remote.append(copy_to(src.at[:, 1 - g], dst, send.at[e, 0], recv.at[e, 0], {"dp": 1 - g}))
+                continue
+            if kind == "spread":
+                place = dst.at[:, g] if groups == 2 else dst
+                self.local.append(pltpu.make_async_copy(src, place, loc.at[e]))
+                if groups == 2:
+                    self.remote.append(copy_to(src, place, send.at[e, 0], recv.at[e, 0], {"dp": 1 - g}))
+                continue
+            if kind == "swaph":
+                few = src.shape[0] != NC
+                piece = lambda to, few=few, src=src: src.at[to >> 1 if few else to, g]
+                for s in range(1, NC):
+                    to = lax.rem(c + s, NC)
+                    self.remote.append(copy_to(piece(to), dst.at[c], send.at[e, s - 1], recv.at[e, s - 1], {"cols": to}))
+                self.local.append(pltpu.make_async_copy(piece(c), dst.at[c], loc.at[e]))
+                continue
             if kind == "dp":
                 for s in range(1, groups):
                     self.remote.append(copy_to(src, dst.at[s - 1], send.at[e, s - 1], recv.at[e, s - 1], {"dp": lax.rem(g + s, groups)}))
@@ -64,14 +83,15 @@
                 own, got = next(held), next(held)
                 first = copy_to(src.at[:, 1 - g], got, send.at[e, 2 * NC - 1], recv.at[e, 2 * NC - 1], other)
                 self.sums.append((first, pltpu.make_async_copy(src.at[:, g], own, loc.at[e]), own, got, pairs))
-                piece = lambda to: own.at[to]
+                piece = lambda to, own=own: own.at[to]
                 keep = pltpu.make_async_copy(own.at[c], dst.at[c, g], loc.at[e])
                 pairs.append((None, keep, copy_to(own.at[c], dst.at[c, g], send.at[e, NC - 1], recv.at[e, NC - 1], other)))
             elif kind == "swap2":
-                piece = lambda to: src.at[to, half]
-                self.local.append(pltpu.make_async_copy(src.at[c], dst.at[c], loc.at[e]))
+                few = src.shape[0] != NC
+                piece = lambda to, few=few, src=src, half=half: src.at[to >> 1 if few else to, half]
+                self.local.append(pltpu.make_async_copy(src.at[c >> 1 if few else c], dst.at[c], loc.at[e]))
             else:
-                piece = lambda to: src.at[half]
+                piece = lambda to, src=src, half=half: src.at[half]
                 self.local.append(pltpu.make_async_copy(src, dst.at[c], loc.at[e]))
             for s in range(1, NC):
                 to, came = lax.rem(c + s, NC), lax.rem(c + NC - s, NC)
@@ -121,7 +141,13 @@
     groups = lax.axis_size("dp")
     shapes = []
     for kind, a in zip(kinds, arrays):
-        lead = {"swap": (), "swap2": (), "reduce": (), "bcast2": (NC,), "dp": (groups - 1,)}[kind]
+        if kind == "swap2":
+            a = jax.ShapeDtypeStruct((NC,) + a.shape[1:], a.dtype)
+        if kind in ("half", "swaph"):
+            a = jax.ShapeDtypeStruct((NC,) + a.shape[2:], a.dtype)
+        if kind == "spread":
+            a = jax.ShapeDtypeStruct((NC,) + (2,) * (groups == 2) + a.shape[1:], a.dtype)
+        lead = {"swap": (), "swap2": (), "half": (), "swaph": (), "spread": (), "reduce": (), "bcast2": (NC,), "dp": (groups - 1,)}[kind]
         shapes.append(jax.ShapeDtypeStruct(lead + a.shape, a.dtype))
     n, most = len(kinds), max(2 * NC, groups)
     sems = [pltpu.SemaphoreType.DMA((n, most)), pltpu.SemaphoreType.DMA((n, most)), pltpu.SemaphoreType.DMA((n,))] if n else []
@@ -139,147 +165,55 @@
     copies = [copy_to(x_ref, others.at[s - 1], dp_s.at[s - 1], dp_r.at[s - 1], {"dp": lax.rem(g + s, groups)}) for s in range(1, groups)]
     for one in copies:
         one.start()
-    total = x_ref[...]
-    for s, one in enumerate(copies):
-        one.wait()
-        total = total + others[s]
-    part = (lax.broadcasted_iota(jnp.int32, total.shape, 0) - SMALL) // n
-    rest = total - total.astype(BF).astype(F32)
-    rest2 = rest - rest.astype(BF).astype(F32)
-    second, third = (part == 1) | (part == 4), (part == 2) | (part == 5)
-    held[...] = jnp.where(second, rest, jnp.where(third, rest2, total)).astype(BF)
-    return held
-
-
-def ag_kernel(native, at, kinds, *refs):
+
+    def settle():
+        total = x_ref[...]
+        for s, one in enumerate(copies):
+            one.wait()
+            total = total + others[s]
+        part = (lax.broadcasted_iota(jnp.int32, total.shape, 0) - SMALL) // n
+        rest = total - total.astype(BF).astype(F32)
+        rest2 = rest - rest.astype(BF).astype(F32)
+        second, third = (part == 1) | (part == 4), (part == 2) | (part == 5)
+        held[...] = jnp.where(second, rest, jnp.where(third, rest2, total)).astype(BF)
+    return settle
+
+
+def ridden(kernel, n_in, n_out, kinds):
     n = len(kinds)
-    x_ref, ins, out_ref, outs = refs[0], refs[1:1 + n], refs[1 + n], refs[2 + n:2 + 2 * n]
-    recv, zr_s, zl_s, y_s, k_s, loc, *sems = refs[2 + 2 * n:]
-    r, c = lax.axis_index("rows"), lax.axis_index("cols")
-    S, W = x_ref.shape
-    greet(r, c, kinds)
-    riding = Riders(kinds, ins, outs, *sems) if n else Riders((), (), (), None, None, None)
-
-    def slab(rr, cc):
-        if native:
-            return out_ref.at[pl.ds(pl.multiple_of(rr * S, 16), S), pl.ds(pl.multiple_of(cc * W, 128), W)]
-        return out_ref.at[pl.ds(pl.multiple_of((rr * NC + cc) * S, 16), S)]
-
-    def right(cc, src):
-        return copy_to(src, slab(r, cc), zr_s.at[cc], recv.at[r * NC + cc], {"cols": c + 1})
-
-    def left(cc, src):
-        return copy_to(src, slab(r, cc), zl_s.at[cc], recv.at[r * NC + cc], {"cols": c - 1})
-
-    def ycopy(cc, src):
-        return copy_to(src, slab(r, cc), y_s.at[cc], recv.at[r * NC + cc], {"rows": r ^ 2})
-
-    def kcopy(rr, cc, src):
-        return copy_to(src, slab(rr, cc), k_s.at[(rr >> 1) * NC + cc], recv.at[rr * NC + cc], {"rows": r ^ 1})
-
-    def got(rr, cc):
-        copy_to(slab(rr, cc), slab(rr, cc), k_s.at[0], recv.at[rr * NC + cc], {"rows": r ^ 1}).wait_recv()
-
-    @pl.when(c < NC - 1)
-    def _():
-        right(c, x_ref).start()
-
-    @pl.when(c > 0)
-    def _():
-        left(c, x_ref).start()
-    ycopy(c, x_ref).start()
-    kcopy(r, c, x_ref).start()
-    own = pltpu.make_async_copy(x_ref, slab(r, c), loc)
-    own.start()
-    if at == 0:
-        riding.start()
-
-    def from_y(cc):
-        got(r ^ 2, cc)
-        kcopy(r ^ 2, cc, slab(r ^ 2, cc)).start()
-
-    for d in range(1, NC):
-        @pl.when(c >= d)
+
+    def run(*refs):
+        ins, rest = refs[:n_in], refs[n_in + n:]
+        outs, tail = rest[:n_out], rest[n_out + n:]
+        riding = Riders(kinds, refs[n_in:n_in + n], rest[n_out:n_out + n], *tail[-3:])
+        step = pl.program_id(0)
+
+        @pl.when(step == 0)
         def _():
-            cc = c - d
-            got(r, cc)
-
-            @pl.when(c < NC - 1)
-            def _():
-                right(cc, slab(r, cc)).start()
-            ycopy(cc, slab(r, cc)).start()
-            kcopy(r, cc, slab(r, cc)).start()
-
-        @pl.when(c + d < NC)
+            greet(lax.axis_index("rows"), lax.axis_index("cols"), kinds, False)
+            riding.start()
+        kernel(*ins, *outs, *tail[:-3])
+
+        @pl.when(step == pl.num_programs(0) - 1)
         def _():
-            cc = c + d
-            got(r, cc)
-
-            @pl.when(c > 0)
-            def _():
-                left(cc, slab(r, cc)).start()
-            ycopy(cc, slab(r, cc)).start()
-            kcopy(r, cc, slab(r, cc)).start()
-        if d == at:
-            riding.start()
-        if d == 1:
-            from_y(c)
-        else:
-            @pl.when(c >= d - 1)
-            def _():
-                from_y(c - (d - 1))
-
-            @pl.when(c + d - 1 < NC)
-            def _():
-                from_y(c + d - 1)
-    d = NC
-
-    @pl.when(c >= d - 1)
-    def _():
-        from_y(c - (d - 1))
-
-    @pl.when(c + d - 1 < NC)
-    def _():
-        from_y(c + d - 1)
-    for cc in range(NC):
-        got(r ^ 1, cc)
-        got(r ^ 3, cc)
-    own.wait()
-    for cc in range(NC):
-        y_c = ycopy(cc, slab(r, cc))
-        y_c.wait_send()
-        kcopy(r, cc, slab(r, cc)).wait_send()
-        kcopy(r ^ 2, cc, slab(r ^ 2, cc)).wait_send()
-
-        @pl.when((cc <= c) & (c < NC - 1))
-        def _():
-            right(cc, slab(r, cc)).wait_send()
-
-        @pl.when((cc >= c) & (c > 0))
-        def _():
-            left(cc, slab(r, cc)).wait_send()
-    riding.relay()
-    riding.finish()
-
-
-def gather16(x, cid, native, kinds, arrays, at=0):
-    S, D = x.shape
+            riding.finish()
+    return run
+
+
+def ridden_call(kernel, cid, grid, ins, in_specs, outs, out_specs, scratch, flops, kinds, arrays):
     shapes, sems = rider_parts(kinds, arrays)
-    any_space = pl.BlockSpec(memory_space=pl.ANY)
+    any_space = [pl.BlockSpec(memory_space=pl.ANY)] * len(kinds)
     return pl.pallas_call(
-        functools.partial(ag_kernel, native, at, tuple(kinds)),
-        out_shape=[jax.ShapeDtypeStruct((4 * S, NC * D) if native else (16 * S, D), BF)] + shapes,
-        in_specs=[pl.BlockSpec(memory_space=pltpu.VMEM)] + [any_space] * len(kinds),
-        out_specs=[pl.BlockSpec(memory_space=pltpu.VMEM)] + [any_space] * len(kinds),
-        scratch_shapes=[pltpu.SemaphoreType.DMA((16,)), pltpu.SemaphoreType.DMA((NC,)), pltpu.SemaphoreType.DMA((NC,)),
-                        pltpu.SemaphoreType.DMA((NC,)), pltpu.SemaphoreType.DMA((2 * NC,)), pltpu.SemaphoreType.DMA] + sems,
-        compiler_params=pltpu.CompilerParams(collective_id=cid, has_side_effects=True, vmem_limit_bytes=48 << 20),
-        cost_estimate=pl.CostEstimate(flops=0, bytes_accessed=64 << 20, transcendentals=0),
-    )(x, *arrays)
-
-
-def gather_native(x, cid, kinds=(), arrays=()):
-    return gather16(x, cid, True, kinds, arrays)
+        ridden(kernel, len(ins), len(outs), tuple(kinds)),
+        grid=(grid,),
+        in_specs=list(in_specs) + any_space,
+        out_specs=list(out_specs) + any_space,
+        out_shape=[jax.ShapeDtypeStruct(*o) for o in outs] + shapes,
+        scratch_shapes=list(scratch) + sems,
+        compiler_params=pltpu.CompilerParams(collective_id=cid, has_side_effects=True, vmem_limit_bytes=56 << 20,
+                                             dimension_semantics=("arbitrary",)),
+        cost_estimate=pl.CostEstimate(flops=flops, bytes_accessed=24 << 20, transcendentals=4 << 20),
+    )(*ins, *arrays)
 
 
 HEAD_DIM = 64
@@ -368,13 +302,25 @@
         return jnp.where(self.lane // HEAD_DIM == h, a, 0.0)
 
 
-def mixer_fwd_kernel(lens, proj, before, cw, pv, mixg, squares, y_out, states, state):
+def mixer_fwd_kernel(lens, hidden, gain, w_bc, w_xz, w_dt, cw, pv, u_out, proj_out, mixg, squares, y_out, states, state, before):
     blk = pl.program_id(0)
 
     @pl.when(blk == 0)
     def _():
         state[...] = jnp.zeros_like(state)
-    k = Block(blk, lens, proj[...], before[...], cw[...], pv[...])
+        before[...] = jnp.zeros_like(before)
+    parts = [hidden[0, i].astype(F32) for i in range(NC)]
+    feat = parts[0].shape[1]
+    squares_in = sum(jnp.sum(p * p, axis=1, keepdims=True) for p in parts)
+    scale = lax.rsqrt(squares_in / (NC * feat) + 1e-05)
+    for i, p in enumerate(parts):
+        at = slice(i * feat, (i + 1) * feat)
+        u_out[:, at] = (p * scale * gain[:, at]).astype(BF)
+    u = u_out[...]
+    proj = jnp.concatenate([mm(u, w_bc[:, :2 * STATE]), mm(u, w_xz[...]), mm(u, w_dt[...])], axis=1)
+    proj_out[...] = proj
+    k = Block(blk, lens, proj, before[...], cw[...], pv[...])
+    before[...] = proj[SPAN - 8:]
     s_in = state[...]
     states[0] = s_in
     y = mm(k.c, s_in, 1, 1) * k.e
@@ -469,41 +415,34 @@
     return block, whole, [pl.BlockSpec(memory_space=pltpu.SMEM), block(MIX + WIDE + 128), before, whole((8, MIX)), whole((8, 256))]
 
 
-def mixer_fwd(lens, proj, cw, pv):
-    T = proj.shape[0]
-    n = T // SPAN
-    block, whole, first = mixer_specs(n, lambda i: i)
-    return pl.pallas_call(
-        mixer_fwd_kernel,
-        grid=(n,),
-        in_specs=first,
-        out_specs=[block(WIDE), block(128), block(WIDE), pl.BlockSpec((1, WIDE, STATE), lambda i: (i, 0, 0))],
-        out_shape=[jax.ShapeDtypeStruct((T, WIDE), BF), jax.ShapeDtypeStruct((T, 128), BF), jax.ShapeDtypeStruct((T, WIDE), F32),
-                   jax.ShapeDtypeStruct((n, WIDE, STATE), F32)],
-        scratch_shapes=[pltpu.VMEM((WIDE, STATE), F32)],
-        compiler_params=pltpu.CompilerParams(vmem_limit_bytes=48 << 20, dimension_semantics=("arbitrary",)),
-        cost_estimate=pl.CostEstimate(flops=4 << 30, bytes_accessed=16 << 20, transcendentals=4 << 20),
-    )(lens, proj, proj, cw, pv)
-
-
-def mixer_bwd(lens, proj, cw, pv, y, states, d_mix, g1_ext):
+def mixer_fwd(cid, lens, hidden, gain, w_bc, w_xz, w_dt, cw, pv, kinds, arrays):
+    _, _, tok, feat = hidden.shape
+    T, D = hidden.shape[0] * tok, NC * feat
+    n, per = T // SPAN, tok // SPAN
+    block, whole, _ = mixer_specs(n, lambda i: i)
+    cols = MIX + WIDE + 128
+    return ridden_call(
+        mixer_fwd_kernel, cid, n, (lens, hidden, gain, w_bc, w_xz, w_dt, cw, pv),
+        [pl.BlockSpec(memory_space=pltpu.SMEM), pl.BlockSpec((1, NC, SPAN, feat), lambda i: (i // per, 0, i % per, 0)),
+         whole((1, D)), whole(w_bc.shape), whole(w_xz.shape), whole(w_dt.shape), whole((8, MIX)), whole((8, 256))],
+        [((T, D), BF), ((T, cols), F32), ((T, WIDE), BF), ((T, 128), BF), ((T, WIDE), F32), ((n, WIDE, STATE), F32)],
+        [block(D), block(cols), block(WIDE), block(128), block(WIDE), pl.BlockSpec((1, WIDE, STATE), lambda i: (i, 0, 0))],
+        [pltpu.VMEM((WIDE, STATE), F32), pltpu.VMEM((8, cols), F32)], 8 << 30, kinds, arrays)
+
+
+def mixer_bwd(cid, lens, proj, cw, pv, y, states, d_mix, g1_ext, kinds, arrays):
     T = proj.shape[0]
     n = T // SPAN
     order = lambda i: n - 1 - i
     block, whole, first = mixer_specs(n, order)
     at = g1_ext.shape[1] // 128 - 1
-    return pl.pallas_call(
-        mixer_bwd_kernel,
-        grid=(n,),
-        in_specs=first + [block(WIDE), pl.BlockSpec((1, WIDE, STATE), lambda i: (order(i), 0, 0)), block(WIDE),
-                          pl.BlockSpec((SPAN, 128), lambda i: (order(i), at))],
-        out_specs=[block(MIX + WIDE + 128), whole((8, MIX)), whole((8, 256))],
-        out_shape=[jax.ShapeDtypeStruct((T, MIX + WIDE + 128), BF), jax.ShapeDtypeStruct((8, MIX), F32),
-                   jax.ShapeDtypeStruct((8, 256), F32)],
-        scratch_shapes=[pltpu.VMEM((WIDE, STATE), F32), pltpu.VMEM((8, MIX), F32)],
-        compiler_params=pltpu.CompilerParams(vmem_limit_bytes=48 << 20, dimension_semantics=("arbitrary",)),
-        cost_estimate=pl.CostEstimate(flops=12 << 30, bytes_accessed=24 << 20, transcendentals=8 << 20),
-    )(lens, proj, proj, cw, pv, y, states, d_mix, g1_ext)
+    return ridden_call(
+        mixer_bwd_kernel, cid, n, (lens, proj, proj, cw, pv, y, states, d_mix, g1_ext),
+        first + [block(WIDE), pl.BlockSpec((1, WIDE, STATE), lambda i: (order(i), 0, 0)), block(WIDE),
+                 pl.BlockSpec((SPAN, 128), lambda i: (order(i), at))],
+        [((T, MIX + WIDE + 128), BF), ((8, MIX), F32), ((8, 256), F32)],
+        [block(MIX + WIDE + 128), whole((8, MIX)), whole((8, 256))],
+        [pltpu.VMEM((WIDE, STATE), F32), pltpu.VMEM((8, MIX), F32)], 12 << 30, kinds, arrays)
 
 
 AHEAD_DIM = 64
@@ -517,12 +456,12 @@
     return (kp <= qp) & (seg_at(kp, lens[0], lens[1]) == seg_at(qp, lens[0], lens[1]))
 
 
-def att_fwd_kernel(lens, odd, qkv, attended, o_ref, lse):
+def att_fwd_kernel(lens, qkv, attended, o_ref, lse):
     i = pl.program_id(0)
     n = o_ref.shape[0]
     lane = lax.broadcasted_iota(jnp.int32, (n, WIDE), 1)
     thin = lax.broadcasted_iota(jnp.int32, (n, 128), 1)
-    mine = jnp.where((i == 0) | (i == 3), 0, 1) == odd[0]
+    mine = jnp.where((i == 0) | (i == 3), 0, 1) == lax.rem(lax.axis_index("cols"), 2)
 
     @pl.when(jnp.logical_not(mine))
     def _():
@@ -561,11 +500,11 @@
         lse[...] = jnp.where(thin == 0, logs[0], jnp.where(thin == 1, logs[1], logs[2]))
 
 
-def att_bwd_kernel(lens, odd, qkv, d_att, o_ref, lse, d_qkv, dk, dv):
+def att_bwd_kernel(lens, qkv, d_att, o_ref, lse, d_qkv, dk, dv):
     i = pl.program_id(0)
     n = lse.shape[0]
     lane = lax.broadcasted_iota(jnp.int32, (n, WIDE), 1)
-    mine = jnp.where((i == 0) | (i == 3), 0, 1) == odd[0]
+    mine = jnp.where((i == 0) | (i == 3), 0, 1) == lax.rem(lax.axis_index("cols"), 2)
 
     @pl.when(i == 0)
     def _():
@@ -608,29 +547,24 @@
         d_qkv[:, 2 * WIDE:] = dv[...].astype(BF)
 
 
-def att_call(kernel, T, ins, blocked, out_specs, out_shape, scratch):
-    n = T // 4
-    smem = pl.BlockSpec(memory_space=pltpu.SMEM)
-    specs = [smem, smem, pl.BlockSpec((T, 3 * WIDE), lambda i: (0, 0))]
-    specs += [pl.BlockSpec((n, a.shape[1]), lambda i: (i, 0)) for a in blocked]
-    return pl.pallas_call(
-        kernel, grid=(4,), in_specs=specs, out_specs=out_specs, out_shape=out_shape, scratch_shapes=scratch,
-        compiler_params=pltpu.CompilerParams(vmem_limit_bytes=56 << 20, dimension_semantics=("arbitrary",)),
-        cost_estimate=pl.CostEstimate(flops=8 << 30, bytes_accessed=16 << 20, transcendentals=8 << 20),
-    )(*ins, *blocked)
-
-
-def att_fwd(lens, odd, qkv):
+def att_call(kernel, cid, lens, qkv, blocked, outs, out_specs, scratch, kinds, arrays):
+    T = qkv.shape[0]
+    specs = [pl.BlockSpec(memory_space=pltpu.SMEM), pl.BlockSpec((T, 3 * WIDE), lambda i: (0, 0))]
+    specs += [pl.BlockSpec((T // 4, a.shape[1]), lambda i: (i, 0)) for a in blocked]
+    return ridden_call(kernel, cid, 4, (lens, qkv) + blocked, specs, outs, out_specs, scratch, 8 << 30, kinds, arrays)
+
+
+def att_fwd(cid, lens, qkv, kinds, arrays):
     T = qkv.shape[0]
     block = lambda w: pl.BlockSpec((T // 4, w), lambda i: (i, 0))
-    return att_call(att_fwd_kernel, T, (lens, odd, qkv), (), [block(WIDE), block(WIDE), block(128)],
-                    [jax.ShapeDtypeStruct((T, WIDE), BF), jax.ShapeDtypeStruct((T, WIDE), F32), jax.ShapeDtypeStruct((T, 128), F32)], [])
-
-
-def att_bwd(lens, odd, qkv, d_att, o, lse):
+    return att_call(att_fwd_kernel, cid, lens, qkv, (), [((T, WIDE), BF), ((T, WIDE), F32), ((T, 128), F32)],
+                    [block(WIDE), block(WIDE), block(128)], [], kinds, arrays)
+
+
+def att_bwd(cid, lens, qkv, d_att, o, lse, kinds, arrays):
     T = qkv.shape[0]
-    return att_call(att_bwd_kernel, T, (lens, odd, qkv), (d_att, o, lse), pl.BlockSpec((T, 3 * WIDE), lambda i: (0, 0)),
-                    jax.ShapeDtypeStruct((T, 3 * WIDE), BF), [pltpu.VMEM((T, WIDE), F32), pltpu.VMEM((T, WIDE), F32)])
+    return att_call(att_bwd_kernel, cid, lens, qkv, (d_att, o, lse), [((T, 3 * WIDE), BF)],
+                    [pl.BlockSpec((T, 3 * WIDE), lambda i: (0, 0))], [pltpu.VMEM((T, WIDE), F32), pltpu.VMEM((T, WIDE), F32)], kinds, arrays)
 
 
 VMEM, ANY = pltpu.VMEM, pl.ANY
@@ -643,14 +577,14 @@
     def __init__(self, r, c, partial, bufs):
         self.r, self.c, self.partial = r, c, partial
         self.yy, self.kk = r >> 1, r & 1
-        (self.part, self.p_out, self.k_buf, self.y_out, self.y_buf, self.zr_out, self.zl_out, self.r_buf, self.l_buf,
+        (self.part, self.p_out, self.k_buf, self.y_out, self.y_buf, self.z_out, self.r_buf, self.l_buf,
          self.k_s, self.k_r, self.y_s, self.y_r, self.zr_s, self.zr_r, self.zl_s, self.zl_r) = bufs
         self.cut = self.part.shape[1] // HALVES
 
     @staticmethod
     def scratch(S, W):
         buf, sem = (lambda *n: VMEM(n + (S, W), BF)), (lambda n: pltpu.SemaphoreType.DMA((n,)))
-        return [VMEM((NC, S, W), F32), buf(2, NC), buf(2, NC)] + [buf(NC)] * 6 + [sem(2 * NC), sem(2 * NC)] + [sem(HALVES * NC)] * 6
+        return [VMEM((NC, S, W), F32), buf(2, NC), buf(2, NC)] + [buf(NC)] * 5 + [sem(2 * NC), sem(2 * NC)] + [sem(HALVES * NC)] * 6
 
     def k_copy(self, y, cc):
         i = y * NC + cc
@@ -664,10 +598,10 @@
         return self.piece(self.y_out, self.y_buf, self.y_s, self.y_r, cc, h, {"rows": self.r ^ 2})
 
     def r_copy(self, cc, h):
-        return self.piece(self.zr_out, self.r_buf, self.zr_s, self.zr_r, cc, h, {"cols": self.c + 1})
+        return self.piece(self.z_out, self.r_buf, self.zr_s, self.zr_r, cc, h, {"cols": self.c + 1})
 
     def l_copy(self, cc, h):
-        return self.piece(self.zl_out, self.l_buf, self.zl_s, self.zl_r, cc, h, {"cols": self.c - 1})
+        return self.piece(self.z_out, self.l_buf, self.zl_s, self.zl_r, cc, h, {"cols": self.c - 1})
 
     def nth(self, j):
         return jnp.where(self.c < NC // 2, NC - 1 - j, j)
@@ -694,9 +628,10 @@
             mine = self.partial((1 - self.yy) * 2 + self.kk, cc)
             self.k_copy(1 - self.yy, cc).wait_recv()
             self.y_out[cc] = (mine + self.k_buf[1 - self.yy, cc].astype(F32)).astype(BF)
-            for h in range(HALVES):
-                self.y_copy(cc, h).start()
+            self.y_copy(cc, 0).start()
         self.each(one)
+        for h in range(1, HALVES):
+            self.each(lambda cc: self.y_copy(cc, h).start())
 
     def own(self):
         def one(cc):
@@ -705,46 +640,43 @@
             self.part[cc] = mine + self.k_buf[self.yy, cc].astype(F32)
         self.each(one)
 
-    def step(self, j):
+    def step(self, j, h):
         c, cc = self.c, self.nth(j)
-        for h in range(HALVES):
-            at = pl.ds(h * self.cut, self.cut)
-            self.y_copy(cc, h).wait_recv()
-            self.part[cc, at] += self.y_buf[cc, at].astype(F32)
-
-            @pl.when(cc > c)
+        at = pl.ds(h * self.cut, self.cut)
+        self.y_copy(cc, h).wait_recv()
+        self.part[cc, at] += self.y_buf[cc, at].astype(F32)
+
+        @pl.when(cc > c)
+        def _():
+            @pl.when(c > 0)
             def _():
-                @pl.when(c > 0)
-                def _():
-                    self.r_copy(cc, h).wait_recv()
-                    self.part[cc, at] += self.r_buf[cc, at].astype(F32)
-                self.zr_out[cc, at] = self.part[cc, at].astype(BF)
-                self.r_copy(cc, h).start()
-
-            @pl.when(cc < c)
+                self.r_copy(cc, h).wait_recv()
+                self.part[cc, at] += self.r_buf[cc, at].astype(F32)
+            self.z_out[cc, at] = self.part[cc, at].astype(BF)
+            self.r_copy(cc, h).start()
+
+        @pl.when(cc < c)
+        def _():
+            @pl.when(c < NC - 1)
             def _():
-                @pl.when(c < NC - 1)
-                def _():
-                    self.l_copy(cc, h).wait_recv()
-                    self.part[cc, at] += self.l_buf[cc, at].astype(F32)
-                self.zl_out[cc, at] = self.part[cc, at].astype(BF)
-                self.l_copy(cc, h).start()
-
-    def last(self, total):
-        c = self.c
-        total[...] = self.part[c]
+                self.l_copy(cc, h).wait_recv()
+                self.part[cc, at] += self.l_buf[cc, at].astype(F32)
+            self.z_out[cc, at] = self.part[cc, at].astype(BF)
+            self.l_copy(cc, h).start()
+
+    def last(self, total, h):
+        c, at = self.c, pl.ds(h * self.cut, self.cut)
+        total[at] = self.part[c, at]
 
         @pl.when(c > 0)
         def _():
-            for h in range(HALVES):
-                self.r_copy(c, h).wait_recv()
-            total[...] += self.r_buf[c].astype(F32)
+            self.r_copy(c, h).wait_recv()
+            total[at] += self.r_buf[c, at].astype(F32)
 
         @pl.when(c < NC - 1)
         def _():
-            for h in range(HALVES):
-                self.l_copy(c, h).wait_recv()
-            total[...] += self.l_buf[c].astype(F32)
+            self.l_copy(c, h).wait_recv()
+            total[at] += self.l_buf[c, at].astype(F32)
 
     def finish(self):
         def one(cc):
@@ -813,27 +745,27 @@
             self.pass_on(self.c, h)
 
     def sides(self, off, f):
-        for h in range(HALVES):
-            for s in (-1, 1):
-                cc = self.c + s * off
-                fits = (cc >= 0) & (cc < NC) & (off < NC)
-                if s == 1:
-                    fits = fits & (off > 0)
-
-                @pl.when(fits)
-                def _():
-                    f(cc, h)
-
-    def forward(self, d):
-        def along(cc, h):
-            self.got(self.r, cc, h)
-            self.pass_on(cc, h)
-
-        def across(cc, h):
-            self.got(self.r ^ 2, cc, h)
-            self.k_copy(self.r ^ 2, cc, h).start()
-        self.sides(d, along)
-        self.sides(d - 1, across)
+        for s in (-1, 1):
+            cc = self.c + s * off
+            fits = (cc >= 0) & (cc < NC) & (off < NC)
+            if s == 1:
+                fits = fits & (off > 0)
+
+            @pl.when(fits)
+            def _():
+                f(cc)
+
+    def forward(self, d, halves=range(HALVES)):
+        for h in halves:
+            def along(cc):
+                self.got(self.r, cc, h)
+                self.pass_on(cc, h)
+
+            def across(cc):
+                self.got(self.r ^ 2, cc, h)
+                self.k_copy(self.r ^ 2, cc, h).start()
+            self.sides(d, along)
+            self.sides(d - 1, across)
 
     def uses(self, d):
         def one(i, carry):
@@ -854,10 +786,6 @@
             return carry
         lax.fori_loop(0, 8, one, 0)
 
-    def stage(self, d):
-        self.forward(d)
-        self.uses(d)
-
     def finish(self):
         def body(cc, carry):
             for h in range(HALVES):
@@ -883,9 +811,69 @@
         in_specs=[pl.BlockSpec(memory_space=s) for s in in_spaces],
         out_specs=[pl.BlockSpec(memory_space=s) for s in out_spaces],
         scratch_shapes=scratch,
-        compiler_params=pltpu.CompilerParams(collective_id=cid, has_side_effects=True, vmem_limit_bytes=60 << 20),
+        compiler_params=pltpu.CompilerParams(collective_id=cid, has_side_effects=True, vmem_limit_bytes=62 << 20),
         cost_estimate=pl.CostEstimate(flops=flops, bytes_accessed=96 << 20, transcendentals=0),
     )(*ins)
+
+
+def entry_kernel(kinds, *refs):
+    n = len(kinds)
+    it = iter(refs)
+    take = lambda k: [next(it) for _ in range(k)]
+    hidden, grad = take(2)
+    ins = take(n)
+    hid_all, g_all, h0 = take(3)
+    outs = take(n)
+    got, = take(1)
+    hid_sems, g_sems, swap_sems, sems = take(5), take(5), take(3), take(3)
+    r, c = lax.axis_index("rows"), lax.axis_index("cols")
+    greet(r, c, kinds)
+    big, S = hidden.shape[0], got.shape[1]
+    feat = hidden.shape[1]
+    first = Gather(r, c, hid_all, big, hid_sems)
+    second = Gather(r, c, g_all, S, g_sems)
+    swap = Riders(("swap",), (grad,), (got,), *swap_sems)
+    riding = Riders(kinds, ins, outs, *sems)
+    hid_all[pl.ds(pl.multiple_of((r * NC + c) * big, 16), big), :] = hidden[...]
+    first.begin()
+    riding.start()
+    swap.start()
+    for d in range(1, NC):
+        first.forward(d)
+        first.uses(d)
+        if d == 1:
+            swap.finish()
+            for i in range(NC):
+                g_all[pl.ds(pl.multiple_of((r * NC + c) * S, 16), S), i * feat:(i + 1) * feat] = got[i]
+            second.begin()
+        if d == 2:
+            riding.relay()
+            second.forward(1)
+            second.uses(1)
+    for i in range(NC):
+        h0[:, i * feat:(i + 1) * feat] = hid_all[pl.ds(pl.multiple_of((r * NC + i) * big + c * S, 16), S), :]
+    for d in range(NC, NC + 2):
+        first.forward(d)
+        first.uses(d)
+        second.forward(d - 2)
+        second.uses(d - 2)
+    for d in range(NC, NC + 2):
+        second.forward(d)
+        second.uses(d)
+    first.finish()
+    second.finish()
+    riding.finish()
+
+
+def entry(cid, hidden, grad, kinds, arrays):
+    big, feat = hidden.shape
+    S, D = big // NC, feat * NC
+    shapes, sems = rider_parts(kinds, arrays)
+    _, swap_sems = rider_parts(("swap",), (grad,))
+    outs = [((4 * NC * big, feat), BF), ((4 * NC * S, D), BF), ((S, D), BF)] + [(s.shape, s.dtype) for s in shapes]
+    scratch = [VMEM(grad.shape, BF)] + Gather.scratch() + Gather.scratch() + swap_sems + sems
+    return link_call(functools.partial(entry_kernel, tuple(kinds)), cid, [hidden, grad] + list(arrays), [VMEM] + [ANY] * (1 + len(kinds)),
+                     outs, [VMEM] * 3 + [ANY] * len(kinds), scratch, 1 << 20)
 
 
 def link_kernel(spec, *refs):
@@ -897,21 +885,20 @@
     mid_in = take(spec["n_mid"])
     w2, = take(1) if spec["w2"] in ("in", "in_t") else [None]
     a2, v2 = maybe("more_sum", 2)
-    slab2, = maybe("more_gather")
+    after_in = take(spec["n_after"])
     early_in = take(len(spec["early"]))
     late_in = take(sum(src is None for _, src in spec["late"]))
     u_all = next(it)
     mid_out = take(spec["n_mid_out"])
     post_out = take(spec["n_post"])
-    sum2, = maybe("more_sum")
-    all2, = maybe("more_gather")
+    after_out = take(spec["n_after_out"])
     early_out, late_out = take(len(spec["early"])), take(len(spec["late"]))
+    final_out = take(len(after_out))
     total, = take(1)
-    sum_bufs, gather_sems = take(17), take(5)
-    sum2_bufs = take(18) if spec["more_sum"] else []
-    gather2_sems = take(6) if spec["more_gather"] else []
+    sum_bufs, gather_sems = take(16), take(5)
+    sum2_bufs = take(17) if spec["more_sum"] else []
     small = take(6) if spec["small"] else None
-    early_sems, late_sems = take(spec["n_early_sems"]), take(spec["n_late_sems"])
+    early_sems, late_sems, final_sems = take(spec["n_early_sems"]), take(spec["n_late_sems"]), take(3 * (len(after_out) > 0))
     r, c = lax.axis_index("rows"), lax.axis_index("cols")
     S, W = total.shape
     D = w1.shape[0] if spec["w1_t"] else w1.shape[1]
@@ -922,6 +909,7 @@
     late_in = iter(late_in)
     sources = [next(late_in) if src is None else mid_out[src] for _, src in spec["late"]]
     late = Riders(late_kinds, sources, late_out, *(late_sems or none))
+    final = Riders(("swap",) * len(after_out), after_out, final_out, *(final_sems or none))
     rows_of = lambda rr, cc: pl.ds(pl.multiple_of((rr * NC + cc) * S, 16), S)
 
     def partial(rr, cc):
@@ -935,68 +923,79 @@
 
     summing = Sum(r, c, partial, sum_bufs)
     gather = Gather(r, c, u_all, S, gather_sems, use if spec["w2"] else None)
-    summing2 = gather2 = None
-    if spec["more_gather"]:
-        gather2 = Gather(r, c, all2, S, gather2_sems[:5])
-        own2 = pltpu.make_async_copy(slab2, gather2.slab(r, c), gather2_sems[5])
-        own2.start()
+    summing2 = None
     summing.to_core()
     early.start()
     summing.to_y()
-    if gather2:
-        own2.wait()
-        gather2.begin()
     if spec["more_sum"]:
-        summing2 = Sum(r, c, lambda rr, cc: mm(a2[rows_of(rr, cc), :], v2[...]), sum2_bufs[:17])
-        summing2.to_core()
+        summing2 = Sum(r, c, lambda rr, cc: mm(a2[rows_of(rr, cc), :], v2[...]), sum2_bufs[:16])
+    summing.own()
+    for j in range(NC):
+        summing.step(j, 0)
+        if spec["small"] and j == 1:
+            early.add()
+        if summing2 and j == 1:
+            summing2.to_core()
+    summing.last(total, 0)
+    if summing2:
         summing2.to_y()
         summing2.own()
-    summing.own()
-    summing.step(0)
-    summing.step(1)
-    early.add()
-    summing.step(2)
-    if gather2:
-        gather2.stage(1)
-    summing.step(3)
-    summing.last(total)
     if spec["small"]:
+        for j in range(NC):
+            summing.step(j, 1)
+        summing.last(total, 1)
         mine, others, held, dp_s, dp_r, loc = small
         spec["mid"](total, mid_in, mid_out, mine)
+        settle = sum_groups(mine, others, held, dp_s, dp_r, 4)
         late.start()
-        sum_groups(mine, others, held, dp_s, dp_r, 4)
+        settle()
         place = pltpu.make_async_copy(held, gather.slab(r, c), loc)
         place.start()
         place.wait()
         gather.begin()
+        early.relay()
     else:
-        u_all[rows_of(r, c), :] = spec["mid"](total, mid_in, mid_out)
-        gather.begin()
+        def advance(h):
+            at = pl.ds(h * (S // HALVES), S // HALVES)
+            off = pl.multiple_of((r * NC + c) * S + h * (S // HALVES), 16)
+            u_all[pl.ds(off, S // HALVES), :] = spec["mid"](total, mid_in, mid_out, at, h)
+            gather.pass_on(c, h)
+        advance(0)
+        early.add()
+        summing.step(0, 1)
+        summing.step(1, 1)
+        gather.forward(1, (0,))
+        summing.step(2, 1)
+        summing.step(3, 1)
+        summing.last(total, 1)
+        advance(1)
         late.start()
     if spec["w2"] == "rider":
         early.relay()
-        gather.forward(1)
         early.finish()
     if spec["w2"]:
         use(r, c)
     for d in range(1, NC + 2):
         if summing2 and d <= NC:
-            summing2.step(d - 1)
-        if gather2 and d < NC + 1:
-            gather2.stage(d + 1)
-        if d > 1 or spec["w2"] != "rider":
+            summing2.step(d - 1, 0)
+            summing2.step(d - 1, 1)
+        if spec["small"]:
             gather.forward(d)
+        else:
+            gather.forward(d, (1,))
+            gather.forward(d + 1, (0,))
         gather.uses(d)
-        if d == 2 and spec["w2"] != "rider":
+        if d == 2 and spec["w2"] != "rider" and not spec["small"]:
             early.relay()
     gather.finish()
     summing.finish()
-    if gather2:
-        gather2.finish()
     if summing2:
-        summing2.last(sum2_bufs[17])
-        sum2[...] = sum2_bufs[17][...]
+        for h in range(HALVES):
+            summing2.last(sum2_bufs[16], h)
+        spec["after"](sum2_bufs[16], after_in, after_out)
+        final.start()
         summing2.finish()
+        final.finish()
     late.add()
     late.relay()
     if spec["w2"] != "rider":
@@ -1005,7 +1004,7 @@
 
 
 def link(cid, a, w1, mid, mid_in, mid_out, *, w1_t=False, side=None, w2=None, w2_kind=None, post=None, post_out=(), early=(), early_in=(),
-         late=(), late_in=(), extra=0, small=0, more_sum=None, more_gather=None):
+         late=(), late_in=(), extra=0, small=0, more_sum=None, after=None, after_in=(), after_out=()):
     T = a.shape[0]
     D = w1.shape[0] if w1_t else w1.shape[1]
     S = T // (4 * NC)
@@ -1015,32 +1014,29 @@
     late_it = iter(late_in)
     late_arrays = [next(late_it) if src is None else jax.ShapeDtypeStruct(*mid_out[src]) for _, src in late]
     late_shapes, late_sems = rider_parts(tuple(k for k, _ in late), late_arrays)
+    final_shapes, final_sems = rider_parts(("swap",) * len(after_out), [jax.ShapeDtypeStruct(*o) for o in after_out])
     spec = dict(w1_t=w1_t, side=side is not None, mid=mid, n_mid=len(mid_in), n_mid_out=len(mid_out), w2=w2_kind, post=post,
                 n_post=len(post_out), early=tuple(early), late=tuple(late), small=small, more_sum=more_sum is not None,
-                more_gather=more_gather is not None, n_early_sems=len(early_sems), n_late_sems=len(late_sems))
+                after=after, n_after=len(after_in), n_after_out=len(after_out), n_early_sems=len(early_sems), n_late_sems=len(late_sems))
     ins = [a, w1] + ([side] if side is not None else []) + list(mid_in) + ([w2] if w2 is not None else [])
-    ins += list(more_sum or ()) + ([more_gather] if more_gather is not None else [])
-    in_spaces = [VMEM] * len(ins) + [ANY] * (len(early_in) + len(late_in))
-    ins += list(early_in) + list(late_in)
+    ins += list(more_sum or ()) + list(after_in)
+    riding = list(early_in) + list(late_in)
+    in_spaces = [VMEM] * len(ins) + [ANY] * len(riding)
+    ins += riding
     outs = [((T, width), BF)] + list(mid_out) + list(post_out)
-    if more_sum is not None:
-        outs.append(((S, D), F32))
-    if more_gather is not None:
-        outs.append(((T, D), BF))
-    out_spaces = [VMEM] * len(outs) + [ANY] * len(early_shapes + late_shapes)
+    outs += list(after_out)
+    out_spaces = [VMEM] * len(outs) + [ANY] * len(early_shapes + late_shapes + final_shapes)
     if w2_kind == "rider":
         out_spaces[len(outs)] = VMEM
-    outs += [(s.shape, s.dtype) for s in early_shapes + late_shapes]
+    outs += [(s.shape, s.dtype) for s in early_shapes + late_shapes + final_shapes]
     scratch = [VMEM((S, W), F32)] + Sum.scratch(S, W) + Gather.scratch()
     if more_sum is not None:
         scratch += Sum.scratch(S, D) + [VMEM((S, D), F32)]
-    if more_gather is not None:
-        scratch += Gather.scratch() + [pltpu.SemaphoreType.DMA]
     if small:
         groups = lax.axis_size("dp")
         scratch += [VMEM((S, small), F32), VMEM((groups - 1, S, small), F32), VMEM((S, small), BF), pltpu.SemaphoreType.DMA((groups - 1,)),
                     pltpu.SemaphoreType.DMA((groups - 1,)), pltpu.SemaphoreType.DMA]
-    scratch += early_sems + late_sems
+    scratch += early_sems + late_sems + final_sems
     return link_call(functools.partial(link_kernel, spec), cid, ins, in_spaces, outs, out_spaces, scratch, 8 << 30)
 
 
@@ -1051,48 +1047,49 @@
     return lax.rsqrt(jnp.mean(x * x, axis=1, keepdims=True) + EPS)
 
 
-def norm_grad(x, gain, up, gain_grad):
+def norm_grad(x, gain, up, gain_grad, h):
     s = norm_scale(x)
-    gain_grad[0:1] = jnp.sum(x * s * up, axis=0, keepdims=True)
+    own = jnp.sum(x * s * up, axis=0, keepdims=True)
+    gain_grad[0:1] = own if h == 0 else gain_grad[0:1] + own
     tilted = up * gain
     return s * tilted - x * (s * s * s * jnp.mean(x * tilted, axis=1, keepdims=True))
 
 
-def mid_mixer(inner, total, ins, outs):
+def mid_mixer(inner, total, ins, outs, at, h):
     h0, gain = ins
     h1, mix_out, gate_scale = outs
     D = h0.shape[1]
-    s = lax.rsqrt(total[:, D:D + 1] / inner + EPS)
-    out = total[:, :D] * s
-    mix_out[...] = out
-    gate_scale[...] = jnp.broadcast_to(s, gate_scale.shape)
-    h = h0[...].astype(F32) + out
-    h1[...] = h
-    return (h * norm_scale(h) * gain[...]).astype(BF)
-
-
-def mid_attention(total, ins, outs):
+    s = lax.rsqrt(total[at, D:D + 1] / inner + EPS)
+    out = total[at, :D] * s
+    mix_out[at] = out
+    gate_scale[at] = jnp.broadcast_to(s, (out.shape[0], gate_scale.shape[1]))
+    x = h0[at].astype(F32) + out
+    h1[at] = x
+    return (x * norm_scale(x) * gain[...]).astype(BF)
+
+
+def mid_attention(total, ins, outs, at, h):
     h1, gain = ins
-    h = h1[...] + total[...]
-    outs[0][...] = h
-    return (h * norm_scale(h) * gain[...]).astype(BF)
-
-
-def mid_ff_back(total, ins, outs):
+    x = h1[at] + total[at]
+    outs[0][at] = x
+    return (x * norm_scale(x) * gain[...]).astype(BF)
+
+
+def mid_ff_back(total, ins, outs, at, h):
     h2, gain, grad = ins
     dh2, gain_grad = outs
-    d = grad[...].astype(F32) + norm_grad(h2[...], gain[...], total[...], gain_grad)
-    dh2[...] = d
+    d = grad[at].astype(F32) + norm_grad(h2[at], gain[...], total[at], gain_grad, h)
+    dh2[at] = d
     return d.astype(BF)
 
 
-def mid_att_back(inner, total, ins, outs):
+def mid_att_back(inner, total, ins, outs, at, h):
     h1, gain, dh2, mix_out, gate_scale = ins
     dh1, gain_grad = outs
-    d = dh2[...] + norm_grad(h1[...], gain[...], total[...], gain_grad)
-    dh1[...] = d
-    s = gate_scale[:, 0:1]
-    tilt = s * s * jnp.sum(d * mix_out[...], axis=1, keepdims=True) / inner
+    d = dh2[at] + norm_grad(h1[at], gain[...], total[at], gain_grad, h)
+    dh1[at] = d
+    s = gate_scale[at, 0:1]
+    tilt = s * s * jnp.sum(d * mix_out[at], axis=1, keepdims=True) / inner
     high = tilt.astype(BF).astype(F32)
     lane = lax.broadcasted_iota(jnp.int32, (d.shape[0], 128), 1)
     return jnp.concatenate([d * s, jnp.where(lane < 64, high, tilt - high)], axis=1).astype(BF)
@@ -1104,10 +1101,10 @@
     D = h0.shape[1]
     thin = small.shape[1]
     four = D // thin
-    d = dh1[...] + norm_grad(h0[...].astype(F32), gain[...], total[:, :D], gain_grad)
+    d = dh1[...] + norm_grad(h0[...].astype(F32), gain[...], total[:, :D], gain_grad, 0)
     feat = D // NC
     for i in range(NC):
-        in_slab[i] = d[:, i * feat:(i + 1) * feat]
+        in_slab[i] = d[:, i * feat:(i + 1) * feat].astype(BF)
     rest = total[:, D:]
     small[...] = jnp.zeros_like(small)
     small[:SMALL] = rest[:SMALL]
@@ -1120,6 +1117,14 @@
             small[at:at + 1] = row[:, j * thin:(j + 1) * thin]
 
 
+def after_output(total, ins, outs):
+    h2, valid = ins
+    x = (h2[...] + total[...]) * valid[:, 0:1]
+    feat = x.shape[1] // NC
+    for i in range(NC):
+        outs[0][i] = x[:, i * feat:(i + 1) * feat].astype(BF)
+
+
 def post_plain(p, at, outs):
     outs[0][at, :] = p.astype(outs[0].dtype)
 
@@ -1129,6 +1134,72 @@
     outs[1][at, :] = (0.5 * p * (1.0 + jnp.tanh(0.7978845608028654 * (p + 0.044715 * (p * p * p))))).astype(BF)
 
 
+def finish_kernel(zx, mix, qkv, o, ff, rest, x_g, z_g, q_g, k_g, v_g, mix_g, o_g, up_g, down_g, bcdt_g, small, gain):
+    i = pl.program_id(0)
+    rows, part = zx.shape[2], ff.shape[2] // 2
+    for h in range(2):
+        at = slice(h * rows, (h + 1) * rows)
+        piece = zx[0, h].astype(F32)
+        x_new, z_new = piece[:, :WIDE], piece[:, WIDE:]
+        three = qkv[0, h].astype(F32)
+        for j in range(NC):
+            @pl.when(i == j)
+            def _():
+                x_g[at, j * WIDE:(j + 1) * WIDE] = x_new
+                z_g[at, j * WIDE:(j + 1) * WIDE] = z_new
+                to = slice((j // 2) * WIDE, (j // 2 + 1) * WIDE)
+                for n, out in enumerate((q_g, k_g, v_g)):
+                    new = three[:, n * WIDE:(n + 1) * WIDE]
+                    out[at, to] = new if j % 2 == 0 else out[at, to] + new
+        half = mix.shape[2]
+        mix_g[h * half:(h + 1) * half] = mix[0, h].astype(F32)
+        o_at = slice(h * half, (h + 1) * half)
+
+        @pl.when(i % 2 == 0)
+        def _():
+            o_g[o_at] = o[0, h].astype(F32)
+
+        @pl.when(i % 2 == 1)
+        def _():
+            o_g[o_at] += o[0, h].astype(F32)
+        down_g[h * part:(h + 1) * part] = ff[0, h, :part].astype(F32)
+        up_g[h * part:(h + 1) * part] = ff[0, h, part:].astype(F32)
+    wide = bcdt_g.shape[1]
+
+    @pl.when(i == 0)
+    def _():
+        gain[...] = jnp.zeros_like(gain)
+    for j in range(NC):
+        slab = rest[j].astype(F32)
+        bcdt_g[j * SMALL:(j + 1) * SMALL] = slab[:SMALL, :wide]
+        tail = slab[SMALL:SMALL + 24]
+        small[j] = tail[0:4] + tail[4:8] + tail[8:12]
+        gain[0:4] += tail[12:16] + tail[16:20] + tail[20:24]
+
+
+def finish(zx, mix, qkv, o, ff, rest, bcdt_width):
+    thin, feat = rest.shape[2], zx.shape[3]
+    D = NC * feat
+    lead = lambda a: pl.BlockSpec((1,) + a.shape[1:], lambda i: (i, 0, 0, 0))
+    whole = lambda r, w: pl.BlockSpec((r, w), lambda i: (0, 0))
+    sds = lambda *s: jax.ShapeDtypeStruct(s, F32)
+    rows, half, part = 2 * zx.shape[2], 2 * mix.shape[2], ff.shape[2]
+    return pl.pallas_call(
+        finish_kernel,
+        grid=(NC,),
+        in_specs=[lead(zx), lead(mix), lead(qkv), lead(o), lead(ff), pl.BlockSpec((NC,) + rest.shape[1:], lambda i: (i, 0, 0))],
+        out_specs=[whole(rows, NC * WIDE)] * 2 + [whole(rows, 2 * WIDE)] * 3 + [
+            pl.BlockSpec((half, feat), lambda i: (i, 0)), pl.BlockSpec((half, feat), lambda i: (i // 2, 0)),
+            pl.BlockSpec((part, feat), lambda i: (0, i)), pl.BlockSpec((part, feat), lambda i: (i, 0)),
+            pl.BlockSpec((NC * SMALL, bcdt_width), lambda i: (i, 0)), pl.BlockSpec((NC, 4, thin), lambda i: (i, 0, 0)), whole(8, thin)],
+        out_shape=[sds(rows, NC * WIDE)] * 2 + [sds(rows, 2 * WIDE)] * 3 + [
+            sds(NC * half, feat), sds(2 * half, feat), sds(part, NC * feat), sds(NC * part, feat), sds(D, bcdt_width),
+            sds(rest.shape[0], 4, thin), sds(8, thin)],
+        compiler_params=pltpu.CompilerParams(vmem_limit_bytes=48 << 20, dimension_semantics=("arbitrary",)),
+        cost_estimate=pl.CostEstimate(flops=1 << 20, bytes_accessed=24 << 20, transcendentals=0),
+    )(zx, mix, qkv, o, ff, rest)
+
+
 P = jax.sharding.PartitionSpec
 
 
@@ -1149,9 +1220,9 @@
     return w.reshape(d, NC, n // NC).transpose(1, 0, 2)
 
 
-def split_pair(w):
+def halves_of(w):
     d, n = w.shape
-    return jnp.repeat(w.reshape(d, 2, n // 2).transpose(1, 0, 2), NC // 2, axis=0)
+    return w.reshape(d, 2, n // 2).transpose(1, 0, 2)
 
 
 def whole_out(got):
@@ -1163,22 +1234,9 @@
     return g.astype(BF).reshape(n, NC, d // NC).transpose(1, 0, 2)
 
 
-def pair_sum(got):
-    return got.astype(F32).reshape((2, NC // 2) + got.shape[1:]).sum(1)
-
-
-def beside(a):
-    k, d, n = a.shape
-    return a.transpose(1, 0, 2).reshape(d, k * n)
-
-
 def place_block(piece, start, full_len, axis):
     shape = piece.shape[:axis] + (full_len,) + piece.shape[axis + 1:]
     return lax.dynamic_update_slice_in_dim(jnp.zeros(shape, piece.dtype), piece, start, axis)
-
-
-def rms_scale(x):
-    return lax.rsqrt(jnp.mean(x * x, axis=1, keepdims=True) + EPS)
 
 
 def per_device(hidden_in, lengths, norm1_gain, z_weight, x_weight, bcdt_weight, conv_x_weight, conv_x_bias,
@@ -1216,74 +1274,79 @@
     bcdt_pad = -bcdt_width % 128
     bcdt_piece = jnp.pad(bcdt_weight, ((0, 0), (0, bcdt_pad))).reshape(2, feat // 2, -1)
     gain_piece = jnp.broadcast_to(jnp.pad(jnp.stack([norm1_gain, norm2_gain, norm3_gain]), ((0, 5), (0, 0)))[None], (2, 8, feat))
-    hidden_all, w_zx, mix_got, w_bcdt, gains = gather_native(
-        hidden_in, 0, (pair, pair, "bcast2", "bcast2"), (zx_pieces, mix_pieces, bcdt_piece, gain_piece))
+    here = lax.dynamic_slice_in_dim(valid, r * tok_rows, tok_rows, 0)[:, None]
+    grad = (grad_output.astype(F32) * here).astype(BF).reshape(NC, S, feat)
+    hidden_all, g3, h0, w_zx, mix_got, w_bcdt, gains = entry(
+        0, hidden_in, grad, (pair, pair, "bcast2", "bcast2"), (zx_pieces, mix_pieces, bcdt_piece, gain_piece))
+    g3_mine = lax.dynamic_slice_in_dim(g3, slab * S, S, 0)
     w_mix = whole_out(joined(mix_got))
     gains = gains[:, 0, :3].transpose(1, 0, 2).reshape(3, D)
-    w_bcdt = w_bcdt.reshape(D, -1)
+    w_bcdt, w_zx = w_bcdt.reshape(D, -1), w_zx.reshape(D, 2 * wide)
     w_dt = jnp.pad(lax.dynamic_slice_in_dim(w_bcdt, 2 * STATE + slab * heads, heads, 1), ((0, 0), (0, 128 - heads)))
-    w_in = jnp.concatenate([w_bcdt[:, :2 * STATE], w_zx.reshape(D, 2 * wide), w_dt], axis=1)
-    qkv_pieces = halved(jnp.concatenate([split_pair(q_weight), split_pair(k_weight), split_pair(v_weight)], axis=2))
-    o_pieces = halved(jnp.repeat(att_out_weight.reshape(2, -1, feat), NC // 2, axis=0))
-
-    hid_all = hidden_all.astype(F32)
-    u1 = (hid_all * rms_scale(hid_all) * gains[0][None, :]).astype(BF)
-    proj = dot(u1, w_in)
+    w_in = jnp.concatenate([w_bcdt[:, :2 * STATE], w_zx, w_dt], axis=1)
+    few = pair == "swap2"
+    twice = lambda a: a if few else jnp.repeat(a, NC // 2, axis=0)
+    one_way = "swaph" if few else "swap"
+    qkv_pieces = halved(twice(jnp.concatenate([halves_of(q_weight), halves_of(k_weight), halves_of(v_weight)], axis=2)))
+    o_pieces = halved(twice(att_out_weight.reshape(2, -1, feat)))
+
     mine = lambda a, n: lax.dynamic_slice_in_dim(a, c * n, n, a.ndim - 1)
     cw = jnp.concatenate([conv_bc_weight, mine(conv_x_weight, wide)], axis=1)
     cw = jnp.concatenate([cw, jnp.concatenate([conv_bc_bias, mine(conv_x_bias, wide)])[None], jnp.zeros((3, MIX), F32)])
     wide_row = lambda a: jnp.pad(a, (0, 256 - a.shape[0]))[None]
     pv = jnp.concatenate([wide_row(mine(gate_gain, wide)), wide_row(jnp.repeat(mine(d_skip, heads), HEAD_DIM)),
                           wide_row(mine(dt_bias, heads)), wide_row(-jnp.exp(mine(a_log, heads))), jnp.zeros((4, 256), F32)])
-    mixg, squares, y, states = mixer_fwd(seq_lens, proj, cw, pv)
-    h0 = lax.dynamic_slice_in_dim(hidden_all, slab * S, S, 0)
+    u1, proj, mixg, squares, y, states, qkv_split = mixer_fwd(
+        6, seq_lens, hidden_all.reshape(rows, NC, tok_rows, feat), gains[0:1], w_bcdt, w_zx, w_dt, cw, pv,
+        (one_way,), (qkv_pieces,))
     att3 = qkv_pieces.shape[-1]
-    u2, h1, mix_out, gate_scale, qkv, qkv_got, o_got, grad_got = link(
+    u2, h1, mix_out, gate_scale, qkv, qkv_got, o_split, down_split = link(
         1, mixg, w_mix, functools.partial(mid_mixer, inner), (h0, gains[1:2]), (one_f32, one_f32, ((S, 128), F32)), side=squares,
-        w2_kind="rider", post=post_plain, post_out=(((T, att3), BF),), early=(pair, pair), early_in=(qkv_pieces, o_pieces),
-        late=(("swap", None),), late_in=(grad_output.reshape(NC, S, feat),))
-    w_qkv, w_o = qkv_got.reshape(D, -1), whole_out(joined(o_got))
-    g3_mine = (grad_got.transpose(1, 0, 2).reshape(S, D).astype(F32) * my_valid).astype(BF)
+        w2_kind="rider", post=post_plain, post_out=(((T, att3), BF),), early=("spread",), early_in=(qkv_split,), late=((one_way, None), (one_way, None)),
+        late_in=(o_pieces, halved(down_weight.reshape(NC, -1, feat))))
+    w_qkv = qkv_got.reshape(D, -1)
     att = att3 // 3
 
-    odd = (c % 2)[None]
-    attended, att_exact, lse = att_fwd(seq_lens, odd, qkv)
+    attended, att_exact, lse, up_split, o_got = att_fwd(
+        7, seq_lens, qkv, (one_way, "spread"), (halved(split_in(up_weight)), o_split))
+    w_o = whole_out(joined(o_got))
     hidden_units = up_weight.shape[1] // NC
-    u3, h2, act, hid, g3, up_got, down_got = link(
+    u3, h2, act, hid, up_got, down_got = link(
         2, attended, w_o, mid_attention, (h1, gains[2:3]), (one_f32,), w2_kind="rider", post=post_gelu,
-        post_out=(((T, hidden_units), F32), ((T, hidden_units), BF)), early=(pair,), early_in=(halved(split_in(up_weight)),),
-        late=((pair, None),), late_in=(halved(down_weight.reshape(NC, -1, feat)),), more_gather=g3_mine)
+        post_out=(((T, hidden_units), F32), ((T, hidden_units), BF)), early=("spread",), early_in=(up_split,),
+        late=(("spread", None),), late_in=(down_split,))
     w_up, w_down = up_got.reshape(D, -1), whole_out(joined(down_got))
     gelu_back = jax.vjp(functools.partial(jax.nn.gelu, approximate=True), act)[1]
 
-    reduce = "reduce" if pair == "swap2" else "swap"
-
-    def settle(got):
-        return joined(got) if reduce == "reduce" else lax.psum(got, "dp")
-
+    reduce = "reduce" if few else "swap"
+
+    def added(pieces, got):
+        if not few:
+            return lax.psum(pieces, "dp")
+        own = lax.dynamic_index_in_dim(pieces, lax.axis_index("dp"), 1, False)
+        return (own.astype(F32) + got[0].astype(F32)).astype(BF)
+
+    x_kinds = lambda n: ("half",) * n if few else ()
+    x_arrays = lambda *arrays: arrays if few else ()
     d_act = gelu_back(dot_t(g3, w_down))[0].astype(BF)
     down_pieces = halved(split_grad(t_dot(hid, g3)))
     up_pieces = halved(t_dot(u3, d_act).astype(BF).reshape(NC, feat, -1))
-    g2, dh2, gain3_rows, d_att, ff_out, down_back, up_back = link(
+    g2, dh2, gain3_rows, d_att, *got = link(
         3, d_act, w_up, mid_ff_back, (h2, gains[2:3], g3_mine), (one_f32, row8), w1_t=True, w2=w_o, w2_kind="in_t", post=post_plain,
-        post_out=(((T, att), BF),), early=(reduce, reduce), early_in=(down_pieces, up_pieces), more_sum=(hid, w_down))
-    out_slab = ((h2 + ff_out) * my_valid).astype(BF)
+        post_out=(((T, att), BF),), early=x_kinds(2), early_in=x_arrays(down_pieces, up_pieces))
+    ff_sum = jnp.concatenate([added(down_pieces, got[:1]), added(up_pieces, got[1:])], axis=1)
     o_pieces = halved(split_grad(t_dot(attended, g2)))
-    d_qkv = att_bwd(seq_lens, odd, qkv, d_att, att_exact, lse)
+    d_qkv, ff_split = att_bwd(8, seq_lens, qkv, d_att, att_exact, lse, ("swap",), (ff_sum,))
     qkv_pieces = halved(t_dot(u2, d_qkv).astype(BF).reshape(NC, feat, -1))
-    g1_ext, dh1, gain2_rows, d_mix, o_back, qkv_back, out_got = link(
+    g1_ext, dh1, gain2_rows, d_mix, ff_back, *got = link(
         4, d_qkv, w_qkv, functools.partial(mid_att_back, inner), (h1, gains[1:2], dh2, mix_out, gate_scale), (one_f32, row8), w1_t=True,
         w2=w_mix, w2_kind="in_t", post=post_plain, post_out=(((T, wide), F32),), extra=128,
-        early=(reduce, reduce), early_in=(o_pieces, qkv_pieces), late=(("swap", None),), late_in=(out_slab.reshape(S, NC, feat).transpose(1, 0, 2),))
+        early=("spread",) + x_kinds(2), early_in=(ff_split,) + x_arrays(o_pieces, qkv_pieces))
+    o_sum, qkv_sum = added(o_pieces, got[:1]), added(qkv_pieces, got[1:])
     g1 = g1_ext[:, :D]
-    output = out_got.reshape(NC * S, feat)
-    down_grad = settle(down_back).astype(F32).reshape(-1, feat)
-    up_grad = beside(settle(up_back)).astype(F32)
-    o_grad = pair_sum(settle(o_back)).reshape(-1, feat)
-    qkv_sum = pair_sum(settle(qkv_back))
-    q_grad, k_grad, v_grad = (beside(qkv_sum[:, :, i * att:(i + 1) * att]) for i in range(3))
     mix_pieces = halved(split_grad(t_dot(mixg, g1)))
-    d_in, tap_grads, row_grads = mixer_bwd(seq_lens, proj, cw, pv, y, states, d_mix, g1_ext)
+    d_in, tap_grads, row_grads, o_split, qkv_split = mixer_bwd(
+        9, seq_lens, proj, cw, pv, y, states, d_mix, g1_ext, ("swap", "swap"), (o_sum, qkv_sum))
     cbw_grad, cxw_grad = tap_grads[:CONV, :2 * STATE], tap_grads[:CONV, 2 * STATE:]
     cbb_grad, cxb_grad = tap_grads[CONV, :2 * STATE], tap_grads[CONV, 2 * STATE:]
     gate_gain_grad, dt_bias_grad, a_log_grad = row_grads[0, :wide], row_grads[2, :heads], row_grads[3, :heads]
@@ -1305,14 +1368,19 @@
     small_hi = small.astype(BF)
     small_lo = (small - small_hi.astype(F32)).astype(BF)
     side = jnp.concatenate([bcdt_part, small_hi, small_lo, jnp.zeros((slabs, S - SMALL - 2 * four, thin), BF)], axis=1)
-    rest_all, _, _, zx_back, mix_back, in_got = link(
-        5, d_in, w_in, mid_mixer_back, (h0, gains[0:1], dh1), (((NC, S, feat), F32), row8), w1_t=True, side=side.reshape(T, thin), small=thin,
-        early=(reduce, reduce), early_in=(zx_pieces, mix_pieces), late=(("swap", 0),))
-    rest_all = rest_all.reshape(slabs, S, thin)
-    bcdt_grad = rest_all[:, :SMALL].reshape(D, thin)[:, :bcdt_width].astype(F32)
-    tail_rows = rest_all[:, SMALL:SMALL + 6 * four].astype(F32).reshape(slabs, 6, D)
-    small = tail_rows[:, 0] + tail_rows[:, 1] + tail_rows[:, 2]
-    gain1_grad = (tail_rows[:, 3] + tail_rows[:, 4] + tail_rows[:, 5]).sum(0)
+    rest_all, _, _, _, zx_back, mix_back, o_back, qkv_back, in_got, out_got = link(
+        5, d_in, w_in, mid_mixer_back, (h0, gains[0:1], dh1), (((NC, S, feat), BF), row8), w1_t=True, side=side.reshape(T, thin), small=thin,
+        early=(reduce, reduce, "spread", "spread"), early_in=(zx_pieces, mix_pieces, o_split, qkv_split), late=(("swap", 0),),
+        more_sum=(hid, w_down), after=after_output, after_in=(h2, jnp.broadcast_to(my_valid, (S, 128))), after_out=(((NC, S, feat), BF),))
+    output = out_got.reshape(NC * S, feat)
+    four_d = lambda a: a if few else a.reshape(NC, 2, -1, a.shape[-1])
+    if not few:
+        n = ff_back.shape[1] // 2
+        ff_back = jnp.concatenate([four_d(ff_back[:, :n]), four_d(ff_back[:, n:])], axis=2)
+        zx_back, mix_back = lax.psum(zx_back, "dp"), lax.psum(mix_back, "dp")
+    (x_grad, z_grad, q_grad, k_grad, v_grad, mix_grad, o_grad, up_grad, down_grad, bcdt_grad, small, gain1) = finish(
+        four_d(zx_back), four_d(mix_back), four_d(qkv_back), four_d(o_back), ff_back, rest_all.reshape(slabs, S, thin), bcdt_width)
+    small, gain1_grad = small.reshape(slabs, D), gain1[:4].reshape(D)
     per_inner = inner // D
     edges = [2 + CONV * per_inner, 2 + (CONV + 1) * per_inner, 2 + (CONV + 2) * per_inner]
     cxw_sum = small[2:edges[0]].reshape(CONV, inner)
@@ -1320,10 +1388,7 @@
     misc = small[edges[2]]
     cbw_sum, cbb_sum = misc[:CONV * 2 * STATE].reshape(CONV, 2 * STATE), misc[CONV * 2 * STATE:(CONV + 1) * 2 * STATE]
     a_log_sum, d_skip_sum, dt_bias_sum = jnp.split(misc[n_misc - 3 * n_heads:n_misc], 3)
-    input_grad = in_got.reshape(NC * S, feat)
-    zx_sum = settle(zx_back).astype(F32)
-    x_grad, z_grad = beside(zx_sum[:, :, :wide]), beside(zx_sum[:, :, wide:])
-    mix_grad = settle(mix_back).astype(F32).reshape(-1, feat)
+    input_grad = in_got.reshape(NC * S, feat).astype(F32)
     return (output, input_grad, gain1_grad, z_grad, x_grad, bcdt_grad, cxw_sum, cxb_sum, cbw_sum, cbb_sum, a_log_sum, d_skip_sum,
             dt_bias_sum, gate_gain_sum, mix_grad, small[0], q_grad, k_grad, v_grad, o_grad, small[1], up_grad, down_grad)
 

time: 933 us -> 862 us (0.924)
  Pallas kernels: 782 us -> 740 us
  other arithmetic: 25.5 us -> 12.9 us
  matrix products: 48.6 us -> 38.9 us
    pallas_call x5, Pallas kernels: 181 us -> 120 us  [the longest x4 112 us: ridden_call(): pl.pallas_call(ridden(kernel, len(ins), len(outs), tuple(kinds)), grid=(g...]
    pallas_call x5 -> x6, Pallas kernels: 600 us -> 620 us  [link_call(): pl.pallas_call(kernel, out_shape=[jax.ShapeDtypeStruct(s, d) for s, d in...]
    unnamed x122 -> x101, local copies, waits for them, and re-layouts: 28.6 us -> 17.9 us
where the time goes in v4:
time: 862 us; the launch traced here: 853 us
  Pallas kernels  740 us (86%)
  local copies, waits for them, and re-layouts  58.4 us (7%)
  matrix products  38.9 us (5%)
  other arithmetic  12.9 us (1%)
    pallas_call x6, Pallas kernels, link_call(): pl.pallas_call(kernel, out_shape=[jax.ShapeDtypeStruct(s, d) for s, d in...  620 us
    pallas_call x4, Pallas kernels, ridden_call(): pl.pallas_call(ridden(kernel, len(ins), len(outs), tuple(kinds)), grid=(g...  112 us
    dot_general x6, matrix products, t_dot(): lax.dot_general(a, b, (((0,), (0,)), ((), ())), preferred_element_type=F32)  30.4 us
    unnamed x101, local copies, waits for them, and re-layouts  17.9 us

profile of v4, /device:TPU:0, one launch (start us, length us, event | category | flops | bytes accessed | tf_op | source)
XLA Modules:
  0.0 853.0 jit_solution(14709078372363492049)
XLA Ops:
  0.7 0.8 dynamic_slice.50
  1.6 0.8 dynamic_slice.49
  4.5 1.3 fusion.21
  7.8 1.9 multiply_convert_fusion
  9.7 1.4 copy.65
  11.6 1.5 copy.67
  13.2 0.8 pad.34.clone
  14.7 114.2 %shard_map.407 = (bf16[8192,384]{1,0:T(8,128)(2,1)}, bf16[2048,1536]{1,0:T(8,128)(2,1)}, bf16[128,1536]{1,0:T(8,128)(2,1)}, bf16[4,2,192,384]{3,2,1,0:T(8,128)(2...) custom-call(bf16[512,384]{1,0:T(8,128)(2,1)} %refs_0_.1, ...), custom_call_target="tpu_custom_call" | custom-call | flops 1048576 | bytes 100663296 | tf_op jit(solution)/shard_map/pallas_call | solution.py:808
  128.9 1.2 constant_dynamic-slice_fusion.2
  130.1 0.8 pad.36.refs_5_
  131.0 0.8 dynamic_slice.48
  132.6 0.8 slice_bitcast_fusion
  134.8 1.3 copy.72
  136.1 30.7 %shard_map.408 = (bf16[2048,1536]{1,0:T(8,128)(2,1)}, f32[2048,768]{1,0:T(8,128)}, bf16[2048,192]{1,0:T(8,128)(2,1)}, bf16[2048,128]{1,0:T(8,128)(2,1)}, f32[204...) custom-call(s32[2]{0:T(128)} %bitcast.197, bf16[4,4,512,384]{3,2,1,0:T(8,128)(2,1)} %bitcast.201, ...), custom_call_target="tpu_custom_call" | custom-call | flops 8589934592 | bytes 25165824 | tf_op jit(solution)/shard_map/pallas_call | solution.py:206
  167.3 0.9 copy.97
  168.2 100.6 %shard_map.409 = (bf16[2048,1536]{1,0:T(8,128)(2,1)}, f32[128,1536]{1,0:T(8,128)}, f32[128,1536]{1,0:T(8,128)}, f32[128,128]{1,0:T(8,128)}, bf16[2048,576]{1,0:T...) custom-call(bf16[2048,192]{1,0:T(8,128)(2,1)} %get-tuple-element.102.refs_, ...), custom_call_target="tpu_custom_call" | custom-call | flops 8589934592 | bytes 100663296 | tf_op jit(solution)/shard_map/pallas_call | solution.py:808
  268.9 1.1 copy.106
  270.0 19.1 %shard_map.410 = (bf16[2048,192]{1,0:T(8,128)(2,1)}, f32[2048,192]{1,0:T(8,128)}, f32[2048,128]{1,0:T(8,128)}, bf16[4,192,384]{2,1,0:T(8,128)(2,1)}, bf16[4,2,96,384]{3,2,1,0:T(8,128)(2,1)}) custom-call(s32[2]{0:T(128)} %bitcast.198, bf16[2048,576]{1,0:T(8,128)(2,1)} %get-tuple-element.107.refs_1_, bf16[4,2,192,384]{3,2,1,0:T(8,128)(2,1)} %bitcast.162, ...), custom_call_target="tpu_custom_call" | custom-call | flops 8589934592 | bytes 25165824 | tf_op jit(solution)/shard_map/pallas_call | solution.py:206
  289.1 1.5 copy.75
  290.6 0.9 copy.98
  291.5 86.1 %shard_map.411 = (bf16[2048,1536]{1,0:T(8,128)(2,1)}, f32[128,1536]{1,0:T(8,128)}, f32[2048,384]{1,0:T(8,128)}, bf16[2048,384]{1,0:T(8,128)(2,1)}, bf16[4,2,192,...) custom-call(bf16[2048,192]{1,0:T(8,128)(2,1)} %get-tuple-element.110.refs_0_, bf16[192,1536]{1,0:T(8,128)(2,1)} %bitcast.172, ...), custom_call_target="tpu_custom_call" | custom-call | flops 8589934592 | bytes 100663296 | tf_op jit(solution)/shard_map/pallas_call | solution.py:808
  377.6 2.3 copy.76
  380.2 8.5 fusion.8.refs_0_
  388.8 4.5 convolution_convert_fusion.2
  393.3 2.6 convolution_convert_fusion.3
  395.9 1.1 copy.105
  397.0 1.8 constant_dynamic-slice_fusion.refs_4_
  398.8 86.8 %shard_map.412 = (bf16[2048,1536]{1,0:T(8,128)(2,1)}, f32[128,1536]{1,0:T(8,128)}, f32[8,1536]{1,0:T(8,128)}, bf16[2048,192]{1,0:T(8,128)(2,1)}, bf16[4,192,384]...) custom-call(bf16[2048,384]{1,0:T(8,128)(2,1)} %copy-done.36, bf16[1536,384]{1,0:T(8,128)(2,1)} %bitcast.205, ...), custom_call_target="tpu_custom_call" | custom-call | flops 8589934592 | bytes 100663296 | tf_op jit(solution)/shard_map/pallas_call | solution.py:808
  485.6 1.8 fusion.13
  487.4 1.1 pad_maximum_fusion.2.refs_5_
  488.5 27.7 %shard_map.413 = (bf16[2048,576]{1,0:T(8,128)(2,1)}, bf16[4,384,384]{2,1,0:T(8,128)(2,1)}) custom-call(s32[2]{0:T(128)} %bitcast.199, bf16[2048,576]{1,0:T(8,128)(2,1)} %get-tuple-element.107.refs_1_, bf16[2048,192]{1,0:T(8,128)(2,1)} %get-tuple-element.121.refs_2_, f32[2048,192]{1,0:T(8,128)} %get-tuple-element.122.refs_3_, ...), custom_call_target="tpu_custom_call" | custom-call | flops 8589934592 | bytes 25165824 | tf_op jit(solution)/shard_map/pallas_call | solution.py:206
  516.2 7.4 convolution_convert_fusion.1
  523.7 2.3 copy.81
  525.9 4.2 convolution_convert_fusion.4
  530.1 0.9 copy.108
  531.0 99.6 %shard_map.414 = (bf16[2048,1664]{1,0:T(8,128)(2,1)}, f32[128,1536]{1,0:T(8,128)}, f32[8,1536]{1,0:T(8,128)}, f32[2048,192]{1,0:T(8,128)}, bf16[4,2,384,384]{3,2...) custom-call(bf16[2048,576]{1,0:T(8,128)(2,1)} %get-tuple-element.126.refs_0_, ...), custom_call_target="tpu_custom_call" | custom-call | flops 8589934592 | bytes 100663296 | tf_op jit(solution)/shard_map/pallas_call | solution.py:808
  630.6 4.3 fusion.9
  635.0 0.9 copy.107
  635.9 1.2 fusion.12.refs_10_
  637.1 0.8 fusion.15.refs_9_
  637.9 34.7 %shard_map.415 = (bf16[2048,768]{1,0:T(8,128)(2,1)}, f32[8,448]{1,0:T(8,128)}, f32[8,256]{1,0:T(8,128)}, bf16[4,96,384]{2,1,0:T(8,128)(2,1)}, bf16[4,192,576]{2,1,0:T(8,128)(2,1)}) custom-call(s32[2]{0:T(128)} %bitcast.200, f32[2048,768]{1,0:T(8,128)} %get-tuple-element.99.refs_1_.refs_2_, f32[2048,768]{1,0:T(8,128)} %get-tuple-element.99.refs_1_.refs_2_, ...), custom_call_target="tpu_custom_call" | custom-call | flops 12884901888 | bytes 25165824 | tf_op jit(solution)/shard_map/pallas_call | solution.py:206
  672.6 7.3 convolution_convert_fusion
  680.0 1.3 copy-done.7
  681.7 0.7 copy.84
  682.5 0.8 slice_reduce_fusion
  683.7 0.8 bitcast_dynamic-update-slice_fusion
  684.5 0.8 bitcast_dynamic-update-slice_fusion.1
  686.5 0.8 slice.132
  687.3 0.8 slice.133
  688.5 1.7 maximum_maximum_fusion
  690.1 1.4 copy.85
  691.8 1.1 copy-done.16
  692.9 1.6 pad_maximum_fusion.refs_1_
  694.4 0.8 dynamic_slice.58
  695.9 132.6 %shard_map.416 = (bf16[2048,384]{1,0:T(8,128)(2,1)}, bf16[4,128,384]{2,1,0:T(8,128)(2,1)}, f32[8,1536]{1,0:T(8,128)}, bf16[4,128,384]{2,1,0:T(8,128)(2,1)}, bf16...) custom-call(bf16[2048,768]{1,0:T(8,128)(2,1)} %get-tuple-element.138, ...), custom_call_target="tpu_custom_call" | custom-call | flops 8589934592 | bytes 100663296 | tf_op jit(solution)/shard_map/pallas_call | solution.py:808
  828.6 1.5 copy-done.2
  830.1 1.4 copy-done.3
  831.5 1.3 copy-done.4
  832.8 1.1 copy-done.5
  833.8 1.1 copy-done.6
  834.9 7.7 shard_map.417
  842.6 3.0 copy.87
  851.1 1.0 bitcast_convert_fusion
  852.0 0.7 copy.124
  (169 shorter events, 16.0 us)
Async XLA Ops:
  0.7 130.3 %copy-start = (f32[4,768]{1,0:T(4,128)S(1)}, f32[4,768]{1,0:T(4,128)}, u32[]{:S(2)}) copy-start(f32[4,768]{1,0:T(4,128)} %param.30) | copy-start | bytes 36868
  0.7 10.4 %copy-start.18 = (bf16[384,768]{1,0:T(8,128)(2,1)S(1)}, bf16[384,768]{1,0:T(8,128)(2,1)}, u32[]{:S(2)}) copy-start(bf16[384,768]{1,0:T(8,128)(2,1)} %param.27) | copy-start | bytes 1769476
  7.1 0.6 copy-start.27
  11.4 1.6 copy-start.26
  11.4 2.6 copy-start.30
  11.4 2.6 copy-start.31
  11.4 2.6 copy-start.32
  14.0 117.8 %copy-start.33 = (f32[256]{0:T(256)S(1)}, f32[256]{0:T(256)}, u32[]{:S(2)}) copy-start(f32[256]{0:T(256)} %param.33) | copy-start | bytes 3076
  14.0 117.9 %copy-start.29 = (f32[4,256]{1,0:T(4,128)S(1)}, f32[4,256]{1,0:T(4,128)}, u32[]{:S(2)}) copy-start(f32[4,256]{1,0:T(4,128)} %param.32) | copy-start | bytes 12292
  14.0 120.0 %copy-start.23 = (bf16[384,384]{1,0:T(8,128)(2,1)S(1)}, bf16[384,384]{1,0:T(8,128)(2,1)}, u32[]{:S(2)}) copy-start(bf16[384,384]{1,0:T(8,128)(2,1)} %param.40) | copy-start | bytes 884740
  14.7 119.5 %copy-start.24 = (bf16[384,384]{1,0:T(8,128)(2,1)S(1)}, bf16[384,384]{1,0:T(8,128)(2,1)}, u32[]{:S(2)}) copy-start(bf16[384,384]{1,0:T(8,128)(2,1)} %param.41) | copy-start | bytes 884740
  14.7 119.7 %copy-start.25 = (bf16[384,384]{1,0:T(8,128)(2,1)S(1)}, bf16[384,384]{1,0:T(8,128)(2,1)}, u32[]{:S(2)}) copy-start(bf16[384,384]{1,0:T(8,128)(2,1)} %param.42) | copy-start | bytes 884740
  136.1 30.8 %copy-start.19 = (bf16[4,2,96,384]{3,2,1,0:T(8,128)(2,1)S(1)}, bf16[4,2,96,384]{3,2,1,0:T(8,128)(2,1)}, u32[]{:S(2)}) copy-start(bf16[4,2,96,384]{3,2,1,0:T(8,128)(2,1)} %get-tuple-element.103) | copy-start | bytes 1769476
  168.2 100.7 %copy-start.13 = (bf16[384,1536]{1,0:T(8,128)(2,1)S(1)}, bf16[384,1536]{1,0:T(8,128)(2,1)}, u32[]{:S(2)}) copy-start(bf16[384,1536]{1,0:T(8,128)(2,1)} %param.45) | copy-start | bytes 3538948
  377.6 2.6 copy-start.37
  380.0 8.8 %slice-start.3 = ((s8[6291456]{0:T(1024)(128)(4,1)}), s8[4194304]{0:T(1024)(128)(4,1)S(1)}, s32[]{:S(2)}) async-start(s8[6291456]{0:T(1024)(128)(4,1)} %bitcast.206), calls=%async_computation.3 | async-start | bytes 8388608
  380.0 13.3 %slice-start.1 = ((s8[6291456]{0:T(1024)(128)(4,1)}), s8[4194304]{0:T(1024)(128)(4,1)S(1)}, s32[]{:S(2)}) async-start(s8[6291456]{0:T(1024)(128)(4,1)} %bitcast.180), calls=%async_computation.1 | async-start | bytes 8388608
  380.2 8.5 copy-start.15
  380.2 8.5 %slice-start.4 = ((s8[6291456]{0:T(1024)(128)(4,1)}), s8[2097152]{0:T(1024)(128)(4,1)S(1)}, s32[]{:S(2)}) async-start(s8[6291456]{0:T(1024)(128)(4,1)} %bitcast.206), calls=%async_computation.4 | async-start | bytes 4194304
  380.2 13.0 %slice-start.2 = ((s8[6291456]{0:T(1024)(128)(4,1)}), s8[2097152]{0:T(1024)(128)(4,1)S(1)}, s32[]{:S(2)}) async-start(s8[6291456]{0:T(1024)(128)(4,1)} %bitcast.180), calls=%async_computation.2 | async-start | bytes 4194304
  388.7 4.5 copy-start.36
  388.8 4.5 copy-start.34
  398.8 86.8 %copy-start.10 = (bf16[48,4,8,384]{3,2,0,1:T(8,128)(2,1)S(1)}, bf16[48,4,8,384]{3,2,0,1:T(8,128)(2,1)}, u32[]{:S(2)}) copy-start(bf16[48,4,8,384]{3,2,0,1:T(8,128)(2,1)} %copy.105) | copy-start | bytes 3538948
  523.7 2.3 copy-start.9
  531.0 99.6 %copy-start.35 = (bf16[2048,192]{1,0:T(8,128)(2,1)S(1)}, bf16[2048,192]{1,0:T(8,128)(2,1)}, u32[]{:S(2)}) copy-start(bf16[2048,192]{1,0:T(8,128)(2,1)} %get-tuple-element.102.refs_0_) | copy-start | bytes 2359300
  630.6 5.3 copy-start.8
  630.6 5.3 copy-start.17
  635.0 2.1 copy-start.12
  635.0 2.1 copy-start.22
  635.9 36.7 %slice-start.5 = ((s8[6291456]{0:T(1024)(128)(4,1)}), s8[4194304]{0:T(1024)(128)(4,1)S(1)}, s32[]{:S(2)}) async-start(s8[6291456]{0:T(1024)(128)(4,1)} %bitcast.208), calls=%async_computation.5 | async-start | bytes 8388608
  637.9 34.7 %slice-start.6 = ((s8[6291456]{0:T(1024)(128)(4,1)}), s8[2097152]{0:T(1024)(128)(4,1)S(1)}, s32[]{:S(2)}) async-start(s8[6291456]{0:T(1024)(128)(4,1)} %bitcast.208), calls=%async_computation.6 | async-start | bytes 4194304
  679.9 1.4 copy-start.7
  681.6 3.6 copy-start.28
  688.5 1.7 slice-start
  690.1 1.4 copy-start.14
  690.1 1.6 copy-start.11
  691.6 1.3 copy-start.16
  828.5 1.5 copy-start.2
  830.1 1.4 copy-start.3
  831.5 1.3 copy-start.4
  832.8 1.1 copy-start.5
  833.8 1.1 copy-start.6
  842.6 8.5 copy-start.21
  842.6 10.2 %copy-start.1 = (f32[4,768]{1,0:T(4,128)S(1)}, f32[4,768]{1,0:T(4,128)}, u32[]{:S(2)}) copy-start(f32[4,768]{1,0:T(4,128)} %param.30) | copy-start | bytes 36868
  842.6 9.5 %copy-start.20 = (bf16[4,128,384]{2,1,0:T(8,128)(2,1)S(1)}, bf16[4,128,384]{2,1,0:T(8,128)(2,1)}, u32[]{:S(2)}) copy-start(bf16[4,128,384]{2,1,0:T(8,128)(2,1)} %get-tuple-element.147) | copy-start | bytes 1179652

commit v5 on v4

--- a/solution.py
+++ b/solution.py
@@ -220,7 +220,6 @@
 STATE = 128
 CONV = 4
 SPAN = 256
-HIGH = lax.Precision.HIGHEST
 WIDE = 192
 MIX = 2 * STATE + WIDE
 
@@ -229,8 +228,14 @@
     return lax.dot_general(a.astype(BF), b.astype(BF), (((ca,), (cb,)), ((), ())), preferred_element_type=F32)
 
 
-def exact(a, b, ca=1, cb=0):
-    return lax.dot_general(a, b, (((ca,), (cb,)), ((), ())), preferred_element_type=F32, precision=HIGH)
+def by_parts(a, mask, ca, cb, parts, mask_first=False):
+    total = None
+    for _ in range(parts):
+        high = a.astype(BF)
+        one = mm(mask, high, ca, cb) if mask_first else mm(high, mask, ca, cb)
+        total = one if total is None else total + one
+        a = a - high.astype(F32)
+    return total
 
 
 def seg_at(place, l0, l1):
@@ -248,7 +253,7 @@
 def head_sums(a):
     i = lax.broadcasted_iota(jnp.int32, (WIDE, 128), 0)
     j = lax.broadcasted_iota(jnp.int32, (WIDE, 128), 1)
-    return exact(a, jnp.where(i // HEAD_DIM == j, 1.0, 0.0).astype(F32))
+    return by_parts(a, jnp.where(i // HEAD_DIM == j, 1.0, 0.0), 1, 0, 2)
 
 
 class Block:
@@ -278,7 +283,7 @@
         i = lax.broadcasted_iota(jnp.int32, (SPAN, SPAN), 0)
         j = lax.broadcasted_iota(jnp.int32, (SPAN, SPAN), 1)
         self.low = jnp.where(j <= i, 1.0, 0.0).astype(F32)
-        self.cum = exact(self.low, self.rate)
+        self.cum = by_parts(self.rate, self.low, 1, 0, 3, True)
         self.cum_t = self.cum.T
         seg_row = seg_at(self.start + lax.broadcasted_iota(jnp.int32, (1, SPAN), 1), self.l0, self.l1)
         self.allowed = (j <= i) & (seg_row == self.seg)
@@ -382,7 +387,7 @@
     at_end = jnp.sum(left, axis=0, keepdims=True) + k.through * own
     is_last = lax.broadcasted_iota(jnp.int32, (SPAN, 128), 0) == SPAN - 1
     d_cum = d_cum + jnp.where(is_last, at_end, 0.0)
-    d_rate = exact(k.low, d_cum, 0, 0)
+    d_rate = by_parts(d_cum, k.low, 0, 0, 3, True)
     d_dt = head_sums(dw * k.x) + d_rate * pv[3:4, :128]
     d_raw = jnp.where(lane < 3, d_dt * sigmoid(k.raw), 0.0)
     d_x = dw * by_head(k.dt, k.lane) + pv[1:2, :WIDE] * dy
@@ -836,17 +841,18 @@
     riding = Riders(kinds, ins, outs, *sems)
     hid_all[pl.ds(pl.multiple_of((r * NC + c) * big, 16), big), :] = hidden[...]
     first.begin()
-    riding.start()
     swap.start()
     for d in range(1, NC):
         first.forward(d)
+        if d == 1:
+            riding.start()
         first.uses(d)
-        if d == 1:
+        if d == 2:
             swap.finish()
             for i in range(NC):
                 g_all[pl.ds(pl.multiple_of((r * NC + c) * S, 16), S), i * feat:(i + 1) * feat] = got[i]
             second.begin()
-        if d == 2:
+        if d == 3:
             riding.relay()
             second.forward(1)
             second.uses(1)
@@ -930,20 +936,33 @@
     if spec["more_sum"]:
         summing2 = Sum(r, c, lambda rr, cc: mm(a2[rows_of(rr, cc), :], v2[...]), sum2_bufs[:16])
     summing.own()
-    for j in range(NC):
-        summing.step(j, 0)
-        if spec["small"] and j == 1:
-            early.add()
-        if summing2 and j == 1:
-            summing2.to_core()
-    summing.last(total, 0)
-    if summing2:
-        summing2.to_y()
-        summing2.own()
+    def advance(h):
+        at = pl.ds(h * (S // HALVES), S // HALVES)
+        off = pl.multiple_of((r * NC + c) * S + h * (S // HALVES), 16)
+        u_all[pl.ds(off, S // HALVES), :] = spec["mid"](total, mid_in, mid_out, at, h)
+        gather.pass_on(c, h)
+
+    for h in range(HALVES):
+        for j in range(NC):
+            summing.step(j, h)
+            if h == 0 and j == 1:
+                if spec["small"]:
+                    early.add()
+                if summing2:
+                    summing2.to_core()
+            if not spec["small"] and j == 1:
+                for g in range(h):
+                    gather.forward(h - g, (g,))
+        summing.last(total, h)
+        if not spec["small"]:
+            advance(h)
+        if h == 0:
+            if summing2:
+                summing2.to_y()
+                summing2.own()
+            if not spec["small"]:
+                early.add()
     if spec["small"]:
-        for j in range(NC):
-            summing.step(j, 1)
-        summing.last(total, 1)
         mine, others, held, dp_s, dp_r, loc = small
         spec["mid"](total, mid_in, mid_out, mine)
         settle = sum_groups(mine, others, held, dp_s, dp_r, 4)
@@ -955,20 +974,6 @@
         gather.begin()
         early.relay()
     else:
-        def advance(h):
-            at = pl.ds(h * (S // HALVES), S // HALVES)
-            off = pl.multiple_of((r * NC + c) * S + h * (S // HALVES), 16)
-            u_all[pl.ds(off, S // HALVES), :] = spec["mid"](total, mid_in, mid_out, at, h)
-            gather.pass_on(c, h)
-        advance(0)
-        early.add()
-        summing.step(0, 1)
-        summing.step(1, 1)
-        gather.forward(1, (0,))
-        summing.step(2, 1)
-        summing.step(3, 1)
-        summing.last(total, 1)
-        advance(1)
         late.start()
     if spec["w2"] == "rider":
         early.relay()
@@ -977,13 +982,14 @@
         use(r, c)
     for d in range(1, NC + 2):
         if summing2 and d <= NC:
-            summing2.step(d - 1, 0)
-            summing2.step(d - 1, 1)
+            for h in range(HALVES):
+                summing2.step(d - 1, h)
         if spec["small"]:
             gather.forward(d)
         else:
-            gather.forward(d, (1,))
-            gather.forward(d + 1, (0,))
+            for g in reversed(range(HALVES)):
+                if HALVES - 1 - g + d <= NC:
+                    gather.forward(HALVES - 1 - g + d, (g,))
         gather.uses(d)
         if d == 2 and spec["w2"] != "rider" and not spec["small"]:
             early.relay()
@@ -1195,9 +1201,69 @@
         out_shape=[sds(rows, NC * WIDE)] * 2 + [sds(rows, 2 * WIDE)] * 3 + [
             sds(NC * half, feat), sds(2 * half, feat), sds(part, NC * feat), sds(NC * part, feat), sds(D, bcdt_width),
             sds(rest.shape[0], 4, thin), sds(8, thin)],
-        compiler_params=pltpu.CompilerParams(vmem_limit_bytes=48 << 20, dimension_semantics=("arbitrary",)),
+        compiler_params=pltpu.CompilerParams(vmem_limit_bytes=62 << 20, dimension_semantics=("arbitrary",)),
         cost_estimate=pl.CostEstimate(flops=1 << 20, bytes_accessed=24 << 20, transcendentals=0),
     )(zx, mix, qkv, o, ff, rest)
+
+
+def side_kernel(in_grad, taps, rows, gain2, gain3, zx, side, small):
+    i = pl.program_id(0)
+    slab = lax.axis_index("rows") * NC + lax.axis_index("cols")
+    thin = side.shape[2]
+    lane = lax.broadcasted_iota(jnp.int32, (1, thin), 1)
+
+    @pl.when(i == 0)
+    def _():
+        small[...] = jnp.zeros_like(small)
+        for n, g in enumerate((gain2, gain3)):
+            for q in range(4):
+                small[n, q:q + 1] = g[0:1, q * thin:(q + 1) * thin]
+
+        def channels(first, v):
+            both = jnp.concatenate([v, v], axis=1)
+            small[first + (slab >> 3), pl.ds((slab & 7) >> 1, 1)] = jnp.where(lane // WIDE == (slab & 1), both, 0.0)
+
+        def heads(at, v):
+            placed = sum(jnp.where(lane == slab * 3 + h, v[:, h:h + 1], 0.0) for h in range(3))
+            small[15, at:at + 1] = placed
+        none = jnp.zeros((1, thin - 2 * STATE), F32)
+        for t in range(CONV):
+            channels(2 + 2 * t, taps[t:t + 1, 2 * STATE:])
+            small[14, t:t + 1] = jnp.concatenate([taps[t:t + 1, :2 * STATE], none], axis=1)
+        channels(10, taps[CONV:CONV + 1, 2 * STATE:])
+        channels(12, rows[0:1, :WIDE])
+        small[15, 0:1] = jnp.concatenate([taps[CONV:CONV + 1, :2 * STATE], none], axis=1)
+        heads(1, rows[3:4, :128])
+        heads(2, head_sums(jnp.broadcast_to(rows[1:2, :WIDE], (8, WIDE)))[0:1])
+        heads(3, rows[2:3, :128])
+    p = in_grad[...]
+    half = p.shape[0] // 2
+    for h in range(2):
+        zx[0, h] = p[h * half:(h + 1) * half, 2 * STATE:2 * STATE + 2 * WIDE].astype(BF)
+    at = lax.broadcasted_iota(jnp.int32, (p.shape[0], 128), 1)
+    dts = sum(jnp.where(at == slab * 3 + h, p[:, MIX + WIDE + h:MIX + WIDE + h + 1], 0.0) for h in range(3))
+    state = jnp.concatenate([p[:, :2 * STATE], dts], axis=1).astype(BF)
+    for j in range(NC):
+        side[j, :SMALL] = state[j * SMALL:(j + 1) * SMALL]
+        own = small[i * NC + j]
+        rest = own - own.astype(BF).astype(F32)
+        side[j, SMALL:] = jnp.concatenate([own, rest, jnp.zeros((side.shape[1] - SMALL - 8, thin), F32)], axis=0).astype(BF)
+
+
+def side_columns(in_grad, taps, rows, gain2, gain3, S):
+    D, cols = in_grad.shape
+    feat, thin = D // NC, cols - 2 * WIDE
+    whole = lambda a: pl.BlockSpec(a.shape, lambda i: (0, 0))
+    return pl.pallas_call(
+        side_kernel,
+        grid=(NC,),
+        in_specs=[pl.BlockSpec((feat, cols), lambda i: (i, 0)), whole(taps), whole(rows), whole(gain2), whole(gain3)],
+        out_specs=[pl.BlockSpec((1, 2, feat // 2, 2 * WIDE), lambda i: (i, 0, 0, 0)), pl.BlockSpec((NC, S, thin), lambda i: (i, 0, 0))],
+        out_shape=[jax.ShapeDtypeStruct((NC, 2, feat // 2, 2 * WIDE), BF), jax.ShapeDtypeStruct((4 * NC, S, thin), BF)],
+        scratch_shapes=[pltpu.VMEM((4 * NC, 4, thin), F32)],
+        compiler_params=pltpu.CompilerParams(vmem_limit_bytes=32 << 20, dimension_semantics=("arbitrary",)),
+        cost_estimate=pl.CostEstimate(flops=1 << 20, bytes_accessed=8 << 20, transcendentals=0),
+    )(in_grad, taps, rows, gain2, gain3)
 
 
 P = jax.sharding.PartitionSpec
@@ -1232,11 +1298,6 @@
 def split_grad(g):
     n, d = g.shape
     return g.astype(BF).reshape(n, NC, d // NC).transpose(1, 0, 2)
-
-
-def place_block(piece, start, full_len, axis):
-    shape = piece.shape[:axis] + (full_len,) + piece.shape[axis + 1:]
-    return lax.dynamic_update_slice_in_dim(jnp.zeros(shape, piece.dtype), piece, start, axis)
 
 
 def per_device(hidden_in, lengths, norm1_gain, z_weight, x_weight, bcdt_weight, conv_x_weight, conv_x_bias,
@@ -1347,27 +1408,11 @@
     mix_pieces = halved(split_grad(t_dot(mixg, g1)))
     d_in, tap_grads, row_grads, o_split, qkv_split = mixer_bwd(
         9, seq_lens, proj, cw, pv, y, states, d_mix, g1_ext, ("swap", "swap"), (o_sum, qkv_sum))
-    cbw_grad, cxw_grad = tap_grads[:CONV, :2 * STATE], tap_grads[:CONV, 2 * STATE:]
-    cbb_grad, cxb_grad = tap_grads[CONV, :2 * STATE], tap_grads[CONV, 2 * STATE:]
-    gate_gain_grad, dt_bias_grad, a_log_grad = row_grads[0, :wide], row_grads[2, :heads], row_grads[3, :heads]
-    d_skip_grad = row_grads[1, :wide].reshape(heads, HEAD_DIM).sum(1)
     in_grad = t_dot(u1, d_in)
-    zx_pieces = halved(in_grad[:, 2 * STATE:2 * STATE + 2 * wide].astype(BF).reshape(NC, feat, -1))
-    slabs = rows * NC
-    dt_grads = place_block(in_grad[:, 2 * STATE + 2 * wide:2 * STATE + 2 * wide + heads].astype(BF), slab * heads, bcdt_width + bcdt_pad - 2 * STATE, 1)
-    bcdt_part = jnp.concatenate([in_grad[:, :2 * STATE].astype(BF), dt_grads], axis=1).reshape(slabs, SMALL, -1)
-    misc = jnp.concatenate([cbw_grad.reshape(-1), cbb_grad] + [
-        place_block(a, slab * heads, n_heads, 0) for a in (a_log_grad, d_skip_grad, dt_bias_grad)])
-    n_misc = misc.shape[0]
-    small = jnp.concatenate([gain2_rows[:1], gain3_rows[:1], place_block(cxw_grad, slab * wide, inner, 1).reshape(-1, D),
-                             place_block(cxb_grad, slab * wide, inner, 0).reshape(-1, D),
-                             place_block(gate_gain_grad, slab * wide, inner, 0).reshape(-1, D), jnp.pad(misc, (0, D - n_misc))[None]])
-    thin = bcdt_width + bcdt_pad
+    slabs, thin = rows * NC, bcdt_width + bcdt_pad
     four = D // thin
-    small = jnp.pad(small, ((0, slabs - small.shape[0]), (0, 0))).reshape(slabs, four, thin)
-    small_hi = small.astype(BF)
-    small_lo = (small - small_hi.astype(F32)).astype(BF)
-    side = jnp.concatenate([bcdt_part, small_hi, small_lo, jnp.zeros((slabs, S - SMALL - 2 * four, thin), BF)], axis=1)
+    zx_pieces, side = side_columns(in_grad, tap_grads, row_grads, gain2_rows, gain3_rows, S)
+    zx_pieces = zx_pieces if few else zx_pieces.reshape(NC, feat, -1)
     rest_all, _, _, _, zx_back, mix_back, o_back, qkv_back, in_got, out_got = link(
         5, d_in, w_in, mid_mixer_back, (h0, gains[0:1], dh1), (((NC, S, feat), BF), row8), w1_t=True, side=side.reshape(T, thin), small=thin,
         early=(reduce, reduce, "spread", "spread"), early_in=(zx_pieces, mix_pieces, o_split, qkv_split), late=(("swap", 0),),
@@ -1380,17 +1425,14 @@
         zx_back, mix_back = lax.psum(zx_back, "dp"), lax.psum(mix_back, "dp")
     (x_grad, z_grad, q_grad, k_grad, v_grad, mix_grad, o_grad, up_grad, down_grad, bcdt_grad, small, gain1) = finish(
         four_d(zx_back), four_d(mix_back), four_d(qkv_back), four_d(o_back), ff_back, rest_all.reshape(slabs, S, thin), bcdt_width)
-    small, gain1_grad = small.reshape(slabs, D), gain1[:4].reshape(D)
-    per_inner = inner // D
-    edges = [2 + CONV * per_inner, 2 + (CONV + 1) * per_inner, 2 + (CONV + 2) * per_inner]
-    cxw_sum = small[2:edges[0]].reshape(CONV, inner)
-    cxb_sum, gate_gain_sum = small[edges[0]:edges[1]].reshape(-1), small[edges[1]:edges[2]].reshape(-1)
-    misc = small[edges[2]]
-    cbw_sum, cbb_sum = misc[:CONV * 2 * STATE].reshape(CONV, 2 * STATE), misc[CONV * 2 * STATE:(CONV + 1) * 2 * STATE]
-    a_log_sum, d_skip_sum, dt_bias_sum = jnp.split(misc[n_misc - 3 * n_heads:n_misc], 3)
+    gain1_grad = gain1[:4].reshape(D)
+    cxw_sum = small[2:10].reshape(CONV, inner)
+    cxb_sum, gate_gain_sum = small[10:12].reshape(-1), small[12:14].reshape(-1)
+    cbw_sum, cbb_sum = small[14, :, :2 * STATE], small[15, 0, :2 * STATE]
+    a_log_sum, d_skip_sum, dt_bias_sum = small[15, 1, :n_heads], small[15, 2, :n_heads], small[15, 3, :n_heads]
     input_grad = in_got.reshape(NC * S, feat).astype(F32)
     return (output, input_grad, gain1_grad, z_grad, x_grad, bcdt_grad, cxw_sum, cxb_sum, cbw_sum, cbb_sum, a_log_sum, d_skip_sum,
-            dt_bias_sum, gate_gain_sum, mix_grad, small[0], q_grad, k_grad, v_grad, o_grad, small[1], up_grad, down_grad)
+            dt_bias_sum, gate_gain_sum, mix_grad, small[0].reshape(D), q_grad, k_grad, v_grad, o_grad, small[1].reshape(D), up_grad, down_grad)
 
 
 def solution(mesh):

time: 862 us -> 830 us (0.963)
  local copies, waits for them, and re-layouts: 58.4 us -> 40.3 us
  Pallas kernels: 740 us -> 728 us
    pallas_call x6, Pallas kernels: 620 us -> 610 us  [link_call(): pl.pallas_call(kernel, out_shape=[jax.ShapeDtypeStruct(s, d) for s, d in...]
    unnamed x101 -> x99, local copies, waits for them, and re-layouts: 17.9 us -> 8.74 us
where the time goes in v5:
time: 830 us; the launch traced here: 821 us
  Pallas kernels  728 us (88%)
  local copies, waits for them, and re-layouts  40.3 us (5%)
  matrix products  38.9 us (5%)
  other arithmetic  11.3 us (1%)
    pallas_call x6, Pallas kernels, link_call(): pl.pallas_call(kernel, out_shape=[jax.ShapeDtypeStruct(s, d) for s, d in...  610 us
    pallas_call x4, Pallas kernels, ridden_call(): pl.pallas_call(ridden(kernel, len(ins), len(outs), tuple(kinds)), grid=(g...  107 us
    dot_general x6, matrix products, t_dot(): lax.dot_general(a, b, (((0,), (0,)), ((), ())), preferred_element_type=F32)  30.4 us

profile of v5, /device:TPU:0, one launch (start us, length us, event | category | flops | bytes accessed | tf_op | source)
XLA Modules:
  0.0 821.3 jit_solution(15863094485402877728)
XLA Ops:
  0.7 0.8 dynamic_slice.50
  1.6 0.8 dynamic_slice.49
  2.4 0.7 dynamic_slice.51
  3.1 0.7 exponential_negate_fusion
  3.9 0.6 concatenate.28.refs_7_.refs_4_
  4.5 1.3 fusion.20
  7.2 1.9 multiply_convert_fusion
  9.1 1.4 copy.63
  11.0 1.5 copy.65
  12.6 0.8 pad.26.clone
  13.5 0.6 broadcast_in_dim.37.refs_5_
  14.1 102.6 %shard_map.407 = (bf16[8192,384]{1,0:T(8,128)(2,1)}, bf16[2048,1536]{1,0:T(8,128)(2,1)}, bf16[128,1536]{1,0:T(8,128)(2,1)}, bf16[4,2,192,384]{3,2,1,0:T(8,128)(2...) custom-call(bf16[512,384]{1,0:T(8,128)(2,1)} %refs_0_.1, ...), custom_call_target="tpu_custom_call" | custom-call | flops 1048576 | bytes 100663296 | tf_op jit(solution)/shard_map/pallas_call | solution.py:813
  116.7 1.2 constant_dynamic-slice_fusion.2
  117.9 0.8 pad.28.refs_5_
  118.8 0.8 dynamic_slice.48
  119.7 0.7 maximum_maximum_fusion.refs_6_.refs_3_
  120.4 0.8 slice_bitcast_fusion
  121.2 0.6 fusion.19
  122.6 1.3 copy.70
  123.9 27.6 %shard_map.408 = (bf16[2048,1536]{1,0:T(8,128)(2,1)}, f32[2048,768]{1,0:T(8,128)}, bf16[2048,192]{1,0:T(8,128)(2,1)}, bf16[2048,128]{1,0:T(8,128)(2,1)}, f32[204...) custom-call(s32[2]{0:T(128)} %bitcast.188, bf16[4,4,512,384]{3,2,1,0:T(8,128)(2,1)} %bitcast.193, ...), custom_call_target="tpu_custom_call" | custom-call | flops 8589934592 | bytes 25165824 | tf_op jit(solution)/shard_map/pallas_call | solution.py:206
  152.0 0.9 copy.93
  152.9 102.4 %shard_map.409 = (bf16[2048,1536]{1,0:T(8,128)(2,1)}, f32[128,1536]{1,0:T(8,128)}, f32[128,1536]{1,0:T(8,128)}, f32[128,128]{1,0:T(8,128)}, bf16[2048,576]{1,0:T...) custom-call(bf16[2048,192]{1,0:T(8,128)(2,1)} %get-tuple-element.104.refs_, ...), custom_call_target="tpu_custom_call" | custom-call | flops 8589934592 | bytes 100663296 | tf_op jit(solution)/shard_map/pallas_call | solution.py:813
  255.3 1.1 copy.101
  256.4 19.2 %shard_map.410 = (bf16[2048,192]{1,0:T(8,128)(2,1)}, f32[2048,192]{1,0:T(8,128)}, f32[2048,128]{1,0:T(8,128)}, bf16[4,192,384]{2,1,0:T(8,128)(2,1)}, bf16[4,2,96,384]{3,2,1,0:T(8,128)(2,1)}) custom-call(s32[2]{0:T(128)} %bitcast.189, bf16[2048,576]{1,0:T(8,128)(2,1)} %get-tuple-element.109.refs_1_, bf16[4,2,192,384]{3,2,1,0:T(8,128)(2,1)} %bitcast.157, ...), custom_call_target="tpu_custom_call" | custom-call | flops 8589934592 | bytes 25165824 | tf_op jit(solution)/shard_map/pallas_call | solution.py:206
  275.7 1.5 copy.73
  277.2 0.9 copy.94
  278.1 86.7 %shard_map.411 = (bf16[2048,1536]{1,0:T(8,128)(2,1)}, f32[128,1536]{1,0:T(8,128)}, f32[2048,384]{1,0:T(8,128)}, bf16[2048,384]{1,0:T(8,128)(2,1)}, bf16[4,2,192,...) custom-call(bf16[2048,192]{1,0:T(8,128)(2,1)} %get-tuple-element.112.refs_0_, bf16[192,1536]{1,0:T(8,128)(2,1)} %bitcast.167, ...), custom_call_target="tpu_custom_call" | custom-call | flops 8589934592 | bytes 100663296 | tf_op jit(solution)/shard_map/pallas_call | solution.py:813
  364.8 2.3 copy.74
  367.4 8.5 %fusion.8.refs_0_ = bf16[2048,384]{1,0:T(8,128)(2,1)S(1)} fusion(f32[2048,384]{1,0:T(8,128)S(1)} %copy-done.37, bf16[2048,1536]{1,0:T(8,128)(2,1)} %get-tuple-element.110, bf16[384,1536]{1,0:T(8,128)(2,1)S(1)} %bitcast.154), kind=kOutput, calls=%fused_computation.10 | convolution fusion | flops 2431647744 | bytes 12189696 | tf_op jit(solution)/shard_map/dot_general | solution.py:1277
  375.9 4.5 convolution_convert_fusion.1
  380.4 2.6 convolution_convert_fusion.2
  383.0 1.1 copy.100
  384.2 1.8 constant_dynamic-slice_fusion.refs_4_
  385.9 87.1 %shard_map.412 = (bf16[2048,1536]{1,0:T(8,128)(2,1)}, f32[128,1536]{1,0:T(8,128)}, f32[8,1536]{1,0:T(8,128)}, bf16[2048,192]{1,0:T(8,128)(2,1)}, bf16[4,192,384]...) custom-call(bf16[2048,384]{1,0:T(8,128)(2,1)} %copy-done.36, bf16[1536,384]{1,0:T(8,128)(2,1)} %bitcast.197, ...), custom_call_target="tpu_custom_call" | custom-call | flops 8589934592 | bytes 100663296 | tf_op jit(solution)/shard_map/pallas_call | solution.py:813
  473.1 1.8 fusion.13
  474.9 1.1 pad_maximum_fusion.2.refs_5_
  476.0 27.7 %shard_map.413 = (bf16[2048,576]{1,0:T(8,128)(2,1)}, bf16[4,384,384]{2,1,0:T(8,128)(2,1)}) custom-call(s32[2]{0:T(128)} %bitcast.190, bf16[2048,576]{1,0:T(8,128)(2,1)} %get-tuple-element.109.refs_1_, bf16[2048,192]{1,0:T(8,128)(2,1)} %get-tuple-element.123.refs_2_, f32[2048,192]{1,0:T(8,128)} %get-tuple-element.124.refs_3_, ...), custom_call_target="tpu_custom_call" | custom-call | flops 8589934592 | bytes 25165824 | tf_op jit(solution)/shard_map/pallas_call | solution.py:206
  503.7 7.4 convolution_convert_fusion
  511.2 2.3 copy.79
  513.5 4.2 convolution_convert_fusion.3
  517.7 0.9 copy.103
  518.5 99.5 %shard_map.414 = (bf16[2048,1664]{1,0:T(8,128)(2,1)}, f32[128,1536]{1,0:T(8,128)}, f32[8,1536]{1,0:T(8,128)}, f32[2048,192]{1,0:T(8,128)}, bf16[4,2,384,384]{3,2...) custom-call(bf16[2048,576]{1,0:T(8,128)(2,1)} %get-tuple-element.128.refs_0_, ...), custom_call_target="tpu_custom_call" | custom-call | flops 8589934592 | bytes 100663296 | tf_op jit(solution)/shard_map/pallas_call | solution.py:813
  618.1 4.4 fusion.9
  622.4 0.9 copy.102
  623.3 1.2 fusion.12.refs_10_
  624.5 0.8 fusion.15.refs_9_
  625.3 32.4 %shard_map.415 = (bf16[2048,768]{1,0:T(8,128)(2,1)}, f32[8,448]{1,0:T(8,128)}, f32[8,256]{1,0:T(8,128)}, bf16[4,96,384]{2,1,0:T(8,128)(2,1)}, bf16[4,192,576]{2,1,0:T(8,128)(2,1)}) custom-call(s32[2]{0:T(128)} %bitcast.191, f32[2048,768]{1,0:T(8,128)} %get-tuple-element.101.refs_1_.refs_2_, f32[2048,768]{1,0:T(8,128)} %get-tuple-element.101.refs_1_.refs_2_, ...), custom_call_target="tpu_custom_call" | custom-call | flops 12884901888 | bytes 25165824 | tf_op jit(solution)/shard_map/pallas_call | solution.py:206
  657.7 7.3 fusion.21.in_grad
  665.1 1.5 shard_map.416
  666.9 1.9 pad_maximum_fusion.refs_1_
  669.0 0.7 broadcast_in_dim.46.refs_9_
  669.7 131.9 %shard_map.417 = (bf16[2048,384]{1,0:T(8,128)(2,1)}, bf16[4,128,384]{2,1,0:T(8,128)(2,1)}, f32[8,1536]{1,0:T(8,128)}, bf16[4,128,384]{2,1,0:T(8,128)(2,1)}, bf16...) custom-call(bf16[2048,768]{1,0:T(8,128)(2,1)} %get-tuple-element.140, ...), custom_call_target="tpu_custom_call" | custom-call | flops 8589934592 | bytes 100663296 | tf_op jit(solution)/shard_map/pallas_call | solution.py:813
  801.6 9.3 %shard_map.418 = (f32[384,768]{1,0:T(8,128)}, f32[384,768]{1,0:T(8,128)}, f32[384,384]{1,0:T(8,128)}, f32[384,384]{1,0:T(8,128)}, f32[384,384]{1,0:T(8,128)}, /*...) custom-call(bf16[4,2,192,384]{3,2,1,0:T(8,128)(2,1)} %get-tuple-elem, ...), custom_call_target="tpu_custom_call" | custom-call | flops 1048576 | bytes 25165824 | tf_op jit(solution)/shard_map/pallas_call | solution.py:1193
  811.0 3.0 copy.83
  814.0 0.7 reshape.210
  814.6 0.6 reshape.211
  815.2 0.6 reshape.212
  815.8 0.6 reshape_squeeze.6
  816.4 0.6 reshape_squeeze.7
  817.1 0.6 reshape.209
  817.7 0.6 slice_bitcast_fusion.1
  818.8 0.6 slice.86
  819.3 1.0 bitcast_convert_fusion
  820.3 0.7 copy.105
  (124 shorter events, 3.6 us)
Async XLA Ops:
  0.7 118.1 %copy-start = (f32[4,768]{1,0:T(4,128)S(1)}, f32[4,768]{1,0:T(4,128)}, u32[]{:S(2)}) copy-start(f32[4,768]{1,0:T(4,128)} %param.30) | copy-start | bytes 36868
  0.7 9.8 %copy-start.18 = (bf16[384,768]{1,0:T(8,128)(2,1)S(1)}, bf16[384,768]{1,0:T(8,128)(2,1)}, u32[]{:S(2)}) copy-start(bf16[384,768]{1,0:T(8,128)(2,1)} %param.27) | copy-start | bytes 1769476
  10.8 1.6 copy-start.26
  10.8 2.6 copy-start.30
  10.8 2.6 copy-start.31
  10.8 2.6 copy-start.32
  13.4 106.2 %copy-start.33 = (f32[256]{0:T(256)S(1)}, f32[256]{0:T(256)}, u32[]{:S(2)}) copy-start(f32[256]{0:T(256)} %param.33) | copy-start | bytes 3076
  13.4 106.3 %copy-start.28 = (f32[4,256]{1,0:T(4,128)S(1)}, f32[4,256]{1,0:T(4,128)}, u32[]{:S(2)}) copy-start(f32[4,256]{1,0:T(4,128)} %param.32) | copy-start | bytes 12292
  13.4 108.4 %copy-start.23 = (bf16[384,384]{1,0:T(8,128)(2,1)S(1)}, bf16[384,384]{1,0:T(8,128)(2,1)}, u32[]{:S(2)}) copy-start(bf16[384,384]{1,0:T(8,128)(2,1)} %param.40) | copy-start | bytes 884740
  14.1 107.9 %copy-start.24 = (bf16[384,384]{1,0:T(8,128)(2,1)S(1)}, bf16[384,384]{1,0:T(8,128)(2,1)}, u32[]{:S(2)}) copy-start(bf16[384,384]{1,0:T(8,128)(2,1)} %param.41) | copy-start | bytes 884740
  14.1 108.1 %copy-start.25 = (bf16[384,384]{1,0:T(8,128)(2,1)S(1)}, bf16[384,384]{1,0:T(8,128)(2,1)}, u32[]{:S(2)}) copy-start(bf16[384,384]{1,0:T(8,128)(2,1)} %param.42) | copy-start | bytes 884740
  123.9 27.6 %copy-start.19 = (bf16[4,2,96,384]{3,2,1,0:T(8,128)(2,1)S(1)}, bf16[4,2,96,384]{3,2,1,0:T(8,128)(2,1)}, u32[]{:S(2)}) copy-start(bf16[4,2,96,384]{3,2,1,0:T(8,128)(2,1)} %get-tuple-element.105) | copy-start | bytes 1769476
  152.9 102.4 %copy-start.13 = (bf16[384,1536]{1,0:T(8,128)(2,1)S(1)}, bf16[384,1536]{1,0:T(8,128)(2,1)}, u32[]{:S(2)}) copy-start(bf16[384,1536]{1,0:T(8,128)(2,1)} %param.45) | copy-start | bytes 3538948
  364.8 2.6 copy-start.37
  367.1 8.8 %slice-start.4 = ((s8[6291456]{0:T(1024)(128)(4,1)}), s8[4194304]{0:T(1024)(128)(4,1)S(1)}, s32[]{:S(2)}) async-start(s8[6291456]{0:T(1024)(128)(4,1)} %bitcast.200), calls=%async_computation.4 | async-start | bytes 8388608
  367.1 13.3 %slice-start = ((s8[6291456]{0:T(1024)(128)(4,1)}), s8[4194304]{0:T(1024)(128)(4,1)S(1)}, s32[]{:S(2)}) async-start(s8[6291456]{0:T(1024)(128)(4,1)} %bitcast.175), calls=%async_computation | async-start | bytes 8388608
  367.3 8.5 %copy-start.15 = (bf16[48,8,4,384]{3,1,2,0:T(8,128)(2,1)}, bf16[48,8,4,384]{3,1,2,0:T(8,128)(2,1)S(1)}, u32[]{:S(2)}) copy-start(bf16[48,8,4,384]{3,1,2,0:T(8,128)(2,1)S(1)} %copy.95) | copy-start | bytes 3538948
  367.3 8.5 %slice-start.5 = ((s8[6291456]{0:T(1024)(128)(4,1)}), s8[2097152]{0:T(1024)(128)(4,1)S(1)}, s32[]{:S(2)}) async-start(s8[6291456]{0:T(1024)(128)(4,1)} %bitcast.200), calls=%async_computation.5 | async-start | bytes 4194304
  367.3 13.0 %slice-start.1 = ((s8[6291456]{0:T(1024)(128)(4,1)}), s8[2097152]{0:T(1024)(128)(4,1)S(1)}, s32[]{:S(2)}) async-start(s8[6291456]{0:T(1024)(128)(4,1)} %bitcast.175), calls=%async_computation.1 | async-start | bytes 4194304
  375.8 4.5 copy-start.36
  375.9 4.5 copy-start.34
  385.9 87.2 %copy-start.10 = (bf16[48,4,8,384]{3,2,0,1:T(8,128)(2,1)S(1)}, bf16[48,4,8,384]{3,2,0,1:T(8,128)(2,1)}, u32[]{:S(2)}) copy-start(bf16[48,4,8,384]{3,2,0,1:T(8,128)(2,1)} %copy.100) | copy-start | bytes 3538948
  511.2 2.3 copy-start.9
  518.5 99.5 %copy-start.35 = (bf16[2048,192]{1,0:T(8,128)(2,1)S(1)}, bf16[2048,192]{1,0:T(8,128)(2,1)}, u32[]{:S(2)}) copy-start(bf16[2048,192]{1,0:T(8,128)(2,1)} %get-tuple-element.104.refs_0_) | copy-start | bytes 2359300
  618.0 5.3 copy-start.8
  618.0 5.3 copy-start.17
  622.4 2.1 copy-start.12
  622.4 2.1 copy-start.22
  623.3 34.4 %slice-start.2 = ((s8[6291456]{0:T(1024)(128)(4,1)}), s8[4194304]{0:T(1024)(128)(4,1)S(1)}, s32[]{:S(2)}) async-start(s8[6291456]{0:T(1024)(128)(4,1)} %bitcast.198), calls=%async_computation.2 | async-start | bytes 8388608
  625.3 32.4 %slice-start.3 = ((s8[6291456]{0:T(1024)(128)(4,1)}), s8[2097152]{0:T(1024)(128)(4,1)S(1)}, s32[]{:S(2)}) async-start(s8[6291456]{0:T(1024)(128)(4,1)} %bitcast.198), calls=%async_computation.3 | async-start | bytes 4194304
  657.7 7.4 copy-start.2
  657.7 7.4 copy-start.3
  657.7 7.4 copy-start.4
  657.7 7.4 copy-start.5
  665.1 1.5 copy-start.14
  665.1 1.6 copy-start.11
  665.1 1.7 copy-start.16
  666.6 2.2 copy-start.6
  666.6 2.3 copy-start.7
  810.9 3.0 copy-start.27
  810.9 6.1 copy-start.29
  810.9 8.4 %copy-start.21 = (bf16[4,128,384]{2,1,0:T(8,128)(2,1)S(1)}, bf16[4,128,384]{2,1,0:T(8,128)(2,1)}, u32[]{:S(2)}) copy-start(bf16[4,128,384]{2,1,0:T(8,128)(2,1)} %get-tuple-element.152) | copy-start | bytes 1179652
  810.9 10.1 %copy-start.1 = (f32[4,768]{1,0:T(4,128)S(1)}, f32[4,768]{1,0:T(4,128)}, u32[]{:S(2)}) copy-start(f32[4,768]{1,0:T(4,128)} %param.30) | copy-start | bytes 36868
  810.9 9.4 %copy-start.20 = (bf16[4,128,384]{2,1,0:T(8,128)(2,1)S(1)}, bf16[4,128,384]{2,1,0:T(8,128)(2,1)}, u32[]{:S(2)}) copy-start(bf16[4,128,384]{2,1,0:T(8,128)(2,1)} %get-tuple-element.151) | copy-start | bytes 1179652

commit v6 on v5

--- a/solution.py
+++ b/solution.py
@@ -1140,7 +1140,7 @@
     outs[1][at, :] = (0.5 * p * (1.0 + jnp.tanh(0.7978845608028654 * (p + 0.044715 * (p * p * p))))).astype(BF)
 
 
-def finish_kernel(zx, mix, qkv, o, ff, rest, x_g, z_g, q_g, k_g, v_g, mix_g, o_g, up_g, down_g, bcdt_g, small, gain):
+def finish_kernel(zx, mix, qkv, o, ff, rest, x_g, z_g, q_g, k_g, v_g, mix_g, o_g, up_g, down_g, bcdt_g, gain2, gain3, cxw, cxb, gate, cbw, cbb, a_log, d_skip, dt_bias, gain1, gain):
     i = pl.program_id(0)
     rows, part = zx.shape[2], ff.shape[2] // 2
     for h in range(2):
@@ -1170,25 +1170,60 @@
             o_g[o_at] += o[0, h].astype(F32)
         down_g[h * part:(h + 1) * part] = ff[0, h, :part].astype(F32)
         up_g[h * part:(h + 1) * part] = ff[0, h, part:].astype(F32)
-    wide = bcdt_g.shape[1]
+    state = jnp.concatenate([rest[j, :SMALL].astype(F32) for j in range(NC)], axis=0)
+    bcdt_g[...] = state.T[:bcdt_g.shape[0]]
+
+    rows_new = []
+    gain_new = jnp.zeros((4, rest.shape[2]), F32)
+    for j in range(NC):
+        tail = rest[j, SMALL:].astype(F32)
+        rows_new.append(tail[0:4] + tail[4:8] + tail[8:12])
+        gain_new = gain_new + tail[12:16] + tail[16:20] + tail[20:24]
 
     @pl.when(i == 0)
     def _():
-        gain[...] = jnp.zeros_like(gain)
-    for j in range(NC):
-        slab = rest[j].astype(F32)
-        bcdt_g[j * SMALL:(j + 1) * SMALL] = slab[:SMALL, :wide]
-        tail = slab[SMALL:SMALL + 24]
-        small[j] = tail[0:4] + tail[4:8] + tail[8:12]
-        gain[0:4] += tail[12:16] + tail[16:20] + tail[20:24]
-
-
-def finish(zx, mix, qkv, o, ff, rest, bcdt_width):
+        gain[...] = gain_new
+
+    @pl.when(i > 0)
+    def _():
+        gain[...] += gain_new
+
+    def line(out, at, four):
+        for q in range(4):
+            width = four.shape[1]
+            out[0:1, at + q * width:at + (q + 1) * width] = four[q:q + 1]
+    D = 4 * rest.shape[2]
+    for step in range(NC):
+        @pl.when(i == step)
+        def _():
+            for j in range(NC):
+                n, new = step * NC + j, rows_new[j]
+                if n < 2:
+                    line((gain2, gain3)[n], 0, new)
+                elif n < 10:
+                    for q in range(4):
+                        at = (n % 2) * D + q * new.shape[1]
+                        cxw[(n - 2) // 2:(n - 2) // 2 + 1, at:at + new.shape[1]] = new[q:q + 1]
+                elif n < 14:
+                    line((cxb, gate)[(n - 10) // 2], (n % 2) * D, new)
+                elif n == 14:
+                    cbw[...] = new[:, :2 * STATE]
+                else:
+                    cbb[...] = new[0:1, :2 * STATE]
+                    a_log[...] = new[1:2, :a_log.shape[1]]
+                    d_skip[...] = new[2:3, :d_skip.shape[1]]
+                    dt_bias[...] = new[3:4, :dt_bias.shape[1]]
+            if step == NC - 1:
+                line(gain1, 0, gain[...])
+
+
+def finish(zx, mix, qkv, o, ff, rest, bcdt_width, inner, n_heads):
     thin, feat = rest.shape[2], zx.shape[3]
     D = NC * feat
     lead = lambda a: pl.BlockSpec((1,) + a.shape[1:], lambda i: (i, 0, 0, 0))
     whole = lambda r, w: pl.BlockSpec((r, w), lambda i: (0, 0))
     sds = lambda *s: jax.ShapeDtypeStruct(s, F32)
+    small = [(1, D), (1, D), (CONV, inner), (1, inner), (1, inner), (CONV, 2 * STATE), (1, 2 * STATE)] + [(1, n_heads)] * 3 + [(1, D)]
     rows, half, part = 2 * zx.shape[2], 2 * mix.shape[2], ff.shape[2]
     return pl.pallas_call(
         finish_kernel,
@@ -1197,10 +1232,11 @@
         out_specs=[whole(rows, NC * WIDE)] * 2 + [whole(rows, 2 * WIDE)] * 3 + [
             pl.BlockSpec((half, feat), lambda i: (i, 0)), pl.BlockSpec((half, feat), lambda i: (i // 2, 0)),
             pl.BlockSpec((part, feat), lambda i: (0, i)), pl.BlockSpec((part, feat), lambda i: (i, 0)),
-            pl.BlockSpec((NC * SMALL, bcdt_width), lambda i: (i, 0)), pl.BlockSpec((NC, 4, thin), lambda i: (i, 0, 0)), whole(8, thin)],
+            pl.BlockSpec((bcdt_width, NC * SMALL), lambda i: (0, i)), *[whole(*s) for s in small]],
         out_shape=[sds(rows, NC * WIDE)] * 2 + [sds(rows, 2 * WIDE)] * 3 + [
-            sds(NC * half, feat), sds(2 * half, feat), sds(part, NC * feat), sds(NC * part, feat), sds(D, bcdt_width),
-            sds(rest.shape[0], 4, thin), sds(8, thin)],
+            sds(NC * half, feat), sds(2 * half, feat), sds(part, NC * feat), sds(NC * part, feat), sds(bcdt_width, D),
+            *[sds(*s) for s in small]],
+        scratch_shapes=[pltpu.VMEM((4, thin), F32)],
         compiler_params=pltpu.CompilerParams(vmem_limit_bytes=62 << 20, dimension_semantics=("arbitrary",)),
         cost_estimate=pl.CostEstimate(flops=1 << 20, bytes_accessed=24 << 20, transcendentals=0),
     )(zx, mix, qkv, o, ff, rest)
@@ -1397,17 +1433,19 @@
         post_out=(((T, att), BF),), early=x_kinds(2), early_in=x_arrays(down_pieces, up_pieces))
     ff_sum = jnp.concatenate([added(down_pieces, got[:1]), added(up_pieces, got[1:])], axis=1)
     o_pieces = halved(split_grad(t_dot(attended, g2)))
-    d_qkv, ff_split = att_bwd(8, seq_lens, qkv, d_att, att_exact, lse, ("swap",), (ff_sum,))
+    d_qkv, ff_split, *got = att_bwd(
+        8, seq_lens, qkv, d_att, att_exact, lse, ("swap",) + x_kinds(1), (ff_sum,) + x_arrays(o_pieces))
+    o_sum = added(o_pieces, got)
     qkv_pieces = halved(t_dot(u2, d_qkv).astype(BF).reshape(NC, feat, -1))
-    g1_ext, dh1, gain2_rows, d_mix, ff_back, *got = link(
+    g1_ext, dh1, gain2_rows, d_mix, ff_back, o_split, *got = link(
         4, d_qkv, w_qkv, functools.partial(mid_att_back, inner), (h1, gains[1:2], dh2, mix_out, gate_scale), (one_f32, row8), w1_t=True,
         w2=w_mix, w2_kind="in_t", post=post_plain, post_out=(((T, wide), F32),), extra=128,
-        early=("spread",) + x_kinds(2), early_in=(ff_split,) + x_arrays(o_pieces, qkv_pieces))
-    o_sum, qkv_sum = added(o_pieces, got[:1]), added(qkv_pieces, got[1:])
+        early=("spread", "swap") + x_kinds(1), early_in=(ff_split, o_sum) + x_arrays(qkv_pieces))
+    qkv_sum = added(qkv_pieces, got)
     g1 = g1_ext[:, :D]
     mix_pieces = halved(split_grad(t_dot(mixg, g1)))
-    d_in, tap_grads, row_grads, o_split, qkv_split = mixer_bwd(
-        9, seq_lens, proj, cw, pv, y, states, d_mix, g1_ext, ("swap", "swap"), (o_sum, qkv_sum))
+    d_in, tap_grads, row_grads, qkv_split = mixer_bwd(
+        9, seq_lens, proj, cw, pv, y, states, d_mix, g1_ext, ("swap",), (qkv_sum,))
     in_grad = t_dot(u1, d_in)
     slabs, thin = rows * NC, bcdt_width + bcdt_pad
     four = D // thin
@@ -1423,16 +1461,15 @@
         n = ff_back.shape[1] // 2
         ff_back = jnp.concatenate([four_d(ff_back[:, :n]), four_d(ff_back[:, n:])], axis=2)
         zx_back, mix_back = lax.psum(zx_back, "dp"), lax.psum(mix_back, "dp")
-    (x_grad, z_grad, q_grad, k_grad, v_grad, mix_grad, o_grad, up_grad, down_grad, bcdt_grad, small, gain1) = finish(
-        four_d(zx_back), four_d(mix_back), four_d(qkv_back), four_d(o_back), ff_back, rest_all.reshape(slabs, S, thin), bcdt_width)
-    gain1_grad = gain1[:4].reshape(D)
-    cxw_sum = small[2:10].reshape(CONV, inner)
-    cxb_sum, gate_gain_sum = small[10:12].reshape(-1), small[12:14].reshape(-1)
-    cbw_sum, cbb_sum = small[14, :, :2 * STATE], small[15, 0, :2 * STATE]
-    a_log_sum, d_skip_sum, dt_bias_sum = small[15, 1, :n_heads], small[15, 2, :n_heads], small[15, 3, :n_heads]
+    (x_grad, z_grad, q_grad, k_grad, v_grad, mix_grad, o_grad, up_grad, down_grad, bcdt_grad, gain2_sum, gain3_sum, cxw_sum, *lines) = finish(
+        four_d(zx_back), four_d(mix_back), four_d(qkv_back), four_d(o_back), ff_back, rest_all.reshape(slabs, S, thin), bcdt_width,
+        inner, n_heads)
+    cxb_sum, gate_gain_sum, cbw_sum, cbb_sum, a_log_sum, d_skip_sum, dt_bias_sum, gain1_grad = lines
+    bcdt_grad = bcdt_grad.T
     input_grad = in_got.reshape(NC * S, feat).astype(F32)
-    return (output, input_grad, gain1_grad, z_grad, x_grad, bcdt_grad, cxw_sum, cxb_sum, cbw_sum, cbb_sum, a_log_sum, d_skip_sum,
-            dt_bias_sum, gate_gain_sum, mix_grad, small[0].reshape(D), q_grad, k_grad, v_grad, o_grad, small[1].reshape(D), up_grad, down_grad)
+    return (output, input_grad, gain1_grad[0], z_grad, x_grad, bcdt_grad, cxw_sum, cxb_sum[0], cbw_sum, cbb_sum[0], a_log_sum[0],
+            d_skip_sum[0], dt_bias_sum[0], gate_gain_sum[0], mix_grad, gain2_sum[0], q_grad, k_grad, v_grad, o_grad, gain3_sum[0],
+            up_grad, down_grad)
 
 
 def solution(mesh):

time: 830 us -> 824 us (level)
  local copies, waits for them, and re-layouts: 40.3 us -> 31.9 us
where the time goes in v6:
time: 824 us; the launch traced here: 816 us
  Pallas kernels  727 us (88%)
  matrix products  39 us (5%)
  local copies, waits for them, and re-layouts  31.9 us (4%)
  other arithmetic  14.9 us (2%)
    pallas_call x6, Pallas kernels, link_call(): pl.pallas_call(kernel, out_shape=[jax.ShapeDtypeStruct(s, d) for s, d in...  608 us
    pallas_call x4, Pallas kernels, ridden_call(): pl.pallas_call(ridden(kernel, len(ins), len(outs), tuple(kinds)), grid=(g...  108 us
    dot_general x6, matrix products, t_dot(): lax.dot_general(a, b, (((0,), (0,)), ((), ())), preferred_element_type=F32)  30.6 us

profile of v6, /device:TPU:0, one launch (start us, length us, event | category | flops | bytes accessed | tf_op | source)
XLA Modules:
  0.0 815.7 jit_solution(1059914398274586572)
XLA Ops:
  0.7 0.8 dynamic_slice.50
  1.6 0.8 dynamic_slice.49
  2.4 0.7 dynamic_slice.51
  3.1 0.7 exponential_negate_fusion
  3.9 0.6 concatenate.28.refs_7_.refs_4_
  4.5 1.3 fusion.18
  7.2 1.9 multiply_convert_fusion
  9.1 1.4 copy.62
  10.5 0.3 copy.63
  11.0 1.5 copy.64
  12.4 0.2 copy.86
  12.6 0.8 pad.26.clone
  13.5 0.6 broadcast_in_dim.37.refs_5_
  14.1 102.7 %shard_map.407 = (bf16[8192,384]{1,0:T(8,128)(2,1)}, bf16[2048,1536]{1,0:T(8,128)(2,1)}, bf16[128,1536]{1,0:T(8,128)(2,1)}, bf16[4,2,192,384]{3,2,1,0:T(8,128)(2...) custom-call(bf16[512,384]{1,0:T(8,128)(2,1)} %refs_0_.1, ...), custom_call_target="tpu_custom_call" | custom-call | flops 1048576 | bytes 100663296 | tf_op jit(solution)/shard_map/pallas_call | solution.py:813
  116.8 1.2 constant_dynamic-slice_fusion.2
  117.9 0.8 pad.28.refs_5_
  118.8 0.8 dynamic_slice.48
  119.7 0.7 maximum_maximum_fusion.refs_6_.refs_3_
  120.4 0.8 slice_bitcast_fusion
  121.2 0.6 fusion.17
  121.8 0.2 copy.66
  122.0 0.2 copy.67
  122.3 0.2 copy.68
  122.6 1.3 copy.69
  123.9 27.6 %shard_map.408 = (bf16[2048,1536]{1,0:T(8,128)(2,1)}, f32[2048,768]{1,0:T(8,128)}, bf16[2048,192]{1,0:T(8,128)(2,1)}, bf16[2048,128]{1,0:T(8,128)(2,1)}, f32[204...) custom-call(s32[2]{0:T(128)} %bitcast.186, bf16[4,4,512,384]{3,2,1,0:T(8,128)(2,1)} %bitcast.190, ...), custom_call_target="tpu_custom_call" | custom-call | flops 8589934592 | bytes 25165824 | tf_op jit(solution)/shard_map/pallas_call | solution.py:206
  151.5 0.5 copy.70
  152.0 0.9 copy.91
  152.9 102.4 %shard_map.409 = (bf16[2048,1536]{1,0:T(8,128)(2,1)}, f32[128,1536]{1,0:T(8,128)}, f32[128,1536]{1,0:T(8,128)}, f32[128,128]{1,0:T(8,128)}, bf16[2048,576]{1,0:T...) custom-call(bf16[2048,192]{1,0:T(8,128)(2,1)} %get-tuple-element.113.refs_, ...), custom_call_target="tpu_custom_call" | custom-call | flops 8589934592 | bytes 100663296 | tf_op jit(solution)/shard_map/pallas_call | solution.py:813
  255.3 1.1 copy.99
  256.4 19.1 %shard_map.410 = (bf16[2048,192]{1,0:T(8,128)(2,1)}, f32[2048,192]{1,0:T(8,128)}, f32[2048,128]{1,0:T(8,128)}, bf16[4,192,384]{2,1,0:T(8,128)(2,1)}, bf16[4,2,96,384]{3,2,1,0:T(8,128)(2,1)}) custom-call(s32[2]{0:T(128)} %bitcast.187, bf16[2048,576]{1,0:T(8,128)(2,1)} %get-tuple-element.118.refs_1_, bf16[4,2,192,384]{3,2,1,0:T(8,128)(2,1)} %bitcast.155, ...), custom_call_target="tpu_custom_call" | custom-call | flops 8589934592 | bytes 25165824 | tf_op jit(solution)/shard_map/pallas_call | solution.py:206
  275.6 1.5 copy.72
  277.1 0.9 copy.92
  278.0 86.6 %shard_map.411 = (bf16[2048,1536]{1,0:T(8,128)(2,1)}, f32[128,1536]{1,0:T(8,128)}, f32[2048,384]{1,0:T(8,128)}, bf16[2048,384]{1,0:T(8,128)(2,1)}, bf16[4,2,192,...) custom-call(bf16[2048,192]{1,0:T(8,128)(2,1)} %get-tuple-element.121.refs_0_, bf16[192,1536]{1,0:T(8,128)(2,1)} %bitcast.165, ...), custom_call_target="tpu_custom_call" | custom-call | flops 8589934592 | bytes 100663296 | tf_op jit(solution)/shard_map/pallas_call | solution.py:813
  364.6 2.3 copy.73
  367.2 8.5 %fusion.8.refs_0_ = bf16[2048,384]{1,0:T(8,128)(2,1)S(1)} fusion(f32[2048,384]{1,0:T(8,128)S(1)} %copy-done.37, bf16[2048,1536]{1,0:T(8,128)(2,1)} %get-tuple-element.119, bf16[384,1536]{1,0:T(8,128)(2,1)S(1)} %bitcast.152), kind=kOutput, calls=%fused_computation.10 | convolution fusion | flops 2431647744 | bytes 12189696 | tf_op jit(solution)/shard_map/dot_general | solution.py:1313
  375.7 4.5 convolution_convert_fusion.1
  380.2 2.6 convolution_convert_fusion.2
  382.9 1.1 copy.98
  384.0 1.8 constant_dynamic-slice_fusion.refs_4_
  385.8 87.2 %shard_map.412 = (bf16[2048,1536]{1,0:T(8,128)(2,1)}, f32[128,1536]{1,0:T(8,128)}, f32[8,1536]{1,0:T(8,128)}, bf16[2048,192]{1,0:T(8,128)(2,1)}, bf16[4,192,384]...) custom-call(bf16[2048,384]{1,0:T(8,128)(2,1)} %copy-done.36, bf16[1536,384]{1,0:T(8,128)(2,1)} %bitcast.201, ...), custom_call_target="tpu_custom_call" | custom-call | flops 8589934592 | bytes 100663296 | tf_op jit(solution)/shard_map/pallas_call | solution.py:813
  473.1 4.4 convolution_convert_fusion.3
  477.4 0.9 copy.101
  478.3 1.4 fusion.13
  479.7 1.1 pad_maximum_fusion.2.refs_5_
  480.9 27.9 %shard_map.413 = (bf16[2048,576]{1,0:T(8,128)(2,1)}, bf16[4,384,384]{2,1,0:T(8,128)(2,1)}, bf16[4,96,384]{2,1,0:T(8,128)(2,1)}) custom-call(s32[2]{0:T(128)} %bitcast.188, bf16[2048,576]{1,0:T(8,128)(2,1)} %get-tuple-element.118.refs_1_, bf16[2048,192]{1,0:T(8,128)(2,1)} %get-tuple-element.132.refs_2_, f32[2048,192]{1,0:T(8,128)} %get-tuple-element.133.refs_3_, ...), custom_call_target="tpu_custom_call" | custom-call | flops 8589934592 | bytes 25165824 | tf_op jit(solution)/shard_map/pallas_call | solution.py:206
  508.8 7.4 convolution_convert_fusion
  516.2 2.3 copy.79
  518.5 0.8 fusion.15.refs_9_
  519.3 98.4 %shard_map.414 = (bf16[2048,1664]{1,0:T(8,128)(2,1)}, f32[128,1536]{1,0:T(8,128)}, f32[8,1536]{1,0:T(8,128)}, f32[2048,192]{1,0:T(8,128)}, bf16[4,2,384,384]{3,2...) custom-call(bf16[2048,576]{1,0:T(8,128)(2,1)} %get-tuple-element.138.refs_0_, ...), custom_call_target="tpu_custom_call" | custom-call | flops 8589934592 | bytes 100663296 | tf_op jit(solution)/shard_map/pallas_call | solution.py:813
  617.8 4.3 fusion.9
  622.1 0.9 copy.100
  623.0 1.2 fusion.12.refs_9_
  624.2 33.2 %shard_map.415 = (bf16[2048,768]{1,0:T(8,128)(2,1)}, f32[8,448]{1,0:T(8,128)}, f32[8,256]{1,0:T(8,128)}, bf16[4,192,576]{2,1,0:T(8,128)(2,1)}) custom-call(s32[2]{0:T(128)} %bitcast.189, f32[2048,768]{1,0:T(8,128)} %get-tuple-element.110.refs_1_.refs_2_, f32[2048,768]{1,0:T(8,128)} %get-tuple-element.110.refs_1_.refs_2_, ...), custom_call_target="tpu_custom_call" | custom-call | flops 12884901888 | bytes 25165824 | tf_op jit(solution)/shard_map/pallas_call | solution.py:206
  657.5 7.3 fusion.19.in_grad
  664.9 1.5 shard_map.416
  666.6 1.9 pad_maximum_fusion.refs_1_
  668.7 0.7 broadcast_in_dim.46.refs_9_
  669.5 130.8 %shard_map.417 = (bf16[2048,384]{1,0:T(8,128)(2,1)}, bf16[4,128,384]{2,1,0:T(8,128)(2,1)}, f32[8,1536]{1,0:T(8,128)}, bf16[4,128,384]{2,1,0:T(8,128)(2,1)}, bf16...) custom-call(bf16[2048,768]{1,0:T(8,128)(2,1)} %get-tuple-element.149, ...), custom_call_target="tpu_custom_call" | custom-call | flops 8589934592 | bytes 100663296 | tf_op jit(solution)/shard_map/pallas_call | solution.py:813
  800.2 9.6 %shard_map.418 = (f32[384,768]{1,0:T(8,128)}, f32[384,768]{1,0:T(8,128)}, f32[384,384]{1,0:T(8,128)}, f32[384,384]{1,0:T(8,128)}, f32[384,384]{1,0:T(8,128)}, /*...) custom-call(bf16[4,2,192,384]{3,2,1,0:T(8,128)(2,1)} %get-tuple-elem, ...), custom_call_target="tpu_custom_call" | custom-call | flops 1048576 | bytes 25165824 | tf_op jit(solution)/shard_map/pallas_call | solution.py:1228
  809.9 1.3 reduce
  811.2 1.3 reduce.1
  812.5 1.3 reduce.2
  813.8 1.0 bitcast_convert_fusion
  814.8 0.7 copy.103
  (113 shorter events, 1.5 us)
Async XLA Ops:
  0.7 118.1 %copy-start = (f32[4,768]{1,0:T(4,128)S(1)}, f32[4,768]{1,0:T(4,128)}, u32[]{:S(2)}) copy-start(f32[4,768]{1,0:T(4,128)} %param.30) | copy-start | bytes 36868
  0.7 9.8 %copy-start.18 = (bf16[384,768]{1,0:T(8,128)(2,1)S(1)}, bf16[384,768]{1,0:T(8,128)(2,1)}, u32[]{:S(2)}) copy-start(bf16[384,768]{1,0:T(8,128)(2,1)} %param.27) | copy-start | bytes 1769476
  10.8 1.6 copy-start.28
  10.8 2.6 copy-start.30
  10.8 2.6 copy-start.31
  10.8 2.6 copy-start.32
  13.4 106.2 %copy-start.33 = (f32[256]{0:T(256)S(1)}, f32[256]{0:T(256)}, u32[]{:S(2)}) copy-start(f32[256]{0:T(256)} %param.33) | copy-start | bytes 3076
  13.4 106.3 %copy-start.29 = (f32[4,256]{1,0:T(4,128)S(1)}, f32[4,256]{1,0:T(4,128)}, u32[]{:S(2)}) copy-start(f32[4,256]{1,0:T(4,128)} %param.32) | copy-start | bytes 12292
  13.4 108.4 %copy-start.25 = (bf16[384,384]{1,0:T(8,128)(2,1)S(1)}, bf16[384,384]{1,0:T(8,128)(2,1)}, u32[]{:S(2)}) copy-start(bf16[384,384]{1,0:T(8,128)(2,1)} %param.40) | copy-start | bytes 884740
  14.1 107.9 %copy-start.26 = (bf16[384,384]{1,0:T(8,128)(2,1)S(1)}, bf16[384,384]{1,0:T(8,128)(2,1)}, u32[]{:S(2)}) copy-start(bf16[384,384]{1,0:T(8,128)(2,1)} %param.41) | copy-start | bytes 884740
  14.1 108.2 %copy-start.27 = (bf16[384,384]{1,0:T(8,128)(2,1)S(1)}, bf16[384,384]{1,0:T(8,128)(2,1)}, u32[]{:S(2)}) copy-start(bf16[384,384]{1,0:T(8,128)(2,1)} %param.42) | copy-start | bytes 884740
  123.9 27.6 %copy-start.19 = (bf16[4,2,96,384]{3,2,1,0:T(8,128)(2,1)S(1)}, bf16[4,2,96,384]{3,2,1,0:T(8,128)(2,1)}, u32[]{:S(2)}) copy-start(bf16[4,2,96,384]{3,2,1,0:T(8,128)(2,1)} %get-tuple-element.114) | copy-start | bytes 1769476
  152.9 102.4 %copy-start.13 = (bf16[384,1536]{1,0:T(8,128)(2,1)S(1)}, bf16[384,1536]{1,0:T(8,128)(2,1)}, u32[]{:S(2)}) copy-start(bf16[384,1536]{1,0:T(8,128)(2,1)} %param.45) | copy-start | bytes 3538948
  364.6 2.6 copy-start.37
  366.9 8.8 %slice-start.4 = ((s8[6291456]{0:T(1024)(128)(4,1)}), s8[4194304]{0:T(1024)(128)(4,1)S(1)}, s32[]{:S(2)}) async-start(s8[6291456]{0:T(1024)(128)(4,1)} %bitcast.204), calls=%async_computation.4 | async-start | bytes 8388608
  367.0 13.3 %slice-start = ((s8[6291456]{0:T(1024)(128)(4,1)}), s8[4194304]{0:T(1024)(128)(4,1)S(1)}, s32[]{:S(2)}) async-start(s8[6291456]{0:T(1024)(128)(4,1)} %bitcast.173), calls=%async_computation | async-start | bytes 8388608
  367.2 8.5 %copy-start.15 = (bf16[48,8,4,384]{3,1,2,0:T(8,128)(2,1)}, bf16[48,8,4,384]{3,1,2,0:T(8,128)(2,1)S(1)}, u32[]{:S(2)}) copy-start(bf16[48,8,4,384]{3,1,2,0:T(8,128)(2,1)S(1)} %copy.93) | copy-start | bytes 3538948
  367.2 8.5 %slice-start.5 = ((s8[6291456]{0:T(1024)(128)(4,1)}), s8[2097152]{0:T(1024)(128)(4,1)S(1)}, s32[]{:S(2)}) async-start(s8[6291456]{0:T(1024)(128)(4,1)} %bitcast.204), calls=%async_computation.5 | async-start | bytes 4194304
  367.2 13.0 %slice-start.1 = ((s8[6291456]{0:T(1024)(128)(4,1)}), s8[2097152]{0:T(1024)(128)(4,1)S(1)}, s32[]{:S(2)}) async-start(s8[6291456]{0:T(1024)(128)(4,1)} %bitcast.173), calls=%async_computation.1 | async-start | bytes 4194304
  375.7 4.5 copy-start.36
  375.7 4.5 copy-start.34
  385.8 87.2 %copy-start.9 = (bf16[2048,192]{1,0:T(8,128)(2,1)S(1)}, bf16[2048,192]{1,0:T(8,128)(2,1)}, u32[]{:S(2)}) copy-start(bf16[2048,192]{1,0:T(8,128)(2,1)} %get-tuple-element.121.refs_0_) | copy-start | bytes 2359300
  473.0 5.3 copy-start.10
  473.0 5.3 copy-start.20
  473.0 5.3 copy-start.21
  516.2 2.3 copy-start.12
  516.2 2.3 copy-start.24
  519.3 98.5 %copy-start.35 = (bf16[2048,192]{1,0:T(8,128)(2,1)S(1)}, bf16[2048,192]{1,0:T(8,128)(2,1)}, u32[]{:S(2)}) copy-start(bf16[2048,192]{1,0:T(8,128)(2,1)} %get-tuple-element.113.refs_0_) | copy-start | bytes 2359300
  617.7 5.3 copy-start.8
  617.8 5.3 copy-start.17
  622.1 35.3 %slice-start.2 = ((s8[6291456]{0:T(1024)(128)(4,1)}), s8[4194304]{0:T(1024)(128)(4,1)S(1)}, s32[]{:S(2)}) async-start(s8[6291456]{0:T(1024)(128)(4,1)} %bitcast.202), calls=%async_computation.2 | async-start | bytes 8388608
  624.2 33.2 %slice-start.3 = ((s8[6291456]{0:T(1024)(128)(4,1)}), s8[2097152]{0:T(1024)(128)(4,1)S(1)}, s32[]{:S(2)}) async-start(s8[6291456]{0:T(1024)(128)(4,1)} %bitcast.202), calls=%async_computation.3 | async-start | bytes 4194304
  657.5 7.4 copy-start.2
  657.5 7.4 copy-start.3
  657.5 7.4 copy-start.4
  657.5 7.4 copy-start.5
  664.9 1.5 copy-start.14
  664.9 1.6 copy-start.11
  664.9 1.7 copy-start.16
  666.4 2.2 copy-start.6
  666.4 2.3 copy-start.7
  800.2 13.6 %copy-start.23 = (bf16[4,128,384]{2,1,0:T(8,128)(2,1)S(1)}, bf16[4,128,384]{2,1,0:T(8,128)(2,1)}, u32[]{:S(2)}) copy-start(bf16[4,128,384]{2,1,0:T(8,128)(2,1)} %get-tuple-element.161) | copy-start | bytes 1179652
  800.2 14.6 %copy-start.22 = (bf16[4,128,384]{2,1,0:T(8,128)(2,1)S(1)}, bf16[4,128,384]{2,1,0:T(8,128)(2,1)}, u32[]{:S(2)}) copy-start(bf16[4,128,384]{2,1,0:T(8,128)(2,1)} %get-tuple-element.160) | copy-start | bytes 1179652
  800.2 15.3 %copy-start.1 = (f32[4,768]{1,0:T(4,128)S(1)}, f32[4,768]{1,0:T(4,128)}, u32[]{:S(2)}) copy-start(f32[4,768]{1,0:T(4,128)} %param.30) | copy-start | bytes 36868
